TPU v7x, 32 devices: a whole 2x2x4 slice. The times are simulated.
32 devices in a mesh: lon: 4 (over z), lat: 4 (over x, core), band: 2 (over y).
Axes of the slice: x: 2, y: 2, z: 4, core: 2. Of those that a mesh axis runs over, the one named last changes fastest.
Arguments:
- spectrum: float32 [64, 64, 576], P('lat', 'lon', 'band'), may hold values from 0.02 to 13, as said below
- sea_mask: int32 [64, 64], P('lat', 'lon'), may hold values 0 or 1
- ice_mask: int32 [64, 64], P('lat', 'lon'), may hold values 0 or 1
- depth_class: int32 [64, 64], P('lat', 'lon'), may hold values from 0 to 7
- speed_table: float32 [8, 16], replicated, may hold values from 0.2 to 0.8
- refraction_table: float32 [8, 16], replicated, may hold values from 0.05 to 0.5
- depth_slope: float32 [2, 64, 64], P(None, 'lat', 'lon'), may hold values from -1 to 1
- wind_speed: float32 [64, 64], P('lat', 'lon'), may hold values from 0.3 to 3
- wind_dir: float32 [64, 64], P('lat', 'lon'), may hold values from -3.140625 to 3.140625
- ice_rate: float32 [16], replicated, may hold values from 0.1 to 1
Outputs:
- spectrum_out: float32 [64, 64, 576], P('lat', 'lon', 'band')
Inputs may be any that keep to these rules, and one draw needn't show every extreme that they name: `spectrum`: densities are positive.
All inputs are finite; a program needn't handle non-finite values. No bound on the sum of `sea_mask` or of `ice_mask` on one device may be relied on, other than what follows from the above.
Results may differ from a plain program's by a relative error of at most 0.0003.
Values sent between devices are 32-bit elements; how exact they have to be, the bound alone decides.
No kernel may reach another device: no remote copies, remote signals or barrier semaphores. Data moves between devices by JAX's collectives and lax.ppermute only.
A program may use at most 64 MiB of HBM per device.

v0:
```python
import math

import jax
import jax.numpy as jnp
from jax import lax
from jax.sharding import PartitionSpec as P

NDIR = 36
ITERS = 4
NCOMP = 576


freq_ratio = 1.1
wind_gain = 0.12
break_coef = 0.05
south_edge = -30.0
band_span = 60.0


def with_halo(cells, sides, width, closed):
    for axis, dim in sides:
        count = lax.axis_size(axis)
        ends = count if closed else count - 1
        head = lax.slice_in_dim(cells, 0, width, axis=dim)
        tail = lax.slice_in_dim(cells, cells.shape[dim] - width, cells.shape[dim], axis=dim)
        cells = jnp.concatenate(
            [
                lax.ppermute(tail, axis, [(i, (i + 1) % count) for i in range(ends)]),
                cells,
                lax.ppermute(head, axis, [((i + 1) % count, i) for i in range(ends)]),
            ],
            axis=dim,
        )
    return cells


def quickest(behind, center, forward, beyond, courant):
    curvature = jnp.where(
        courant >= 0.0, forward - 2.0 * center + behind, beyond - 2.0 * forward + center
    )
    face_value = (
        0.5 * (center + forward)
        - 0.5 * courant * (forward - center)
        - (1.0 - courant * courant) / 6.0 * curvature
    )
    return courant * face_value


def advect(density, cell_speed, axis_dim):
    length = density.shape[axis_dim]

    def piece(array, low, high):
        return lax.slice_in_dim(array, low, high, axis=axis_dim)

    courant = 0.5 * (piece(cell_speed, 1, length - 2) + piece(cell_speed, 2, length - 1))
    fluxes = quickest(
        piece(density, 0, length - 3),
        piece(density, 1, length - 2),
        piece(density, 2, length - 1),
        piece(density, 3, length),
        courant,
    )
    faces = fluxes.shape[axis_dim]
    return piece(density, 2, length - 2) - (piece(fluxes, 1, faces) - piece(fluxes, 0, faces - 1))


def rotate(density, offset):
    dir_index = jnp.arange(density.shape[-1]) % NDIR
    target = dir_index + offset
    inner_roll = jnp.roll(density, -offset, axis=-1)
    if offset > 0:
        outer_roll = jnp.roll(density, NDIR - offset, axis=-1)
        return jnp.where(target >= NDIR, outer_roll, inner_roll)
    outer_roll = jnp.roll(density, -(offset + NDIR), axis=-1)
    return jnp.where(target < 0, outer_roll, inner_roll)


def refract(density, courant):
    fluxes = quickest(rotate(density, -1), density, rotate(density, 1), rotate(density, 2), courant)
    return density - (fluxes - rotate(fluxes, -1))


def expand(per_freq, spread):
    return jnp.dot(per_freq, spread, precision=lax.Precision.HIGHEST)


def lookup(classes, lookup_table):
    onehot = (classes[..., None] == jnp.arange(lookup_table.shape[0])).astype(jnp.float32)
    return jnp.dot(onehot, lookup_table, precision=lax.Precision.HIGHEST)


def stretch(rows, total_rows):
    latitude = (south_edge + band_span * (rows.astype(jnp.float32) + 0.5) / total_rows) * (
        math.pi / 180.0
    )
    return 1.0 / jnp.cos(latitude)


def sources(
    density,
    energy_sum,
    moment,
    levels,
    heading,
    ice_loss,
    sea_share,
    ice_share,
    wind_speed,
    wind_dir,
):
    mean_level = jnp.maximum(moment, 1.0) / jnp.maximum(energy_sum, 1.0)
    energy = energy_sum / NCOMP
    breaking = break_coef * levels * levels / mean_level[..., None] * (energy * energy)[..., None]
    growth = (
        wind_gain
        * wind_speed[..., None]
        * levels
        * jnp.maximum(jnp.cos(heading - wind_dir[..., None]), 0.0)
    )
    damping = ice_share[..., None] * ice_loss
    return sea_share[..., None] * density * jnp.exp(growth - breaking - damping)


def edge_cols(stacked):
    return with_halo(stacked, (("lon", 1),), 2, True)


def edge_rows(stacked):
    return with_halo(stacked, (("lat", 0),), 2, False)


def per_device(
    spectrum,
    sea_mask,
    ice_mask,
    depth_class,
    speed_table,
    refraction_table,
    depth_slope,
    wind_speed,
    wind_dir,
    ice_rate,
):
    rows_dev, cols_dev, comps_dev = spectrum.shape
    freqs_dev = comps_dev // NDIR
    band_index = lax.axis_index("band")
    first_comp = band_index * comps_dev
    local_comp = jnp.arange(comps_dev)
    comp_index = first_comp + local_comp
    spread = (local_comp[None, :] // NDIR == jnp.arange(freqs_dev)[:, None]).astype(jnp.float32)
    heading = 2.0 * math.pi * (comp_index % NDIR).astype(jnp.float32) / NDIR
    face_angle = heading + math.pi / NDIR
    cos_head = jnp.cos(heading)
    sin_head = jnp.sin(heading)
    sin_face = jnp.sin(face_angle)
    cos_face = jnp.cos(face_angle)
    ice_loss_all = jnp.repeat(ice_rate, NDIR)
    sea_share = sea_mask.astype(jnp.float32)
    ice_share = ice_mask.astype(jnp.float32)
    speed_local = lax.dynamic_slice_in_dim(speed_table, band_index * freqs_dev, freqs_dev, 1)
    refr_local = lax.dynamic_slice_in_dim(refraction_table, band_index * freqs_dev, freqs_dev, 1)
    group_speed = lookup(depth_class, speed_local) * sea_share[..., None]
    turning = lookup(depth_class, refr_local) * sea_share[..., None]
    turn_x = turning * depth_slope[0][..., None]
    turn_y = turning * depth_slope[1][..., None]
    total_rows = rows_dev * lax.axis_size("lat")
    first_row = lax.axis_index("lat") * rows_dev
    density = spectrum * sea_share[..., None]
    stretch_rows = stretch(first_row + jnp.arange(rows_dev), total_rows)
    along_t = expand(turn_x, spread) * sin_face - expand(turn_y, spread) * cos_face
    for substep in range(ITERS):
        if substep == 0:
            wide_rims = edge_cols(jnp.concatenate([density, group_speed], axis=-1))
            along_x = (
                expand(wide_rims[..., comps_dev:], spread) * cos_head * stretch_rows[:, None, None]
            )
        else:
            wide_rims = edge_cols(density)
        density = advect(wide_rims[..., :comps_dev], along_x, 1)
        if substep == 0:
            tall_rims = edge_rows(jnp.concatenate([density, group_speed], axis=-1))
            along_y = expand(tall_rims[..., comps_dev:], spread) * sin_head
        else:
            tall_rims = edge_rows(density)
        density = advect(tall_rims[..., :comps_dev], along_y, 0)
        density = refract(density, along_t)
    points = lax.all_to_all(density, "band", split_axis=1, concat_axis=2, tiled=True)
    half_cols = points.shape[1]
    first_col = band_index * half_cols

    def slice_cols(array):
        return lax.dynamic_slice_in_dim(array, first_col, half_cols, 1)

    all_comp = jnp.arange(NCOMP)
    heading_all = 2.0 * math.pi * (all_comp % NDIR).astype(jnp.float32) / NDIR
    levels_all = jnp.exp(math.log(freq_ratio) * (all_comp // NDIR).astype(jnp.float32))
    energy_sum = jnp.sum(points, axis=-1)
    moment = jnp.sum(points * levels_all, axis=-1)
    result = sources(
        points,
        energy_sum,
        moment,
        levels_all,
        heading_all,
        ice_loss_all,
        slice_cols(sea_share),
        slice_cols(ice_share),
        slice_cols(wind_speed),
        slice_cols(wind_dir),
    )
    return lax.all_to_all(result, "band", split_axis=2, concat_axis=1, tiled=True)


def solution(mesh):
    return jax.shard_map(
        per_device,
        mesh=mesh,
        in_specs=(
            P("lat", "lon", "band"),
            P("lat", "lon"),
            P("lat", "lon"),
            P("lat", "lon"),
            P(),
            P(),
            P(None, "lat", "lon"),
            P("lat", "lon"),
            P("lat", "lon"),
            P(),
        ),
        out_specs=P("lat", "lon", "band"),
        check_vma=False,
    )
```

profile of v0, /device:TPU:0, one launch (start us, length us, event | category | flops | bytes accessed | tf_op | source)
XLA Modules:
  0.0 99.9 jit_solution(6769597955886237830)
XLA Ops:
  0.7 1.1 %broadcast_multiply_fusion = f32[16,16,288]{2,1,0:T(8,128)S(1)} fusion(f32[16,16,288]{2,1,0:T(8,128)} %param.10, f32[16,16]{1,0:T(8,128)S(1)} %convert_element_type.54), kind=kLoop, calls=%fused_computation.197 | loop fusion | flops 73728 | bytes 590848 | tf_op jit(solution)/shard_map/mul | solution.py:168
  1.8 1.0 convolution_multiply_fusion.5
  3.0 3.1 %collective-permute-start = (f32[16,2,296]{2,0,1:T(8,128)S(1)}, f32[16,2,296]{2,0,1:T(8,128)S(1)}, u32[]{:S(2)}, u32[]{:S(2)}) collective-permute-start(f32[16,2,296]{2,0,1:T(8,128)S(1)} %copy.421), channel_id=1, source_target_pairs={{0,8},{8,16},{16,24},{24,0},{1,9},{9,17},{17,25},{25,1},{2,10},{10... | collective-permute-start | bytes 113672 | tf_op jit(solution)/shard_map/ppermute | solution.py:28
  6.0 2.1 %collective-permute-start.1 = (f32[16,2,296]{2,0,1:T(8,128)S(1)}, f32[16,2,296]{2,0,1:T(8,128)S(1)}, u32[]{:S(2)}, u32[]{:S(2)}) collective-permute-start(f32[16,2,296]{2,0,1:T(8,128)S(1)} %copy.422), channel_id=1, source_target_pairs={{8,0},{16,8},{24,16},{0,24},{9,1},{17,9},{25,17},{1,25},{10,2},{18... | collective-permute-start | bytes 113672 | tf_op jit(solution)/shard_map/ppermute | solution.py:30
  8.3 1.0 %convolution_multiply_fusion.4 = f32[16,16,8]{2,1,0:T(8,128)S(1)} fusion(f32[16,16]{1,0:T(8,128)S(1)} %convert_element_type.54, s32[16,16]{1,0:T(8,128)} %param.13, f32[8,16]{1,0:T(8,128)} %param.15, s32[]{:T(128)S(6)} %select_n.223), kind=kOutput, calls=%fused_computation.6 | convolution fusion | flops 202752 | bytes 10756 | tf_op jit(solution)/shard_map/dot_general | solution.py:89
  12.5 1.3 %collective-permute-start.2 = (f32[2,16,296]{2,1,0:T(8,128)S(1)}, f32[2,16,296]{2,1,0:T(8,128)S(1)}, u32[]{:S(2)}, u32[]{:S(2)}) collective-permute-start(f32[2,16,296]{2,1,0:T(8,128)S(1)} %get-tuple-element.13), channel_id=1, source_target_pairs={{0,2},{2,4},{4,6},{1,3},{3,5},{5,7},{8,10},{10,12},{12,14},{9,11},... | collective-permute-start | bytes 113672 | tf_op jit(solution)/shard_map/ppermute | solution.py:28
  13.9 1.3 %collective-permute-start.3 = (f32[2,16,296]{2,1,0:T(8,128)S(1)}, f32[2,16,296]{2,1,0:T(8,128)S(1)}, u32[]{:S(2)}, u32[]{:S(2)}) collective-permute-start(f32[2,16,296]{2,1,0:T(8,128)S(1)} %get-tuple-element.14), channel_id=1, source_target_pairs={{2,0},{4,2},{6,4},{3,1},{5,3},{7,5},{10,8},{12,10},{14,12},{11,9},... | collective-permute-start | bytes 113672 | tf_op jit(solution)/shard_map/ppermute | solution.py:30
  15.2 3.5 %collective-permute-done.3 = f32[2,16,296]{2,1,0:T(8,128)S(1)} collective-permute-done((f32[2,16,296]{2,1,0:T(8,128)S(1)}, f32[2,16,296]{2,1,0:T(8,128)S(1)}, u32[]{:S(2)}, u32[]{:S(2)}) %collective-permute-start.3) | collective-permute-done | bytes 37920 | tf_op jit(solution)/shard_map/ppermute | solution.py:30
  21.9 1.1 %collective-permute-start.4 = (f32[16,2,288]{2,0,1:T(8,128)S(1)}, f32[16,2,288]{2,0,1:T(8,128)S(1)}, u32[]{:S(2)}, u32[]{:S(2)}) collective-permute-start(f32[16,2,288]{2,0,1:T(8,128)S(1)} %copy.434), channel_id=1, source_target_pairs={{0,8},{8,16},{16,24},{24,0},{1,9},{9,17},{17,25},{25,1},{2,10},{10... | collective-permute-start | bytes 110600 | tf_op jit(solution)/shard_map/ppermute | solution.py:28
  22.9 2.8 %collective-permute-start.5 = (f32[16,2,288]{2,0,1:T(8,128)S(1)}, f32[16,2,288]{2,0,1:T(8,128)S(1)}, u32[]{:S(2)}, u32[]{:S(2)}) collective-permute-start(f32[16,2,288]{2,0,1:T(8,128)S(1)} %copy.436), channel_id=1, source_target_pairs={{8,0},{16,8},{24,16},{0,24},{9,1},{17,9},{25,17},{1,25},{10,2},{18... | collective-permute-start | bytes 110600 | tf_op jit(solution)/shard_map/ppermute | solution.py:30
  25.8 2.1 %collective-permute-done.4 = f32[16,2,288]{2,0,1:T(8,128)S(1)} collective-permute-done((f32[16,2,288]{2,0,1:T(8,128)S(1)}, f32[16,2,288]{2,0,1:T(8,128)S(1)}, u32[]{:S(2)}, u32[]{:S(2)}) %collective-permute-start.4) | collective-permute-done | bytes 36896 | tf_op jit(solution)/shard_map/ppermute | solution.py:28
  28.6 4.0 %collective-permute-start.6 = (f32[2,16,288]{2,1,0:T(8,128)S(1)}, f32[2,16,288]{2,1,0:T(8,128)S(1)}, u32[]{:S(2)}, u32[]{:S(2)}) collective-permute-start(f32[2,16,288]{2,1,0:T(8,128)S(1)} %get-tuple-element.51), channel_id=1, source_target_pairs={{0,2},{2,4},{4,6},{1,3},{3,5},{5,7},{8,10},{10,12},{12,14},{9,11},... | collective-permute-start | bytes 110600 | tf_op jit(solution)/shard_map/ppermute | solution.py:28
  32.6 1.3 %collective-permute-start.7 = (f32[2,16,288]{2,1,0:T(8,128)S(1)}, f32[2,16,288]{2,1,0:T(8,128)S(1)}, u32[]{:S(2)}, u32[]{:S(2)}) collective-permute-start(f32[2,16,288]{2,1,0:T(8,128)S(1)} %get-tuple-element.52), channel_id=1, source_target_pairs={{2,0},{4,2},{6,4},{3,1},{5,3},{7,5},{10,8},{12,10},{14,12},{11,9},... | collective-permute-start | bytes 110600 | tf_op jit(solution)/shard_map/ppermute | solution.py:30
  33.9 2.0 %collective-permute-done.7 = f32[2,16,288]{2,1,0:T(8,128)S(1)} collective-permute-done((f32[2,16,288]{2,1,0:T(8,128)S(1)}, f32[2,16,288]{2,1,0:T(8,128)S(1)}, u32[]{:S(2)}, u32[]{:S(2)}) %collective-permute-start.7) | collective-permute-done | bytes 36896 | tf_op jit(solution)/shard_map/ppermute | solution.py:30
  38.3 1.1 %collective-permute-start.8 = (f32[16,2,288]{2,0,1:T(8,128)S(1)}, f32[16,2,288]{2,0,1:T(8,128)S(1)}, u32[]{:S(2)}, u32[]{:S(2)}) collective-permute-start(f32[16,2,288]{2,0,1:T(8,128)S(1)} %copy.438), channel_id=1, source_target_pairs={{0,8},{8,16},{16,24},{24,0},{1,9},{9,17},{17,25},{25,1},{2,10},{10... | collective-permute-start | bytes 110600 | tf_op jit(solution)/shard_map/ppermute | solution.py:28
  39.3 2.8 %collective-permute-start.9 = (f32[16,2,288]{2,0,1:T(8,128)S(1)}, f32[16,2,288]{2,0,1:T(8,128)S(1)}, u32[]{:S(2)}, u32[]{:S(2)}) collective-permute-start(f32[16,2,288]{2,0,1:T(8,128)S(1)} %copy.440), channel_id=1, source_target_pairs={{8,0},{16,8},{24,16},{0,24},{9,1},{17,9},{25,17},{1,25},{10,2},{18... | collective-permute-start | bytes 110600 | tf_op jit(solution)/shard_map/ppermute | solution.py:30
  42.2 2.0 %collective-permute-done.8 = f32[16,2,288]{2,0,1:T(8,128)S(1)} collective-permute-done((f32[16,2,288]{2,0,1:T(8,128)S(1)}, f32[16,2,288]{2,0,1:T(8,128)S(1)}, u32[]{:S(2)}, u32[]{:S(2)}) %collective-permute-start.8) | collective-permute-done | bytes 36896 | tf_op jit(solution)/shard_map/ppermute | solution.py:28
  45.0 4.3 %collective-permute-start.10 = (f32[2,16,288]{2,1,0:T(8,128)S(1)}, f32[2,16,288]{2,1,0:T(8,128)S(1)}, u32[]{:S(2)}, u32[]{:S(2)}) collective-permute-start(f32[2,16,288]{2,1,0:T(8,128)S(1)} %get-tuple-element.39), channel_id=1, source_target_pairs={{0,2},{2,4},{4,6},{1,3},{3,5},{5,7},{8,10},{10,12},{12,14},{9,11},... | collective-permute-start | bytes 110600 | tf_op jit(solution)/shard_map/ppermute | solution.py:28
  49.3 1.3 %collective-permute-start.11 = (f32[2,16,288]{2,1,0:T(8,128)S(1)}, f32[2,16,288]{2,1,0:T(8,128)S(1)}, u32[]{:S(2)}, u32[]{:S(2)}) collective-permute-start(f32[2,16,288]{2,1,0:T(8,128)S(1)} %get-tuple-element.40), channel_id=1, source_target_pairs={{2,0},{4,2},{6,4},{3,1},{5,3},{7,5},{10,8},{12,10},{14,12},{11,9},... | collective-permute-start | bytes 110600 | tf_op jit(solution)/shard_map/ppermute | solution.py:30
  50.6 1.8 %collective-permute-done.11 = f32[2,16,288]{2,1,0:T(8,128)S(1)} collective-permute-done((f32[2,16,288]{2,1,0:T(8,128)S(1)}, f32[2,16,288]{2,1,0:T(8,128)S(1)}, u32[]{:S(2)}, u32[]{:S(2)}) %collective-permute-start.11) | collective-permute-done | bytes 36896 | tf_op jit(solution)/shard_map/ppermute | solution.py:30
  54.8 0.9 collective-permute-start.12
  55.7 3.0 %collective-permute-start.13 = (f32[16,2,288]{2,0,1:T(8,128)S(1)}, f32[16,2,288]{2,0,1:T(8,128)S(1)}, u32[]{:S(2)}, u32[]{:S(2)}) collective-permute-start(f32[16,2,288]{2,0,1:T(8,128)S(1)} %copy.444), channel_id=1, source_target_pairs={{8,0},{16,8},{24,16},{0,24},{9,1},{17,9},{25,17},{1,25},{10,2},{18... | collective-permute-start | bytes 110600 | tf_op jit(solution)/shard_map/ppermute | solution.py:30
  58.8 1.9 %collective-permute-done.12 = f32[16,2,288]{2,0,1:T(8,128)S(1)} collective-permute-done((f32[16,2,288]{2,0,1:T(8,128)S(1)}, f32[16,2,288]{2,0,1:T(8,128)S(1)}, u32[]{:S(2)}, u32[]{:S(2)}) %collective-permute-start.12) | collective-permute-done | bytes 36896 | tf_op jit(solution)/shard_map/ppermute | solution.py:28
  61.5 4.2 %collective-permute-start.14 = (f32[2,16,288]{2,1,0:T(8,128)S(1)}, f32[2,16,288]{2,1,0:T(8,128)S(1)}, u32[]{:S(2)}, u32[]{:S(2)}) collective-permute-start(f32[2,16,288]{2,1,0:T(8,128)S(1)} %get-tuple-element.27), channel_id=1, source_target_pairs={{0,2},{2,4},{4,6},{1,3},{3,5},{5,7},{8,10},{10,12},{12,14},{9,11},... | collective-permute-start | bytes 110600 | tf_op jit(solution)/shard_map/ppermute | solution.py:28
  65.7 1.3 %collective-permute-start.15 = (f32[2,16,288]{2,1,0:T(8,128)S(1)}, f32[2,16,288]{2,1,0:T(8,128)S(1)}, u32[]{:S(2)}, u32[]{:S(2)}) collective-permute-start(f32[2,16,288]{2,1,0:T(8,128)S(1)} %get-tuple-element.28), channel_id=1, source_target_pairs={{2,0},{4,2},{6,4},{3,1},{5,3},{7,5},{10,8},{12,10},{14,12},{11,9},... | collective-permute-start | bytes 110600 | tf_op jit(solution)/shard_map/ppermute | solution.py:30
  67.0 1.8 %collective-permute-done.15 = f32[2,16,288]{2,1,0:T(8,128)S(1)} collective-permute-done((f32[2,16,288]{2,1,0:T(8,128)S(1)}, f32[2,16,288]{2,1,0:T(8,128)S(1)}, u32[]{:S(2)}, u32[]{:S(2)}) %collective-permute-start.15) | collective-permute-done | bytes 36896 | tf_op jit(solution)/shard_map/ppermute | solution.py:30
  72.1 3.5 %all-to-all-start = ((f32[16,16,288]{2,0,1:T(8,128)}), f32[16,16,288]{2,0,1:T(8,128)S(1)}, u32[]{:S(2)}, u32[]{:S(2)}) async-start(f32[16,16,288]{2,0,1:T(8,128)} %copy.446), calls=%async_computation | async-start | bytes 786432 | tf_op jit(solution)/shard_map/all_to_all | solution.py:187
  75.8 6.0 %all-to-all-done = f32[16,16,288]{2,0,1:T(8,128)S(1)} async-done(((f32[16,16,288]{2,0,1:T(8,128)}), f32[16,16,288]{2,0,1:T(8,128)S(1)}, u32[]{:S(2)}, u32[]{:S(2)}) %all-to-all-start) | async-done | bytes 294944 | tf_op jit(solution)/shard_map/all_to_all | solution.py:187
  82.6 1.3 %fusion.108 = f32[16,8,576]{2,1,0:T(8,128)S(1)} fusion(f32[16,8,576]{2,1,0:T(8,128)S(1)} %all_to_all.29, f32[576]{0:T(1024)S(1)} %mul.613, f32[16,8]{1,0:T(8,128)S(1)} %dynamic-slice_convert_fusion, f32[16,8]{1,0:T(8,128)S(1)} %get-tuple-element.66, f32[16,8]{1,0:T(8,128)S(1)} %get-tuple-element.65, f32[576]{0:T(1024)S(1)} %get-tuple-element.75, ...), kind=kLoop, calls=%fused_computation.190 | loop fusion | flops 811008 | bytes 602112 | tf_op jit(solution)/shard_map/mul | solution.py:121
  85.7 8.8 %all_to_all.36 = f32[2,1,36864]{2,1,0:T(1,128)S(1)} all-to-all(f32[2,1,36864]{2,1,0:T(1,128)S(1)} %reshape.114), channel_id=1, replica_groups=mesh['lon'=4,'lat'=4,'band'=2] {'band'}, dimensions={0} | all-to-all | bytes 589824 | tf_op jit(solution)/shard_map/all_to_all | solution.py:211
  95.1 1.6 %reduce.2 = f32[2,36864]{1,0:T(2,128)S(1)} reduce(f32[2,1,36864]{2,1,0:T(1,128)S(1)} %all_to_all.36, f32[]{:T(128)} %broadcast.442), dimensions={1}, to_apply=%all_to_all.30.reduce_sub_computation | reduce | bytes 589828 | tf_op jit(solution)/shard_map/all_to_all | solution.py:211
  97.5 1.7 %copy.458 = f32[16,8,2,288]{3,2,1,0:T(2,128)S(1)} copy(f32[16,8,2,288]{0,1,3,2:T(8,128)S(1)} %bitcast.40) | data formatting | bytes 589824 | tf_op jit(solution)/shard_map/all_to_all | solution.py:211
  (145 shorter events, 22.1 us)
Async XLA Ops:
  0.0 1.8 %copy-start = (f32[8,16]{1,0:T(8,128)S(1)}, f32[8,16]{1,0:T(8,128)}, u32[]{:S(2)}) copy-start(f32[8,16]{1,0:T(8,128)} %param.14) | copy-start | bytes 1540
  3.0 7.5 %collective-permute-start = (f32[16,2,296]{2,0,1:T(8,128)S(1)}, f32[16,2,296]{2,0,1:T(8,128)S(1)}, u32[]{:S(2)}, u32[]{:S(2)}) collective-permute-start(f32[16,2,296]{2,0,1:T(8,128)S(1)} %copy.421), channel_id=1, source_target_pairs={{0,8},{8,16},{16,24},{24,0},{1,9},{9,17},{17,25},{25,1},{2,10},{10... | collective-permute-start | bytes 113672 | tf_op jit(solution)/shard_map/ppermute | solution.py:28
  6.0 4.6 %collective-permute-start.1 = (f32[16,2,296]{2,0,1:T(8,128)S(1)}, f32[16,2,296]{2,0,1:T(8,128)S(1)}, u32[]{:S(2)}, u32[]{:S(2)}) collective-permute-start(f32[16,2,296]{2,0,1:T(8,128)S(1)} %copy.422), channel_id=1, source_target_pairs={{8,0},{16,8},{24,16},{0,24},{9,1},{17,9},{25,17},{1,25},{10,2},{18... | collective-permute-start | bytes 113672 | tf_op jit(solution)/shard_map/ppermute | solution.py:30
  11.3 1.0 copy-start.1
  12.5 2.7 %collective-permute-start.2 = (f32[2,16,296]{2,1,0:T(8,128)S(1)}, f32[2,16,296]{2,1,0:T(8,128)S(1)}, u32[]{:S(2)}, u32[]{:S(2)}) collective-permute-start(f32[2,16,296]{2,1,0:T(8,128)S(1)} %get-tuple-element.13), channel_id=1, source_target_pairs={{0,2},{2,4},{4,6},{1,3},{3,5},{5,7},{8,10},{10,12},{12,14},{9,11},... | collective-permute-start | bytes 113672 | tf_op jit(solution)/shard_map/ppermute | solution.py:28
  13.9 4.8 %collective-permute-start.3 = (f32[2,16,296]{2,1,0:T(8,128)S(1)}, f32[2,16,296]{2,1,0:T(8,128)S(1)}, u32[]{:S(2)}, u32[]{:S(2)}) collective-permute-start(f32[2,16,296]{2,1,0:T(8,128)S(1)} %get-tuple-element.14), channel_id=1, source_target_pairs={{2,0},{4,2},{6,4},{3,1},{5,3},{7,5},{10,8},{12,10},{14,12},{11,9},... | collective-permute-start | bytes 113672 | tf_op jit(solution)/shard_map/ppermute | solution.py:30
  21.9 6.0 %collective-permute-start.4 = (f32[16,2,288]{2,0,1:T(8,128)S(1)}, f32[16,2,288]{2,0,1:T(8,128)S(1)}, u32[]{:S(2)}, u32[]{:S(2)}) collective-permute-start(f32[16,2,288]{2,0,1:T(8,128)S(1)} %copy.434), channel_id=1, source_target_pairs={{0,8},{8,16},{16,24},{24,0},{1,9},{9,17},{17,25},{25,1},{2,10},{10... | collective-permute-start | bytes 110600 | tf_op jit(solution)/shard_map/ppermute | solution.py:28
  22.9 4.9 %collective-permute-start.5 = (f32[16,2,288]{2,0,1:T(8,128)S(1)}, f32[16,2,288]{2,0,1:T(8,128)S(1)}, u32[]{:S(2)}, u32[]{:S(2)}) collective-permute-start(f32[16,2,288]{2,0,1:T(8,128)S(1)} %copy.436), channel_id=1, source_target_pairs={{8,0},{16,8},{24,16},{0,24},{9,1},{17,9},{25,17},{1,25},{10,2},{18... | collective-permute-start | bytes 110600 | tf_op jit(solution)/shard_map/ppermute | solution.py:30
  28.6 5.3 %collective-permute-start.6 = (f32[2,16,288]{2,1,0:T(8,128)S(1)}, f32[2,16,288]{2,1,0:T(8,128)S(1)}, u32[]{:S(2)}, u32[]{:S(2)}) collective-permute-start(f32[2,16,288]{2,1,0:T(8,128)S(1)} %get-tuple-element.51), channel_id=1, source_target_pairs={{0,2},{2,4},{4,6},{1,3},{3,5},{5,7},{8,10},{10,12},{12,14},{9,11},... | collective-permute-start | bytes 110600 | tf_op jit(solution)/shard_map/ppermute | solution.py:28
  32.6 3.3 %collective-permute-start.7 = (f32[2,16,288]{2,1,0:T(8,128)S(1)}, f32[2,16,288]{2,1,0:T(8,128)S(1)}, u32[]{:S(2)}, u32[]{:S(2)}) collective-permute-start(f32[2,16,288]{2,1,0:T(8,128)S(1)} %get-tuple-element.52), channel_id=1, source_target_pairs={{2,0},{4,2},{6,4},{3,1},{5,3},{7,5},{10,8},{12,10},{14,12},{11,9},... | collective-permute-start | bytes 110600 | tf_op jit(solution)/shard_map/ppermute | solution.py:30
  38.3 5.9 %collective-permute-start.8 = (f32[16,2,288]{2,0,1:T(8,128)S(1)}, f32[16,2,288]{2,0,1:T(8,128)S(1)}, u32[]{:S(2)}, u32[]{:S(2)}) collective-permute-start(f32[16,2,288]{2,0,1:T(8,128)S(1)} %copy.438), channel_id=1, source_target_pairs={{0,8},{8,16},{16,24},{24,0},{1,9},{9,17},{17,25},{25,1},{2,10},{10... | collective-permute-start | bytes 110600 | tf_op jit(solution)/shard_map/ppermute | solution.py:28
  39.3 4.9 %collective-permute-start.9 = (f32[16,2,288]{2,0,1:T(8,128)S(1)}, f32[16,2,288]{2,0,1:T(8,128)S(1)}, u32[]{:S(2)}, u32[]{:S(2)}) collective-permute-start(f32[16,2,288]{2,0,1:T(8,128)S(1)} %copy.440), channel_id=1, source_target_pairs={{8,0},{16,8},{24,16},{0,24},{9,1},{17,9},{25,17},{1,25},{10,2},{18... | collective-permute-start | bytes 110600 | tf_op jit(solution)/shard_map/ppermute | solution.py:30
  45.0 5.7 %collective-permute-start.10 = (f32[2,16,288]{2,1,0:T(8,128)S(1)}, f32[2,16,288]{2,1,0:T(8,128)S(1)}, u32[]{:S(2)}, u32[]{:S(2)}) collective-permute-start(f32[2,16,288]{2,1,0:T(8,128)S(1)} %get-tuple-element.39), channel_id=1, source_target_pairs={{0,2},{2,4},{4,6},{1,3},{3,5},{5,7},{8,10},{10,12},{12,14},{9,11},... | collective-permute-start | bytes 110600 | tf_op jit(solution)/shard_map/ppermute | solution.py:28
  49.3 3.1 %collective-permute-start.11 = (f32[2,16,288]{2,1,0:T(8,128)S(1)}, f32[2,16,288]{2,1,0:T(8,128)S(1)}, u32[]{:S(2)}, u32[]{:S(2)}) collective-permute-start(f32[2,16,288]{2,1,0:T(8,128)S(1)} %get-tuple-element.40), channel_id=1, source_target_pairs={{2,0},{4,2},{6,4},{3,1},{5,3},{7,5},{10,8},{12,10},{14,12},{11,9},... | collective-permute-start | bytes 110600 | tf_op jit(solution)/shard_map/ppermute | solution.py:30
  54.2 4.5 %copy-start.2 = (s32[16,16]{1,0:T(8,128)S(1)}, s32[16,16]{1,0:T(8,128)}, u32[]{:S(2)}) copy-start(s32[16,16]{1,0:T(8,128)} %param.12) | copy-start | bytes 3076
  54.8 5.9 %collective-permute-start.12 = (f32[16,2,288]{2,0,1:T(8,128)S(1)}, f32[16,2,288]{2,0,1:T(8,128)S(1)}, u32[]{:S(2)}, u32[]{:S(2)}) collective-permute-start(f32[16,2,288]{2,0,1:T(8,128)S(1)} %copy.442), channel_id=1, source_target_pairs={{0,8},{8,16},{16,24},{24,0},{1,9},{9,17},{17,25},{25,1},{2,10},{10... | collective-permute-start | bytes 110600 | tf_op jit(solution)/shard_map/ppermute | solution.py:28
  55.7 5.0 %collective-permute-start.13 = (f32[16,2,288]{2,0,1:T(8,128)S(1)}, f32[16,2,288]{2,0,1:T(8,128)S(1)}, u32[]{:S(2)}, u32[]{:S(2)}) collective-permute-start(f32[16,2,288]{2,0,1:T(8,128)S(1)} %copy.444), channel_id=1, source_target_pairs={{8,0},{16,8},{24,16},{0,24},{9,1},{17,9},{25,17},{1,25},{10,2},{18... | collective-permute-start | bytes 110600 | tf_op jit(solution)/shard_map/ppermute | solution.py:30
  61.5 5.5 %collective-permute-start.14 = (f32[2,16,288]{2,1,0:T(8,128)S(1)}, f32[2,16,288]{2,1,0:T(8,128)S(1)}, u32[]{:S(2)}, u32[]{:S(2)}) collective-permute-start(f32[2,16,288]{2,1,0:T(8,128)S(1)} %get-tuple-element.27), channel_id=1, source_target_pairs={{0,2},{2,4},{4,6},{1,3},{3,5},{5,7},{8,10},{10,12},{12,14},{9,11},... | collective-permute-start | bytes 110600 | tf_op jit(solution)/shard_map/ppermute | solution.py:28
  65.7 3.1 %collective-permute-start.15 = (f32[2,16,288]{2,1,0:T(8,128)S(1)}, f32[2,16,288]{2,1,0:T(8,128)S(1)}, u32[]{:S(2)}, u32[]{:S(2)}) collective-permute-start(f32[2,16,288]{2,1,0:T(8,128)S(1)} %get-tuple-element.28), channel_id=1, source_target_pairs={{2,0},{4,2},{6,4},{3,1},{5,3},{7,5},{10,8},{12,10},{14,12},{11,9},... | collective-permute-start | bytes 110600 | tf_op jit(solution)/shard_map/ppermute | solution.py:30
  70.7 4.9 %copy-start.5 = (f32[16]{0:T(128)S(1)}, f32[16]{0:T(128)}, u32[]{:S(2)}) copy-start(f32[16]{0:T(128)} %param.19) | copy-start | bytes 196
  70.7 5.1 %copy-start.3 = (f32[16,16]{1,0:T(8,128)S(1)}, f32[16,16]{1,0:T(8,128)}, u32[]{:S(2)}) copy-start(f32[16,16]{1,0:T(8,128)} %param.17) | copy-start | bytes 3076
  70.7 5.1 %copy-start.4 = (f32[16,16]{1,0:T(8,128)S(1)}, f32[16,16]{1,0:T(8,128)}, u32[]{:S(2)}) copy-start(f32[16,16]{1,0:T(8,128)} %param.18) | copy-start | bytes 3076
  72.1 9.7 %all-to-all-start = ((f32[16,16,288]{2,0,1:T(8,128)}), f32[16,16,288]{2,0,1:T(8,128)S(1)}, u32[]{:S(2)}, u32[]{:S(2)}) async-start(f32[16,16,288]{2,0,1:T(8,128)} %copy.446), calls=%async_computation | async-start | bytes 786432 | tf_op jit(solution)/shard_map/all_to_all | solution.py:187
where the time goes:
time: 101 us; the launch traced here: 99.9 us
  starting transfers between devices  39.4 us (39%)
  waiting for transfers between devices  21.2 us (21%)
  local copies, waits for them, and re-layouts  12.8 us (13%)
  other arithmetic  12.7 us (13%)
  blocking collectives  8.82 us (9%)
  matrix products  4.06 us (4%)
    ppermute x8, starting transfers between devices, with_halo(): lax.ppermute(tail, axis, [(i, (i + 1) % count) for i in range(ends)])  20.1 us
    ppermute x8, starting transfers between devices, with_halo(): lax.ppermute(head, axis, [((i + 1) % count, i) for i in range(ends)])  15.9 us
    ppermute x8, waiting for transfers between devices, with_halo(): lax.ppermute(head, axis, [((i + 1) % count, i) for i in range(ends)])  9.2 us
    all_to_all x1, blocking collectives, per_device(): lax.all_to_all(result, 'band', split_axis=2, concat_axis=1, tiled=True)  8.82 us
    ppermute x8, waiting for transfers between devices, with_halo(): lax.ppermute(tail, axis, [(i, (i + 1) % count) for i in range(ends)])  5.99 us
    all_to_all x1, waiting for transfers between devices, per_device(): lax.all_to_all(density, 'band', split_axis=1, concat_axis=2, tiled=True)  5.98 us
    mul x11, other arithmetic, quickest(): return courant * face_value  5.36 us
    all_to_all x1, starting transfers between devices, per_device(): lax.all_to_all(density, 'band', split_axis=1, concat_axis=2, tiled=True)  3.47 us
  transfers between devices with their start and end apart: 17, of which 9 were waited for; matrix products, arithmetic and copies ran while one was open for 3% of the time, Pallas kernels for 0%

commit v1 on v0

v1 whole, which is shorter than its diff:
```python
import math

import jax
import jax.numpy as jnp
import numpy as np
from jax import lax
from jax.experimental import pallas as pl
from jax.experimental.pallas import tpu as pltpu
from jax.sharding import PartitionSpec as P

NDIR = 36
NCOMP = 576
ITERS = 4
NCLASS = 8
FREQ = 8
HALO = 8
STATIC = NDIR
SLABS = NDIR + 1
SEA, DEPTH, SLOPE_X, SLOPE_Y, ICE, WIND, WDIR = range(7)

freq_ratio = 1.1
wind_gain = 0.12
break_coef = 0.05
south_edge = -30.0
band_span = 60.0

COS = [math.cos(2.0 * math.pi * d / NDIR) for d in range(NDIR)]
SIN = [math.sin(2.0 * math.pi * d / NDIR) for d in range(NDIR)]
COS_FACE = [math.cos(2.0 * math.pi * (d + 0.5) / NDIR) for d in range(NDIR)]
SIN_FACE = [math.sin(2.0 * math.pi * (d + 0.5) / NDIR) for d in range(NDIR)]

TAB_SPEED, TAB_TURN, STRETCH, LIVE, ICE_RATE, LEVEL = 0, 8, 16, 17, 18, 19

f32 = jnp.float32


def lanes():
    return lax.broadcasted_iota(jnp.int32, (8, 128), 1)


def roll(x, shift):
    shift = shift % 128
    return pltpu.roll(x, shift, 1) if shift else x


def pack_kernel(spec, sea, ice, depth, slope, wspeed, wdir, own, to_east, to_west, flat0, flat1, wide):
    grid = spec[...].reshape(256, NDIR * FREQ)
    for low, high in ((0, 128), (128, 256), (256, 288)):
        turned = grid[:, low:high].T
        flat0[low:high, :] = turned[:, :128]
        flat1[low:high, :] = turned[:, 128:]
    wide[...] = jnp.zeros_like(wide)
    group = lax.broadcasted_iota(jnp.int32, (16, 128), 1) // 16
    row = lax.broadcasted_iota(jnp.int32, (16, 128), 0) % 8
    own[STATIC] = jnp.zeros((2, 8, 128), f32)

    def place(field, values):
        wide[:, :16] = values
        moved = pltpu.roll(wide[...], 0, 1, stride=16, stride_axis=0)
        kept = jnp.where(group == row, moved, 0.0)
        for half in range(2):
            own[STATIC, half, field : field + 1, :] = jnp.sum(
                kept[8 * half : 8 * half + 8], axis=0, keepdims=True
            )

    place(SEA, sea[...].astype(f32))
    place(DEPTH, depth[...].astype(f32))
    place(SLOPE_X, slope[0])
    place(SLOPE_Y, slope[1])
    place(ICE, ice[...].astype(f32))
    place(WIND, wspeed[...])
    place(WDIR, wdir[...])
    inner = lanes() % 16
    sea0 = own[STATIC, 0, SEA : SEA + 1, :]
    sea1 = own[STATIC, 1, SEA : SEA + 1, :]
    for slab in range(SLABS):
        if slab < NDIR:
            own0 = flat0[pl.ds(slab, FREQ, stride=NDIR), :] * sea0
            own1 = flat1[pl.ds(slab, FREQ, stride=NDIR), :] * sea1
            own[slab, 0] = own0
            own[slab, 1] = own1
        else:
            own0 = own[slab, 0]
            own1 = own[slab, 1]
        to_east[slab] = jnp.where(inner >= 8, own0, roll(own1, -8))
        to_west[slab] = jnp.where(inner < 8, own0, roll(own1, 8))


def growth_kernel(own, consts, gain):
    for half in range(2):
        point = own[STATIC, half]
        turn = point[WDIR : WDIR + 1]
        cos_w = jnp.cos(turn)
        sin_w = jnp.sin(turn)
        force = wind_gain * point[WIND : WIND + 1] * consts[LEVEL]
        share = point[SEA : SEA + 1]
        for d in range(NDIR):
            along = jnp.maximum(COS[d] * cos_w + SIN[d] * sin_w, 0.0)
            gain[d, half] = jnp.exp(force * along) * share


def join_kernel(own, from_west, from_east, rows):
    inner = lanes() % 16
    even = (lanes() // 16) % 2 == 0

    def body(slab, carry):
        west = from_west[slab]
        east = from_east[slab]
        rim0 = jnp.where(inner < 8, roll(east, 16), roll(west, -16))
        rim1 = jnp.where(inner < 8, roll(east, 8), roll(west, -8))
        own0 = own[slab, 0]
        own1 = own[slab, 1]
        rows[0, slab, 0] = jnp.where(even, own0, rim0)
        rows[0, slab, 1] = jnp.where(even, rim0, own0)
        rows[1, slab, 0] = jnp.where(even, own1, rim1)
        rows[1, slab, 1] = jnp.where(even, rim1, own1)
        return carry

    lax.fori_loop(0, SLABS, body, 0, unroll=True)


def flux(q, diff, curve, k):
    return k * (q + (0.5 - 0.5 * k) * (diff - (1.0 / 3.0 + (1.0 / 3.0) * k) * curve))


def sweep_lon(tiles, kx, cos_d, positive):
    out = []
    for q, face in zip(tiles, kx):
        k = cos_d * face
        diff = roll(q, -1) - q
        if positive:
            curve = diff - roll(diff, 1)
        else:
            curve = roll(diff, -1) - diff
        f = flux(q, diff, curve, k)
        out.append(q - f + roll(f, 1))
    return out


def sweep_lat(tiles, ky, sin_d, positive, live):
    ahead = tiles[1:] + [roll(tiles[0], -32)]
    diff = [n - m for n, m in zip(ahead, tiles)]
    if positive:
        before = [roll(diff[7], 32)] + diff[:7]
        curve = [a - b for a, b in zip(diff, before)]
    else:
        after = diff[1:] + [roll(diff[0], -32)]
        curve = [a - b for a, b in zip(after, diff)]
    fluxes = [flux(q, a, b, sin_d * face) for q, a, b, face in zip(tiles, diff, curve, ky)]
    behind = [roll(fluxes[7], 32)] + fluxes[:7]
    return [(q - f + b) * live for q, f, b in zip(tiles, fluxes, behind)]


def sweep_dir(cells, tx, ty):
    courant = [SIN_FACE[d] * tx - COS_FACE[d] * ty for d in range(NDIR)]
    first = cells[0]
    diff = [None] * NDIR
    for d in range(NDIR):
        diff[d] = cells[(d + 1) % NDIR] - cells[d]
    curve = [diff[d] - diff[d - 1] for d in range(NDIR)]
    fluxes = []
    for d in range(NDIR):
        k = courant[d]
        bend = jnp.where(k >= 0.0, curve[d], curve[(d + 1) % NDIR])
        fluxes.append(flux(cells[d], diff[d], bend, k))
    return [cells[d] - fluxes[d] + fluxes[d - 1] for d in range(NDIR)]


def march_kernel(rows, from_south, from_north, consts, own, sums, q, kx, ky, tx, ty, trig):
    lane = lanes()

    def assemble(slab, carry):
        for p in range(2):
            parts = [
                from_south[slab, p],
                roll(rows[0, slab, p], 32),
                roll(rows[1, slab, p], 64),
                roll(from_north[slab, p], 96),
            ]
            for t in range(p, 8, 2):
                which = ((lane - (16 * t - 8)) % 128) // 32
                mixed = jnp.where(
                    which < 2,
                    jnp.where(which == 0, parts[0], parts[1]),
                    jnp.where(which == 2, parts[2], parts[3]),
                )
                q[slab, t] = roll(mixed, 8 - 16 * t)
        return carry

    lax.fori_loop(0, SLABS, assemble, 0, unroll=2)

    for d in range(NDIR):
        trig[0, d] = jnp.float32(COS[d])
        trig[1, d] = jnp.float32(SIN[d])

    speed = []
    for t in range(8):
        point = q[STATIC, t]
        depth = jnp.broadcast_to(point[DEPTH : DEPTH + 1], (8, 128))
        share = point[SEA : SEA + 1]
        pace = jnp.zeros((8, 128), f32)
        turning = jnp.zeros((8, 128), f32)
        for c in range(NCLASS):
            hit = depth == float(c)
            pace = jnp.where(hit, consts[TAB_SPEED + c], pace)
            turning = jnp.where(hit, consts[TAB_TURN + c], turning)
        pace = pace * share
        turning = turning * share
        speed.append(pace)
        kx[t] = 0.5 * (pace + roll(pace, -1)) * consts[STRETCH, t : t + 1, :]
        tx[t] = turning * point[SLOPE_X : SLOPE_X + 1]
        ty[t] = turning * point[SLOPE_Y : SLOPE_Y + 1]
    for t in range(8):
        ahead = speed[t + 1] if t < 7 else roll(speed[0], -32)
        ky[t] = 0.5 * (speed[t] + ahead)

    live = consts[LIVE]

    def substep(step, carry):
        for quadrant in range(4):
            east = quadrant in (0, 3)
            north = quadrant in (0, 1)

            def one(i, c, quadrant=quadrant, east=east, north=north):
                d = quadrant * 9 + i
                tiles = [q[d, t] for t in range(8)]
                tiles = sweep_lon(tiles, [kx[t] for t in range(8)], trig[0, d], east)
                tiles = sweep_lat(tiles, [ky[t] for t in range(8)], trig[1, d], north, live)
                for t in range(8):
                    q[d, t] = tiles[t]
                return c

            lax.fori_loop(0, 9, one, 0, unroll=3)

        def turn(t, c):
            cells = sweep_dir([q[d, t] for d in range(NDIR)], tx[t], ty[t])
            for d in range(NDIR):
                q[d, t] = cells[d]
            return c

        lax.fori_loop(0, 8, turn, 0)
        return carry

    lax.fori_loop(0, ITERS, substep, 0)

    def take(d, carry):
        sum0, sum1 = carry
        half0 = jnp.zeros((8, 128), f32)
        half1 = jnp.zeros((8, 128), f32)
        for t in range(8):
            moved = roll(q[d, t], 16 * t - 40)
            half0 = jnp.where(lane // 16 == t, moved, half0)
            half1 = jnp.where(lane // 16 == (t + 2) % 8, moved, half1)
        half1 = roll(half1, -32)
        own[d, 0] = half0
        own[d, 1] = half1
        return sum0 + half0, sum1 + half1

    zero = jnp.zeros((8, 128), f32)
    totals = lax.fori_loop(0, NDIR, take, (zero, zero), unroll=3)
    level = consts[LEVEL]
    sums[...] = zero
    for half in range(2):
        sums[half : half + 1, :] = jnp.sum(totals[half], axis=0, keepdims=True)
        sums[2 + half : 3 + half, :] = jnp.sum(totals[half] * level, axis=0, keepdims=True)


def finish_kernel(own, gain, static, sums, other, consts, out, flat0, flat1):
    total = sums[...] + other[...]
    for half, flat in ((0, flat0), (1, flat1)):
        energy = total[half : half + 1]
        moment = total[2 + half : 3 + half]
        mean_level = jnp.maximum(moment, 1.0) / jnp.maximum(energy, 1.0)
        mean = energy / NCOMP
        level = consts[LEVEL]
        breaking = break_coef * level * level / mean_level * (mean * mean)
        damping = static[0, half, ICE : ICE + 1] * consts[ICE_RATE]
        loss = jnp.exp(-breaking - damping)
        for d in range(NDIR):
            flat[pl.ds(d, FREQ, stride=NDIR), :] = own[d, half] * gain[d, half] * loss
        for low, high in ((0, 128), (128, 256), (256, 288)):
            turned = flat[low:high, :].T
            out[8 * half : 8 * half + 8, :, low:high] = turned.reshape(8, 16, high - low)


def vmem(count):
    return [pl.BlockSpec(memory_space=pltpu.VMEM)] * count


PARAMS = pltpu.CompilerParams(vmem_limit_bytes=32 * 2**20)


def call(kernel, ins, outs, scratch=(), name=None):
    return pl.pallas_call(
        kernel,
        out_shape=[jax.ShapeDtypeStruct(shape, f32) for shape in outs],
        in_specs=vmem(ins),
        out_specs=vmem(len(outs)),
        scratch_shapes=list(scratch),
        compiler_params=PARAMS,
        name=name,
    )


def shift(array, axis, step, closed):
    count = lax.axis_size(axis)
    pairs = []
    for i in range(count):
        j = i + step
        if closed or 0 <= j < count:
            pairs.append((i, j % count))
    return lax.ppermute(array, axis, pairs)


def per_device(
    spectrum,
    sea_mask,
    ice_mask,
    depth_class,
    speed_table,
    refraction_table,
    depth_slope,
    wind_speed,
    wind_dir,
    ice_rate,
):
    band = lax.axis_index("band")
    lat = lax.axis_index("lat")
    lats = lax.axis_size("lat")
    rows_dev = spectrum.shape[0]

    def spread(table):
        mine = lax.dynamic_slice_in_dim(table, band * FREQ, FREQ, 1)
        return jnp.broadcast_to(mine[:, :, None], (NCLASS, FREQ, 128))

    group = jnp.arange(128) // 32
    row = lat * rows_dev - HALO + 8 * group[None, :] + jnp.arange(8)[:, None]
    latitude = (south_edge + band_span * (row.astype(f32) + 0.5) / (rows_dev * lats)) * (math.pi / 180.0)
    stretch = 1.0 / jnp.cos(latitude)
    live = 1.0 - (((group == 0) & (lat == 0)) | ((group == 3) & (lat == lats - 1))).astype(f32)
    ice = lax.dynamic_slice_in_dim(ice_rate, band * FREQ, FREQ, 0)
    level = jnp.exp(math.log(freq_ratio) * (band * FREQ + jnp.arange(FREQ)).astype(f32))
    consts = jnp.concatenate(
        [
            spread(speed_table),
            spread(refraction_table),
            stretch[None],
            jnp.broadcast_to(live[None, None, :], (1, 8, 128)),
            jnp.broadcast_to(ice[None, :, None], (1, 8, 128)),
            jnp.broadcast_to(level[None, :, None], (1, 8, 128)),
        ]
    )

    tile = (8, 128)
    own, to_east, to_west = call(
        pack_kernel,
        7,
        [(SLABS, 2) + tile, (SLABS,) + tile, (SLABS,) + tile],
        [pltpu.VMEM((NDIR * FREQ, 128), f32)] * 2 + [pltpu.VMEM((16, 128), f32)],
        name="pack",
    )(spectrum, sea_mask, ice_mask, depth_class, depth_slope, wind_speed, wind_dir)
    from_west = shift(to_east, "lon", 1, True)
    from_east = shift(to_west, "lon", -1, True)
    (gain,) = call(growth_kernel, 2, [(NDIR, 2) + tile], name="growth")(own, consts)
    (rows,) = call(join_kernel, 3, [(2, SLABS, 2) + tile], name="join")(own, from_west, from_east)
    from_south = shift(rows[1], "lat", 1, False)
    from_north = shift(rows[0], "lat", -1, False)
    block = pltpu.VMEM((8,) + tile, f32)
    last, sums = call(
        march_kernel,
        4,
        [(NDIR, 2) + tile, tile],
        [pltpu.VMEM((SLABS, 8) + tile, f32), block, block, block, block, pltpu.SMEM((2, NDIR), f32)],
        name="march",
    )(rows, from_south, from_north, consts)
    other = lax.ppermute(sums, "band", [(i, 1 - i) for i in range(2)])
    (out,) = call(
        finish_kernel,
        6,
        [spectrum.shape],
        [pltpu.VMEM((NDIR * FREQ, 128), f32)] * 2,
        name="finish",
    )(last, gain, own[STATIC:], sums, other, consts)
    return out


def solution(mesh):
    return jax.shard_map(
        per_device,
        mesh=mesh,
        in_specs=(
            P("lat", "lon", "band"),
            P("lat", "lon"),
            P("lat", "lon"),
            P("lat", "lon"),
            P(),
            P(),
            P(None, "lat", "lon"),
            P("lat", "lon"),
            P("lat", "lon"),
            P(),
        ),
        out_specs=P("lat", "lon", "band"),
        check_vma=False,
    )
```

time: 101 us -> 58 us (0.57)
  the two profiles are of different devices: /device:TPU:0 before, /device:TPU:1 now
where the time goes in v1:
time: 58 us; the launch traced here: 57.4 us
  Pallas kernels  26.9 us (46%)
  waiting for transfers between devices  11.8 us (20%)
  starting transfers between devices  11.6 us (20%)
  local copies, waits for them, and re-layouts  7.03 us (12%)
    pallas_call x1, Pallas kernels, per_device(): call(march_kernel, 4, [(NDIR, 2) + tile, tile], [pltpu.VMEM((SLABS, 8) +...  25.2 us
    ppermute x4, waiting for transfers between devices, shift(): return lax.ppermute(array, axis, pairs)  10.7 us
    ppermute x4, starting transfers between devices, shift(): return lax.ppermute(array, axis, pairs)  10.3 us
    unnamed x24, local copies, waits for them, and re-layouts  6.77 us
    ppermute x1, starting transfers between devices, per_device(): other = lax.ppermute(sums, 'band', [(i, 1 - i) for i in range(2)])  1.26 us
  transfers between devices with their start and end apart: 5, of which 5 were waited for; matrix products, arithmetic and copies ran while one was open for 1% of the time, Pallas kernels for 0%

profile of v1, /device:TPU:1, one launch (start us, length us, event | category | flops | bytes accessed | tf_op | source)
XLA Modules:
  0.0 57.4 jit_solution(3559255932788319763)
XLA Ops:
  0.0 0.0 copy-start
  0.0 1.0 %copy-done = f32[16,16,288]{2,1,0:T(8,128)S(1)} copy-done((f32[16,16,288]{2,1,0:T(8,128)S(1)}, f32[16,16,288]{2,1,0:T(8,128)}, u32[]{:S(2)}) %copy-start) | copy-done | bytes 294936
  1.0 0.7 %copy-done.1 = f32[2,16,16]{2,1,0:T(8,128)S(1)} copy-done((f32[2,16,16]{2,1,0:T(8,128)S(1)}, f32[2,16,16]{2,1,0:T(8,128)}, u32[]{:S(2)}) %copy-start.1) | copy-done | bytes 2072
  1.7 0.7 %copy-done.2 = s32[16,16]{1,0:T(8,128)S(1)} copy-done((s32[16,16]{1,0:T(8,128)S(1)}, s32[16,16]{1,0:T(8,128)}, u32[]{:S(2)}) %copy-start.2) | copy-done | bytes 1048
  2.4 0.7 %copy-done.3 = s32[16,16]{1,0:T(8,128)S(1)} copy-done((s32[16,16]{1,0:T(8,128)S(1)}, s32[16,16]{1,0:T(8,128)}, u32[]{:S(2)}) %copy-start.3) | copy-done | bytes 1048
  3.1 0.7 %copy-done.4 = s32[16,16]{1,0:T(8,128)S(1)} copy-done((s32[16,16]{1,0:T(8,128)S(1)}, s32[16,16]{1,0:T(8,128)}, u32[]{:S(2)}) %copy-start.4) | copy-done | bytes 1048
  3.8 0.7 %copy-done.5 = f32[16,16]{1,0:T(8,128)S(1)} copy-done((f32[16,16]{1,0:T(8,128)S(1)}, f32[16,16]{1,0:T(8,128)}, u32[]{:S(2)}) %copy-start.5) | copy-done | bytes 1048
  4.5 0.7 %copy-done.6 = f32[16,16]{1,0:T(8,128)S(1)} copy-done((f32[16,16]{1,0:T(8,128)S(1)}, f32[16,16]{1,0:T(8,128)}, u32[]{:S(2)}) %copy-start.6) | copy-done | bytes 1048
  5.2 0.3 pack.1
  5.6 2.2 %collective-permute-start = (f32[37,8,128]{2,1,0:T(8,128)S(1)}, f32[37,8,128]{2,1,0:T(8,128)S(1)}, u32[]{:S(2)}, u32[]{:S(2)}) collective-permute-start(f32[37,8,128]{2,1,0:T(8,128)S(1)} %get-tuple-element.11), channel_id=1, source_target_pairs={{0,8},{8,16},{16,24},{24,0},{1,9},{9,17},{17,25},{25,1},{2,10},{10... | collective-permute-start | bytes 454664 | tf_op jit(solution)/shard_map/ppermute | solution.py:312
  7.7 2.1 %collective-permute-start.1 = (f32[37,8,128]{2,1,0:T(8,128)S(1)}, f32[37,8,128]{2,1,0:T(8,128)S(1)}, u32[]{:S(2)}, u32[]{:S(2)}) collective-permute-start(f32[37,8,128]{2,1,0:T(8,128)S(1)} %get-tuple-element.12), channel_id=1, source_target_pairs={{0,24},{8,0},{16,8},{24,16},{1,25},{9,1},{17,9},{25,17},{2,26},{10... | collective-permute-start | bytes 454664 | tf_op jit(solution)/shard_map/ppermute | solution.py:312
  9.8 0.7 %copy-done.8 = f32[8,16]{1,0:T(8,128)S(1)} copy-done((f32[8,16]{1,0:T(8,128)S(1)}, f32[8,16]{1,0:T(8,128)}, u32[]{:S(2)}) %copy-start.8) | copy-done | bytes 536
  10.5 0.0 copy-done.7
  10.5 0.1 constant_dynamic-slice_fusion
  10.6 0.1 broadcast_dynamic-update-slice_fusion.1
  10.7 0.7 %copy-done.9 = f32[16]{0:T(128)S(1)} copy-done((f32[16]{0:T(128)S(1)}, f32[16]{0:T(128)}, u32[]{:S(2)}) %copy-start.9) | copy-done | bytes 88
  11.3 0.1 dynamic_slice.11
  11.4 0.1 broadcast_dynamic-update-slice_fusion
  11.6 0.1 constant_dynamic-update-slice_fusion.1
  11.6 1.8 %collective-permute-done.from_west = f32[37,8,128]{2,1,0:T(8,128)S(1)} collective-permute-done((f32[37,8,128]{2,1,0:T(8,128)S(1)}, f32[37,8,128]{2,1,0:T(8,128)S(1)}, u32[]{:S(2)}, u32[]{:S(2)}) %collective-permute-start) | collective-permute-done | bytes 151584 | tf_op jit(solution)/shard_map/ppermute | solution.py:312
  13.5 2.8 %collective-permute-done.1.from_east = f32[37,8,128]{2,1,0:T(8,128)S(1)} collective-permute-done((f32[37,8,128]{2,1,0:T(8,128)S(1)}, f32[37,8,128]{2,1,0:T(8,128)S(1)}, u32[]{:S(2)}, u32[]{:S(2)}) %collective-permute-start.1) | collective-permute-done | bytes 151584 | tf_op jit(solution)/shard_map/ppermute | solution.py:312
  16.2 0.2 join.1.rows
  16.5 4.1 %collective-permute-start.2 = (f32[37,2,8,128]{3,2,1,0:T(8,128)S(1)}, f32[37,2,8,128]{3,2,1,0:T(8,128)S(1)}, u32[]{:S(2)}, u32[]{:S(2)}) collective-permute-start(f32[37,2,8,128]{3,2,1,0:T(8,128)S(1)} %get-tuple-element.16), channel_id=1, source_target_pairs={{0,2},{2,4},{4,6},{1,3},{3,5},{5,7},{8,10},{10,12},{12,14},{9,11},... | collective-permute-start | bytes 909320 | tf_op jit(solution)/shard_map/ppermute | solution.py:312
  20.6 1.9 %collective-permute-start.3 = (f32[37,2,8,128]{3,2,1,0:T(8,128)S(1)}, f32[37,2,8,128]{3,2,1,0:T(8,128)S(1)}, u32[]{:S(2)}, u32[]{:S(2)}) collective-permute-start(f32[37,2,8,128]{3,2,1,0:T(8,128)S(1)} %get-tuple-element.15), channel_id=1, source_target_pairs={{2,0},{4,2},{6,4},{3,1},{5,3},{7,5},{10,8},{12,10},{14,12},{11,9},... | collective-permute-start | bytes 909320 | tf_op jit(solution)/shard_map/ppermute | solution.py:312
  22.6 0.1 constant_dynamic-update-slice_fusion.consts
  22.6 1.7 %collective-permute-done.2.from_south = f32[37,2,8,128]{3,2,1,0:T(8,128)S(1)} collective-permute-done((f32[37,2,8,128]{3,2,1,0:T(8,128)S(1)}, f32[37,2,8,128]{3,2,1,0:T(8,128)S(1)}, u32[]{:S(2)}, u32[]{:S(2)}) %collective-permute-start.2) | collective-permute-done | bytes 303136 | tf_op jit(solution)/shard_map/ppermute | solution.py:312
  24.4 4.4 %collective-permute-done.3.from_north = f32[37,2,8,128]{3,2,1,0:T(8,128)S(1)} collective-permute-done((f32[37,2,8,128]{3,2,1,0:T(8,128)S(1)}, f32[37,2,8,128]{3,2,1,0:T(8,128)S(1)}, u32[]{:S(2)}, u32[]{:S(2)}) %collective-permute-start.3) | collective-permute-done | bytes 303136 | tf_op jit(solution)/shard_map/ppermute | solution.py:312
  28.8 25.2 %march.1 = (f32[36,2,8,128]{3,2,1,0:T(8,128)S(1)}, f32[8,128]{1,0:T(8,128)S(1)}) custom-call(f32[2,37,2,8,128]{4,3,2,1,0:T(8,128)S(1)} %join.1.rows, f32[37,2,8,128]{3,2,1,0:T(8,128)S(1)} %collective-permute-done.2.from_south, f32[37,2,8,128]{3,2,1,0:T(8,128)S(1)} %collective-permute-done.3.from_north, f32[20,8,128]{2,1,0:T(8,128)S(1)} %constant_dynamic-update-slice_fusion.consts), custom_call_target="tpu_custom_call" | custom-call | tf_op jit(solution)/shard_map/march/pallas_call | solution.py:369
  54.0 1.3 %collective-permute-start.4 = (f32[8,128]{1,0:T(8,128)S(1)}, f32[8,128]{1,0:T(8,128)S(1)}, u32[]{:S(2)}, u32[]{:S(2)}) collective-permute-start(f32[8,128]{1,0:T(8,128)S(1)} %get-tuple-element.14.sums), channel_id=1, source_target_pairs={{0,1},{1,0},{2,3},{3,2},{4,5},{5,4},{6,7},{7,6},{8,9},{9,8},{10,11... | collective-permute-start | bytes 12296 | tf_op jit(solution)/shard_map/ppermute | solution.py:376
  55.2 0.1 growth.1.gain
  55.4 1.1 %collective-permute-done.4.other = f32[8,128]{1,0:T(8,128)S(1)} collective-permute-done((f32[8,128]{1,0:T(8,128)S(1)}, f32[8,128]{1,0:T(8,128)S(1)}, u32[]{:S(2)}, u32[]{:S(2)}) %collective-permute-start.4) | collective-permute-done | bytes 4128 | tf_op jit(solution)/shard_map/ppermute | solution.py:376
  56.4 1.0 %finish.1 = f32[16,16,288]{2,1,0:T(8,128)} custom-call(f32[36,2,8,128]{3,2,1,0:T(8,128)S(1)} %get-tuple-element.13.own, f32[36,2,8,128]{3,2,1,0:T(8,128)S(1)} %growth.1.gain, f32[1,2,8,128]{3,2,1,0:T(8,128)S(1)} %slice.11.static, f32[8,128]{1,0:T(8,128)S(1)} %get-tuple-element.14.sums, f32[8,128]{1,0:T(8,128)S(1)} %collective-permute-done.4.other, ...), custom_call_target="tpu_custom_call" | custom-call | tf_op jit(solution)/shard_map/finish/pallas_call | solution.py:377
  (16 shorter events, 0.1 us)
Async XLA Ops:
  0.0 1.0 %copy-start = (f32[16,16,288]{2,1,0:T(8,128)S(1)}, f32[16,16,288]{2,1,0:T(8,128)}, u32[]{:S(2)}) copy-start(f32[16,16,288]{2,1,0:T(8,128)} %spec.1) | copy-start | bytes 884740
  1.0 0.7 %copy-start.1 = (f32[2,16,16]{2,1,0:T(8,128)S(1)}, f32[2,16,16]{2,1,0:T(8,128)}, u32[]{:S(2)}) copy-start(f32[2,16,16]{2,1,0:T(8,128)} %slope.1) | copy-start | bytes 6148
  1.7 0.7 %copy-start.2 = (s32[16,16]{1,0:T(8,128)S(1)}, s32[16,16]{1,0:T(8,128)}, u32[]{:S(2)}) copy-start(s32[16,16]{1,0:T(8,128)} %sea.1) | copy-start | bytes 3076
  2.4 0.7 %copy-start.3 = (s32[16,16]{1,0:T(8,128)S(1)}, s32[16,16]{1,0:T(8,128)}, u32[]{:S(2)}) copy-start(s32[16,16]{1,0:T(8,128)} %ice.1) | copy-start | bytes 3076
  3.1 0.7 %copy-start.4 = (s32[16,16]{1,0:T(8,128)S(1)}, s32[16,16]{1,0:T(8,128)}, u32[]{:S(2)}) copy-start(s32[16,16]{1,0:T(8,128)} %depth.1) | copy-start | bytes 3076
  3.8 0.7 %copy-start.5 = (f32[16,16]{1,0:T(8,128)S(1)}, f32[16,16]{1,0:T(8,128)}, u32[]{:S(2)}) copy-start(f32[16,16]{1,0:T(8,128)} %wspeed.1) | copy-start | bytes 3076
  4.5 0.7 %copy-start.6 = (f32[16,16]{1,0:T(8,128)S(1)}, f32[16,16]{1,0:T(8,128)}, u32[]{:S(2)}) copy-start(f32[16,16]{1,0:T(8,128)} %wdir.1) | copy-start | bytes 3076
  5.6 7.9 %collective-permute-start = (f32[37,8,128]{2,1,0:T(8,128)S(1)}, f32[37,8,128]{2,1,0:T(8,128)S(1)}, u32[]{:S(2)}, u32[]{:S(2)}) collective-permute-start(f32[37,8,128]{2,1,0:T(8,128)S(1)} %get-tuple-element.11), channel_id=1, source_target_pairs={{0,8},{8,16},{16,24},{24,0},{1,9},{9,17},{17,25},{25,1},{2,10},{10... | collective-permute-start | bytes 454664 | tf_op jit(solution)/shard_map/ppermute | solution.py:312
  7.7 8.5 %collective-permute-start.1 = (f32[37,8,128]{2,1,0:T(8,128)S(1)}, f32[37,8,128]{2,1,0:T(8,128)S(1)}, u32[]{:S(2)}, u32[]{:S(2)}) collective-permute-start(f32[37,8,128]{2,1,0:T(8,128)S(1)} %get-tuple-element.12), channel_id=1, source_target_pairs={{0,24},{8,0},{16,8},{24,16},{1,25},{9,1},{17,9},{25,17},{2,26},{10... | collective-permute-start | bytes 454664 | tf_op jit(solution)/shard_map/ppermute | solution.py:312
  9.8 0.7 %copy-start.8 = (f32[8,16]{1,0:T(8,128)S(1)}, f32[8,16]{1,0:T(8,128)}, u32[]{:S(2)}) copy-start(f32[8,16]{1,0:T(8,128)} %param.14) | copy-start | bytes 1540
  9.8 0.7 %copy-start.7 = (f32[8,16]{1,0:T(8,128)S(1)}, f32[8,16]{1,0:T(8,128)}, u32[]{:S(2)}) copy-start(f32[8,16]{1,0:T(8,128)} %param.15) | copy-start | bytes 1540
  10.7 0.7 %copy-start.9 = (f32[16]{0:T(128)S(1)}, f32[16]{0:T(128)}, u32[]{:S(2)}) copy-start(f32[16]{0:T(128)} %param.19) | copy-start | bytes 196
  16.5 7.9 %collective-permute-start.2 = (f32[37,2,8,128]{3,2,1,0:T(8,128)S(1)}, f32[37,2,8,128]{3,2,1,0:T(8,128)S(1)}, u32[]{:S(2)}, u32[]{:S(2)}) collective-permute-start(f32[37,2,8,128]{3,2,1,0:T(8,128)S(1)} %get-tuple-element.16), channel_id=1, source_target_pairs={{0,2},{2,4},{4,6},{1,3},{3,5},{5,7},{8,10},{10,12},{12,14},{9,11},... | collective-permute-start | bytes 909320 | tf_op jit(solution)/shard_map/ppermute | solution.py:312
  20.6 8.1 %collective-permute-start.3 = (f32[37,2,8,128]{3,2,1,0:T(8,128)S(1)}, f32[37,2,8,128]{3,2,1,0:T(8,128)S(1)}, u32[]{:S(2)}, u32[]{:S(2)}) collective-permute-start(f32[37,2,8,128]{3,2,1,0:T(8,128)S(1)} %get-tuple-element.15), channel_id=1, source_target_pairs={{2,0},{4,2},{6,4},{3,1},{5,3},{7,5},{10,8},{12,10},{14,12},{11,9},... | collective-permute-start | bytes 909320 | tf_op jit(solution)/shard_map/ppermute | solution.py:312
  54.0 2.5 %collective-permute-start.4 = (f32[8,128]{1,0:T(8,128)S(1)}, f32[8,128]{1,0:T(8,128)S(1)}, u32[]{:S(2)}, u32[]{:S(2)}) collective-permute-start(f32[8,128]{1,0:T(8,128)S(1)} %get-tuple-element.14.sums), channel_id=1, source_target_pairs={{0,1},{1,0},{2,3},{3,2},{4,5},{5,4},{6,7},{7,6},{8,9},{9,8},{10,11... | collective-permute-start | bytes 12296 | tf_op jit(solution)/shard_map/ppermute | solution.py:376

commit v2 on v1

--- a/solution.py
+++ b/solution.py
@@ -43,16 +43,19 @@
     return pltpu.roll(x, shift, 1) if shift else x
 
 
-def pack_kernel(spec, sea, ice, depth, slope, wspeed, wdir, own, to_east, to_west, flat0, flat1, wide):
-    grid = spec[...].reshape(256, NDIR * FREQ)
-    for low, high in ((0, 128), (128, 256), (256, 288)):
-        turned = grid[:, low:high].T
-        flat0[low:high, :] = turned[:, :128]
-        flat1[low:high, :] = turned[:, 128:]
+def pack_kernel(*refs):
+    sources, (own, to_east, to_west), landed = refs[:7], refs[7:10], refs[10:17]
+    flat0, flat1, wide, sems = refs[17:]
+    copies = [pltpu.make_async_copy(src, dst, sems.at[i]) for i, (src, dst) in enumerate(zip(sources, landed))]
+    for copy in copies:
+        copy.start()
     wide[...] = jnp.zeros_like(wide)
     group = lax.broadcasted_iota(jnp.int32, (16, 128), 1) // 16
     row = lax.broadcasted_iota(jnp.int32, (16, 128), 0) % 8
     own[STATIC] = jnp.zeros((2, 8, 128), f32)
+    for copy in copies:
+        copy.wait()
+    spec, sea, ice, depth, slope, wspeed, wdir = landed
 
     def place(field, values):
         wide[:, :16] = values
@@ -70,6 +73,11 @@
     place(ICE, ice[...].astype(f32))
     place(WIND, wspeed[...])
     place(WDIR, wdir[...])
+    grid = spec[...].reshape(256, NDIR * FREQ)
+    for low, high in ((0, 128), (128, 256), (256, 288)):
+        turned = grid[:, low:high].T
+        flat0[low:high, :] = turned[:, :128]
+        flat1[low:high, :] = turned[:, 128:]
     inner = lanes() % 16
     sea0 = own[STATIC, 0, SEA : SEA + 1, :]
     sea1 = own[STATIC, 1, SEA : SEA + 1, :]
@@ -99,82 +107,31 @@
             gain[d, half] = jnp.exp(force * along) * share
 
 
-def join_kernel(own, from_west, from_east, rows):
+def join_kernel(own, from_west, from_east, south_rows, north_rows):
     inner = lanes() % 16
     even = (lanes() // 16) % 2 == 0
-
-    def body(slab, carry):
+    for slab in range(SLABS):
         west = from_west[slab]
         east = from_east[slab]
         rim0 = jnp.where(inner < 8, roll(east, 16), roll(west, -16))
         rim1 = jnp.where(inner < 8, roll(east, 8), roll(west, -8))
         own0 = own[slab, 0]
         own1 = own[slab, 1]
-        rows[0, slab, 0] = jnp.where(even, own0, rim0)
-        rows[0, slab, 1] = jnp.where(even, rim0, own0)
-        rows[1, slab, 0] = jnp.where(even, own1, rim1)
-        rows[1, slab, 1] = jnp.where(even, rim1, own1)
-        return carry
-
-    lax.fori_loop(0, SLABS, body, 0, unroll=True)
-
-
-def flux(q, diff, curve, k):
-    return k * (q + (0.5 - 0.5 * k) * (diff - (1.0 / 3.0 + (1.0 / 3.0) * k) * curve))
-
-
-def sweep_lon(tiles, kx, cos_d, positive):
-    out = []
-    for q, face in zip(tiles, kx):
-        k = cos_d * face
-        diff = roll(q, -1) - q
-        if positive:
-            curve = diff - roll(diff, 1)
-        else:
-            curve = roll(diff, -1) - diff
-        f = flux(q, diff, curve, k)
-        out.append(q - f + roll(f, 1))
-    return out
-
-
-def sweep_lat(tiles, ky, sin_d, positive, live):
-    ahead = tiles[1:] + [roll(tiles[0], -32)]
-    diff = [n - m for n, m in zip(ahead, tiles)]
-    if positive:
-        before = [roll(diff[7], 32)] + diff[:7]
-        curve = [a - b for a, b in zip(diff, before)]
-    else:
-        after = diff[1:] + [roll(diff[0], -32)]
-        curve = [a - b for a, b in zip(after, diff)]
-    fluxes = [flux(q, a, b, sin_d * face) for q, a, b, face in zip(tiles, diff, curve, ky)]
-    behind = [roll(fluxes[7], 32)] + fluxes[:7]
-    return [(q - f + b) * live for q, f, b in zip(tiles, fluxes, behind)]
-
-
-def sweep_dir(cells, tx, ty):
-    courant = [SIN_FACE[d] * tx - COS_FACE[d] * ty for d in range(NDIR)]
-    first = cells[0]
-    diff = [None] * NDIR
-    for d in range(NDIR):
-        diff[d] = cells[(d + 1) % NDIR] - cells[d]
-    curve = [diff[d] - diff[d - 1] for d in range(NDIR)]
-    fluxes = []
-    for d in range(NDIR):
-        k = courant[d]
-        bend = jnp.where(k >= 0.0, curve[d], curve[(d + 1) % NDIR])
-        fluxes.append(flux(cells[d], diff[d], bend, k))
-    return [cells[d] - fluxes[d] + fluxes[d - 1] for d in range(NDIR)]
-
-
-def march_kernel(rows, from_south, from_north, consts, own, sums, q, kx, ky, tx, ty, trig):
+        south_rows[slab, 0] = jnp.where(even, own0, rim0)
+        south_rows[slab, 1] = jnp.where(even, rim0, own0)
+        north_rows[slab, 0] = jnp.where(even, own1, rim1)
+        north_rows[slab, 1] = jnp.where(even, rim1, own1)
+
+
+def place_kernel(south_rows, north_rows, from_south, from_north, consts, q, kx, ky, tx, ty):
     lane = lanes()
 
     def assemble(slab, carry):
         for p in range(2):
             parts = [
                 from_south[slab, p],
-                roll(rows[0, slab, p], 32),
-                roll(rows[1, slab, p], 64),
+                roll(south_rows[slab, p], 32),
+                roll(north_rows[slab, p], 64),
                 roll(from_north[slab, p], 96),
             ]
             for t in range(p, 8, 2):
@@ -187,12 +144,7 @@
                 q[slab, t] = roll(mixed, 8 - 16 * t)
         return carry
 
-    lax.fori_loop(0, SLABS, assemble, 0, unroll=2)
-
-    for d in range(NDIR):
-        trig[0, d] = jnp.float32(COS[d])
-        trig[1, d] = jnp.float32(SIN[d])
-
+    assemble(STATIC, 0)
     speed = []
     for t in range(8):
         point = q[STATIC, t]
@@ -214,39 +166,130 @@
         ahead = speed[t + 1] if t < 7 else roll(speed[0], -32)
         ky[t] = 0.5 * (speed[t] + ahead)
 
+    lax.fori_loop(0, NDIR, assemble, 0, unroll=3)
+
+
+def flux(q, diff, curve, k, u, w):
+    return k * (q + u * (diff - w * curve))
+
+
+def halves(k):
+    return 0.5 - 0.5 * k, (1.0 / 3.0) + (1.0 / 3.0) * k
+
+
+def lon_kernel(q, kx, out):
+    def one(t, c):
+        face = kx[t]
+        for base in range(10):
+            if base == 0:
+                forth, back = [0], [18]
+            elif base == 9:
+                forth, back = [27], [9]
+            else:
+                forth, back = [base, 36 - base], [18 - base, 18 + base]
+            k = COS[base] * face
+            u, w = halves(k)
+            for d in forth:
+                cell = q[d, t]
+                diff = roll(cell, -1) - cell
+                f = flux(cell, diff, diff - roll(diff, 1), k, u, w)
+                out[d, t] = cell - f + roll(f, 1)
+            for d in back:
+                cell = q[d, t]
+                ahead = roll(cell, -1)
+                diff = cell - ahead
+                f = flux(ahead, diff, diff - roll(diff, -1), k, u, w)
+                out[d, t] = cell + f - roll(f, 1)
+        return c
+
+    lax.fori_loop(0, 8, one, 0)
+
+
+def lat_kernel(q, ky, consts, out):
     live = consts[LIVE]
 
-    def substep(step, carry):
-        for quadrant in range(4):
-            east = quadrant in (0, 3)
-            north = quadrant in (0, 1)
-
-            def one(i, c, quadrant=quadrant, east=east, north=north):
-                d = quadrant * 9 + i
-                tiles = [q[d, t] for t in range(8)]
-                tiles = sweep_lon(tiles, [kx[t] for t in range(8)], trig[0, d], east)
-                tiles = sweep_lat(tiles, [ky[t] for t in range(8)], trig[1, d], north, live)
-                for t in range(8):
-                    q[d, t] = tiles[t]
-                return c
-
-            lax.fori_loop(0, 9, one, 0, unroll=3)
-
-        def turn(t, c):
-            cells = sweep_dir([q[d, t] for d in range(NDIR)], tx[t], ty[t])
-            for d in range(NDIR):
-                q[d, t] = cells[d]
-            return c
-
-        lax.fori_loop(0, 8, turn, 0)
-        return carry
-
-    lax.fori_loop(0, ITERS, substep, 0)
+    def forth(d, ks, us, ws):
+        tiles = [q[d, t] for t in range(8)]
+        diff = [tiles[t + 1] - tiles[t] for t in range(7)]
+        diff.append(roll(tiles[0], -32) - tiles[7])
+        before = roll(diff[7], 32)
+        fluxes = []
+        for t in range(8):
+            fluxes.append(flux(tiles[t], diff[t], diff[t] - before, ks[t], us[t], ws[t]))
+            before = diff[t]
+        behind = roll(fluxes[7], 32)
+        for t in range(8):
+            out[d, t] = (tiles[t] - fluxes[t] + behind) * live
+            behind = fluxes[t]
+
+    def back(d, ks, us, ws):
+        tiles = [q[d, t] for t in range(8)]
+        ahead = tiles[1:] + [roll(tiles[0], -32)]
+        diff = [tiles[t] - ahead[t] for t in range(8)]
+        after = diff[1:] + [roll(diff[0], -32)]
+        fluxes = [flux(ahead[t], diff[t], diff[t] - after[t], ks[t], us[t], ws[t]) for t in range(8)]
+        behind = roll(fluxes[7], 32)
+        for t in range(8):
+            out[d, t] = (tiles[t] + fluxes[t] - behind) * live
+            behind = fluxes[t]
+
+    for base in range(10):
+        ks = [SIN[base] * ky[t] for t in range(8)]
+        us, ws = zip(*[halves(k) for k in ks])
+        if base == 0:
+            north, south = [0], [18]
+        elif base == 9:
+            north, south = [9], [27]
+        else:
+            north, south = [base, 18 - base], [18 + base, 36 - base]
+        for d in north:
+            forth(d, ks, us, ws)
+        for d in south:
+            back(d, ks, us, ws)
+
+
+def turn_kernel(q, tx, ty, out):
+    def one(t, c):
+        x = tx[t]
+        y = ty[t]
+
+        def courant(d):
+            return SIN_FACE[d] * x - COS_FACE[d] * y
+
+        def face(d, cell, diff, curve, curve_ahead):
+            k = courant(d)
+            u, w = halves(k)
+            return flux(cell, diff, jnp.where(k >= 0.0, curve, curve_ahead), k, u, w)
+
+        cell, ahead = q[0, t], q[1, t]
+        before, last = q[NDIR - 1, t], q[NDIR - 2, t]
+        diff0 = before - last
+        diff1 = cell - before
+        diff2 = ahead - cell
+        curve1 = diff1 - diff0
+        curve2 = diff2 - diff1
+        f_before = face(NDIR - 1, before, diff1, curve1, curve2)
+        diff, curve = diff2, curve2
+        for d in range(NDIR):
+            beyond = q[(d + 2) % NDIR, t]
+            diff_ahead = beyond - ahead
+            curve_ahead = diff_ahead - diff
+            f = face(d, cell, diff, curve, curve_ahead)
+            out[d, t] = cell - f + f_before
+            cell, ahead, diff, curve, f_before = ahead, beyond, diff_ahead, curve_ahead, f
+        return c
+
+    lax.fori_loop(0, 8, one, 0)
+
+
+def gather_kernel(q, consts, own, sums):
+    lane = lanes()
+    zero = jnp.zeros((8, 128), f32)
 
     def take(d, carry):
         sum0, sum1 = carry
-        half0 = jnp.zeros((8, 128), f32)
-        half1 = jnp.zeros((8, 128), f32)
+        half0 = zero
+        half1 = zero
         for t in range(8):
             moved = roll(q[d, t], 16 * t - 40)
             half0 = jnp.where(lane // 16 == t, moved, half0)
@@ -256,7 +299,6 @@
         own[d, 1] = half1
         return sum0 + half0, sum1 + half1
 
-    zero = jnp.zeros((8, 128), f32)
     totals = lax.fori_loop(0, NDIR, take, (zero, zero), unroll=3)
     level = consts[LEVEL]
     sums[...] = zero
@@ -283,19 +325,15 @@
             out[8 * half : 8 * half + 8, :, low:high] = turned.reshape(8, 16, high - low)
 
 
-def vmem(count):
-    return [pl.BlockSpec(memory_space=pltpu.VMEM)] * count
-
-
 PARAMS = pltpu.CompilerParams(vmem_limit_bytes=32 * 2**20)
 
 
-def call(kernel, ins, outs, scratch=(), name=None):
+def call(kernel, ins, outs, scratch=(), name=None, space=pltpu.VMEM):
     return pl.pallas_call(
         kernel,
         out_shape=[jax.ShapeDtypeStruct(shape, f32) for shape in outs],
-        in_specs=vmem(ins),
-        out_specs=vmem(len(outs)),
+        in_specs=[pl.BlockSpec(memory_space=space)] * ins,
+        out_specs=[pl.BlockSpec(memory_space=pltpu.VMEM)] * len(outs),
         scratch_shapes=list(scratch),
         compiler_params=PARAMS,
         name=name,
@@ -352,27 +390,33 @@
     )
 
     tile = (8, 128)
+    inputs = [spectrum, sea_mask, ice_mask, depth_class, depth_slope, wind_speed, wind_dir]
     own, to_east, to_west = call(
         pack_kernel,
         7,
         [(SLABS, 2) + tile, (SLABS,) + tile, (SLABS,) + tile],
-        [pltpu.VMEM((NDIR * FREQ, 128), f32)] * 2 + [pltpu.VMEM((16, 128), f32)],
+        [pltpu.VMEM(x.shape, x.dtype) for x in inputs]
+        + [pltpu.VMEM((NDIR * FREQ, 128), f32)] * 2
+        + [pltpu.VMEM((16, 128), f32), pltpu.SemaphoreType.DMA((7,))],
         name="pack",
-    )(spectrum, sea_mask, ice_mask, depth_class, depth_slope, wind_speed, wind_dir)
+        space=pltpu.HBM,
+    )(*[pltpu.with_memory_space_constraint(x, pltpu.HBM) for x in inputs])
     from_west = shift(to_east, "lon", 1, True)
     from_east = shift(to_west, "lon", -1, True)
     (gain,) = call(growth_kernel, 2, [(NDIR, 2) + tile], name="growth")(own, consts)
-    (rows,) = call(join_kernel, 3, [(2, SLABS, 2) + tile], name="join")(own, from_west, from_east)
-    from_south = shift(rows[1], "lat", 1, False)
-    from_north = shift(rows[0], "lat", -1, False)
-    block = pltpu.VMEM((8,) + tile, f32)
-    last, sums = call(
-        march_kernel,
-        4,
-        [(NDIR, 2) + tile, tile],
-        [pltpu.VMEM((SLABS, 8) + tile, f32), block, block, block, block, pltpu.SMEM((2, NDIR), f32)],
-        name="march",
-    )(rows, from_south, from_north, consts)
+    south_rows, north_rows = call(join_kernel, 3, [(SLABS, 2) + tile] * 2, name="join")(own, from_west, from_east)
+    from_south = shift(north_rows, "lat", 1, False)
+    from_north = shift(south_rows, "lat", -1, False)
+    block = (8,) + tile
+    q, kx, ky, tx, ty = call(place_kernel, 5, [(SLABS,) + block] + [block] * 4, name="place")(
+        south_rows, north_rows, from_south, from_north, consts
+    )
+    cells = [(NDIR,) + block]
+    for substep in range(ITERS):
+        (q,) = call(lon_kernel, 2, cells, name="lon")(q, kx)
+        (q,) = call(lat_kernel, 3, cells, name="lat")(q, ky, consts)
+        (q,) = call(turn_kernel, 3, cells, name="turn")(q, tx, ty)
+    last, sums = call(gather_kernel, 2, [(NDIR, 2) + tile, tile], name="gather")(q, consts)
     other = lax.ppermute(sums, "band", [(i, 1 - i) for i in range(2)])
     (out,) = call(
         finish_kernel,

time: 58 us -> 44.3 us (0.76)
  the two profiles are of different devices: /device:TPU:1 before, /device:TPU:2 now
where the time goes in v2:
time: 44.3 us; the launch traced here: 44 us
  Pallas kernels  20 us (45%)
  waiting for transfers between devices  12.2 us (28%)
  starting transfers between devices  9.8 us (22%)
  local copies, waits for them, and re-layouts  1.79 us (4%)
    ppermute x4, waiting for transfers between devices, shift(): return lax.ppermute(array, axis, pairs)  10.2 us
    ppermute x4, starting transfers between devices, shift(): return lax.ppermute(array, axis, pairs)  8.22 us
    pallas_call x4, Pallas kernels, per_device(): q, = call(lon_kernel, 2, cells, name='lon')(q, kx)  8.02 us
    pallas_call x4, Pallas kernels, per_device(): q, = call(turn_kernel, 3, cells, name='turn')(q, tx, ty)  2.89 us
    pallas_call x1, Pallas kernels, per_device(): call(place_kernel, 5, [(SLABS,) + block] + [block] * 4, name='place')  2.21 us
    pallas_call x4, Pallas kernels, per_device(): q, = call(lat_kernel, 3, cells, name='lat')(q, ky, consts)  2.17 us
    ppermute x1, waiting for transfers between devices, per_device(): other = lax.ppermute(sums, 'band', [(i, 1 - i) for i in range(2)])  1.95 us
    pallas_call x1, Pallas kernels, per_device(): call(gather_kernel, 2, [(NDIR, 2) + tile, tile], name='gather')(q, consts)  1.94 us
  transfers between devices with their start and end apart: 5, of which 5 were waited for; matrix products, arithmetic and copies ran while one was open for 4% of the time, Pallas kernels for 0%

profile of v2, /device:TPU:2, one launch (start us, length us, event | category | flops | bytes accessed | tf_op | source)
XLA Modules:
  0.0 44.0 jit_solution(8453524099204338663)
XLA Ops:
  0.0 1.4 %pack.1 = (f32[37,2,8,128]{3,2,1,0:T(8,128)S(1)}, f32[37,8,128]{2,1,0:T(8,128)S(1)}, f32[37,8,128]{2,1,0:T(8,128)S(1)}) custom-call(f32[16,16,288]{2,1,0:T(8,128)} %refs_0_.1, s32[16,16]{1,0:T(8,128)} %refs_1_.1, s32[16,16]{1,0:T(8,128)} %refs_2_.1, s32[16,16]{1,0:T(8,128)} %refs_3_.1, f32[2,16,16]{2,1,0:T(8,128)} %refs_4_.1, f32[16,16]{1,0:T(8,128)} %refs_5_.1, ...), custom_call_target="tpu_custom_call" | custom-call | tf_op jit(solution)/shard_map/pack/pallas_call | solution.py:394
  1.4 1.6 %collective-permute-start = (f32[37,8,128]{2,1,0:T(8,128)S(1)}, f32[37,8,128]{2,1,0:T(8,128)S(1)}, u32[]{:S(2)}, u32[]{:S(2)}) collective-permute-start(f32[37,8,128]{2,1,0:T(8,128)S(1)} %get-tuple-element.18), channel_id=1, source_target_pairs={{0,8},{8,16},{16,24},{24,0},{1,9},{9,17},{17,25},{25,1},{2,10},{10... | collective-permute-start | bytes 454664 | tf_op jit(solution)/shard_map/ppermute | solution.py:350
  3.1 2.2 %collective-permute-start.1 = (f32[37,8,128]{2,1,0:T(8,128)S(1)}, f32[37,8,128]{2,1,0:T(8,128)S(1)}, u32[]{:S(2)}, u32[]{:S(2)}) collective-permute-start(f32[37,8,128]{2,1,0:T(8,128)S(1)} %get-tuple-element.19), channel_id=1, source_target_pairs={{0,24},{8,0},{16,8},{24,16},{1,25},{9,1},{17,9},{25,17},{2,26},{10... | collective-permute-start | bytes 454664 | tf_op jit(solution)/shard_map/ppermute | solution.py:350
  5.3 0.7 %dynamic_slice.11 = f32[8]{0:T(128)S(1)} dynamic-slice(f32[16]{0:T(128)} %param.19, s32[]{:T(128)S(6)} %select_n.22), dynamic_slice_sizes={8} | dynamic-slice | bytes 68 | tf_op jit(solution)/shard_map/dynamic_slice | solution.py:379
  6.0 0.8 %constant_dynamic-slice_fusion = (f32[8,8]{1,0:T(8,128)S(1)}, f32[8,8]{1,0:T(8,128)S(1)}) fusion(f32[8,16]{1,0:T(8,128)} %param.15, s32[]{:T(128)S(6)} %select_n.22, f32[8,16]{1,0:T(8,128)} %param.14), kind=kLoop, calls=%fused_computation.13 | loop fusion | bytes 1028 | tf_op jit(solution)/shard_map/dynamic_slice | solution.py:371
  6.8 0.1 broadcast_dynamic-update-slice_fusion.1
  6.9 0.1 broadcast_dynamic-update-slice_fusion
  7.1 3.0 %collective-permute-done.from_west = f32[37,8,128]{2,1,0:T(8,128)S(1)} collective-permute-done((f32[37,8,128]{2,1,0:T(8,128)S(1)}, f32[37,8,128]{2,1,0:T(8,128)S(1)}, u32[]{:S(2)}, u32[]{:S(2)}) %collective-permute-start) | collective-permute-done | bytes 151584 | tf_op jit(solution)/shard_map/ppermute | solution.py:350
  10.1 1.6 %collective-permute-done.1.from_east = f32[37,8,128]{2,1,0:T(8,128)S(1)} collective-permute-done((f32[37,8,128]{2,1,0:T(8,128)S(1)}, f32[37,8,128]{2,1,0:T(8,128)S(1)}, u32[]{:S(2)}, u32[]{:S(2)}) %collective-permute-start.1) | collective-permute-done | bytes 151584 | tf_op jit(solution)/shard_map/ppermute | solution.py:350
  11.7 0.2 join.1
  11.9 1.9 %collective-permute-start.3 = (f32[37,2,8,128]{3,2,1,0:T(8,128)S(1)}, f32[37,2,8,128]{3,2,1,0:T(8,128)S(1)}, u32[]{:S(2)}, u32[]{:S(2)}) collective-permute-start(f32[37,2,8,128]{3,2,1,0:T(8,128)S(1)} %get-tuple-element.20.south_rows), channel_id=1, source_target_pairs={{2,0},{4,2},{6,4},{3,1},{5,3},{7,5},{10,8},{12,10},{14,12},{11,9},... | collective-permute-start | bytes 909320 | tf_op jit(solution)/shard_map/ppermute | solution.py:350
  13.9 2.4 %collective-permute-start.2 = (f32[37,2,8,128]{3,2,1,0:T(8,128)S(1)}, f32[37,2,8,128]{3,2,1,0:T(8,128)S(1)}, u32[]{:S(2)}, u32[]{:S(2)}) collective-permute-start(f32[37,2,8,128]{3,2,1,0:T(8,128)S(1)} %get-tuple-element.21.north_rows), channel_id=1, source_target_pairs={{0,2},{2,4},{4,6},{1,3},{3,5},{5,7},{8,10},{10,12},{12,14},{9,11},... | collective-permute-start | bytes 909320 | tf_op jit(solution)/shard_map/ppermute | solution.py:350
  16.4 1.8 %collective-permute-done.3.from_north = f32[37,2,8,128]{3,2,1,0:T(8,128)S(1)} collective-permute-done((f32[37,2,8,128]{3,2,1,0:T(8,128)S(1)}, f32[37,2,8,128]{3,2,1,0:T(8,128)S(1)}, u32[]{:S(2)}, u32[]{:S(2)}) %collective-permute-start.3) | collective-permute-done | bytes 303136 | tf_op jit(solution)/shard_map/ppermute | solution.py:350
  18.2 3.8 %collective-permute-done.2.from_south = f32[37,2,8,128]{3,2,1,0:T(8,128)S(1)} collective-permute-done((f32[37,2,8,128]{3,2,1,0:T(8,128)S(1)}, f32[37,2,8,128]{3,2,1,0:T(8,128)S(1)}, u32[]{:S(2)}, u32[]{:S(2)}) %collective-permute-start.2) | collective-permute-done | bytes 303136 | tf_op jit(solution)/shard_map/ppermute | solution.py:350
  22.0 2.2 %place.1 = (f32[37,8,8,128]{3,2,1,0:T(8,128)S(1)}, f32[8,8,128]{2,1,0:T(8,128)S(1)}, f32[8,8,128]{2,1,0:T(8,128)S(1)}, f32[8,8,128]{2,1,0:T(8,128)S(1)}, f32[8,8,128]{2,1,0:T(8,128)S(1)}) custom-call(f32[37,2,8,128]{3,2,1,0:T(8,128)S(1)} %get-tuple-element.20.south_rows, f32[37,2,8,128]{3,2,1,0:T(8,128)S(1)} %get-tuple-element.21.north_rows, ...), custom_call_target="tpu_custom_call" | custom-call | tf_op jit(solution)/shard_map/place/pallas_call | solution.py:411
  24.2 2.0 %lon.4.q = f32[36,8,8,128]{3,2,1,0:T(8,128)S(1)} custom-call(f32[37,8,8,128]{3,2,1,0:T(8,128)S(1)} %get-tuple-element.22.q, f32[8,8,128]{2,1,0:T(8,128)S(1)} %get-tuple-element.23.kx), custom_call_target="tpu_custom_call" | custom-call | tf_op jit(solution)/shard_map/lon/pallas_call | solution.py:416
  26.2 0.5 %lat.4.q = f32[36,8,8,128]{3,2,1,0:T(8,128)S(1)} custom-call(f32[36,8,8,128]{3,2,1,0:T(8,128)S(1)} %lon.4.q, f32[8,8,128]{2,1,0:T(8,128)S(1)} %get-tuple-element.24.ky, f32[20,8,128]{2,1,0:T(8,128)S(1)} %constant_dynamic-update-slice_fusion.consts), custom_call_target="tpu_custom_call" | custom-call | tf_op jit(solution)/shard_map/lat/pallas_call | solution.py:417
  26.8 0.7 %turn.4.q = f32[36,8,8,128]{3,2,1,0:T(8,128)S(1)} custom-call(f32[36,8,8,128]{3,2,1,0:T(8,128)S(1)} %lat.4.q, f32[8,8,128]{2,1,0:T(8,128)S(1)} %get-tuple-element.25.tx, f32[8,8,128]{2,1,0:T(8,128)S(1)} %get-tuple-element.26.ty), custom_call_target="tpu_custom_call" | custom-call | tf_op jit(solution)/shard_map/turn/pallas_call | solution.py:418
  27.5 2.0 %lon.5.q = f32[36,8,8,128]{3,2,1,0:T(8,128)S(1)} custom-call(f32[36,8,8,128]{3,2,1,0:T(8,128)S(1)} %turn.4.q, f32[8,8,128]{2,1,0:T(8,128)S(1)} %get-tuple-element.23.kx), custom_call_target="tpu_custom_call" | custom-call | tf_op jit(solution)/shard_map/lon/pallas_call | solution.py:416
  29.5 0.5 %lat.5.q = f32[36,8,8,128]{3,2,1,0:T(8,128)S(1)} custom-call(f32[36,8,8,128]{3,2,1,0:T(8,128)S(1)} %lon.5.q, f32[8,8,128]{2,1,0:T(8,128)S(1)} %get-tuple-element.24.ky, f32[20,8,128]{2,1,0:T(8,128)S(1)} %constant_dynamic-update-slice_fusion.consts), custom_call_target="tpu_custom_call" | custom-call | tf_op jit(solution)/shard_map/lat/pallas_call | solution.py:417
  30.1 0.7 %turn.5.q = f32[36,8,8,128]{3,2,1,0:T(8,128)S(1)} custom-call(f32[36,8,8,128]{3,2,1,0:T(8,128)S(1)} %lat.5.q, f32[8,8,128]{2,1,0:T(8,128)S(1)} %get-tuple-element.25.tx, f32[8,8,128]{2,1,0:T(8,128)S(1)} %get-tuple-element.26.ty), custom_call_target="tpu_custom_call" | custom-call | tf_op jit(solution)/shard_map/turn/pallas_call | solution.py:418
  30.8 2.0 %lon.6.q = f32[36,8,8,128]{3,2,1,0:T(8,128)S(1)} custom-call(f32[36,8,8,128]{3,2,1,0:T(8,128)S(1)} %turn.5.q, f32[8,8,128]{2,1,0:T(8,128)S(1)} %get-tuple-element.23.kx), custom_call_target="tpu_custom_call" | custom-call | tf_op jit(solution)/shard_map/lon/pallas_call | solution.py:416
  32.8 0.5 %lat.6.q = f32[36,8,8,128]{3,2,1,0:T(8,128)S(1)} custom-call(f32[36,8,8,128]{3,2,1,0:T(8,128)S(1)} %lon.6.q, f32[8,8,128]{2,1,0:T(8,128)S(1)} %get-tuple-element.24.ky, f32[20,8,128]{2,1,0:T(8,128)S(1)} %constant_dynamic-update-slice_fusion.consts), custom_call_target="tpu_custom_call" | custom-call | tf_op jit(solution)/shard_map/lat/pallas_call | solution.py:417
  33.4 0.7 %turn.6.q = f32[36,8,8,128]{3,2,1,0:T(8,128)S(1)} custom-call(f32[36,8,8,128]{3,2,1,0:T(8,128)S(1)} %lat.6.q, f32[8,8,128]{2,1,0:T(8,128)S(1)} %get-tuple-element.25.tx, f32[8,8,128]{2,1,0:T(8,128)S(1)} %get-tuple-element.26.ty), custom_call_target="tpu_custom_call" | custom-call | tf_op jit(solution)/shard_map/turn/pallas_call | solution.py:418
  34.1 2.0 %lon.7.q = f32[36,8,8,128]{3,2,1,0:T(8,128)S(1)} custom-call(f32[36,8,8,128]{3,2,1,0:T(8,128)S(1)} %turn.6.q, f32[8,8,128]{2,1,0:T(8,128)S(1)} %get-tuple-element.23.kx), custom_call_target="tpu_custom_call" | custom-call | tf_op jit(solution)/shard_map/lon/pallas_call | solution.py:416
  36.1 0.5 %lat.7.q = f32[36,8,8,128]{3,2,1,0:T(8,128)S(1)} custom-call(f32[36,8,8,128]{3,2,1,0:T(8,128)S(1)} %lon.7.q, f32[8,8,128]{2,1,0:T(8,128)S(1)} %get-tuple-element.24.ky, f32[20,8,128]{2,1,0:T(8,128)S(1)} %constant_dynamic-update-slice_fusion.consts), custom_call_target="tpu_custom_call" | custom-call | tf_op jit(solution)/shard_map/lat/pallas_call | solution.py:417
  36.7 0.7 %turn.7.q = f32[36,8,8,128]{3,2,1,0:T(8,128)S(1)} custom-call(f32[36,8,8,128]{3,2,1,0:T(8,128)S(1)} %lat.7.q, f32[8,8,128]{2,1,0:T(8,128)S(1)} %get-tuple-element.25.tx, f32[8,8,128]{2,1,0:T(8,128)S(1)} %get-tuple-element.26.ty), custom_call_target="tpu_custom_call" | custom-call | tf_op jit(solution)/shard_map/turn/pallas_call | solution.py:418
  37.4 1.9 %gather.1 = (f32[36,2,8,128]{3,2,1,0:T(8,128)S(1)}, f32[8,128]{1,0:T(8,128)S(1)}) custom-call(f32[36,8,8,128]{3,2,1,0:T(8,128)S(1)} %turn.7.q, f32[20,8,128]{2,1,0:T(8,128)S(1)} %constant_dynamic-update-slice_fusion.consts), custom_call_target="tpu_custom_call" | custom-call | tf_op jit(solution)/shard_map/gather/pallas_call | solution.py:419
  39.3 1.6 %collective-permute-start.4 = (f32[8,128]{1,0:T(8,128)S(1)}, f32[8,128]{1,0:T(8,128)S(1)}, u32[]{:S(2)}, u32[]{:S(2)}) collective-permute-start(f32[8,128]{1,0:T(8,128)S(1)} %get-tuple-element.28.sums), channel_id=1, source_target_pairs={{0,1},{1,0},{2,3},{3,2},{4,5},{5,4},{6,7},{7,6},{8,9},{9,8},{10,11... | collective-permute-start | bytes 12296 | tf_op jit(solution)/shard_map/ppermute | solution.py:420
  40.9 0.1 growth.1.gain
  41.0 2.0 %collective-permute-done.4.other = f32[8,128]{1,0:T(8,128)S(1)} collective-permute-done((f32[8,128]{1,0:T(8,128)S(1)}, f32[8,128]{1,0:T(8,128)S(1)}, u32[]{:S(2)}, u32[]{:S(2)}) %collective-permute-start.4) | collective-permute-done | bytes 4128 | tf_op jit(solution)/shard_map/ppermute | solution.py:420
  43.0 1.0 %finish.1 = f32[16,16,288]{2,1,0:T(8,128)} custom-call(f32[36,2,8,128]{3,2,1,0:T(8,128)S(1)} %get-tuple-element.27.own, f32[36,2,8,128]{3,2,1,0:T(8,128)S(1)} %growth.1.gain, f32[1,2,8,128]{3,2,1,0:T(8,128)S(1)} %slice.3.static, f32[8,128]{1,0:T(8,128)S(1)} %get-tuple-element.28.sums, f32[8,128]{1,0:T(8,128)S(1)} %collective-permute-done.4.other, ...), custom_call_target="tpu_custom_call" | custom-call | tf_op jit(solution)/shard_map/finish/pallas_call | solution.py:421
  (8 shorter events, 0.2 us)
Async XLA Ops:
  1.4 8.7 %collective-permute-start = (f32[37,8,128]{2,1,0:T(8,128)S(1)}, f32[37,8,128]{2,1,0:T(8,128)S(1)}, u32[]{:S(2)}, u32[]{:S(2)}) collective-permute-start(f32[37,8,128]{2,1,0:T(8,128)S(1)} %get-tuple-element.18), channel_id=1, source_target_pairs={{0,8},{8,16},{16,24},{24,0},{1,9},{9,17},{17,25},{25,1},{2,10},{10... | collective-permute-start | bytes 454664 | tf_op jit(solution)/shard_map/ppermute | solution.py:350
  3.1 8.6 %collective-permute-start.1 = (f32[37,8,128]{2,1,0:T(8,128)S(1)}, f32[37,8,128]{2,1,0:T(8,128)S(1)}, u32[]{:S(2)}, u32[]{:S(2)}) collective-permute-start(f32[37,8,128]{2,1,0:T(8,128)S(1)} %get-tuple-element.19), channel_id=1, source_target_pairs={{0,24},{8,0},{16,8},{24,16},{1,25},{9,1},{17,9},{25,17},{2,26},{10... | collective-permute-start | bytes 454664 | tf_op jit(solution)/shard_map/ppermute | solution.py:350
  11.9 6.2 %collective-permute-start.3 = (f32[37,2,8,128]{3,2,1,0:T(8,128)S(1)}, f32[37,2,8,128]{3,2,1,0:T(8,128)S(1)}, u32[]{:S(2)}, u32[]{:S(2)}) collective-permute-start(f32[37,2,8,128]{3,2,1,0:T(8,128)S(1)} %get-tuple-element.20.south_rows), channel_id=1, source_target_pairs={{2,0},{4,2},{6,4},{3,1},{5,3},{7,5},{10,8},{12,10},{14,12},{11,9},... | collective-permute-start | bytes 909320 | tf_op jit(solution)/shard_map/ppermute | solution.py:350
  13.9 8.1 %collective-permute-start.2 = (f32[37,2,8,128]{3,2,1,0:T(8,128)S(1)}, f32[37,2,8,128]{3,2,1,0:T(8,128)S(1)}, u32[]{:S(2)}, u32[]{:S(2)}) collective-permute-start(f32[37,2,8,128]{3,2,1,0:T(8,128)S(1)} %get-tuple-element.21.north_rows), channel_id=1, source_target_pairs={{0,2},{2,4},{4,6},{1,3},{3,5},{5,7},{8,10},{10,12},{12,14},{9,11},... | collective-permute-start | bytes 909320 | tf_op jit(solution)/shard_map/ppermute | solution.py:350
  39.3 3.7 %collective-permute-start.4 = (f32[8,128]{1,0:T(8,128)S(1)}, f32[8,128]{1,0:T(8,128)S(1)}, u32[]{:S(2)}, u32[]{:S(2)}) collective-permute-start(f32[8,128]{1,0:T(8,128)S(1)} %get-tuple-element.28.sums), channel_id=1, source_target_pairs={{0,1},{1,0},{2,3},{3,2},{4,5},{5,4},{6,7},{7,6},{8,9},{9,8},{10,11... | collective-permute-start | bytes 12296 | tf_op jit(solution)/shard_map/ppermute | solution.py:420

commit v3 on v2

--- a/solution.py
+++ b/solution.py
@@ -43,8 +43,12 @@
     return pltpu.roll(x, shift, 1) if shift else x
 
 
+def is_even(axis):
+    return lax.axis_index(axis) % 2 == 0
+
+
 def pack_kernel(*refs):
-    sources, (own, to_east, to_west), landed = refs[:7], refs[7:10], refs[10:17]
+    sources, (own, to_first, to_second), landed = refs[:7], refs[7:10], refs[10:17]
     flat0, flat1, wide, sems = refs[17:]
     copies = [pltpu.make_async_copy(src, dst, sems.at[i]) for i, (src, dst) in enumerate(zip(sources, landed))]
     for copy in copies:
@@ -79,6 +83,7 @@
         flat0[low:high, :] = turned[:, :128]
         flat1[low:high, :] = turned[:, 128:]
     inner = lanes() % 16
+    even = is_even("lon")
     sea0 = own[STATIC, 0, SEA : SEA + 1, :]
     sea1 = own[STATIC, 1, SEA : SEA + 1, :]
     for slab in range(SLABS):
@@ -90,8 +95,10 @@
         else:
             own0 = own[slab, 0]
             own1 = own[slab, 1]
-        to_east[slab] = jnp.where(inner >= 8, own0, roll(own1, -8))
-        to_west[slab] = jnp.where(inner < 8, own0, roll(own1, 8))
+        to_east = jnp.where(inner >= 8, own0, roll(own1, -8))
+        to_west = jnp.where(inner < 8, own0, roll(own1, 8))
+        to_first[slab] = jnp.where(even, to_east, to_west)
+        to_second[slab] = jnp.where(even, to_west, to_east)
 
 
 def growth_kernel(own, consts, gain):
@@ -107,32 +114,40 @@
             gain[d, half] = jnp.exp(force * along) * share
 
 
-def join_kernel(own, from_west, from_east, south_rows, north_rows):
+def join_kernel(own, from_first, from_second, to_first, to_second):
     inner = lanes() % 16
-    even = (lanes() // 16) % 2 == 0
+    even_group = (lanes() // 16) % 2 == 0
+    even_lon = is_even("lon")
+    even_lat = is_even("lat")
     for slab in range(SLABS):
-        west = from_west[slab]
-        east = from_east[slab]
+        first, second = from_first[slab], from_second[slab]
+        east = jnp.where(even_lon, first, second)
+        west = jnp.where(even_lon, second, first)
         rim0 = jnp.where(inner < 8, roll(east, 16), roll(west, -16))
         rim1 = jnp.where(inner < 8, roll(east, 8), roll(west, -8))
         own0 = own[slab, 0]
         own1 = own[slab, 1]
-        south_rows[slab, 0] = jnp.where(even, own0, rim0)
-        south_rows[slab, 1] = jnp.where(even, rim0, own0)
-        north_rows[slab, 0] = jnp.where(even, own1, rim1)
-        north_rows[slab, 1] = jnp.where(even, rim1, own1)
-
-
-def place_kernel(south_rows, north_rows, from_south, from_north, consts, q, kx, ky, tx, ty):
+        for p in range(2):
+            pick = even_group if p == 0 else ~even_group
+            south_rows = jnp.where(pick, own0, rim0)
+            north_rows = jnp.where(pick, own1, rim1)
+            to_first[slab, p] = jnp.where(even_lat, north_rows, south_rows)
+            to_second[slab, p] = jnp.where(even_lat, south_rows, north_rows)
+
+
+def place_kernel(to_first, to_second, from_first, from_second, consts, q, kx, ky, tx, ty):
     lane = lanes()
-
-    def assemble(slab, carry):
+    even = is_even("lat")
+
+    def assemble(slab):
         for p in range(2):
+            to1, to2 = to_first[slab, p], to_second[slab, p]
+            from1, from2 = from_first[slab, p], from_second[slab, p]
             parts = [
-                from_south[slab, p],
-                roll(south_rows[slab, p], 32),
-                roll(north_rows[slab, p], 64),
-                roll(from_north[slab, p], 96),
+                jnp.where(even, from2, from1),
+                roll(jnp.where(even, to2, to1), 32),
+                roll(jnp.where(even, to1, to2), 64),
+                roll(jnp.where(even, from1, from2), 96),
             ]
             for t in range(p, 8, 2):
                 which = ((lane - (16 * t - 8)) % 128) // 32
@@ -142,9 +157,8 @@
                     jnp.where(which == 2, parts[2], parts[3]),
                 )
                 q[slab, t] = roll(mixed, 8 - 16 * t)
-        return carry
-
-    assemble(STATIC, 0)
+
+    assemble(STATIC)
     speed = []
     for t in range(8):
         point = q[STATIC, t]
@@ -166,7 +180,8 @@
         ahead = speed[t + 1] if t < 7 else roll(speed[0], -32)
         ky[t] = 0.5 * (speed[t] + ahead)
 
-    lax.fori_loop(0, NDIR, assemble, 0, unroll=3)
+    for d in range(NDIR):
+        assemble(d)
 
 
 def flux(q, diff, curve, k, u, w):
@@ -178,7 +193,7 @@
 
 
 def lon_kernel(q, kx, out):
-    def one(t, c):
+    for t in range(8):
         face = kx[t]
         for base in range(10):
             if base == 0:
@@ -200,9 +215,6 @@
                 diff = cell - ahead
                 f = flux(ahead, diff, diff - roll(diff, -1), k, u, w)
                 out[d, t] = cell + f - roll(f, 1)
-        return c
-
-    lax.fori_loop(0, 8, one, 0)
 
 
 def lat_kernel(q, ky, consts, out):
@@ -249,7 +261,7 @@
 
 
 def turn_kernel(q, tx, ty, out):
-    def one(t, c):
+    def one(t):
         x = tx[t]
         y = ty[t]
 
@@ -277,29 +289,26 @@
             f = face(d, cell, diff, curve, curve_ahead)
             out[d, t] = cell - f + f_before
             cell, ahead, diff, curve, f_before = ahead, beyond, diff_ahead, curve_ahead, f
-        return c
-
-    lax.fori_loop(0, 8, one, 0)
+
+    for t in range(8):
+        one(t)
 
 
 def gather_kernel(q, consts, own, sums):
     lane = lanes()
     zero = jnp.zeros((8, 128), f32)
 
-    def take(d, carry):
-        sum0, sum1 = carry
-        half0 = zero
-        half1 = zero
+    totals = [zero, zero]
+    for d in range(NDIR):
+        halves_of = [zero, zero]
         for t in range(8):
             moved = roll(q[d, t], 16 * t - 40)
-            half0 = jnp.where(lane // 16 == t, moved, half0)
-            half1 = jnp.where(lane // 16 == (t + 2) % 8, moved, half1)
-        half1 = roll(half1, -32)
-        own[d, 0] = half0
-        own[d, 1] = half1
-        return sum0 + half0, sum1 + half1
-
-    totals = lax.fori_loop(0, NDIR, take, (zero, zero), unroll=3)
+            halves_of[0] = jnp.where(lane // 16 == t, moved, halves_of[0])
+            halves_of[1] = jnp.where(lane // 16 == (t + 2) % 8, moved, halves_of[1])
+        halves_of[1] = roll(halves_of[1], -32)
+        for half in range(2):
+            own[d, half] = halves_of[half]
+            totals[half] = totals[half] + halves_of[half]
     level = consts[LEVEL]
     sums[...] = zero
     for half in range(2):
@@ -340,13 +349,13 @@
     )
 
 
-def shift(array, axis, step, closed):
+def swap(array, axis, first, closed=False):
     count = lax.axis_size(axis)
     pairs = []
-    for i in range(count):
-        j = i + step
-        if closed or 0 <= j < count:
-            pairs.append((i, j % count))
+    for i in range(first, count, 2):
+        if i + 1 < count or closed:
+            j = (i + 1) % count
+            pairs += [(i, j), (j, i)]
     return lax.ppermute(array, axis, pairs)
 
 
@@ -391,7 +400,7 @@
 
     tile = (8, 128)
     inputs = [spectrum, sea_mask, ice_mask, depth_class, depth_slope, wind_speed, wind_dir]
-    own, to_east, to_west = call(
+    own, to_first, to_second = call(
         pack_kernel,
         7,
         [(SLABS, 2) + tile, (SLABS,) + tile, (SLABS,) + tile],
@@ -401,15 +410,15 @@
         name="pack",
         space=pltpu.HBM,
     )(*[pltpu.with_memory_space_constraint(x, pltpu.HBM) for x in inputs])
-    from_west = shift(to_east, "lon", 1, True)
-    from_east = shift(to_west, "lon", -1, True)
+    from_second = swap(to_second, "lon", 1, True)
+    from_first = swap(to_first, "lon", 0, True)
     (gain,) = call(growth_kernel, 2, [(NDIR, 2) + tile], name="growth")(own, consts)
-    south_rows, north_rows = call(join_kernel, 3, [(SLABS, 2) + tile] * 2, name="join")(own, from_west, from_east)
-    from_south = shift(north_rows, "lat", 1, False)
-    from_north = shift(south_rows, "lat", -1, False)
+    to_first, to_second = call(join_kernel, 3, [(SLABS, 2) + tile] * 2, name="join")(own, from_first, from_second)
+    from_second = swap(to_second, "lat", 1)
+    from_first = swap(to_first, "lat", 0)
     block = (8,) + tile
     q, kx, ky, tx, ty = call(place_kernel, 5, [(SLABS,) + block] + [block] * 4, name="place")(
-        south_rows, north_rows, from_south, from_north, consts
+        to_first, to_second, from_first, from_second, consts
     )
     cells = [(NDIR,) + block]
     for substep in range(ITERS):
@@ -417,7 +426,7 @@
         (q,) = call(lat_kernel, 3, cells, name="lat")(q, ky, consts)
         (q,) = call(turn_kernel, 3, cells, name="turn")(q, tx, ty)
     last, sums = call(gather_kernel, 2, [(NDIR, 2) + tile, tile], name="gather")(q, consts)
-    other = lax.ppermute(sums, "band", [(i, 1 - i) for i in range(2)])
+    other = swap(sums, "band", 0)
     (out,) = call(
         finish_kernel,
         6,

time: 44.3 us -> 105 us (2.37)
  Pallas kernels: 20 us -> 81.7 us
  starting transfers between devices: 9.8 us -> 8.28 us
    pallas_call x4, Pallas kernels: 8.02 us -> 68.1 us  [per_device(): q, = call(lon_kernel, 2, cells, name='lon')(q, kx)]
    pallas_call x1, Pallas kernels: 2.21 us -> 4.26 us  [per_device(): call(place_kernel, 5, [(SLABS,) + block] + [block] * 4, name='place')]
    ppermute x5, starting transfers between devices: 9.8 us -> 8.28 us  [swap(): return lax.ppermute(array, axis, pairs)]
  transfers between devices with their start and end apart: 5 -> 5, of which waited for: 5 -> 3; matrix products, arithmetic and copies ran while one was open for 4% -> 2% of each run, Pallas kernels for 0% -> 0%
where the time goes in v3:
time: 105 us
  Pallas kernels  81.7 us (78%)
  waiting for transfers between devices  12.7 us (12%)
  starting transfers between devices  8.28 us (8%)
  local copies, waits for them, and re-layouts  1.79 us (2%)
    pallas_call x4, Pallas kernels, per_device(): q, = call(lon_kernel, 2, cells, name='lon')(q, kx)  68.1 us
    ppermute x5, waiting for transfers between devices, swap(): return lax.ppermute(array, axis, pairs)  12.7 us
    ppermute x5, starting transfers between devices, swap(): return lax.ppermute(array, axis, pairs)  8.28 us
    pallas_call x1, Pallas kernels, per_device(): call(place_kernel, 5, [(SLABS,) + block] + [block] * 4, name='place')  4.26 us
    pallas_call x4, Pallas kernels, per_device(): q, = call(turn_kernel, 3, cells, name='turn')(q, tx, ty)  2.66 us
    pallas_call x4, Pallas kernels, per_device(): q, = call(lat_kernel, 3, cells, name='lat')(q, ky, consts)  2.17 us
  transfers between devices with their start and end apart: 5, of which 3 were waited for; matrix products, arithmetic and copies ran while one was open for 2% of the time, Pallas kernels for 0%

profile of v3, /device:TPU:2, one launch (start us, length us, event | category | flops | bytes accessed | tf_op | source)
XLA Modules:
  0.0 104.7 jit_solution(14733969835146137083)
XLA Ops:
  0.0 1.4 %pack.1 = (f32[37,2,8,128]{3,2,1,0:T(8,128)S(1)}, f32[37,8,128]{2,1,0:T(8,128)S(1)}, f32[37,8,128]{2,1,0:T(8,128)S(1)}) custom-call(f32[16,16,288]{2,1,0:T(8,128)} %refs_0_.1, s32[16,16]{1,0:T(8,128)} %refs_1_.1, s32[16,16]{1,0:T(8,128)} %refs_2_.1, s32[16,16]{1,0:T(8,128)} %refs_3_.1, f32[2,16,16]{2,1,0:T(8,128)} %refs_4_.1, f32[16,16]{1,0:T(8,128)} %refs_5_.1, ...), custom_call_target="tpu_custom_call" | custom-call | tf_op jit(solution)/shard_map/pack/pallas_call | solution.py:403
  1.4 1.6 %collective-permute-start = (f32[37,8,128]{2,1,0:T(8,128)S(1)}, f32[37,8,128]{2,1,0:T(8,128)S(1)}, u32[]{:S(2)}, u32[]{:S(2)}) collective-permute-start(f32[37,8,128]{2,1,0:T(8,128)S(1)} %get-tuple-element.18), channel_id=1, source_target_pairs={{0,8},{8,0},{16,24},{24,16},{1,9},{9,1},{17,25},{25,17},{2,10},{10... | collective-permute-start | bytes 454664 | tf_op jit(solution)/shard_map/ppermute | solution.py:359
  3.1 2.5 %collective-permute-start.1 = (f32[37,8,128]{2,1,0:T(8,128)S(1)}, f32[37,8,128]{2,1,0:T(8,128)S(1)}, u32[]{:S(2)}, u32[]{:S(2)}) collective-permute-start(f32[37,8,128]{2,1,0:T(8,128)S(1)} %get-tuple-element.19), channel_id=1, source_target_pairs={{8,16},{16,8},{24,0},{0,24},{9,17},{17,9},{25,1},{1,25},{10,18},{1... | collective-permute-start | bytes 454664 | tf_op jit(solution)/shard_map/ppermute | solution.py:359
  5.6 0.7 dynamic_slice.11
  6.3 0.8 constant_dynamic-slice_fusion
  7.1 0.1 broadcast_dynamic-update-slice_fusion.1
  7.1 0.1 broadcast_dynamic-update-slice_fusion
  7.3 0.1 constant_dynamic-update-slice_fusion.1
  7.4 5.2 %collective-permute-done.1.from_second = f32[37,8,128]{2,1,0:T(8,128)S(1)} collective-permute-done((f32[37,8,128]{2,1,0:T(8,128)S(1)}, f32[37,8,128]{2,1,0:T(8,128)S(1)}, u32[]{:S(2)}, u32[]{:S(2)}) %collective-permute-start.1) | collective-permute-done | bytes 151584 | tf_op jit(solution)/shard_map/ppermute | solution.py:359
  12.6 0.2 join.1
  12.8 0.1 collective-permute-start.2
  12.9 2.5 %collective-permute-start.3 = (f32[37,2,8,128]{3,2,1,0:T(8,128)S(1)}, f32[37,2,8,128]{3,2,1,0:T(8,128)S(1)}, u32[]{:S(2)}, u32[]{:S(2)}) collective-permute-start(f32[37,2,8,128]{3,2,1,0:T(8,128)S(1)} %get-tuple-element.21.to_second), channel_id=1, source_target_pairs={{2,4},{4,2},{3,5},{5,3},{10,12},{12,10},{11,13},{13,11},{18,20},{2... | collective-permute-start | bytes 909320 | tf_op jit(solution)/shard_map/ppermute | solution.py:359
  15.4 0.1 constant_dynamic-update-slice_fusion.consts
  15.5 5.5 %collective-permute-done.3.from_second = f32[37,2,8,128]{3,2,1,0:T(8,128)S(1)} collective-permute-done((f32[37,2,8,128]{3,2,1,0:T(8,128)S(1)}, f32[37,2,8,128]{3,2,1,0:T(8,128)S(1)}, u32[]{:S(2)}, u32[]{:S(2)}) %collective-permute-start.3) | collective-permute-done | bytes 303136 | tf_op jit(solution)/shard_map/ppermute | solution.py:359
  21.0 4.3 %place.1 = (f32[37,8,8,128]{3,2,1,0:T(8,128)S(1)}, f32[8,8,128]{2,1,0:T(8,128)S(1)}, f32[8,8,128]{2,1,0:T(8,128)S(1)}, f32[8,8,128]{2,1,0:T(8,128)S(1)}, f32[8,8,128]{2,1,0:T(8,128)S(1)}) custom-call(f32[37,2,8,128]{3,2,1,0:T(8,128)S(1)} %get-tuple-element.20.to_first, f32[37,2,8,128]{3,2,1,0:T(8,128)S(1)} %get-tuple-element.21.to_second, ...), custom_call_target="tpu_custom_call" | custom-call | tf_op jit(solution)/shard_map/place/pallas_call | solution.py:420
  25.3 17.0 %lon.4.q = f32[36,8,8,128]{3,2,1,0:T(8,128)S(1)} custom-call(f32[37,8,8,128]{3,2,1,0:T(8,128)S(1)} %get-tuple-element.22.q, f32[8,8,128]{2,1,0:T(8,128)S(1)} %get-tuple-element.23.kx), custom_call_target="tpu_custom_call" | custom-call | tf_op jit(solution)/shard_map/lon/pallas_call | solution.py:425
  42.3 0.5 lat.4.q
  42.8 0.7 turn.4.q
  43.5 17.0 %lon.5.q = f32[36,8,8,128]{3,2,1,0:T(8,128)S(1)} custom-call(f32[36,8,8,128]{3,2,1,0:T(8,128)S(1)} %turn.4.q, f32[8,8,128]{2,1,0:T(8,128)S(1)} %get-tuple-element.23.kx), custom_call_target="tpu_custom_call" | custom-call | tf_op jit(solution)/shard_map/lon/pallas_call | solution.py:425
  60.5 0.5 lat.5.q
  61.0 0.7 turn.5.q
  61.7 17.0 %lon.6.q = f32[36,8,8,128]{3,2,1,0:T(8,128)S(1)} custom-call(f32[36,8,8,128]{3,2,1,0:T(8,128)S(1)} %turn.5.q, f32[8,8,128]{2,1,0:T(8,128)S(1)} %get-tuple-element.23.kx), custom_call_target="tpu_custom_call" | custom-call | tf_op jit(solution)/shard_map/lon/pallas_call | solution.py:425
  78.7 0.5 lat.6.q
  79.3 0.7 turn.6.q
  79.9 17.1 %lon.7.q = f32[36,8,8,128]{3,2,1,0:T(8,128)S(1)} custom-call(f32[36,8,8,128]{3,2,1,0:T(8,128)S(1)} %turn.6.q, f32[8,8,128]{2,1,0:T(8,128)S(1)} %get-tuple-element.23.kx), custom_call_target="tpu_custom_call" | custom-call | tf_op jit(solution)/shard_map/lon/pallas_call | solution.py:425
  97.1 0.5 lat.7.q
  97.6 0.7 turn.7.q
  98.3 1.8 %gather.1 = (f32[36,2,8,128]{3,2,1,0:T(8,128)S(1)}, f32[8,128]{1,0:T(8,128)S(1)}) custom-call(f32[36,8,8,128]{3,2,1,0:T(8,128)S(1)} %turn.7.q, f32[20,8,128]{2,1,0:T(8,128)S(1)} %constant_dynamic-update-slice_fusion.consts), custom_call_target="tpu_custom_call" | custom-call | tf_op jit(solution)/shard_map/gather/pallas_call | solution.py:428
  100.1 1.6 %collective-permute-start.4 = (f32[8,128]{1,0:T(8,128)S(1)}, f32[8,128]{1,0:T(8,128)S(1)}, u32[]{:S(2)}, u32[]{:S(2)}) collective-permute-start(f32[8,128]{1,0:T(8,128)S(1)} %get-tuple-element.28.sums), channel_id=1, source_target_pairs={{0,1},{1,0},{2,3},{3,2},{4,5},{5,4},{6,7},{7,6},{8,9},{9,8},{10,11... | collective-permute-start | bytes 12296 | tf_op jit(solution)/shard_map/ppermute | solution.py:359
  101.6 0.1 growth.1.gain
  101.8 2.0 %collective-permute-done.4.other = f32[8,128]{1,0:T(8,128)S(1)} collective-permute-done((f32[8,128]{1,0:T(8,128)S(1)}, f32[8,128]{1,0:T(8,128)S(1)}, u32[]{:S(2)}, u32[]{:S(2)}) %collective-permute-start.4) | collective-permute-done | bytes 4128 | tf_op jit(solution)/shard_map/ppermute | solution.py:359
  103.7 1.0 finish.1
  (8 shorter events, 0.1 us)
Async XLA Ops:
  1.4 5.9 %collective-permute-start = (f32[37,8,128]{2,1,0:T(8,128)S(1)}, f32[37,8,128]{2,1,0:T(8,128)S(1)}, u32[]{:S(2)}, u32[]{:S(2)}) collective-permute-start(f32[37,8,128]{2,1,0:T(8,128)S(1)} %get-tuple-element.18), channel_id=1, source_target_pairs={{0,8},{8,0},{16,24},{24,16},{1,9},{9,1},{17,25},{25,17},{2,10},{10... | collective-permute-start | bytes 454664 | tf_op jit(solution)/shard_map/ppermute | solution.py:359
  3.1 9.5 %collective-permute-start.1 = (f32[37,8,128]{2,1,0:T(8,128)S(1)}, f32[37,8,128]{2,1,0:T(8,128)S(1)}, u32[]{:S(2)}, u32[]{:S(2)}) collective-permute-start(f32[37,8,128]{2,1,0:T(8,128)S(1)} %get-tuple-element.19), channel_id=1, source_target_pairs={{8,16},{16,8},{24,0},{0,24},{9,17},{17,9},{25,1},{1,25},{10,18},{1... | collective-permute-start | bytes 454664 | tf_op jit(solution)/shard_map/ppermute | solution.py:359
  12.8 2.7 %collective-permute-start.2 = (f32[37,2,8,128]{3,2,1,0:T(8,128)S(1)}, f32[37,2,8,128]{3,2,1,0:T(8,128)S(1)}, u32[]{:S(2)}, u32[]{:S(2)}) collective-permute-start(f32[37,2,8,128]{3,2,1,0:T(8,128)S(1)} %get-tuple-element.20.to_first), channel_id=1, source_target_pairs={{0,2},{2,0},{4,6},{6,4},{1,3},{3,1},{5,7},{7,5},{8,10},{10,8},{12,... | collective-permute-start | bytes 909320 | tf_op jit(solution)/shard_map/ppermute | solution.py:359
  12.9 8.1 %collective-permute-start.3 = (f32[37,2,8,128]{3,2,1,0:T(8,128)S(1)}, f32[37,2,8,128]{3,2,1,0:T(8,128)S(1)}, u32[]{:S(2)}, u32[]{:S(2)}) collective-permute-start(f32[37,2,8,128]{3,2,1,0:T(8,128)S(1)} %get-tuple-element.21.to_second), channel_id=1, source_target_pairs={{2,4},{4,2},{3,5},{5,3},{10,12},{12,10},{11,13},{13,11},{18,20},{2... | collective-permute-start | bytes 909320 | tf_op jit(solution)/shard_map/ppermute | solution.py:359
  100.1 3.6 %collective-permute-start.4 = (f32[8,128]{1,0:T(8,128)S(1)}, f32[8,128]{1,0:T(8,128)S(1)}, u32[]{:S(2)}, u32[]{:S(2)}) collective-permute-start(f32[8,128]{1,0:T(8,128)S(1)} %get-tuple-element.28.sums), channel_id=1, source_target_pairs={{0,1},{1,0},{2,3},{3,2},{4,5},{5,4},{6,7},{7,6},{8,9},{9,8},{10,11... | collective-permute-start | bytes 12296 | tf_op jit(solution)/shard_map/ppermute | solution.py:359

commit v4 on v3

--- a/solution.py
+++ b/solution.py
@@ -32,6 +32,7 @@
 TAB_SPEED, TAB_TURN, STRETCH, LIVE, ICE_RATE, LEVEL = 0, 8, 16, 17, 18, 19
 
 f32 = jnp.float32
+bf16 = jnp.bfloat16
 
 
 def lanes():
@@ -48,15 +49,15 @@
 
 
 def pack_kernel(*refs):
-    sources, (own, to_first, to_second), landed = refs[:7], refs[7:10], refs[10:17]
-    flat0, flat1, wide, sems = refs[17:]
+    sources, (own, to_first, to_second, rows_first, rows_second), landed = refs[:7], refs[7:12], refs[12:19]
+    flat0, flat1, wide, sems = refs[19:]
     copies = [pltpu.make_async_copy(src, dst, sems.at[i]) for i, (src, dst) in enumerate(zip(sources, landed))]
     for copy in copies:
         copy.start()
     wide[...] = jnp.zeros_like(wide)
     group = lax.broadcasted_iota(jnp.int32, (16, 128), 1) // 16
     row = lax.broadcasted_iota(jnp.int32, (16, 128), 0) % 8
-    own[STATIC] = jnp.zeros((2, 8, 128), f32)
+    own[:, STATIC] = jnp.zeros((2, 8, 128), f32)
     for copy in copies:
         copy.wait()
     spec, sea, ice, depth, slope, wspeed, wdir = landed
@@ -66,7 +67,7 @@
         moved = pltpu.roll(wide[...], 0, 1, stride=16, stride_axis=0)
         kept = jnp.where(group == row, moved, 0.0)
         for half in range(2):
-            own[STATIC, half, field : field + 1, :] = jnp.sum(
+            own[half, STATIC, field : field + 1, :] = jnp.sum(
                 kept[8 * half : 8 * half + 8], axis=0, keepdims=True
             )
 
@@ -84,26 +85,29 @@
         flat1[low:high, :] = turned[:, 128:]
     inner = lanes() % 16
     even = is_even("lon")
-    sea0 = own[STATIC, 0, SEA : SEA + 1, :]
-    sea1 = own[STATIC, 1, SEA : SEA + 1, :]
+    even_lat = is_even("lat")
+    sea0 = own[0, STATIC, SEA : SEA + 1, :]
+    sea1 = own[1, STATIC, SEA : SEA + 1, :]
     for slab in range(SLABS):
         if slab < NDIR:
             own0 = flat0[pl.ds(slab, FREQ, stride=NDIR), :] * sea0
             own1 = flat1[pl.ds(slab, FREQ, stride=NDIR), :] * sea1
-            own[slab, 0] = own0
-            own[slab, 1] = own1
+            own[0, slab] = own0
+            own[1, slab] = own1
         else:
-            own0 = own[slab, 0]
-            own1 = own[slab, 1]
+            own0 = own[0, slab]
+            own1 = own[1, slab]
         to_east = jnp.where(inner >= 8, own0, roll(own1, -8))
         to_west = jnp.where(inner < 8, own0, roll(own1, 8))
         to_first[slab] = jnp.where(even, to_east, to_west)
         to_second[slab] = jnp.where(even, to_west, to_east)
+        rows_first[slab] = jnp.where(even_lat, own1, own0)
+        rows_second[slab] = jnp.where(even_lat, own0, own1)
 
 
 def growth_kernel(own, consts, gain):
     for half in range(2):
-        point = own[STATIC, half]
+        point = own[half, STATIC]
         turn = point[WDIR : WDIR + 1]
         cos_w = jnp.cos(turn)
         sin_w = jnp.sin(turn)
@@ -114,51 +118,92 @@
             gain[d, half] = jnp.exp(force * along) * share
 
 
-def join_kernel(own, from_first, from_second, to_first, to_second):
-    inner = lanes() % 16
-    even_group = (lanes() // 16) % 2 == 0
+def tables_kernel(place, shifts, gather):
+    chunk = lax.broadcasted_iota(jnp.int32, (16, 128), 0)
+    lane = lax.broadcasted_iota(jnp.int32, (16, 128), 1)
+    low = chunk < 8
+    targets = [
+        40 + chunk,
+        72 + chunk,
+        jnp.where(low, 64 + chunk, 24 + chunk),
+        jnp.where(low, 56 + chunk, 80 + chunk),
+        8 + chunk,
+        jnp.where(low, chunk, 16 + chunk),
+        104 + chunk,
+        jnp.where(low, 120 + chunk, 88 + chunk),
+    ]
+    place[...] = jnp.zeros_like(place)
+    for s, target in enumerate(targets):
+        stripe = (lane == target).astype(f32).astype(bf16)
+        for part in range(2):
+            for t in range(8):
+                row = part * 1024 + s * 128 + 16 * t
+                place[row : row + 16, 128 * t : 128 * t + 128] = stripe
+    row = lax.broadcasted_iota(jnp.int32, (128, 128), 0)
+    col = lax.broadcasted_iota(jnp.int32, (128, 128), 1)
+    for sign, taps in ((0, FORTH_TAPS), (1, BACK_TAPS)):
+        for i, tap in enumerate(taps):
+            moved = (row == (col + tap) % 128).astype(f32).astype(bf16)
+            for part in range(2):
+                shifts[sign, 128 * part : 128 * part + 128, 128 * i : 128 * i + 128] = moved
+    for t in range(8):
+        for half in range(2):
+            from_row = 40 + 32 * half + col % 16
+            moved = ((col // 16 == t) & (row == from_row)).astype(f32).astype(bf16)
+            for part in range(2):
+                at = part * 1024 + 128 * t
+                gather[at : at + 128, 128 * half : 128 * half + 128] = moved
+
+
+def corner_kernel(from_first, from_second, to_first, to_second):
+    low = lanes() % 16 < 8
     even_lon = is_even("lon")
     even_lat = is_even("lat")
     for slab in range(SLABS):
         first, second = from_first[slab], from_second[slab]
         east = jnp.where(even_lon, first, second)
         west = jnp.where(even_lon, second, first)
-        rim0 = jnp.where(inner < 8, roll(east, 16), roll(west, -16))
-        rim1 = jnp.where(inner < 8, roll(east, 8), roll(west, -8))
-        own0 = own[slab, 0]
-        own1 = own[slab, 1]
-        for p in range(2):
-            pick = even_group if p == 0 else ~even_group
-            south_rows = jnp.where(pick, own0, rim0)
-            north_rows = jnp.where(pick, own1, rim1)
-            to_first[slab, p] = jnp.where(even_lat, north_rows, south_rows)
-            to_second[slab, p] = jnp.where(even_lat, south_rows, north_rows)
-
-
-def place_kernel(to_first, to_second, from_first, from_second, consts, q, kx, ky, tx, ty):
-    lane = lanes()
-    even = is_even("lat")
-
-    def assemble(slab):
-        for p in range(2):
-            to1, to2 = to_first[slab, p], to_second[slab, p]
-            from1, from2 = from_first[slab, p], from_second[slab, p]
-            parts = [
-                jnp.where(even, from2, from1),
-                roll(jnp.where(even, to2, to1), 32),
-                roll(jnp.where(even, to1, to2), 64),
-                roll(jnp.where(even, from1, from2), 96),
-            ]
-            for t in range(p, 8, 2):
-                which = ((lane - (16 * t - 8)) % 128) // 32
-                mixed = jnp.where(
-                    which < 2,
-                    jnp.where(which == 0, parts[0], parts[1]),
-                    jnp.where(which == 2, parts[2], parts[3]),
-                )
-                q[slab, t] = roll(mixed, 8 - 16 * t)
-
-    assemble(STATIC)
+        north = jnp.where(low, west, east)
+        south = jnp.where(low, east, west)
+        to_first[slab] = jnp.where(even_lat, north, south)
+        to_second[slab] = jnp.where(even_lat, south, north)
+
+
+def split(x):
+    high = x.astype(bf16)
+    return high, (x - high.astype(f32)).astype(bf16)
+
+
+def place_kernel(
+    own, cols_first, cols_second, rows_first, rows_second, rims_first, rims_second, consts, matrix,
+    q, taps, ky, tx, ty, lhs,
+):
+    even_lon = is_even("lon")
+    even_lat = is_even("lat")
+    blank = jnp.zeros((8, 128), f32)
+
+    def fill(s, array):
+        x = jnp.concatenate([array.reshape(8 * SLABS, 128), blank], axis=0)
+        high, low = split(x)
+        lhs[:, 128 * s : 128 * s + 128] = high
+        lhs[:, 1024 + 128 * s : 1024 + 128 * s + 128] = low
+
+    def pick(flag, first, second):
+        return jnp.where(flag, first[...], second[...])
+
+    fill(0, own[0])
+    fill(1, own[1])
+    fill(2, pick(even_lon, cols_second, cols_first))
+    fill(3, pick(even_lon, cols_first, cols_second))
+    fill(4, pick(even_lat, rows_second, rows_first))
+    fill(5, pick(even_lat, rims_second, rims_first))
+    fill(6, pick(even_lat, rows_first, rows_second))
+    fill(7, pick(even_lat, rims_first, rims_second))
+    for pair in range(4):
+        moved = jnp.dot(lhs[...], matrix[:, 256 * pair : 256 * pair + 256], preferred_element_type=f32)
+        for i in range(2):
+            q[:, 2 * pair + i] = moved[: 8 * SLABS, 128 * i : 128 * i + 128].reshape(SLABS, 8, 128)
+
     speed = []
     for t in range(8):
         point = q[STATIC, t]
@@ -173,16 +218,26 @@
         pace = pace * share
         turning = turning * share
         speed.append(pace)
-        kx[t] = 0.5 * (pace + roll(pace, -1)) * consts[STRETCH, t : t + 1, :]
         tx[t] = turning * point[SLOPE_X : SLOPE_X + 1]
         ty[t] = turning * point[SLOPE_Y : SLOPE_Y + 1]
+        stretch = consts[STRETCH, t : t + 1, :]
+        right = 0.5 * (pace + roll(pace, -1)) * stretch
+        left = 0.5 * (pace + roll(pace, 1)) * stretch
+        for base in range(10):
+            a1, b1, c1 = weights(COS[base] * right)
+            a0, b0, c0 = weights(COS[base] * left)
+            taps[base, 0, 0, t] = 1.0 - a1 + b0
+            taps[base, 0, 1, t] = -b1
+            taps[base, 0, 2, t] = a0 - c1
+            taps[base, 0, 3, t] = c0
+            taps[base, 1, 0, t] = 1.0 + b1 - a0
+            taps[base, 1, 1, t] = a1 - c0
+            taps[base, 1, 2, t] = -b0
+            taps[base, 1, 3, t] = c1
     for t in range(8):
         ahead = speed[t + 1] if t < 7 else roll(speed[0], -32)
         ky[t] = 0.5 * (speed[t] + ahead)
 
-    for d in range(NDIR):
-        assemble(d)
-
 
 def flux(q, diff, curve, k, u, w):
     return k * (q + u * (diff - w * curve))
@@ -192,29 +247,35 @@
     return 0.5 - 0.5 * k, (1.0 / 3.0) + (1.0 / 3.0) * k
 
 
-def lon_kernel(q, kx, out):
-    for t in range(8):
-        face = kx[t]
+def weights(k):
+    u, w = halves(k)
+    bend = k * u * w
+    return k - k * u + 2.0 * bend, k * u - bend, -bend
+
+
+FORTH_TAPS = (1, -1, -2)
+BACK_TAPS = (1, -1, 2)
+
+
+def lon_kernel(q, taps, shifts, out, moved):
+    for quadrant, sign in ((0, 0), (3, 0), (1, 1), (2, 1)):
+        x = q[9 * quadrant : 9 * quadrant + 9].reshape(576, 128)
+        lhs = jnp.concatenate(split(x), axis=1)
+        moved[quadrant] = jnp.dot(lhs, shifts[sign], preferred_element_type=f32)
+    for sign in range(2):
         for base in range(10):
             if base == 0:
-                forth, back = [0], [18]
+                dirs = [[0], [18]][sign]
             elif base == 9:
-                forth, back = [27], [9]
+                dirs = [[27], [9]][sign]
             else:
-                forth, back = [base, 36 - base], [18 - base, 18 + base]
-            k = COS[base] * face
-            u, w = halves(k)
-            for d in forth:
-                cell = q[d, t]
-                diff = roll(cell, -1) - cell
-                f = flux(cell, diff, diff - roll(diff, 1), k, u, w)
-                out[d, t] = cell - f + roll(f, 1)
-            for d in back:
-                cell = q[d, t]
-                ahead = roll(cell, -1)
-                diff = cell - ahead
-                f = flux(ahead, diff, diff - roll(diff, -1), k, u, w)
-                out[d, t] = cell + f - roll(f, 1)
+                dirs = [[base, 36 - base], [18 - base, 18 + base]][sign]
+            for t in range(8):
+                tap = [taps[base, sign, i, t] for i in range(4)]
+                for d in dirs:
+                    at = 64 * (d % 9) + 8 * t
+                    near = [moved[d // 9, at : at + 8, 128 * i : 128 * i + 128] for i in range(3)]
+                    out[d, t] = (tap[0] * q[d, t] + tap[1] * near[0]) + (tap[2] * near[1] + tap[3] * near[2])
 
 
 def lat_kernel(q, ky, consts, out):
@@ -294,21 +355,17 @@
         one(t)
 
 
-def gather_kernel(q, consts, own, sums):
-    lane = lanes()
+def gather_kernel(q, consts, matrix, own, sums, lhs):
     zero = jnp.zeros((8, 128), f32)
-
+    for t in range(8):
+        high, low = split(q[:, t].reshape(8 * NDIR, 128))
+        lhs[:, 128 * t : 128 * t + 128] = high
+        lhs[:, 1024 + 128 * t : 1024 + 128 * t + 128] = low
+    moved = jnp.dot(lhs[...], matrix[...], preferred_element_type=f32)
     totals = [zero, zero]
-    for d in range(NDIR):
-        halves_of = [zero, zero]
-        for t in range(8):
-            moved = roll(q[d, t], 16 * t - 40)
-            halves_of[0] = jnp.where(lane // 16 == t, moved, halves_of[0])
-            halves_of[1] = jnp.where(lane // 16 == (t + 2) % 8, moved, halves_of[1])
-        halves_of[1] = roll(halves_of[1], -32)
-        for half in range(2):
-            own[d, half] = halves_of[half]
-            totals[half] = totals[half] + halves_of[half]
+    for half in range(2):
+        own[half] = moved[:, 128 * half : 128 * half + 128].reshape(NDIR, 8, 128)
+        totals[half] = jnp.sum(own[half], axis=0)
     level = consts[LEVEL]
     sums[...] = zero
     for half in range(2):
@@ -325,22 +382,22 @@
         mean = energy / NCOMP
         level = consts[LEVEL]
         breaking = break_coef * level * level / mean_level * (mean * mean)
-        damping = static[0, half, ICE : ICE + 1] * consts[ICE_RATE]
+        damping = static[half, 0, ICE : ICE + 1] * consts[ICE_RATE]
         loss = jnp.exp(-breaking - damping)
         for d in range(NDIR):
-            flat[pl.ds(d, FREQ, stride=NDIR), :] = own[d, half] * gain[d, half] * loss
+            flat[pl.ds(d, FREQ, stride=NDIR), :] = own[half, d] * gain[d, half] * loss
         for low, high in ((0, 128), (128, 256), (256, 288)):
             turned = flat[low:high, :].T
             out[8 * half : 8 * half + 8, :, low:high] = turned.reshape(8, 16, high - low)
 
 
-PARAMS = pltpu.CompilerParams(vmem_limit_bytes=32 * 2**20)
-
-
-def call(kernel, ins, outs, scratch=(), name=None, space=pltpu.VMEM):
+PARAMS = pltpu.CompilerParams(vmem_limit_bytes=40 * 2**20)
+
+
+def call(kernel, ins, outs, scratch=(), name=None, space=pltpu.VMEM, dtype=f32):
     return pl.pallas_call(
         kernel,
-        out_shape=[jax.ShapeDtypeStruct(shape, f32) for shape in outs],
+        out_shape=[jax.ShapeDtypeStruct(shape, dtype) for shape in outs],
         in_specs=[pl.BlockSpec(memory_space=space)] * ins,
         out_specs=[pl.BlockSpec(memory_space=pltpu.VMEM)] * len(outs),
         scratch_shapes=list(scratch),
@@ -400,32 +457,44 @@
 
     tile = (8, 128)
     inputs = [spectrum, sea_mask, ice_mask, depth_class, depth_slope, wind_speed, wind_dir]
-    own, to_first, to_second = call(
+    slabs = (SLABS,) + tile
+    own, to_first, to_second, edge_first, edge_second = call(
         pack_kernel,
         7,
-        [(SLABS, 2) + tile, (SLABS,) + tile, (SLABS,) + tile],
+        [(2,) + slabs] + [slabs] * 4,
         [pltpu.VMEM(x.shape, x.dtype) for x in inputs]
         + [pltpu.VMEM((NDIR * FREQ, 128), f32)] * 2
         + [pltpu.VMEM((16, 128), f32), pltpu.SemaphoreType.DMA((7,))],
         name="pack",
         space=pltpu.HBM,
     )(*[pltpu.with_memory_space_constraint(x, pltpu.HBM) for x in inputs])
-    from_second = swap(to_second, "lon", 1, True)
-    from_first = swap(to_first, "lon", 0, True)
+    cols_second = swap(to_second, "lon", 1, True)
+    cols_first = swap(to_first, "lon", 0, True)
+    rows_second = swap(edge_second, "lat", 1)
+    rows_first = swap(edge_first, "lat", 0)
     (gain,) = call(growth_kernel, 2, [(NDIR, 2) + tile], name="growth")(own, consts)
-    to_first, to_second = call(join_kernel, 3, [(SLABS, 2) + tile] * 2, name="join")(own, from_first, from_second)
-    from_second = swap(to_second, "lat", 1)
-    from_first = swap(to_first, "lat", 0)
+    place, shifts, gather = call(
+        tables_kernel, 0, [(2048, 1024), (2, 256, 384), (2048, 256)], name="tables", dtype=bf16
+    )()
+    to_first, to_second = call(corner_kernel, 2, [slabs] * 2, name="corner")(cols_first, cols_second)
+    rims_second = swap(to_second, "lat", 1)
+    rims_first = swap(to_first, "lat", 0)
     block = (8,) + tile
-    q, kx, ky, tx, ty = call(place_kernel, 5, [(SLABS,) + block] + [block] * 4, name="place")(
-        to_first, to_second, from_first, from_second, consts
-    )
+    q, taps, ky, tx, ty = call(
+        place_kernel,
+        9,
+        [(SLABS,) + block, (10, 2, 4) + block] + [block] * 3,
+        [pltpu.VMEM((8 * SLABS + 8, 2048), bf16)],
+        name="place",
+    )(own, cols_first, cols_second, rows_first, rows_second, rims_first, rims_second, consts, place)
     cells = [(NDIR,) + block]
     for substep in range(ITERS):
-        (q,) = call(lon_kernel, 2, cells, name="lon")(q, kx)
+        (q,) = call(lon_kernel, 3, cells, [pltpu.VMEM((4, 576, 384), f32)], name="lon")(q, taps, shifts)
         (q,) = call(lat_kernel, 3, cells, name="lat")(q, ky, consts)
         (q,) = call(turn_kernel, 3, cells, name="turn")(q, tx, ty)
-    last, sums = call(gather_kernel, 2, [(NDIR, 2) + tile, tile], name="gather")(q, consts)
+    last, sums = call(
+        gather_kernel, 3, [(2, NDIR) + tile, tile], [pltpu.VMEM((8 * NDIR, 2048), bf16)], name="gather"
+    )(q, consts, gather)
     other = swap(sums, "band", 0)
     (out,) = call(
         finish_kernel,
@@ -433,7 +502,7 @@
         [spectrum.shape],
         [pltpu.VMEM((NDIR * FREQ, 128), f32)] * 2,
         name="finish",
-    )(last, gain, own[STATIC:], sums, other, consts)
+    )(last, gain, own[:, STATIC:], sums, other, consts)
     return out
 
 

time: 105 us -> 35 us (0.33)
  Pallas kernels: 81.7 us -> 13.6 us
  waiting for transfers between devices: 12.7 us -> 7.91 us
  starting transfers between devices: 8.28 us -> 10.8 us
    pallas_call x8 -> x9, Pallas kernels: 75.8 us -> 7.66 us  [the longest x4 3.13 us: per_device(): call(lon_kernel, 3, cells, [pltpu.VMEM((4, 576, 384), f32)], name='lon')]
    ppermute x5 -> x7, waiting for transfers between devices: 12.7 us -> 7.91 us  [swap(): return lax.ppermute(array, axis, pairs)]
    ppermute x5 -> x7, starting transfers between devices: 8.28 us -> 10.8 us  [swap(): return lax.ppermute(array, axis, pairs)]
  transfers between devices with their start and end apart: 5 -> 7, of which waited for: 3 -> 3; matrix products, arithmetic and copies ran while one was open for 2% -> 5% of each run, Pallas kernels for 0% -> 2%
where the time goes in v4:
time: 35 us; the launch traced here: 34.4 us
  Pallas kernels  13.6 us (39%)
  starting transfers between devices  10.8 us (31%)
  waiting for transfers between devices  7.91 us (23%)
  local copies, waits for them, and re-layouts  1.81 us (5%)
    ppermute x7, starting transfers between devices, swap(): return lax.ppermute(array, axis, pairs)  10.8 us
    ppermute x7, waiting for transfers between devices, swap(): return lax.ppermute(array, axis, pairs)  7.91 us
    pallas_call x4, Pallas kernels, per_device(): call(lon_kernel, 3, cells, [pltpu.VMEM((4, 576, 384), f32)], name='lon')  3.13 us
    pallas_call x4, Pallas kernels, per_device(): q, = call(turn_kernel, 3, cells, name='turn')(q, tx, ty)  2.66 us
    pallas_call x4, Pallas kernels, per_device(): q, = call(lat_kernel, 3, cells, name='lat')(q, ky, consts)  2.17 us
    pallas_call x1, Pallas kernels, per_device(): call(place_kernel, 9, [(SLABS,) + block, (10, 2, 4) + block] + [block] *...  2.01 us
    pallas_call x1, Pallas kernels, per_device(): call(pack_kernel, 7, [(2,) + slabs] + [slabs] * 4, [pltpu.VMEM(x.shape, x...  1.43 us
    pallas_call x1, Pallas kernels, per_device(): call(finish_kernel, 6, [spectrum.shape], [pltpu.VMEM((NDIR * FREQ, 128),...  0.97 us
  transfers between devices with their start and end apart: 7, of which 3 were waited for; matrix products, arithmetic and copies ran while one was open for 5% of the time, Pallas kernels for 2%

profile of v4, /device:TPU:2, one launch (start us, length us, event | category | flops | bytes accessed | tf_op | source)
XLA Modules:
  0.0 34.4 jit_solution(8808246630400285144)
XLA Ops:
  0.0 1.4 %pack.1 = (f32[2,37,8,128]{3,2,1,0:T(8,128)S(1)}, f32[37,8,128]{2,1,0:T(8,128)S(1)}, f32[37,8,128]{2,1,0:T(8,128)S(1)}, f32[37,8,128]{2,1,0:T(8,128)S(1)}, f32[37,8,128]{2,1,0:T(8,128)S(1)}) custom-call(f32[16,16,288]{2,1,0:T(8,128)} %refs_0_.1, s32[16,16]{1,0:T(8,128)} %refs_1_.1, s32[16,16]{1,0:T(8,128)} %refs_2_.1, s32[16,16]{1,0:T(8,128)} %refs_3_.1, ...), custom_call_target="tpu_custom_call" | custom-call | tf_op jit(solution)/shard_map/pack/pallas_call | solution.py:461
  1.4 1.6 %collective-permute-start = (f32[37,8,128]{2,1,0:T(8,128)S(1)}, f32[37,8,128]{2,1,0:T(8,128)S(1)}, u32[]{:S(2)}, u32[]{:S(2)}) collective-permute-start(f32[37,8,128]{2,1,0:T(8,128)S(1)} %get-tuple-element.23), channel_id=1, source_target_pairs={{0,8},{8,0},{16,24},{24,16},{1,9},{9,1},{17,25},{25,17},{2,10},{10... | collective-permute-start | bytes 454664 | tf_op jit(solution)/shard_map/ppermute | solution.py:416
  3.1 2.5 %collective-permute-start.1 = (f32[37,8,128]{2,1,0:T(8,128)S(1)}, f32[37,8,128]{2,1,0:T(8,128)S(1)}, u32[]{:S(2)}, u32[]{:S(2)}) collective-permute-start(f32[37,8,128]{2,1,0:T(8,128)S(1)} %get-tuple-element.24), channel_id=1, source_target_pairs={{8,16},{16,8},{24,0},{0,24},{9,17},{17,9},{25,1},{1,25},{10,18},{1... | collective-permute-start | bytes 454664 | tf_op jit(solution)/shard_map/ppermute | solution.py:416
  5.6 2.5 %collective-permute-start.3 = (f32[37,8,128]{2,1,0:T(8,128)S(1)}, f32[37,8,128]{2,1,0:T(8,128)S(1)}, u32[]{:S(2)}, u32[]{:S(2)}) collective-permute-start(f32[37,8,128]{2,1,0:T(8,128)S(1)} %get-tuple-element.26), channel_id=1, source_target_pairs={{2,4},{4,2},{3,5},{5,3},{10,12},{12,10},{11,13},{13,11},{18,20},{2... | collective-permute-start | bytes 454664 | tf_op jit(solution)/shard_map/ppermute | solution.py:416
  8.1 0.8 %constant_dynamic-slice_fusion = (f32[8,8]{1,0:T(8,128)S(1)}, f32[8,8]{1,0:T(8,128)S(1)}) fusion(f32[8,16]{1,0:T(8,128)} %param.15, s32[]{:T(128)S(6)} %select_n.22, f32[8,16]{1,0:T(8,128)} %param.14), kind=kLoop, calls=%fused_computation.13 | loop fusion | bytes 1028 | tf_op jit(solution)/shard_map/dynamic_slice | solution.py:437
  8.9 0.1 broadcast_dynamic-update-slice_fusion.1
  9.0 0.7 %dynamic_slice.11 = f32[8]{0:T(128)S(1)} dynamic-slice(f32[16]{0:T(128)} %param.19, s32[]{:T(128)S(6)} %select_n.22), dynamic_slice_sizes={8} | dynamic-slice | bytes 68 | tf_op jit(solution)/shard_map/dynamic_slice | solution.py:445
  9.7 0.1 broadcast_dynamic-update-slice_fusion
  9.9 0.1 constant_dynamic-update-slice_fusion.1
  9.9 0.5 %tables.1 = (bf16[2048,1024]{1,0:T(8,128)(2,1)S(1)}, bf16[2,256,384]{2,1,0:T(8,128)(2,1)S(1)}, bf16[2048,256]{1,0:T(8,128)(2,1)S(1)}) custom-call(), custom_call_target="tpu_custom_call" | custom-call | tf_op jit(solution)/shard_map/tables/pallas_call | solution.py:476
  10.5 2.1 %collective-permute-done.1.from_second.cols_second = f32[37,8,128]{2,1,0:T(8,128)S(1)} collective-permute-done((f32[37,8,128]{2,1,0:T(8,128)S(1)}, f32[37,8,128]{2,1,0:T(8,128)S(1)}, u32[]{:S(2)}, u32[]{:S(2)}) %collective-permute-start.1) | collective-permute-done | bytes 151584 | tf_op jit(solution)/shard_map/ppermute | solution.py:416
  12.6 0.1 collective-permute-start.4
  12.7 2.5 %collective-permute-start.5 = (f32[37,8,128]{2,1,0:T(8,128)S(1)}, f32[37,8,128]{2,1,0:T(8,128)S(1)}, u32[]{:S(2)}, u32[]{:S(2)}) collective-permute-start(f32[37,8,128]{2,1,0:T(8,128)S(1)} %get-tuple-element.28), channel_id=1, source_target_pairs={{2,4},{4,2},{3,5},{5,3},{10,12},{12,10},{11,13},{13,11},{18,20},{2... | collective-permute-start | bytes 454664 | tf_op jit(solution)/shard_map/ppermute | solution.py:416
  15.3 3.9 %collective-permute-done.5.rims_second = f32[37,8,128]{2,1,0:T(8,128)S(1)} collective-permute-done((f32[37,8,128]{2,1,0:T(8,128)S(1)}, f32[37,8,128]{2,1,0:T(8,128)S(1)}, u32[]{:S(2)}, u32[]{:S(2)}) %collective-permute-start.5) | collective-permute-done | bytes 151584 | tf_op jit(solution)/shard_map/ppermute | solution.py:416
  19.2 2.0 %place.1 = (f32[37,8,8,128]{3,2,1,0:T(8,128)S(1)}, f32[10,2,4,8,8,128]{5,4,3,2,1,0:T(8,128)S(1)}, f32[8,8,128]{2,1,0:T(8,128)S(1)}, f32[8,8,128]{2,1,0:T(8,128)S(1)}, f32[8,8,128]{2,1,0:T(8,128)S(1)}) custom-call(f32[2,37,8,128]{3,2,1,0:T(8,128)S(1)} %get-tuple-element.22.own, f32[37,8,128]{2,1,0:T(8,128)S(1)} %collective-permute-done.from_first.cols_first, ...), custom_call_target="tpu_custom_call" | custom-call | tf_op jit(solution)/shard_map/place/pallas_call | solution.py:483
  21.2 0.8 %lon.4.q = f32[36,8,8,128]{3,2,1,0:T(8,128)S(1)} custom-call(f32[37,8,8,128]{3,2,1,0:T(8,128)S(1)} %get-tuple-element.30.q, f32[10,2,4,8,8,128]{5,4,3,2,1,0:T(8,128)S(1)} %get-tuple-element.31.taps, bf16[2,256,384]{2,1,0:T(8,128)(2,1)S(1)} %get-tuple-element.32.shifts), custom_call_target="tpu_custom_call" | custom-call | tf_op jit(solution)/shard_map/lon/pallas_call | solution.py:492
  22.0 0.5 %lat.4.q = f32[36,8,8,128]{3,2,1,0:T(8,128)S(1)} custom-call(f32[36,8,8,128]{3,2,1,0:T(8,128)S(1)} %lon.4.q, f32[8,8,128]{2,1,0:T(8,128)S(1)} %get-tuple-element.33.ky, f32[20,8,128]{2,1,0:T(8,128)S(1)} %constant_dynamic-update-slice_fusion.consts), custom_call_target="tpu_custom_call" | custom-call | tf_op jit(solution)/shard_map/lat/pallas_call | solution.py:493
  22.5 0.7 %turn.4.q = f32[36,8,8,128]{3,2,1,0:T(8,128)S(1)} custom-call(f32[36,8,8,128]{3,2,1,0:T(8,128)S(1)} %lat.4.q, f32[8,8,128]{2,1,0:T(8,128)S(1)} %get-tuple-element.34.tx, f32[8,8,128]{2,1,0:T(8,128)S(1)} %get-tuple-element.35.ty), custom_call_target="tpu_custom_call" | custom-call | tf_op jit(solution)/shard_map/turn/pallas_call | solution.py:494
  23.2 0.8 %lon.5.q = f32[36,8,8,128]{3,2,1,0:T(8,128)S(1)} custom-call(f32[36,8,8,128]{3,2,1,0:T(8,128)S(1)} %turn.4.q, f32[10,2,4,8,8,128]{5,4,3,2,1,0:T(8,128)S(1)} %get-tuple-element.31.taps, bf16[2,256,384]{2,1,0:T(8,128)(2,1)S(1)} %get-tuple-element.32.shifts), custom_call_target="tpu_custom_call" | custom-call | tf_op jit(solution)/shard_map/lon/pallas_call | solution.py:492
  24.0 0.5 %lat.5.q = f32[36,8,8,128]{3,2,1,0:T(8,128)S(1)} custom-call(f32[36,8,8,128]{3,2,1,0:T(8,128)S(1)} %lon.5.q, f32[8,8,128]{2,1,0:T(8,128)S(1)} %get-tuple-element.33.ky, f32[20,8,128]{2,1,0:T(8,128)S(1)} %constant_dynamic-update-slice_fusion.consts), custom_call_target="tpu_custom_call" | custom-call | tf_op jit(solution)/shard_map/lat/pallas_call | solution.py:493
  24.6 0.7 %turn.5.q = f32[36,8,8,128]{3,2,1,0:T(8,128)S(1)} custom-call(f32[36,8,8,128]{3,2,1,0:T(8,128)S(1)} %lat.5.q, f32[8,8,128]{2,1,0:T(8,128)S(1)} %get-tuple-element.34.tx, f32[8,8,128]{2,1,0:T(8,128)S(1)} %get-tuple-element.35.ty), custom_call_target="tpu_custom_call" | custom-call | tf_op jit(solution)/shard_map/turn/pallas_call | solution.py:494
  25.2 0.8 %lon.6.q = f32[36,8,8,128]{3,2,1,0:T(8,128)S(1)} custom-call(f32[36,8,8,128]{3,2,1,0:T(8,128)S(1)} %turn.5.q, f32[10,2,4,8,8,128]{5,4,3,2,1,0:T(8,128)S(1)} %get-tuple-element.31.taps, bf16[2,256,384]{2,1,0:T(8,128)(2,1)S(1)} %get-tuple-element.32.shifts), custom_call_target="tpu_custom_call" | custom-call | tf_op jit(solution)/shard_map/lon/pallas_call | solution.py:492
  26.0 0.5 %lat.6.q = f32[36,8,8,128]{3,2,1,0:T(8,128)S(1)} custom-call(f32[36,8,8,128]{3,2,1,0:T(8,128)S(1)} %lon.6.q, f32[8,8,128]{2,1,0:T(8,128)S(1)} %get-tuple-element.33.ky, f32[20,8,128]{2,1,0:T(8,128)S(1)} %constant_dynamic-update-slice_fusion.consts), custom_call_target="tpu_custom_call" | custom-call | tf_op jit(solution)/shard_map/lat/pallas_call | solution.py:493
  26.6 0.7 %turn.6.q = f32[36,8,8,128]{3,2,1,0:T(8,128)S(1)} custom-call(f32[36,8,8,128]{3,2,1,0:T(8,128)S(1)} %lat.6.q, f32[8,8,128]{2,1,0:T(8,128)S(1)} %get-tuple-element.34.tx, f32[8,8,128]{2,1,0:T(8,128)S(1)} %get-tuple-element.35.ty), custom_call_target="tpu_custom_call" | custom-call | tf_op jit(solution)/shard_map/turn/pallas_call | solution.py:494
  27.2 0.8 %lon.7.q = f32[36,8,8,128]{3,2,1,0:T(8,128)S(1)} custom-call(f32[36,8,8,128]{3,2,1,0:T(8,128)S(1)} %turn.6.q, f32[10,2,4,8,8,128]{5,4,3,2,1,0:T(8,128)S(1)} %get-tuple-element.31.taps, bf16[2,256,384]{2,1,0:T(8,128)(2,1)S(1)} %get-tuple-element.32.shifts), custom_call_target="tpu_custom_call" | custom-call | tf_op jit(solution)/shard_map/lon/pallas_call | solution.py:492
  28.0 0.5 %lat.7.q = f32[36,8,8,128]{3,2,1,0:T(8,128)S(1)} custom-call(f32[36,8,8,128]{3,2,1,0:T(8,128)S(1)} %lon.7.q, f32[8,8,128]{2,1,0:T(8,128)S(1)} %get-tuple-element.33.ky, f32[20,8,128]{2,1,0:T(8,128)S(1)} %constant_dynamic-update-slice_fusion.consts), custom_call_target="tpu_custom_call" | custom-call | tf_op jit(solution)/shard_map/lat/pallas_call | solution.py:493
  28.6 0.7 %turn.7.q = f32[36,8,8,128]{3,2,1,0:T(8,128)S(1)} custom-call(f32[36,8,8,128]{3,2,1,0:T(8,128)S(1)} %lat.7.q, f32[8,8,128]{2,1,0:T(8,128)S(1)} %get-tuple-element.34.tx, f32[8,8,128]{2,1,0:T(8,128)S(1)} %get-tuple-element.35.ty), custom_call_target="tpu_custom_call" | custom-call | tf_op jit(solution)/shard_map/turn/pallas_call | solution.py:494
  29.2 0.5 %gather.1 = (f32[2,36,8,128]{3,2,1,0:T(8,128)S(1)}, f32[8,128]{1,0:T(8,128)S(1)}) custom-call(f32[36,8,8,128]{3,2,1,0:T(8,128)S(1)} %turn.7.q, f32[20,8,128]{2,1,0:T(8,128)S(1)} %constant_dynamic-update-slice_fusion.consts, bf16[2048,256]{1,0:T(8,128)(2,1)S(1)} %get-tuple-element.36.matrix), custom_call_target="tpu_custom_call" | custom-call | tf_op jit(solution)/shard_map/gather/pallas_call | solution.py:495
  29.8 1.6 %collective-permute-start.6 = (f32[8,128]{1,0:T(8,128)S(1)}, f32[8,128]{1,0:T(8,128)S(1)}, u32[]{:S(2)}, u32[]{:S(2)}) collective-permute-start(f32[8,128]{1,0:T(8,128)S(1)} %get-tuple-element.38.sums), channel_id=1, source_target_pairs={{0,1},{1,0},{2,3},{3,2},{4,5},{5,4},{6,7},{7,6},{8,9},{9,8},{10,11... | collective-permute-start | bytes 12296 | tf_op jit(solution)/shard_map/ppermute | solution.py:416
  31.4 0.1 growth.1.gain
  31.5 1.9 %collective-permute-done.6.other = f32[8,128]{1,0:T(8,128)S(1)} collective-permute-done((f32[8,128]{1,0:T(8,128)S(1)}, f32[8,128]{1,0:T(8,128)S(1)}, u32[]{:S(2)}, u32[]{:S(2)}) %collective-permute-start.6) | collective-permute-done | bytes 4128 | tf_op jit(solution)/shard_map/ppermute | solution.py:416
  33.5 1.0 %finish.1 = f32[16,16,288]{2,1,0:T(8,128)} custom-call(f32[2,36,8,128]{3,2,1,0:T(8,128)S(1)} %get-tuple-element.37.own, f32[36,2,8,128]{3,2,1,0:T(8,128)S(1)} %growth.1.gain, f32[2,1,8,128]{3,2,1,0:T(8,128)S(1)} %slice.3.static, f32[8,128]{1,0:T(8,128)S(1)} %get-tuple-element.38.sums, f32[8,128]{1,0:T(8,128)S(1)} %collective-permute-done.6.other, ...), custom_call_target="tpu_custom_call" | custom-call | tf_op jit(solution)/shard_map/finish/pallas_call | solution.py:499
  (13 shorter events, 0.2 us)
Async XLA Ops:
  1.4 9.0 %collective-permute-start = (f32[37,8,128]{2,1,0:T(8,128)S(1)}, f32[37,8,128]{2,1,0:T(8,128)S(1)}, u32[]{:S(2)}, u32[]{:S(2)}) collective-permute-start(f32[37,8,128]{2,1,0:T(8,128)S(1)} %get-tuple-element.23), channel_id=1, source_target_pairs={{0,8},{8,0},{16,24},{24,16},{1,9},{9,1},{17,25},{25,17},{2,10},{10... | collective-permute-start | bytes 454664 | tf_op jit(solution)/shard_map/ppermute | solution.py:416
  3.1 9.5 %collective-permute-start.1 = (f32[37,8,128]{2,1,0:T(8,128)S(1)}, f32[37,8,128]{2,1,0:T(8,128)S(1)}, u32[]{:S(2)}, u32[]{:S(2)}) collective-permute-start(f32[37,8,128]{2,1,0:T(8,128)S(1)} %get-tuple-element.24), channel_id=1, source_target_pairs={{8,16},{16,8},{24,0},{0,24},{9,17},{17,9},{25,1},{1,25},{10,18},{1... | collective-permute-start | bytes 454664 | tf_op jit(solution)/shard_map/ppermute | solution.py:416
  5.6 9.7 %collective-permute-start.2 = (f32[37,8,128]{2,1,0:T(8,128)S(1)}, f32[37,8,128]{2,1,0:T(8,128)S(1)}, u32[]{:S(2)}, u32[]{:S(2)}) collective-permute-start(f32[37,8,128]{2,1,0:T(8,128)S(1)} %get-tuple-element.25), channel_id=1, source_target_pairs={{0,2},{2,0},{4,6},{6,4},{1,3},{3,1},{5,7},{7,5},{8,10},{10,8},{12,... | collective-permute-start | bytes 454664 | tf_op jit(solution)/shard_map/ppermute | solution.py:416
  5.6 9.7 %collective-permute-start.3 = (f32[37,8,128]{2,1,0:T(8,128)S(1)}, f32[37,8,128]{2,1,0:T(8,128)S(1)}, u32[]{:S(2)}, u32[]{:S(2)}) collective-permute-start(f32[37,8,128]{2,1,0:T(8,128)S(1)} %get-tuple-element.26), channel_id=1, source_target_pairs={{2,4},{4,2},{3,5},{5,3},{10,12},{12,10},{11,13},{13,11},{18,20},{2... | collective-permute-start | bytes 454664 | tf_op jit(solution)/shard_map/ppermute | solution.py:416
  12.6 2.7 %collective-permute-start.4 = (f32[37,8,128]{2,1,0:T(8,128)S(1)}, f32[37,8,128]{2,1,0:T(8,128)S(1)}, u32[]{:S(2)}, u32[]{:S(2)}) collective-permute-start(f32[37,8,128]{2,1,0:T(8,128)S(1)} %get-tuple-element.27), channel_id=1, source_target_pairs={{0,2},{2,0},{4,6},{6,4},{1,3},{3,1},{5,7},{7,5},{8,10},{10,8},{12,... | collective-permute-start | bytes 454664 | tf_op jit(solution)/shard_map/ppermute | solution.py:416
  12.7 6.5 %collective-permute-start.5 = (f32[37,8,128]{2,1,0:T(8,128)S(1)}, f32[37,8,128]{2,1,0:T(8,128)S(1)}, u32[]{:S(2)}, u32[]{:S(2)}) collective-permute-start(f32[37,8,128]{2,1,0:T(8,128)S(1)} %get-tuple-element.28), channel_id=1, source_target_pairs={{2,4},{4,2},{3,5},{5,3},{10,12},{12,10},{11,13},{13,11},{18,20},{2... | collective-permute-start | bytes 454664 | tf_op jit(solution)/shard_map/ppermute | solution.py:416
  29.8 3.7 %collective-permute-start.6 = (f32[8,128]{1,0:T(8,128)S(1)}, f32[8,128]{1,0:T(8,128)S(1)}, u32[]{:S(2)}, u32[]{:S(2)}) collective-permute-start(f32[8,128]{1,0:T(8,128)S(1)} %get-tuple-element.38.sums), channel_id=1, source_target_pairs={{0,1},{1,0},{2,3},{3,2},{4,5},{5,4},{6,7},{7,6},{8,9},{9,8},{10,11... | collective-permute-start | bytes 12296 | tf_op jit(solution)/shard_map/ppermute | solution.py:416

commit v5 on v4

--- a/solution.py
+++ b/solution.py
@@ -1,3 +1,4 @@
+import functools
 import math
 
 import jax
@@ -14,6 +15,7 @@
 NCLASS = 8
 FREQ = 8
 HALO = 8
+ROWS = 16
 STATIC = NDIR
 SLABS = NDIR + 1
 SEA, DEPTH, SLOPE_X, SLOPE_Y, ICE, WIND, WDIR = range(7)
@@ -49,9 +51,12 @@
 
 
 def pack_kernel(*refs):
-    sources, (own, to_first, to_second, rows_first, rows_second), landed = refs[:7], refs[7:12], refs[12:19]
-    flat0, flat1, wide, sems = refs[19:]
-    copies = [pltpu.make_async_copy(src, dst, sems.at[i]) for i, (src, dst) in enumerate(zip(sources, landed))]
+    sources, own, tables = refs[:10], refs[10], refs[11:14]
+    landed = refs[14:21]
+    flat0, flat1, wide, sems = refs[21:]
+    copies = [
+        pltpu.make_async_copy(src, dst, sems.at[i]) for i, (src, dst) in enumerate(zip(sources, landed + tables))
+    ]
     for copy in copies:
         copy.start()
     wide[...] = jnp.zeros_like(wide)
@@ -83,26 +88,29 @@
         turned = grid[:, low:high].T
         flat0[low:high, :] = turned[:, :128]
         flat1[low:high, :] = turned[:, 128:]
-    inner = lanes() % 16
-    even = is_even("lon")
-    even_lat = is_even("lat")
     sea0 = own[0, STATIC, SEA : SEA + 1, :]
     sea1 = own[1, STATIC, SEA : SEA + 1, :]
+    for d in range(NDIR):
+        own[0, d] = flat0[pl.ds(d, FREQ, stride=NDIR), :] * sea0
+        own[1, d] = flat1[pl.ds(d, FREQ, stride=NDIR), :] * sea1
+
+
+def column_kernel(second, own, message):
+    inner = lanes() % 16
+    to_east = is_even("lon") != second
     for slab in range(SLABS):
-        if slab < NDIR:
-            own0 = flat0[pl.ds(slab, FREQ, stride=NDIR), :] * sea0
-            own1 = flat1[pl.ds(slab, FREQ, stride=NDIR), :] * sea1
-            own[0, slab] = own0
-            own[1, slab] = own1
-        else:
-            own0 = own[0, slab]
-            own1 = own[1, slab]
-        to_east = jnp.where(inner >= 8, own0, roll(own1, -8))
-        to_west = jnp.where(inner < 8, own0, roll(own1, 8))
-        to_first[slab] = jnp.where(even, to_east, to_west)
-        to_second[slab] = jnp.where(even, to_west, to_east)
-        rows_first[slab] = jnp.where(even_lat, own1, own0)
-        rows_second[slab] = jnp.where(even_lat, own0, own1)
+        own0, own1 = own[0, slab], own[1, slab]
+        east = jnp.where(inner >= 8, own0, roll(own1, -8))
+        west = jnp.where(inner < 8, own0, roll(own1, 8))
+        message[slab] = jnp.where(to_east, east, west)
+
+
+def edge_kernel(second, own, edge):
+    even = is_even("lat")
+    if second:
+        edge[...] = jnp.where(even, own[0], own[1])
+    else:
+        edge[...] = jnp.where(even, own[1], own[0])
 
 
 def growth_kernel(own, consts, gain):
@@ -118,7 +126,36 @@
             gain[d, half] = jnp.exp(force * along) * share
 
 
-def tables_kernel(place, shifts, gather):
+def tables_kernel(speed_table, refraction_table, ice_rate, place, rims, shifts, gather, spread, consts):
+    first = lax.axis_index("band") * FREQ
+    sub = lax.broadcasted_iota(jnp.int32, (8, 128), 0)
+    mine = lanes() == first + sub
+
+    def column(row):
+        picked = jnp.where(mine, jnp.broadcast_to(row, (8, 128)), 0.0)
+        return jnp.broadcast_to(jnp.sum(picked, axis=1, keepdims=True), (8, 128))
+
+    def widen(values):
+        return jnp.concatenate([values, jnp.zeros((values.shape[0], 112), f32)], axis=1)
+
+    for at, table in ((TAB_SPEED, speed_table), (TAB_TURN, refraction_table)):
+        wide = widen(table[...])
+        for c in range(NCLASS):
+            consts[at + c] = column(wide[c : c + 1])
+    consts[ICE_RATE] = column(widen(ice_rate[...].reshape(1, 16)))
+    consts[LEVEL] = jnp.exp(math.log(freq_ratio) * (first + sub).astype(f32))
+    lat = lax.axis_index("lat")
+    lats = lax.axis_size("lat")
+    group = lanes() // 32
+    rows = lat * ROWS - HALO + 8 * group + sub
+    latitude = (south_edge + band_span * (rows.astype(f32) + 0.5) / (ROWS * lats)) * (math.pi / 180.0)
+    consts[STRETCH] = 1.0 / jnp.cos(latitude)
+    ghost = ((group == 0) & (lat == 0)) | ((group == 3) & (lat == lats - 1))
+    consts[LIVE] = jnp.where(ghost, 0.0, 1.0)
+    comp = lax.broadcasted_iota(jnp.int32, (16, NDIR * FREQ), 1) // NDIR
+    freq = lax.broadcasted_iota(jnp.int32, (16, NDIR * FREQ), 0) % FREQ
+    spread[...] = (comp == freq).astype(f32).astype(bf16)
+
     chunk = lax.broadcasted_iota(jnp.int32, (16, 128), 0)
     lane = lax.broadcasted_iota(jnp.int32, (16, 128), 1)
     low = chunk < 8
@@ -128,17 +165,17 @@
         jnp.where(low, 64 + chunk, 24 + chunk),
         jnp.where(low, 56 + chunk, 80 + chunk),
         8 + chunk,
-        jnp.where(low, chunk, 16 + chunk),
         104 + chunk,
-        jnp.where(low, 120 + chunk, 88 + chunk),
     ]
-    place[...] = jnp.zeros_like(place)
-    for s, target in enumerate(targets):
-        stripe = (lane == target).astype(f32).astype(bf16)
-        for part in range(2):
-            for t in range(8):
-                row = part * 1024 + s * 128 + 16 * t
-                place[row : row + 16, 128 * t : 128 * t + 128] = stripe
+    corners = [jnp.where(low, chunk, 16 + chunk), jnp.where(low, 120 + chunk, 88 + chunk)]
+    for matrix, lists in ((place, targets), (rims, corners)):
+        matrix[...] = jnp.zeros_like(matrix)
+        for s, target in enumerate(lists):
+            stripe = (lane == target).astype(f32).astype(bf16)
+            for part in range(2):
+                for t in range(8):
+                    row = part * 128 * len(lists) + s * 128 + 16 * t
+                    matrix[row : row + 16, 128 * t : 128 * t + 128] = stripe
     row = lax.broadcasted_iota(jnp.int32, (128, 128), 0)
     col = lax.broadcasted_iota(jnp.int32, (128, 128), 1)
     for sign, taps in ((0, FORTH_TAPS), (1, BACK_TAPS)):
@@ -155,18 +192,17 @@
                 gather[at : at + 128, 128 * half : 128 * half + 128] = moved
 
 
-def corner_kernel(from_first, from_second, to_first, to_second):
+def corner_kernel(second, cols_second, cols_first, rim):
     low = lanes() % 16 < 8
     even_lon = is_even("lon")
     even_lat = is_even("lat")
+    to_north = ~even_lat if second else even_lat
+    west_low = low == to_north
     for slab in range(SLABS):
-        first, second = from_first[slab], from_second[slab]
-        east = jnp.where(even_lon, first, second)
-        west = jnp.where(even_lon, second, first)
-        north = jnp.where(low, west, east)
-        south = jnp.where(low, east, west)
-        to_first[slab] = jnp.where(even_lat, north, south)
-        to_second[slab] = jnp.where(even_lat, south, north)
+        one, two = cols_first[slab], cols_second[slab]
+        east = jnp.where(even_lon, one, two)
+        west = jnp.where(even_lon, two, one)
+        rim[slab] = jnp.where(west_low, west, east)
 
 
 def split(x):
@@ -174,49 +210,51 @@
     return high, (x - high.astype(f32)).astype(bf16)
 
 
-def place_kernel(
-    own, cols_first, cols_second, rows_first, rows_second, rims_first, rims_second, consts, matrix,
-    q, taps, ky, tx, ty, lhs,
-):
+def fill_parts(lhs, count, s, array):
+    x = jnp.concatenate([array.reshape(8 * SLABS, 128), jnp.zeros((8, 128), f32)], axis=0)
+    high, low = split(x)
+    lhs[:, 128 * s : 128 * s + 128] = high
+    lhs[:, 128 * (count + s) : 128 * (count + s) + 128] = low
+
+
+def place_kernel(own, cols_second, cols_first, rows_second, rows_first, matrix, q, lhs):
     even_lon = is_even("lon")
     even_lat = is_even("lat")
-    blank = jnp.zeros((8, 128), f32)
-
-    def fill(s, array):
-        x = jnp.concatenate([array.reshape(8 * SLABS, 128), blank], axis=0)
-        high, low = split(x)
-        lhs[:, 128 * s : 128 * s + 128] = high
-        lhs[:, 1024 + 128 * s : 1024 + 128 * s + 128] = low
-
-    def pick(flag, first, second):
-        return jnp.where(flag, first[...], second[...])
-
-    fill(0, own[0])
-    fill(1, own[1])
-    fill(2, pick(even_lon, cols_second, cols_first))
-    fill(3, pick(even_lon, cols_first, cols_second))
-    fill(4, pick(even_lat, rows_second, rows_first))
-    fill(5, pick(even_lat, rims_second, rims_first))
-    fill(6, pick(even_lat, rows_first, rows_second))
-    fill(7, pick(even_lat, rims_first, rims_second))
+    fill_parts(lhs, 6, 0, own[0])
+    fill_parts(lhs, 6, 1, own[1])
+    fill_parts(lhs, 6, 2, jnp.where(even_lon, cols_second[...], cols_first[...]))
+    fill_parts(lhs, 6, 3, jnp.where(even_lon, cols_first[...], cols_second[...]))
+    fill_parts(lhs, 6, 4, jnp.where(even_lat, rows_second[...], rows_first[...]))
+    fill_parts(lhs, 6, 5, jnp.where(even_lat, rows_first[...], rows_second[...]))
     for pair in range(4):
         moved = jnp.dot(lhs[...], matrix[:, 256 * pair : 256 * pair + 256], preferred_element_type=f32)
         for i in range(2):
             q[:, 2 * pair + i] = moved[: 8 * SLABS, 128 * i : 128 * i + 128].reshape(SLABS, 8, 128)
 
+
+def lookup(point, consts, at):
+    depth = jnp.broadcast_to(point[DEPTH : DEPTH + 1], (8, 128))
+    value = jnp.zeros((8, 128), f32)
+    for c in range(NCLASS):
+        value = jnp.where(depth == float(c), consts[at + c], value)
+    return value * point[SEA : SEA + 1]
+
+
+def rims_kernel(partial, rims_second, rims_first, consts, matrix, q, taps, ky, tx, ty, lhs):
+    even_lat = is_even("lat")
+    fill_parts(lhs, 2, 0, jnp.where(even_lat, rims_second[...], rims_first[...]))
+    fill_parts(lhs, 2, 1, jnp.where(even_lat, rims_first[...], rims_second[...]))
+    for pair in range(4):
+        moved = jnp.dot(lhs[...], matrix[:, 256 * pair : 256 * pair + 256], preferred_element_type=f32)
+        for i in range(2):
+            t = 2 * pair + i
+            q[:, t] = partial[:, t] + moved[: 8 * SLABS, 128 * i : 128 * i + 128].reshape(SLABS, 8, 128)
+
     speed = []
     for t in range(8):
         point = q[STATIC, t]
-        depth = jnp.broadcast_to(point[DEPTH : DEPTH + 1], (8, 128))
-        share = point[SEA : SEA + 1]
-        pace = jnp.zeros((8, 128), f32)
-        turning = jnp.zeros((8, 128), f32)
-        for c in range(NCLASS):
-            hit = depth == float(c)
-            pace = jnp.where(hit, consts[TAB_SPEED + c], pace)
-            turning = jnp.where(hit, consts[TAB_TURN + c], turning)
-        pace = pace * share
-        turning = turning * share
+        pace = lookup(point, consts, TAB_SPEED)
+        turning = lookup(point, consts, TAB_TURN)
         speed.append(pace)
         tx[t] = turning * point[SLOPE_X : SLOPE_X + 1]
         ty[t] = turning * point[SLOPE_Y : SLOPE_Y + 1]
@@ -321,38 +359,63 @@
             back(d, ks, us, ws)
 
 
-def turn_kernel(q, tx, ty, out):
-    def one(t):
-        x = tx[t]
-        y = ty[t]
-
-        def courant(d):
-            return SIN_FACE[d] * x - COS_FACE[d] * y
-
-        def face(d, cell, diff, curve, curve_ahead):
-            k = courant(d)
-            u, w = halves(k)
-            return flux(cell, diff, jnp.where(k >= 0.0, curve, curve_ahead), k, u, w)
-
-        cell, ahead = q[0, t], q[1, t]
-        before, last = q[NDIR - 1, t], q[NDIR - 2, t]
-        diff0 = before - last
+def turn_around(get, put, x, y):
+    def factors(d):
+        k = SIN_FACE[d] * x - COS_FACE[d] * y
+        half, third = 0.5 * k, (1.0 / 3.0) * k
+        return k, 0.5 - half, 1.0 / 3.0 + third, 0.5 + half, 1.0 / 3.0 - third
+
+    half_turn = NDIR // 2
+    k, u, w, u_back, w_back = factors(half_turn - 1)
+    state = []
+    ends = []
+    for at in (0, half_turn):
+        cell, ahead = get(at), get(at + 1)
+        before, last = get((at - 1) % NDIR), get((at - 2) % NDIR)
+        diff = ahead - cell
         diff1 = cell - before
-        diff2 = ahead - cell
-        curve1 = diff1 - diff0
-        curve2 = diff2 - diff1
-        f_before = face(NDIR - 1, before, diff1, curve1, curve2)
-        diff, curve = diff2, curve2
-        for d in range(NDIR):
-            beyond = q[(d + 2) % NDIR, t]
+        curve = diff - diff1
+        curve1 = diff1 - (before - last)
+        if at == 0:
+            f = flux(before, diff1, jnp.where(k >= 0.0, curve, curve1), k, u_back, w_back)
+        else:
+            f = flux(before, diff1, jnp.where(k >= 0.0, curve1, curve), k, u, w)
+        state.append([cell, ahead, diff, curve])
+        ends.append(f)
+    f_first, f_second = -ends[0], -ends[1]
+    for d in range(half_turn):
+        if d < half_turn - 1:
+            k, u, w, u_back, w_back = factors(d)
+            positive = k >= 0.0
+        for at in (0, half_turn):
+            cell, ahead, diff, curve = state[at // half_turn]
+            beyond = get((at + d + 2) % NDIR)
             diff_ahead = beyond - ahead
             curve_ahead = diff_ahead - diff
-            f = face(d, cell, diff, curve, curve_ahead)
-            out[d, t] = cell - f + f_before
-            cell, ahead, diff, curve, f_before = ahead, beyond, diff_ahead, curve_ahead, f
-
+            if at == 0:
+                if d < half_turn - 1:
+                    f = flux(cell, diff, jnp.where(positive, curve, curve_ahead), k, u, w)
+                else:
+                    f = ends[1]
+                put(d, cell - f + f_first)
+                f_first = f
+            else:
+                if d < half_turn - 1:
+                    f = flux(cell, diff, jnp.where(positive, curve_ahead, curve), k, u_back, w_back)
+                else:
+                    f = ends[0]
+                put(at + d, cell + f - f_second)
+                f_second = f
+            state[at // half_turn] = [ahead, beyond, diff_ahead, curve_ahead]
+
+
+def turn_kernel(q, tx, ty, out):
     for t in range(8):
-        one(t)
+
+        def put(d, value, t=t):
+            out[d, t] = value
+
+        turn_around(lambda d, t=t: q[d, t], put, tx[t], ty[t])
 
 
 def gather_kernel(q, consts, matrix, own, sums, lhs):
@@ -373,9 +436,27 @@
         sums[2 + half : 3 + half, :] = jnp.sum(totals[half] * level, axis=0, keepdims=True)
 
 
-def finish_kernel(own, gain, static, sums, other, consts, out, flat0, flat1):
+def last_turn_kernel(own, static, gain, consts, early, flat0, flat1):
+    for half, flat in ((0, flat0), (1, flat1)):
+        point = static[half, 0]
+        turning = lookup(point, consts, TAB_TURN)
+
+        def put(d, value, half=half, flat=flat):
+            flat[pl.ds(d, FREQ, stride=NDIR), :] = value * gain[d, half]
+
+        turn_around(
+            lambda d, half=half: own[half, d],
+            put,
+            turning * point[SLOPE_X : SLOPE_X + 1],
+            turning * point[SLOPE_Y : SLOPE_Y + 1],
+        )
+        for low, high in ((0, 128), (128, 256), (256, 288)):
+            early[128 * half : 128 * half + 128, low:high] = flat[low:high, :].T
+
+
+def finish_kernel(early, static, sums, other, consts, spread, out):
     total = sums[...] + other[...]
-    for half, flat in ((0, flat0), (1, flat1)):
+    for half in range(2):
         energy = total[half : half + 1]
         moment = total[2 + half : 3 + half]
         mean_level = jnp.maximum(moment, 1.0) / jnp.maximum(energy, 1.0)
@@ -384,20 +465,20 @@
         breaking = break_coef * level * level / mean_level * (mean * mean)
         damping = static[half, 0, ICE : ICE + 1] * consts[ICE_RATE]
         loss = jnp.exp(-breaking - damping)
-        for d in range(NDIR):
-            flat[pl.ds(d, FREQ, stride=NDIR), :] = own[half, d] * gain[d, half] * loss
-        for low, high in ((0, 128), (128, 256), (256, 288)):
-            turned = flat[low:high, :].T
-            out[8 * half : 8 * half + 8, :, low:high] = turned.reshape(8, 16, high - low)
+        parts = jnp.concatenate(split(loss.T), axis=1)
+        wide = jnp.dot(parts, spread[...], preferred_element_type=f32)
+        result = early[128 * half : 128 * half + 128, :] * wide
+        out[8 * half : 8 * half + 8] = result.reshape(8, 16, NDIR * FREQ)
 
 
 PARAMS = pltpu.CompilerParams(vmem_limit_bytes=40 * 2**20)
 
 
 def call(kernel, ins, outs, scratch=(), name=None, space=pltpu.VMEM, dtype=f32):
+    types = dtype if isinstance(dtype, list) else [dtype] * len(outs)
     return pl.pallas_call(
         kernel,
-        out_shape=[jax.ShapeDtypeStruct(shape, dtype) for shape in outs],
+        out_shape=[jax.ShapeDtypeStruct(shape, kind) for shape, kind in zip(outs, types)],
         in_specs=[pl.BlockSpec(memory_space=space)] * ins,
         out_specs=[pl.BlockSpec(memory_space=pltpu.VMEM)] * len(outs),
         scratch_shapes=list(scratch),
@@ -428,81 +509,74 @@
     wind_dir,
     ice_rate,
 ):
-    band = lax.axis_index("band")
-    lat = lax.axis_index("lat")
-    lats = lax.axis_size("lat")
-    rows_dev = spectrum.shape[0]
-
-    def spread(table):
-        mine = lax.dynamic_slice_in_dim(table, band * FREQ, FREQ, 1)
-        return jnp.broadcast_to(mine[:, :, None], (NCLASS, FREQ, 128))
-
-    group = jnp.arange(128) // 32
-    row = lat * rows_dev - HALO + 8 * group[None, :] + jnp.arange(8)[:, None]
-    latitude = (south_edge + band_span * (row.astype(f32) + 0.5) / (rows_dev * lats)) * (math.pi / 180.0)
-    stretch = 1.0 / jnp.cos(latitude)
-    live = 1.0 - (((group == 0) & (lat == 0)) | ((group == 3) & (lat == lats - 1))).astype(f32)
-    ice = lax.dynamic_slice_in_dim(ice_rate, band * FREQ, FREQ, 0)
-    level = jnp.exp(math.log(freq_ratio) * (band * FREQ + jnp.arange(FREQ)).astype(f32))
-    consts = jnp.concatenate(
-        [
-            spread(speed_table),
-            spread(refraction_table),
-            stretch[None],
-            jnp.broadcast_to(live[None, None, :], (1, 8, 128)),
-            jnp.broadcast_to(ice[None, :, None], (1, 8, 128)),
-            jnp.broadcast_to(level[None, :, None], (1, 8, 128)),
-        ]
-    )
-
     tile = (8, 128)
+    block = (8,) + tile
+    slabs = (SLABS,) + tile
     inputs = [spectrum, sea_mask, ice_mask, depth_class, depth_slope, wind_speed, wind_dir]
-    slabs = (SLABS,) + tile
-    own, to_first, to_second, edge_first, edge_second = call(
+    tables = [speed_table, refraction_table, ice_rate]
+    own, speeds, turnings, ices = call(
         pack_kernel,
-        7,
-        [(2,) + slabs] + [slabs] * 4,
+        10,
+        [(2,) + slabs] + [x.shape for x in tables],
         [pltpu.VMEM(x.shape, x.dtype) for x in inputs]
         + [pltpu.VMEM((NDIR * FREQ, 128), f32)] * 2
-        + [pltpu.VMEM((16, 128), f32), pltpu.SemaphoreType.DMA((7,))],
+        + [pltpu.VMEM((16, 128), f32), pltpu.SemaphoreType.DMA((10,))],
         name="pack",
         space=pltpu.HBM,
-    )(*[pltpu.with_memory_space_constraint(x, pltpu.HBM) for x in inputs])
+    )(*[pltpu.with_memory_space_constraint(x, pltpu.HBM) for x in inputs + tables])
+    (to_second,) = call(functools.partial(column_kernel, True), 1, [slabs], name="column_far")(own)
     cols_second = swap(to_second, "lon", 1, True)
+    (to_first,) = call(functools.partial(column_kernel, False), 1, [slabs], name="column_near")(own)
     cols_first = swap(to_first, "lon", 0, True)
+    (edge_second,) = call(functools.partial(edge_kernel, True), 1, [slabs], name="edge_far")(own)
     rows_second = swap(edge_second, "lat", 1)
+    (edge_first,) = call(functools.partial(edge_kernel, False), 1, [slabs], name="edge_near")(own)
     rows_first = swap(edge_first, "lat", 0)
+    place, rims, shifts, gather, spread, consts = call(
+        tables_kernel,
+        3,
+        [(1536, 1024), (512, 1024), (2, 256, 384), (2048, 256), (16, NDIR * FREQ), (20,) + tile],
+        name="tables",
+        dtype=[bf16] * 5 + [f32],
+    )(speeds, turnings, ices)
     (gain,) = call(growth_kernel, 2, [(NDIR, 2) + tile], name="growth")(own, consts)
-    place, shifts, gather = call(
-        tables_kernel, 0, [(2048, 1024), (2, 256, 384), (2048, 256)], name="tables", dtype=bf16
-    )()
-    to_first, to_second = call(corner_kernel, 2, [slabs] * 2, name="corner")(cols_first, cols_second)
+    (to_second,) = call(functools.partial(corner_kernel, True), 2, [slabs], name="corner_far")(cols_second, cols_first)
     rims_second = swap(to_second, "lat", 1)
+    (to_first,) = call(functools.partial(corner_kernel, False), 2, [slabs], name="corner_near")(cols_second, cols_first)
     rims_first = swap(to_first, "lat", 0)
-    block = (8,) + tile
+    (partial,) = call(
+        place_kernel,
+        6,
+        [(SLABS,) + block],
+        [pltpu.VMEM((8 * SLABS + 8, 1536), bf16)],
+        name="place",
+    )(own, cols_second, cols_first, rows_second, rows_first, place)
     q, taps, ky, tx, ty = call(
-        place_kernel,
-        9,
+        rims_kernel,
+        5,
         [(SLABS,) + block, (10, 2, 4) + block] + [block] * 3,
-        [pltpu.VMEM((8 * SLABS + 8, 2048), bf16)],
-        name="place",
-    )(own, cols_first, cols_second, rows_first, rows_second, rims_first, rims_second, consts, place)
+        [pltpu.VMEM((8 * SLABS + 8, 512), bf16)],
+        name="rims",
+    )(partial, rims_second, rims_first, consts, rims)
     cells = [(NDIR,) + block]
     for substep in range(ITERS):
         (q,) = call(lon_kernel, 3, cells, [pltpu.VMEM((4, 576, 384), f32)], name="lon")(q, taps, shifts)
         (q,) = call(lat_kernel, 3, cells, name="lat")(q, ky, consts)
-        (q,) = call(turn_kernel, 3, cells, name="turn")(q, tx, ty)
+        if substep < ITERS - 1:
+            (q,) = call(turn_kernel, 3, cells, name="turn")(q, tx, ty)
     last, sums = call(
         gather_kernel, 3, [(2, NDIR) + tile, tile], [pltpu.VMEM((8 * NDIR, 2048), bf16)], name="gather"
     )(q, consts, gather)
     other = swap(sums, "band", 0)
-    (out,) = call(
-        finish_kernel,
-        6,
-        [spectrum.shape],
+    static = own[:, STATIC:]
+    (early,) = call(
+        last_turn_kernel,
+        4,
+        [(256, NDIR * FREQ)],
         [pltpu.VMEM((NDIR * FREQ, 128), f32)] * 2,
-        name="finish",
-    )(last, gain, own[:, STATIC:], sums, other, consts)
+        name="last_turn",
+    )(last, static, gain, consts)
+    (out,) = call(finish_kernel, 6, [spectrum.shape], name="finish")(early, static, sums, other, consts, spread)
     return out
 
 

time: 35 us -> 33.1 us (0.946)
  local copies, waits for them, and re-layouts: 1.81 us -> 0.01 us
  starting transfers between devices: 10.8 us -> 9.31 us
  waiting for transfers between devices: 7.91 us -> 9.26 us
    ppermute x7, starting transfers between devices: 10.8 us -> 9.31 us  [swap(): return lax.ppermute(array, axis, pairs)]
    dynamic_slice x2 -> x0, local copies, waits for them, and re-layouts: 1.52 us -> none  [the longest x1 0.78 us: spread(): mine = lax.dynamic_slice_in_dim(table, band * FREQ, FREQ, 1)]
    ppermute x7, waiting for transfers between devices: 7.91 us -> 9.26 us  [swap(): return lax.ppermute(array, axis, pairs)]
    pallas_call x5 -> x12, Pallas kernels: 4.98 us -> 5.95 us  [the longest x1 1.32 us: per_device(): call(pack_kernel, 10, [(2,) + slabs] + [x.shape for x in tables], [pltpu....]
    pallas_call x4 -> x3, Pallas kernels: 2.66 us -> 1.73 us  [per_device(): q, = call(turn_kernel, 3, cells, name='turn')(q, tx, ty)]
  transfers between devices with their start and end apart: 7 -> 7, of which waited for: 3 -> 4; matrix products, arithmetic and copies ran while one was open for 5% -> 0% of each run, Pallas kernels for 2% -> 8%
where the time goes in v5:
time: 33.1 us; the launch traced here: 32.6 us
  Pallas kernels  13.8 us (42%)
  starting transfers between devices  9.31 us (28%)
  waiting for transfers between devices  9.26 us (28%)
    ppermute x7, starting transfers between devices, swap(): return lax.ppermute(array, axis, pairs)  9.31 us
    ppermute x7, waiting for transfers between devices, swap(): return lax.ppermute(array, axis, pairs)  9.26 us
    pallas_call x4, Pallas kernels, per_device(): call(lon_kernel, 3, cells, [pltpu.VMEM((4, 576, 384), f32)], name='lon')  3.28 us
    pallas_call x4, Pallas kernels, per_device(): q, = call(lat_kernel, 3, cells, name='lat')(q, ky, consts)  2.17 us
    pallas_call x3, Pallas kernels, per_device(): q, = call(turn_kernel, 3, cells, name='turn')(q, tx, ty)  1.73 us
    pallas_call x1, Pallas kernels, per_device(): call(pack_kernel, 10, [(2,) + slabs] + [x.shape for x in tables], [pltpu....  1.32 us
    pallas_call x1, Pallas kernels, per_device(): call(place_kernel, 6, [(SLABS,) + block], [pltpu.VMEM((8 * SLABS + 8, 153...  1.2 us
    pallas_call x1, Pallas kernels, per_device(): call(finish_kernel, 6, [spectrum.shape], name='finish')  1.11 us
  transfers between devices with their start and end apart: 7, of which 4 were waited for; matrix products, arithmetic and copies ran while one was open for 0% of the time, Pallas kernels for 8%

profile of v5, /device:TPU:2, one launch (start us, length us, event | category | flops | bytes accessed | tf_op | source)
XLA Modules:
  0.0 32.6 jit_solution(6011168695374384040)
XLA Ops:
  0.0 1.3 %pack.1 = (f32[2,37,8,128]{3,2,1,0:T(8,128)S(1)}, f32[8,16]{1,0:T(8,128)S(1)}, f32[8,16]{1,0:T(8,128)S(1)}, f32[16]{0:T(128)S(1)}) custom-call(f32[16,16,288]{2,1,0:T(8,128)} %refs_0_.1, s32[16,16]{1,0:T(8,128)} %refs_1_.1, s32[16,16]{1,0:T(8,128)} %refs_2_.1, s32[16,16]{1,0:T(8,128)} %refs_3_.1, f32[2,16,16]{2,1,0:T(8,128)} %refs_4_.1, f32[16,16]{1,0:T(8,128)} %refs_5_.1, ...), custom_call_target="tpu_custom_call" | custom-call | tf_op jit(solution)/shard_map/pack/pallas_call | solution.py:517
  1.3 0.1 column_far.1
  1.5 3.7 %collective-permute-start = (f32[37,8,128]{2,1,0:T(8,128)S(1)}, f32[37,8,128]{2,1,0:T(8,128)S(1)}, u32[]{:S(2)}, u32[]{:S(2)}) collective-permute-start(f32[37,8,128]{2,1,0:T(8,128)S(1)} %column_far.1), channel_id=1, source_target_pairs={{8,16},{16,8},{24,0},{0,24},{9,17},{17,9},{25,1},{1,25},{10,18},{1... | collective-permute-start | bytes 454664 | tf_op jit(solution)/shard_map/ppermute | solution.py:497
  5.1 0.1 column_near.1
  5.3 0.1 collective-permute-start.1
  5.4 1.9 %collective-permute-start.2 = (f32[37,8,128]{2,1,0:T(8,128)S(1)}, f32[37,8,128]{2,1,0:T(8,128)S(1)}, u32[]{:S(2)}, u32[]{:S(2)}) collective-permute-start(f32[37,8,128]{2,1,0:T(8,128)S(1)} %edge_far.1), channel_id=1, source_target_pairs={{2,4},{4,2},{3,5},{5,3},{10,12},{12,10},{11,13},{13,11},{18,20},{2... | collective-permute-start | bytes 454664 | tf_op jit(solution)/shard_map/ppermute | solution.py:497
  7.4 0.1 collective-permute-start.3
  7.5 2.7 %collective-permute-done.cols_second = f32[37,8,128]{2,1,0:T(8,128)S(1)} collective-permute-done((f32[37,8,128]{2,1,0:T(8,128)S(1)}, f32[37,8,128]{2,1,0:T(8,128)S(1)}, u32[]{:S(2)}, u32[]{:S(2)}) %collective-permute-start) | collective-permute-done | bytes 151584 | tf_op jit(solution)/shard_map/ppermute | solution.py:497
  10.2 2.3 %collective-permute-done.1.cols_first = f32[37,8,128]{2,1,0:T(8,128)S(1)} collective-permute-done((f32[37,8,128]{2,1,0:T(8,128)S(1)}, f32[37,8,128]{2,1,0:T(8,128)S(1)}, u32[]{:S(2)}, u32[]{:S(2)}) %collective-permute-start.1) | collective-permute-done | bytes 151584 | tf_op jit(solution)/shard_map/ppermute | solution.py:497
  12.5 1.9 %collective-permute-start.4 = (f32[37,8,128]{2,1,0:T(8,128)S(1)}, f32[37,8,128]{2,1,0:T(8,128)S(1)}, u32[]{:S(2)}, u32[]{:S(2)}) collective-permute-start(f32[37,8,128]{2,1,0:T(8,128)S(1)} %corner_far.1), channel_id=1, source_target_pairs={{2,4},{4,2},{3,5},{5,3},{10,12},{12,10},{11,13},{13,11},{18,20},{2... | collective-permute-start | bytes 454664 | tf_op jit(solution)/shard_map/ppermute | solution.py:497
  14.4 0.1 collective-permute-start.5
  14.5 0.6 %tables.1 = (bf16[1536,1024]{1,0:T(8,128)(2,1)S(1)}, bf16[512,1024]{1,0:T(8,128)(2,1)S(1)}, bf16[2,256,384]{2,1,0:T(8,128)(2,1)S(1)}, bf16[2048,256]{1,0:T(8,128...) custom-call(f32[8,16]{1,0:T(8,128)S(1)} %get-tuple-element.23.speed_table, ...), custom_call_target="tpu_custom_call" | custom-call | tf_op jit(solution)/shard_map/tables/pallas_call | solution.py:535
  15.1 1.2 %place.1.partial = f32[37,8,8,128]{3,2,1,0:T(8,128)S(1)} custom-call(f32[2,37,8,128]{3,2,1,0:T(8,128)S(1)} %get-tuple-element.22.own, f32[37,8,128]{2,1,0:T(8,128)S(1)} %collective-permute-done.cols_second, f32[37,8,128]{2,1,0:T(8,128)S(1)} %collective-permute-done.1.cols_first, f32[37,8,128]{2,1,0:T(8,128)S(1)} %collective-permute-done.2.rows_second, ...), custom_call_target="tpu_custom_call" | custom-call | tf_op jit(solution)/shard_map/place/pallas_call | solution.py:547
  16.3 2.7 %collective-permute-done.4.rims_second = f32[37,8,128]{2,1,0:T(8,128)S(1)} collective-permute-done((f32[37,8,128]{2,1,0:T(8,128)S(1)}, f32[37,8,128]{2,1,0:T(8,128)S(1)}, u32[]{:S(2)}, u32[]{:S(2)}) %collective-permute-start.4) | collective-permute-done | bytes 151584 | tf_op jit(solution)/shard_map/ppermute | solution.py:497
  19.0 1.0 %rims.1 = (f32[37,8,8,128]{3,2,1,0:T(8,128)S(1)}, f32[10,2,4,8,8,128]{5,4,3,2,1,0:T(8,128)S(1)}, f32[8,8,128]{2,1,0:T(8,128)S(1)}, f32[8,8,128]{2,1,0:T(8,128)S(1)}, f32[8,8,128]{2,1,0:T(8,128)S(1)}) custom-call(f32[37,8,8,128]{3,2,1,0:T(8,128)S(1)} %place.1.partial, f32[37,8,128]{2,1,0:T(8,128)S(1)} %collective-permute-done.4.rims_second, ...), custom_call_target="tpu_custom_call" | custom-call | tf_op jit(solution)/shard_map/rims/pallas_call | solution.py:554
  20.0 0.8 %lon.4.q = f32[36,8,8,128]{3,2,1,0:T(8,128)S(1)} custom-call(f32[37,8,8,128]{3,2,1,0:T(8,128)S(1)} %get-tuple-element.29.q, f32[10,2,4,8,8,128]{5,4,3,2,1,0:T(8,128)S(1)} %get-tuple-element.30.taps, bf16[2,256,384]{2,1,0:T(8,128)(2,1)S(1)} %get-tuple-element.31.shifts), custom_call_target="tpu_custom_call" | custom-call | tf_op jit(solution)/shard_map/lon/pallas_call | solution.py:563
  20.8 0.5 %lat.4.q = f32[36,8,8,128]{3,2,1,0:T(8,128)S(1)} custom-call(f32[36,8,8,128]{3,2,1,0:T(8,128)S(1)} %lon.4.q, f32[8,8,128]{2,1,0:T(8,128)S(1)} %get-tuple-element.32.ky, f32[20,8,128]{2,1,0:T(8,128)S(1)} %get-tuple-element.27.consts), custom_call_target="tpu_custom_call" | custom-call | tf_op jit(solution)/shard_map/lat/pallas_call | solution.py:564
  21.4 0.6 %turn.3.q = f32[36,8,8,128]{3,2,1,0:T(8,128)S(1)} custom-call(f32[36,8,8,128]{3,2,1,0:T(8,128)S(1)} %lat.4.q, f32[8,8,128]{2,1,0:T(8,128)S(1)} %get-tuple-element.33.tx, f32[8,8,128]{2,1,0:T(8,128)S(1)} %get-tuple-element.34.ty), custom_call_target="tpu_custom_call" | custom-call | tf_op jit(solution)/shard_map/turn/pallas_call | solution.py:566
  22.0 0.8 %lon.5.q = f32[36,8,8,128]{3,2,1,0:T(8,128)S(1)} custom-call(f32[36,8,8,128]{3,2,1,0:T(8,128)S(1)} %turn.3.q, f32[10,2,4,8,8,128]{5,4,3,2,1,0:T(8,128)S(1)} %get-tuple-element.30.taps, bf16[2,256,384]{2,1,0:T(8,128)(2,1)S(1)} %get-tuple-element.31.shifts), custom_call_target="tpu_custom_call" | custom-call | tf_op jit(solution)/shard_map/lon/pallas_call | solution.py:563
  22.8 0.5 %lat.5.q = f32[36,8,8,128]{3,2,1,0:T(8,128)S(1)} custom-call(f32[36,8,8,128]{3,2,1,0:T(8,128)S(1)} %lon.5.q, f32[8,8,128]{2,1,0:T(8,128)S(1)} %get-tuple-element.32.ky, f32[20,8,128]{2,1,0:T(8,128)S(1)} %get-tuple-element.27.consts), custom_call_target="tpu_custom_call" | custom-call | tf_op jit(solution)/shard_map/lat/pallas_call | solution.py:564
  23.3 0.6 %turn.4.q = f32[36,8,8,128]{3,2,1,0:T(8,128)S(1)} custom-call(f32[36,8,8,128]{3,2,1,0:T(8,128)S(1)} %lat.5.q, f32[8,8,128]{2,1,0:T(8,128)S(1)} %get-tuple-element.33.tx, f32[8,8,128]{2,1,0:T(8,128)S(1)} %get-tuple-element.34.ty), custom_call_target="tpu_custom_call" | custom-call | tf_op jit(solution)/shard_map/turn/pallas_call | solution.py:566
  23.9 0.8 %lon.6.q = f32[36,8,8,128]{3,2,1,0:T(8,128)S(1)} custom-call(f32[36,8,8,128]{3,2,1,0:T(8,128)S(1)} %turn.4.q, f32[10,2,4,8,8,128]{5,4,3,2,1,0:T(8,128)S(1)} %get-tuple-element.30.taps, bf16[2,256,384]{2,1,0:T(8,128)(2,1)S(1)} %get-tuple-element.31.shifts), custom_call_target="tpu_custom_call" | custom-call | tf_op jit(solution)/shard_map/lon/pallas_call | solution.py:563
  24.8 0.5 %lat.6.q = f32[36,8,8,128]{3,2,1,0:T(8,128)S(1)} custom-call(f32[36,8,8,128]{3,2,1,0:T(8,128)S(1)} %lon.6.q, f32[8,8,128]{2,1,0:T(8,128)S(1)} %get-tuple-element.32.ky, f32[20,8,128]{2,1,0:T(8,128)S(1)} %get-tuple-element.27.consts), custom_call_target="tpu_custom_call" | custom-call | tf_op jit(solution)/shard_map/lat/pallas_call | solution.py:564
  25.3 0.6 %turn.5.q = f32[36,8,8,128]{3,2,1,0:T(8,128)S(1)} custom-call(f32[36,8,8,128]{3,2,1,0:T(8,128)S(1)} %lat.6.q, f32[8,8,128]{2,1,0:T(8,128)S(1)} %get-tuple-element.33.tx, f32[8,8,128]{2,1,0:T(8,128)S(1)} %get-tuple-element.34.ty), custom_call_target="tpu_custom_call" | custom-call | tf_op jit(solution)/shard_map/turn/pallas_call | solution.py:566
  25.9 0.8 %lon.7.q = f32[36,8,8,128]{3,2,1,0:T(8,128)S(1)} custom-call(f32[36,8,8,128]{3,2,1,0:T(8,128)S(1)} %turn.5.q, f32[10,2,4,8,8,128]{5,4,3,2,1,0:T(8,128)S(1)} %get-tuple-element.30.taps, bf16[2,256,384]{2,1,0:T(8,128)(2,1)S(1)} %get-tuple-element.31.shifts), custom_call_target="tpu_custom_call" | custom-call | tf_op jit(solution)/shard_map/lon/pallas_call | solution.py:563
  26.7 0.5 %lat.7.q = f32[36,8,8,128]{3,2,1,0:T(8,128)S(1)} custom-call(f32[36,8,8,128]{3,2,1,0:T(8,128)S(1)} %lon.7.q, f32[8,8,128]{2,1,0:T(8,128)S(1)} %get-tuple-element.32.ky, f32[20,8,128]{2,1,0:T(8,128)S(1)} %get-tuple-element.27.consts), custom_call_target="tpu_custom_call" | custom-call | tf_op jit(solution)/shard_map/lat/pallas_call | solution.py:564
  27.3 0.5 %gather.1 = (f32[2,36,8,128]{3,2,1,0:T(8,128)S(1)}, f32[8,128]{1,0:T(8,128)S(1)}) custom-call(f32[36,8,8,128]{3,2,1,0:T(8,128)S(1)} %lat.7.q, f32[20,8,128]{2,1,0:T(8,128)S(1)} %get-tuple-element.27.consts, bf16[2048,256]{1,0:T(8,128)(2,1)S(1)} %get-tuple-element.35.matrix), custom_call_target="tpu_custom_call" | custom-call | tf_op jit(solution)/shard_map/gather/pallas_call | solution.py:567
  27.8 1.6 %collective-permute-start.6 = (f32[8,128]{1,0:T(8,128)S(1)}, f32[8,128]{1,0:T(8,128)S(1)}, u32[]{:S(2)}, u32[]{:S(2)}) collective-permute-start(f32[8,128]{1,0:T(8,128)S(1)} %get-tuple-element.37.sums), channel_id=1, source_target_pairs={{0,1},{1,0},{2,3},{3,2},{4,5},{5,4},{6,7},{7,6},{8,9},{9,8},{10,11... | collective-permute-start | bytes 12296 | tf_op jit(solution)/shard_map/ppermute | solution.py:497
  29.4 0.1 growth.1.gain
  29.5 0.3 last_turn.1.early
  29.9 1.6 %collective-permute-done.6.other = f32[8,128]{1,0:T(8,128)S(1)} collective-permute-done((f32[8,128]{1,0:T(8,128)S(1)}, f32[8,128]{1,0:T(8,128)S(1)}, u32[]{:S(2)}, u32[]{:S(2)}) %collective-permute-start.6) | collective-permute-done | bytes 4128 | tf_op jit(solution)/shard_map/ppermute | solution.py:497
  31.5 1.1 %finish.1 = f32[16,16,288]{2,1,0:T(8,128)} custom-call(f32[256,288]{1,0:T(8,128)S(1)} %last_turn.1.early, f32[2,1,8,128]{3,2,1,0:T(8,128)S(1)} %slice.3.static, f32[8,128]{1,0:T(8,128)S(1)} %get-tuple-element.37.sums, f32[8,128]{1,0:T(8,128)S(1)} %collective-permute-done.6.other, f32[20,8,128]{2,1,0:T(8,128)S(1)} %get-tuple-element.27.consts, ...), custom_call_target="tpu_custom_call" | custom-call | tf_op jit(solution)/shard_map/finish/pallas_call | solution.py:579
  (8 shorter events, 0.1 us)
Async XLA Ops:
  1.5 8.7 %collective-permute-start = (f32[37,8,128]{2,1,0:T(8,128)S(1)}, f32[37,8,128]{2,1,0:T(8,128)S(1)}, u32[]{:S(2)}, u32[]{:S(2)}) collective-permute-start(f32[37,8,128]{2,1,0:T(8,128)S(1)} %column_far.1), channel_id=1, source_target_pairs={{8,16},{16,8},{24,0},{0,24},{9,17},{17,9},{25,1},{1,25},{10,18},{1... | collective-permute-start | bytes 454664 | tf_op jit(solution)/shard_map/ppermute | solution.py:497
  5.3 7.1 %collective-permute-start.1 = (f32[37,8,128]{2,1,0:T(8,128)S(1)}, f32[37,8,128]{2,1,0:T(8,128)S(1)}, u32[]{:S(2)}, u32[]{:S(2)}) collective-permute-start(f32[37,8,128]{2,1,0:T(8,128)S(1)} %column_near.1), channel_id=1, source_target_pairs={{0,8},{8,0},{16,24},{24,16},{1,9},{9,1},{17,25},{25,17},{2,10},{10... | collective-permute-start | bytes 454664 | tf_op jit(solution)/shard_map/ppermute | solution.py:497
  5.4 9.7 %collective-permute-start.2 = (f32[37,8,128]{2,1,0:T(8,128)S(1)}, f32[37,8,128]{2,1,0:T(8,128)S(1)}, u32[]{:S(2)}, u32[]{:S(2)}) collective-permute-start(f32[37,8,128]{2,1,0:T(8,128)S(1)} %edge_far.1), channel_id=1, source_target_pairs={{2,4},{4,2},{3,5},{5,3},{10,12},{12,10},{11,13},{13,11},{18,20},{2... | collective-permute-start | bytes 454664 | tf_op jit(solution)/shard_map/ppermute | solution.py:497
  7.4 7.7 %collective-permute-start.3 = (f32[37,8,128]{2,1,0:T(8,128)S(1)}, f32[37,8,128]{2,1,0:T(8,128)S(1)}, u32[]{:S(2)}, u32[]{:S(2)}) collective-permute-start(f32[37,8,128]{2,1,0:T(8,128)S(1)} %edge_near.1), channel_id=1, source_target_pairs={{0,2},{2,0},{4,6},{6,4},{1,3},{3,1},{5,7},{7,5},{8,10},{10,8},{12,... | collective-permute-start | bytes 454664 | tf_op jit(solution)/shard_map/ppermute | solution.py:497
  12.5 6.5 %collective-permute-start.4 = (f32[37,8,128]{2,1,0:T(8,128)S(1)}, f32[37,8,128]{2,1,0:T(8,128)S(1)}, u32[]{:S(2)}, u32[]{:S(2)}) collective-permute-start(f32[37,8,128]{2,1,0:T(8,128)S(1)} %corner_far.1), channel_id=1, source_target_pairs={{2,4},{4,2},{3,5},{5,3},{10,12},{12,10},{11,13},{13,11},{18,20},{2... | collective-permute-start | bytes 454664 | tf_op jit(solution)/shard_map/ppermute | solution.py:497
  14.4 4.5 %collective-permute-start.5 = (f32[37,8,128]{2,1,0:T(8,128)S(1)}, f32[37,8,128]{2,1,0:T(8,128)S(1)}, u32[]{:S(2)}, u32[]{:S(2)}) collective-permute-start(f32[37,8,128]{2,1,0:T(8,128)S(1)} %corner_near.1), channel_id=1, source_target_pairs={{0,2},{2,0},{4,6},{6,4},{1,3},{3,1},{5,7},{7,5},{8,10},{10,8},{12,... | collective-permute-start | bytes 454664 | tf_op jit(solution)/shard_map/ppermute | solution.py:497
  27.8 3.7 %collective-permute-start.6 = (f32[8,128]{1,0:T(8,128)S(1)}, f32[8,128]{1,0:T(8,128)S(1)}, u32[]{:S(2)}, u32[]{:S(2)}) collective-permute-start(f32[8,128]{1,0:T(8,128)S(1)} %get-tuple-element.37.sums), channel_id=1, source_target_pairs={{0,1},{1,0},{2,3},{3,2},{4,5},{5,4},{6,7},{7,6},{8,9},{9,8},{10,11... | collective-permute-start | bytes 12296 | tf_op jit(solution)/shard_map/ppermute | solution.py:497

commit v6 on v5

--- a/solution.py
+++ b/solution.py
@@ -192,17 +192,21 @@
                 gather[at : at + 128, 128 * half : 128 * half + 128] = moved
 
 
-def corner_kernel(second, cols_second, cols_first, rim):
+def corner_kernel(cols_second, cols_first, rows_second, rows_first, consts, rim):
+    del rows_second, rows_first, consts
     low = lanes() % 16 < 8
     even_lon = is_even("lon")
-    even_lat = is_even("lat")
-    to_north = ~even_lat if second else even_lat
-    west_low = low == to_north
+    west_low = low == is_even("lat")
     for slab in range(SLABS):
         one, two = cols_first[slab], cols_second[slab]
         east = jnp.where(even_lon, one, two)
         west = jnp.where(even_lon, two, one)
-        rim[slab] = jnp.where(west_low, west, east)
+        rim[0, slab] = jnp.where(west_low, west, east)
+        rim[1, slab] = jnp.where(west_low, east, west)
+
+
+def relay_kernel(rims_pair, beyond):
+    beyond[...] = rims_pair[1]
 
 
 def split(x):
@@ -240,10 +244,10 @@
     return value * point[SEA : SEA + 1]
 
 
-def rims_kernel(partial, rims_second, rims_first, consts, matrix, q, taps, ky, tx, ty, lhs):
+def rims_kernel(partial, rims_second, rims_pair, consts, matrix, q, taps, ky, tx, ty, lhs):
     even_lat = is_even("lat")
-    fill_parts(lhs, 2, 0, jnp.where(even_lat, rims_second[...], rims_first[...]))
-    fill_parts(lhs, 2, 1, jnp.where(even_lat, rims_first[...], rims_second[...]))
+    fill_parts(lhs, 2, 0, jnp.where(even_lat, rims_second[...], rims_pair[0]))
+    fill_parts(lhs, 2, 1, jnp.where(even_lat, rims_pair[0], rims_second[...]))
     for pair in range(4):
         moved = jnp.dot(lhs[...], matrix[:, 256 * pair : 256 * pair + 256], preferred_element_type=f32)
         for i in range(2):
@@ -291,8 +295,8 @@
     return k - k * u + 2.0 * bend, k * u - bend, -bend
 
 
-FORTH_TAPS = (1, -1, -2)
-BACK_TAPS = (1, -1, 2)
+FORTH_TAPS = (-1, -2)
+BACK_TAPS = (-1, 2)
 
 
 def lon_kernel(q, taps, shifts, out, moved):
@@ -312,12 +316,19 @@
                 tap = [taps[base, sign, i, t] for i in range(4)]
                 for d in dirs:
                     at = 64 * (d % 9) + 8 * t
-                    near = [moved[d // 9, at : at + 8, 128 * i : 128 * i + 128] for i in range(3)]
-                    out[d, t] = (tap[0] * q[d, t] + tap[1] * near[0]) + (tap[2] * near[1] + tap[3] * near[2])
-
-
-def lat_kernel(q, ky, consts, out):
+                    cell = q[d, t]
+                    near = [moved[d // 9, at : at + 8, 128 * i : 128 * i + 128] for i in range(2)]
+                    out[d, t] = (tap[0] * cell + tap[1] * roll(cell, -1)) + (tap[2] * near[0] + tap[3] * near[1])
+
+
+def lat_kernel(q, ky, consts, out, sums=None):
     live = consts[LIVE]
+    totals = [jnp.zeros((8, 128), f32)] * 8
+
+    def put(d, t, value):
+        out[d, t] = value
+        if sums is not None:
+            totals[t] = totals[t] + value
 
     def forth(d, ks, us, ws):
         tiles = [q[d, t] for t in range(8)]
@@ -330,7 +341,7 @@
             before = diff[t]
         behind = roll(fluxes[7], 32)
         for t in range(8):
-            out[d, t] = (tiles[t] - fluxes[t] + behind) * live
+            put(d, t, (tiles[t] - fluxes[t] + behind) * live)
             behind = fluxes[t]
 
     def back(d, ks, us, ws):
@@ -341,7 +352,7 @@
         fluxes = [flux(ahead[t], diff[t], diff[t] - after[t], ks[t], us[t], ws[t]) for t in range(8)]
         behind = roll(fluxes[7], 32)
         for t in range(8):
-            out[d, t] = (tiles[t] + fluxes[t] - behind) * live
+            put(d, t, (tiles[t] + fluxes[t] - behind) * live)
             behind = fluxes[t]
 
     for base in range(10):
@@ -357,6 +368,19 @@
             forth(d, ks, us, ws)
         for d in south:
             back(d, ks, us, ws)
+    if sums is None:
+        return
+    lane = lanes()
+    halves_of = [jnp.zeros((8, 128), f32)] * 2
+    for t in range(8):
+        moved = roll(totals[t], 16 * t - 40)
+        halves_of[0] = jnp.where(lane // 16 == t, moved, halves_of[0])
+        halves_of[1] = jnp.where(lane // 16 == (t + 2) % 8, moved, halves_of[1])
+    halves_of[1] = roll(halves_of[1], -32)
+    sums[...] = jnp.zeros((8, 128), f32)
+    for half in range(2):
+        sums[half : half + 1, :] = jnp.sum(halves_of[half], axis=0, keepdims=True)
+        sums[2 + half : 3 + half, :] = jnp.sum(halves_of[half] * consts[LEVEL], axis=0, keepdims=True)
 
 
 def turn_around(get, put, x, y):
@@ -418,22 +442,14 @@
         turn_around(lambda d, t=t: q[d, t], put, tx[t], ty[t])
 
 
-def gather_kernel(q, consts, matrix, own, sums, lhs):
-    zero = jnp.zeros((8, 128), f32)
+def gather_kernel(q, matrix, own, lhs):
     for t in range(8):
         high, low = split(q[:, t].reshape(8 * NDIR, 128))
         lhs[:, 128 * t : 128 * t + 128] = high
         lhs[:, 1024 + 128 * t : 1024 + 128 * t + 128] = low
     moved = jnp.dot(lhs[...], matrix[...], preferred_element_type=f32)
-    totals = [zero, zero]
     for half in range(2):
         own[half] = moved[:, 128 * half : 128 * half + 128].reshape(NDIR, 8, 128)
-        totals[half] = jnp.sum(own[half], axis=0)
-    level = consts[LEVEL]
-    sums[...] = zero
-    for half in range(2):
-        sums[half : half + 1, :] = jnp.sum(totals[half], axis=0, keepdims=True)
-        sums[2 + half : 3 + half, :] = jnp.sum(totals[half] * level, axis=0, keepdims=True)
 
 
 def last_turn_kernel(own, static, gain, consts, early, flat0, flat1):
@@ -454,7 +470,7 @@
             early[128 * half : 128 * half + 128, low:high] = flat[low:high, :].T
 
 
-def finish_kernel(early, static, sums, other, consts, spread, out):
+def finish_kernel(early, static, sums, other, consts, spread, out, ready, sems):
     total = sums[...] + other[...]
     for half in range(2):
         energy = total[half : half + 1]
@@ -468,19 +484,24 @@
         parts = jnp.concatenate(split(loss.T), axis=1)
         wide = jnp.dot(parts, spread[...], preferred_element_type=f32)
         result = early[128 * half : 128 * half + 128, :] * wide
-        out[8 * half : 8 * half + 8] = result.reshape(8, 16, NDIR * FREQ)
+        mine = pl.ds(8 * half, 8)
+        ready[mine] = result.reshape(8, 16, NDIR * FREQ)
+        pltpu.make_async_copy(ready.at[mine], out.at[mine], sems.at[half]).start()
+    for half in range(2):
+        mine = pl.ds(8 * half, 8)
+        pltpu.make_async_copy(ready.at[mine], out.at[mine], sems.at[half]).wait()
 
 
 PARAMS = pltpu.CompilerParams(vmem_limit_bytes=40 * 2**20)
 
 
-def call(kernel, ins, outs, scratch=(), name=None, space=pltpu.VMEM, dtype=f32):
+def call(kernel, ins, outs, scratch=(), name=None, space=pltpu.VMEM, dtype=f32, result=pltpu.VMEM):
     types = dtype if isinstance(dtype, list) else [dtype] * len(outs)
     return pl.pallas_call(
         kernel,
         out_shape=[jax.ShapeDtypeStruct(shape, kind) for shape, kind in zip(outs, types)],
         in_specs=[pl.BlockSpec(memory_space=space)] * ins,
-        out_specs=[pl.BlockSpec(memory_space=pltpu.VMEM)] * len(outs),
+        out_specs=[pl.BlockSpec(memory_space=result)] * len(outs),
         scratch_shapes=list(scratch),
         compiler_params=PARAMS,
         name=name,
@@ -494,6 +515,12 @@
         if i + 1 < count or closed:
             j = (i + 1) % count
             pairs += [(i, j), (j, i)]
+    return lax.ppermute(array, axis, pairs)
+
+
+def skip(array, axis):
+    count = lax.axis_size(axis)
+    pairs = [(i, i + 2) for i in range(0, count - 2, 2)] + [(i, i - 2) for i in range(3, count, 2)]
     return lax.ppermute(array, axis, pairs)
 
 
@@ -535,15 +562,17 @@
     place, rims, shifts, gather, spread, consts = call(
         tables_kernel,
         3,
-        [(1536, 1024), (512, 1024), (2, 256, 384), (2048, 256), (16, NDIR * FREQ), (20,) + tile],
+        [(1536, 1024), (512, 1024), (2, 256, 256), (2048, 256), (16, NDIR * FREQ), (20,) + tile],
         name="tables",
         dtype=[bf16] * 5 + [f32],
     )(speeds, turnings, ices)
     (gain,) = call(growth_kernel, 2, [(NDIR, 2) + tile], name="growth")(own, consts)
-    (to_second,) = call(functools.partial(corner_kernel, True), 2, [slabs], name="corner_far")(cols_second, cols_first)
-    rims_second = swap(to_second, "lat", 1)
-    (to_first,) = call(functools.partial(corner_kernel, False), 2, [slabs], name="corner_near")(cols_second, cols_first)
-    rims_first = swap(to_first, "lat", 0)
+    (rim,) = call(corner_kernel, 5, [(2,) + slabs], name="corner")(
+        cols_second, cols_first, rows_second, rows_first, consts
+    )
+    rims_pair = swap(rim, "lat", 0)
+    (beyond,) = call(relay_kernel, 1, [slabs], name="relay")(rims_pair)
+    rims_second = skip(beyond, "lat")
     (partial,) = call(
         place_kernel,
         6,
@@ -557,17 +586,19 @@
         [(SLABS,) + block, (10, 2, 4) + block] + [block] * 3,
         [pltpu.VMEM((8 * SLABS + 8, 512), bf16)],
         name="rims",
-    )(partial, rims_second, rims_first, consts, rims)
+    )(partial, rims_second, rims_pair, consts, rims)
     cells = [(NDIR,) + block]
     for substep in range(ITERS):
-        (q,) = call(lon_kernel, 3, cells, [pltpu.VMEM((4, 576, 384), f32)], name="lon")(q, taps, shifts)
-        (q,) = call(lat_kernel, 3, cells, name="lat")(q, ky, consts)
-        if substep < ITERS - 1:
+        (q,) = call(lon_kernel, 3, cells, [pltpu.VMEM((4, 576, 256), f32)], name="lon")(q, taps, shifts)
+        if substep == ITERS - 1:
+            q, sums = call(lat_kernel, 3, cells + [tile], name="lat_sums")(q, ky, consts)
+        else:
+            (q,) = call(lat_kernel, 3, cells, name="lat")(q, ky, consts)
             (q,) = call(turn_kernel, 3, cells, name="turn")(q, tx, ty)
-    last, sums = call(
-        gather_kernel, 3, [(2, NDIR) + tile, tile], [pltpu.VMEM((8 * NDIR, 2048), bf16)], name="gather"
-    )(q, consts, gather)
     other = swap(sums, "band", 0)
+    (last,) = call(
+        gather_kernel, 2, [(2, NDIR) + tile], [pltpu.VMEM((8 * NDIR, 2048), bf16)], name="gather"
+    )(q, gather)
     static = own[:, STATIC:]
     (early,) = call(
         last_turn_kernel,
@@ -576,7 +607,14 @@
         [pltpu.VMEM((NDIR * FREQ, 128), f32)] * 2,
         name="last_turn",
     )(last, static, gain, consts)
-    (out,) = call(finish_kernel, 6, [spectrum.shape], name="finish")(early, static, sums, other, consts, spread)
+    (out,) = call(
+        finish_kernel,
+        6,
+        [spectrum.shape],
+        [pltpu.VMEM(spectrum.shape, f32), pltpu.SemaphoreType.DMA((2,))],
+        name="finish",
+        result=pltpu.HBM,
+    )(early, static, sums, other, consts, spread)
     return out
 
 

time: 33.1 us -> 34.7 us (1.048)
  waiting for transfers between devices: 9.26 us -> 11.7 us
  starting transfers between devices: 9.31 us -> 8.63 us
    ppermute x0 -> x1, waiting for transfers between devices: none -> 4.61 us  [skip(): return lax.ppermute(array, axis, pairs)]
    ppermute x7 -> x6, waiting for transfers between devices: 9.26 us -> 7.1 us  [swap(): return lax.ppermute(array, axis, pairs)]
    ppermute x7 -> x6, starting transfers between devices: 9.31 us -> 7.33 us  [swap(): return lax.ppermute(array, axis, pairs)]
    ppermute x0 -> x1, starting transfers between devices: none -> 1.29 us  [skip(): return lax.ppermute(array, axis, pairs)]
    pallas_call x4 -> x3, Pallas kernels: 2.17 us -> 1.63 us  [per_device(): q, = call(lat_kernel, 3, cells, name='lat')(q, ky, consts)]
    pallas_call x9 -> x10, Pallas kernels: 5.56 us -> 5.83 us  [the longest x4 2.91 us: per_device(): call(lon_kernel, 3, cells, [pltpu.VMEM((4, 576, 256), f32)], name='lon')]
  transfers between devices with their start and end apart: 7 -> 7, of which waited for: 4 -> 5; matrix products, arithmetic and copies ran while one was open for 0% -> 0% of each run, Pallas kernels for 8% -> 8%
where the time goes in v6:
time: 34.7 us; the launch traced here: 34 us
  Pallas kernels  13.5 us (39%)
  waiting for transfers between devices  11.7 us (34%)
  starting transfers between devices  8.63 us (25%)
    ppermute x6, starting transfers between devices, swap(): return lax.ppermute(array, axis, pairs)  7.33 us
    ppermute x6, waiting for transfers between devices, swap(): return lax.ppermute(array, axis, pairs)  7.1 us
    ppermute x1, waiting for transfers between devices, skip(): return lax.ppermute(array, axis, pairs)  4.61 us
    pallas_call x4, Pallas kernels, per_device(): call(lon_kernel, 3, cells, [pltpu.VMEM((4, 576, 256), f32)], name='lon')  2.91 us
    pallas_call x3, Pallas kernels, per_device(): q, = call(turn_kernel, 3, cells, name='turn')(q, tx, ty)  1.73 us
    pallas_call x3, Pallas kernels, per_device(): q, = call(lat_kernel, 3, cells, name='lat')(q, ky, consts)  1.63 us
    pallas_call x1, Pallas kernels, per_device(): call(pack_kernel, 10, [(2,) + slabs] + [x.shape for x in tables], [pltpu....  1.32 us
    ppermute x1, starting transfers between devices, skip(): return lax.ppermute(array, axis, pairs)  1.29 us
  transfers between devices with their start and end apart: 7, of which 5 were waited for; matrix products, arithmetic and copies ran while one was open for 0% of the time, Pallas kernels for 8%

profile of v6, /device:TPU:2, one launch (start us, length us, event | category | flops | bytes accessed | tf_op | source)
XLA Modules:
  0.0 34.0 jit_solution(13095521579394980132)
XLA Ops:
  0.0 1.3 %pack.1 = (f32[2,37,8,128]{3,2,1,0:T(8,128)S(1)}, f32[8,16]{1,0:T(8,128)S(1)}, f32[8,16]{1,0:T(8,128)S(1)}, f32[16]{0:T(128)S(1)}) custom-call(f32[16,16,288]{2,1,0:T(8,128)} %refs_0_.1, s32[16,16]{1,0:T(8,128)} %refs_1_.1, s32[16,16]{1,0:T(8,128)} %refs_2_.1, s32[16,16]{1,0:T(8,128)} %refs_3_.1, f32[2,16,16]{2,1,0:T(8,128)} %refs_4_.1, f32[16,16]{1,0:T(8,128)} %refs_5_.1, ...), custom_call_target="tpu_custom_call" | custom-call | tf_op jit(solution)/shard_map/pack/pallas_call | solution.py:544
  1.3 0.1 column_far.1
  1.5 3.7 %collective-permute-start = (f32[37,8,128]{2,1,0:T(8,128)S(1)}, f32[37,8,128]{2,1,0:T(8,128)S(1)}, u32[]{:S(2)}, u32[]{:S(2)}) collective-permute-start(f32[37,8,128]{2,1,0:T(8,128)S(1)} %column_far.1), channel_id=1, source_target_pairs={{8,16},{16,8},{24,0},{0,24},{9,17},{17,9},{25,1},{1,25},{10,18},{1... | collective-permute-start | bytes 454664 | tf_op jit(solution)/shard_map/ppermute | solution.py:518
  5.1 0.1 column_near.1
  5.3 0.1 collective-permute-start.1
  5.4 1.9 %collective-permute-start.2 = (f32[37,8,128]{2,1,0:T(8,128)S(1)}, f32[37,8,128]{2,1,0:T(8,128)S(1)}, u32[]{:S(2)}, u32[]{:S(2)}) collective-permute-start(f32[37,8,128]{2,1,0:T(8,128)S(1)} %edge_far.1), channel_id=1, source_target_pairs={{2,4},{4,2},{3,5},{5,3},{10,12},{12,10},{11,13},{13,11},{18,20},{2... | collective-permute-start | bytes 454664 | tf_op jit(solution)/shard_map/ppermute | solution.py:518
  7.4 0.1 collective-permute-start.3
  7.5 0.6 %tables.1 = (bf16[1536,1024]{1,0:T(8,128)(2,1)S(1)}, bf16[512,1024]{1,0:T(8,128)(2,1)S(1)}, bf16[2,256,256]{2,1,0:T(8,128)(2,1)S(1)}, bf16[2048,256]{1,0:T(8,128...) custom-call(f32[8,16]{1,0:T(8,128)S(1)} %get-tuple-element.23.speed_table, ...), custom_call_target="tpu_custom_call" | custom-call | tf_op jit(solution)/shard_map/tables/pallas_call | solution.py:562
  8.0 2.1 %collective-permute-done.cols_second = f32[37,8,128]{2,1,0:T(8,128)S(1)} collective-permute-done((f32[37,8,128]{2,1,0:T(8,128)S(1)}, f32[37,8,128]{2,1,0:T(8,128)S(1)}, u32[]{:S(2)}, u32[]{:S(2)}) %collective-permute-start) | collective-permute-done | bytes 151584 | tf_op jit(solution)/shard_map/ppermute | solution.py:518
  10.2 2.3 %collective-permute-done.1.cols_first = f32[37,8,128]{2,1,0:T(8,128)S(1)} collective-permute-done((f32[37,8,128]{2,1,0:T(8,128)S(1)}, f32[37,8,128]{2,1,0:T(8,128)S(1)}, u32[]{:S(2)}, u32[]{:S(2)}) %collective-permute-start.1) | collective-permute-done | bytes 151584 | tf_op jit(solution)/shard_map/ppermute | solution.py:518
  12.6 1.6 %collective-permute-done.4.rims_pair = f32[2,37,8,128]{3,2,1,0:T(8,128)S(1)} collective-permute-done((f32[2,37,8,128]{3,2,1,0:T(8,128)S(1)}, f32[2,37,8,128]{3,2,1,0:T(8,128)S(1)}, u32[]{:S(2)}, u32[]{:S(2)}) %collective-permute-start.4) | collective-permute-done | bytes 303136 | tf_op jit(solution)/shard_map/ppermute | solution.py:518
  14.2 1.3 %collective-permute-start.5 = (f32[37,8,128]{2,1,0:T(8,128)S(1)}, f32[37,8,128]{2,1,0:T(8,128)S(1)}, u32[]{:S(2)}, u32[]{:S(2)}) collective-permute-start(f32[37,8,128]{2,1,0:T(8,128)S(1)} %relay.1), channel_id=1, source_target_pairs={{0,4},{6,2},{1,5},{7,3},{8,12},{14,10},{9,13},{15,11},{16,20},{22,... | collective-permute-start | bytes 454664 | tf_op jit(solution)/shard_map/ppermute | solution.py:524
  15.5 1.2 %place.1.partial = f32[37,8,8,128]{3,2,1,0:T(8,128)S(1)} custom-call(f32[2,37,8,128]{3,2,1,0:T(8,128)S(1)} %get-tuple-element.22.own, f32[37,8,128]{2,1,0:T(8,128)S(1)} %collective-permute-done.cols_second, f32[37,8,128]{2,1,0:T(8,128)S(1)} %collective-permute-done.1.cols_first, f32[37,8,128]{2,1,0:T(8,128)S(1)} %collective-permute-done.2.rows_second, ...), custom_call_target="tpu_custom_call" | custom-call | tf_op jit(solution)/shard_map/place/pallas_call | solution.py:576
  16.6 4.6 %collective-permute-done.5.rims_second = f32[37,8,128]{2,1,0:T(8,128)S(1)} collective-permute-done((f32[37,8,128]{2,1,0:T(8,128)S(1)}, f32[37,8,128]{2,1,0:T(8,128)S(1)}, u32[]{:S(2)}, u32[]{:S(2)}) %collective-permute-start.5) | collective-permute-done | bytes 151584 | tf_op jit(solution)/shard_map/ppermute | solution.py:524
  21.2 1.0 %rims.1 = (f32[37,8,8,128]{3,2,1,0:T(8,128)S(1)}, f32[10,2,4,8,8,128]{5,4,3,2,1,0:T(8,128)S(1)}, f32[8,8,128]{2,1,0:T(8,128)S(1)}, f32[8,8,128]{2,1,0:T(8,128)S(1)}, f32[8,8,128]{2,1,0:T(8,128)S(1)}) custom-call(f32[37,8,8,128]{3,2,1,0:T(8,128)S(1)} %place.1.partial, f32[37,8,128]{2,1,0:T(8,128)S(1)} %collective-permute-done.5.rims_second, ...), custom_call_target="tpu_custom_call" | custom-call | tf_op jit(solution)/shard_map/rims/pallas_call | solution.py:583
  22.3 0.7 %lon.4.q = f32[36,8,8,128]{3,2,1,0:T(8,128)S(1)} custom-call(f32[37,8,8,128]{3,2,1,0:T(8,128)S(1)} %get-tuple-element.29.q, f32[10,2,4,8,8,128]{5,4,3,2,1,0:T(8,128)S(1)} %get-tuple-element.30.taps, bf16[2,256,256]{2,1,0:T(8,128)(2,1)S(1)} %get-tuple-element.31.shifts), custom_call_target="tpu_custom_call" | custom-call | tf_op jit(solution)/shard_map/lon/pallas_call | solution.py:592
  23.0 0.5 %lat.3.q = f32[36,8,8,128]{3,2,1,0:T(8,128)S(1)} custom-call(f32[36,8,8,128]{3,2,1,0:T(8,128)S(1)} %lon.4.q, f32[8,8,128]{2,1,0:T(8,128)S(1)} %get-tuple-element.32.ky, f32[20,8,128]{2,1,0:T(8,128)S(1)} %get-tuple-element.27.consts), custom_call_target="tpu_custom_call" | custom-call | tf_op jit(solution)/shard_map/lat/pallas_call | solution.py:596
  23.6 0.6 %turn.3.q = f32[36,8,8,128]{3,2,1,0:T(8,128)S(1)} custom-call(f32[36,8,8,128]{3,2,1,0:T(8,128)S(1)} %lat.3.q, f32[8,8,128]{2,1,0:T(8,128)S(1)} %get-tuple-element.33.tx, f32[8,8,128]{2,1,0:T(8,128)S(1)} %get-tuple-element.34.ty), custom_call_target="tpu_custom_call" | custom-call | tf_op jit(solution)/shard_map/turn/pallas_call | solution.py:597
  24.2 0.7 %lon.5.q = f32[36,8,8,128]{3,2,1,0:T(8,128)S(1)} custom-call(f32[36,8,8,128]{3,2,1,0:T(8,128)S(1)} %turn.3.q, f32[10,2,4,8,8,128]{5,4,3,2,1,0:T(8,128)S(1)} %get-tuple-element.30.taps, bf16[2,256,256]{2,1,0:T(8,128)(2,1)S(1)} %get-tuple-element.31.shifts), custom_call_target="tpu_custom_call" | custom-call | tf_op jit(solution)/shard_map/lon/pallas_call | solution.py:592
  24.9 0.5 %lat.4.q = f32[36,8,8,128]{3,2,1,0:T(8,128)S(1)} custom-call(f32[36,8,8,128]{3,2,1,0:T(8,128)S(1)} %lon.5.q, f32[8,8,128]{2,1,0:T(8,128)S(1)} %get-tuple-element.32.ky, f32[20,8,128]{2,1,0:T(8,128)S(1)} %get-tuple-element.27.consts), custom_call_target="tpu_custom_call" | custom-call | tf_op jit(solution)/shard_map/lat/pallas_call | solution.py:596
  25.4 0.6 %turn.4.q = f32[36,8,8,128]{3,2,1,0:T(8,128)S(1)} custom-call(f32[36,8,8,128]{3,2,1,0:T(8,128)S(1)} %lat.4.q, f32[8,8,128]{2,1,0:T(8,128)S(1)} %get-tuple-element.33.tx, f32[8,8,128]{2,1,0:T(8,128)S(1)} %get-tuple-element.34.ty), custom_call_target="tpu_custom_call" | custom-call | tf_op jit(solution)/shard_map/turn/pallas_call | solution.py:597
  26.0 0.7 %lon.6.q = f32[36,8,8,128]{3,2,1,0:T(8,128)S(1)} custom-call(f32[36,8,8,128]{3,2,1,0:T(8,128)S(1)} %turn.4.q, f32[10,2,4,8,8,128]{5,4,3,2,1,0:T(8,128)S(1)} %get-tuple-element.30.taps, bf16[2,256,256]{2,1,0:T(8,128)(2,1)S(1)} %get-tuple-element.31.shifts), custom_call_target="tpu_custom_call" | custom-call | tf_op jit(solution)/shard_map/lon/pallas_call | solution.py:592
  26.8 0.5 %lat.5.q = f32[36,8,8,128]{3,2,1,0:T(8,128)S(1)} custom-call(f32[36,8,8,128]{3,2,1,0:T(8,128)S(1)} %lon.6.q, f32[8,8,128]{2,1,0:T(8,128)S(1)} %get-tuple-element.32.ky, f32[20,8,128]{2,1,0:T(8,128)S(1)} %get-tuple-element.27.consts), custom_call_target="tpu_custom_call" | custom-call | tf_op jit(solution)/shard_map/lat/pallas_call | solution.py:596
  27.3 0.6 %turn.5.q = f32[36,8,8,128]{3,2,1,0:T(8,128)S(1)} custom-call(f32[36,8,8,128]{3,2,1,0:T(8,128)S(1)} %lat.5.q, f32[8,8,128]{2,1,0:T(8,128)S(1)} %get-tuple-element.33.tx, f32[8,8,128]{2,1,0:T(8,128)S(1)} %get-tuple-element.34.ty), custom_call_target="tpu_custom_call" | custom-call | tf_op jit(solution)/shard_map/turn/pallas_call | solution.py:597
  27.9 0.7 %lon.7.q = f32[36,8,8,128]{3,2,1,0:T(8,128)S(1)} custom-call(f32[36,8,8,128]{3,2,1,0:T(8,128)S(1)} %turn.5.q, f32[10,2,4,8,8,128]{5,4,3,2,1,0:T(8,128)S(1)} %get-tuple-element.30.taps, bf16[2,256,256]{2,1,0:T(8,128)(2,1)S(1)} %get-tuple-element.31.shifts), custom_call_target="tpu_custom_call" | custom-call | tf_op jit(solution)/shard_map/lon/pallas_call | solution.py:592
  28.6 0.7 %lat_sums.1 = (f32[36,8,8,128]{3,2,1,0:T(8,128)S(1)}, f32[8,128]{1,0:T(8,128)S(1)}) custom-call(f32[36,8,8,128]{3,2,1,0:T(8,128)S(1)} %lon.7.q, f32[8,8,128]{2,1,0:T(8,128)S(1)} %get-tuple-element.32.ky, f32[20,8,128]{2,1,0:T(8,128)S(1)} %get-tuple-element.27.consts), custom_call_target="tpu_custom_call" | custom-call | tf_op jit(solution)/shard_map/lat_sums/pallas_call | solution.py:594
  29.3 1.5 %collective-permute-start.6 = (f32[8,128]{1,0:T(8,128)S(1)}, f32[8,128]{1,0:T(8,128)S(1)}, u32[]{:S(2)}, u32[]{:S(2)}) collective-permute-start(f32[8,128]{1,0:T(8,128)S(1)} %get-tuple-element.37.sums), channel_id=1, source_target_pairs={{0,1},{1,0},{2,3},{3,2},{4,5},{5,4},{6,7},{7,6},{8,9},{9,8},{10,11... | collective-permute-start | bytes 12296 | tf_op jit(solution)/shard_map/ppermute | solution.py:518
  30.9 0.1 growth.1.gain
  31.0 0.5 %gather.1.own = f32[2,36,8,128]{3,2,1,0:T(8,128)S(1)} custom-call(f32[36,8,8,128]{3,2,1,0:T(8,128)S(1)} %get-tuple-element.35.q, bf16[2048,256]{1,0:T(8,128)(2,1)S(1)} %get-tuple-element.36.matrix), custom_call_target="tpu_custom_call" | custom-call | tf_op jit(solution)/shard_map/gather/pallas_call | solution.py:599
  31.5 0.3 last_turn.1.early
  31.9 1.1 %collective-permute-done.6.other = f32[8,128]{1,0:T(8,128)S(1)} collective-permute-done((f32[8,128]{1,0:T(8,128)S(1)}, f32[8,128]{1,0:T(8,128)S(1)}, u32[]{:S(2)}, u32[]{:S(2)}) %collective-permute-start.6) | collective-permute-done | bytes 4128 | tf_op jit(solution)/shard_map/ppermute | solution.py:518
  33.0 1.1 %finish.1 = f32[16,16,288]{2,1,0:T(8,128)} custom-call(f32[256,288]{1,0:T(8,128)S(1)} %last_turn.1.early, f32[2,1,8,128]{3,2,1,0:T(8,128)S(1)} %slice.3.static, f32[8,128]{1,0:T(8,128)S(1)} %get-tuple-element.37.sums, f32[8,128]{1,0:T(8,128)S(1)} %collective-permute-done.6.other, f32[20,8,128]{2,1,0:T(8,128)S(1)} %get-tuple-element.27.consts, ...), custom_call_target="tpu_custom_call" | custom-call | tf_op jit(solution)/shard_map/finish/pallas_call | solution.py:610
  (8 shorter events, 0.2 us)
Async XLA Ops:
  1.5 8.7 %collective-permute-start = (f32[37,8,128]{2,1,0:T(8,128)S(1)}, f32[37,8,128]{2,1,0:T(8,128)S(1)}, u32[]{:S(2)}, u32[]{:S(2)}) collective-permute-start(f32[37,8,128]{2,1,0:T(8,128)S(1)} %column_far.1), channel_id=1, source_target_pairs={{8,16},{16,8},{24,0},{0,24},{9,17},{17,9},{25,1},{1,25},{10,18},{1... | collective-permute-start | bytes 454664 | tf_op jit(solution)/shard_map/ppermute | solution.py:518
  5.3 7.1 %collective-permute-start.1 = (f32[37,8,128]{2,1,0:T(8,128)S(1)}, f32[37,8,128]{2,1,0:T(8,128)S(1)}, u32[]{:S(2)}, u32[]{:S(2)}) collective-permute-start(f32[37,8,128]{2,1,0:T(8,128)S(1)} %column_near.1), channel_id=1, source_target_pairs={{0,8},{8,0},{16,24},{24,16},{1,9},{9,1},{17,25},{25,17},{2,10},{10... | collective-permute-start | bytes 454664 | tf_op jit(solution)/shard_map/ppermute | solution.py:518
  5.4 7.0 %collective-permute-start.2 = (f32[37,8,128]{2,1,0:T(8,128)S(1)}, f32[37,8,128]{2,1,0:T(8,128)S(1)}, u32[]{:S(2)}, u32[]{:S(2)}) collective-permute-start(f32[37,8,128]{2,1,0:T(8,128)S(1)} %edge_far.1), channel_id=1, source_target_pairs={{2,4},{4,2},{3,5},{5,3},{10,12},{12,10},{11,13},{13,11},{18,20},{2... | collective-permute-start | bytes 454664 | tf_op jit(solution)/shard_map/ppermute | solution.py:518
  7.4 5.1 %collective-permute-start.3 = (f32[37,8,128]{2,1,0:T(8,128)S(1)}, f32[37,8,128]{2,1,0:T(8,128)S(1)}, u32[]{:S(2)}, u32[]{:S(2)}) collective-permute-start(f32[37,8,128]{2,1,0:T(8,128)S(1)} %edge_near.1), channel_id=1, source_target_pairs={{0,2},{2,0},{4,6},{6,4},{1,3},{3,1},{5,7},{7,5},{8,10},{10,8},{12,... | collective-permute-start | bytes 454664 | tf_op jit(solution)/shard_map/ppermute | solution.py:518
  12.5 1.7 %collective-permute-start.4 = (f32[2,37,8,128]{3,2,1,0:T(8,128)S(1)}, f32[2,37,8,128]{3,2,1,0:T(8,128)S(1)}, u32[]{:S(2)}, u32[]{:S(2)}) collective-permute-start(f32[2,37,8,128]{3,2,1,0:T(8,128)S(1)} %corner.1), channel_id=1, source_target_pairs={{0,2},{2,0},{4,6},{6,4},{1,3},{3,1},{5,7},{7,5},{8,10},{10,8},{12,... | collective-permute-start | bytes 909320 | tf_op jit(solution)/shard_map/ppermute | solution.py:518
  14.2 7.1 %collective-permute-start.5 = (f32[37,8,128]{2,1,0:T(8,128)S(1)}, f32[37,8,128]{2,1,0:T(8,128)S(1)}, u32[]{:S(2)}, u32[]{:S(2)}) collective-permute-start(f32[37,8,128]{2,1,0:T(8,128)S(1)} %relay.1), channel_id=1, source_target_pairs={{0,4},{6,2},{1,5},{7,3},{8,12},{14,10},{9,13},{15,11},{16,20},{22,... | collective-permute-start | bytes 454664 | tf_op jit(solution)/shard_map/ppermute | solution.py:524
  29.3 3.6 %collective-permute-start.6 = (f32[8,128]{1,0:T(8,128)S(1)}, f32[8,128]{1,0:T(8,128)S(1)}, u32[]{:S(2)}, u32[]{:S(2)}) collective-permute-start(f32[8,128]{1,0:T(8,128)S(1)} %get-tuple-element.37.sums), channel_id=1, source_target_pairs={{0,1},{1,0},{2,3},{3,2},{4,5},{5,4},{6,7},{7,6},{8,9},{9,8},{10,11... | collective-permute-start | bytes 12296 | tf_op jit(solution)/shard_map/ppermute | solution.py:518

commit v7 on v6

--- a/solution.py
+++ b/solution.py
@@ -95,22 +95,52 @@
         own[1, d] = flat1[pl.ds(d, FREQ, stride=NDIR), :] * sea1
 
 
+WEST_PAIRS = [(33, 0), (34, 1), (35, 2)]
+EAST_PAIRS = [(15, 18), (16, 19), (17, 20)]
+
+
+def slots(pairs):
+    paired = [d for pair in pairs for d in pair]
+    return [d for d in range(SLABS) if d not in paired]
+
+
+SENT = SLABS - 3
+
+
 def column_kernel(second, own, message):
     inner = lanes() % 16
     to_east = is_even("lon") != second
-    for slab in range(SLABS):
-        own0, own1 = own[0, slab], own[1, slab]
-        east = jnp.where(inner >= 8, own0, roll(own1, -8))
-        west = jnp.where(inner < 8, own0, roll(own1, 8))
-        message[slab] = jnp.where(to_east, east, west)
-
-
-def edge_kernel(second, own, edge):
-    even = is_even("lat")
-    if second:
-        edge[...] = jnp.where(even, own[0], own[1])
-    else:
-        edge[...] = jnp.where(even, own[1], own[0])
+    from_own0 = (inner >= 8) == to_east
+    shift = jnp.where(to_east, 120, 8)
+
+    def edge(slab):
+        return jnp.where(from_own0, own[0, slab], pltpu.roll(own[1, slab], shift, 1))
+
+    for i, (east, west) in enumerate(zip(slots(EAST_PAIRS), slots(WEST_PAIRS))):
+        if east == west:
+            message[i] = edge(east)
+        else:
+            message[i] = edge(jnp.where(to_east, east, west))
+    near = (inner % 8 >= 4) == to_east
+    for i, (east, west) in enumerate(zip(EAST_PAIRS, WEST_PAIRS)):
+        one = edge(jnp.where(to_east, east[0], west[0]))
+        two = edge(jnp.where(to_east, east[1], west[1]))
+        message[SENT - 3 + i] = jnp.where(near, one, pltpu.roll(two, jnp.where(to_east, 124, 4), 1))
+
+
+NORTH_PAIRS = [(24, 27), (25, 28), (26, 29)]
+SOUTH_PAIRS = [(6, 9), (7, 10), (8, 11)]
+
+
+def edge_kernel(second, own, message):
+    to_north = is_even("lat") != second
+    for i, (north, south) in enumerate(zip(slots(NORTH_PAIRS), slots(SOUTH_PAIRS))):
+        message[i] = jnp.where(to_north, own[1, north], own[0, south])
+    near = (lanes() >= 64) == to_north
+    for i, (north, south) in enumerate(zip(NORTH_PAIRS, SOUTH_PAIRS)):
+        one = jnp.where(to_north, own[1, north[0]], own[0, south[0]])
+        two = jnp.where(to_north, own[1, north[1]], own[0, south[1]])
+        message[SENT - 3 + i] = jnp.where(near, one, roll(two, 64))
 
 
 def growth_kernel(own, consts, gain):
@@ -152,9 +182,10 @@
     consts[STRETCH] = 1.0 / jnp.cos(latitude)
     ghost = ((group == 0) & (lat == 0)) | ((group == 3) & (lat == lats - 1))
     consts[LIVE] = jnp.where(ghost, 0.0, 1.0)
-    comp = lax.broadcasted_iota(jnp.int32, (16, NDIR * FREQ), 1) // NDIR
-    freq = lax.broadcasted_iota(jnp.int32, (16, NDIR * FREQ), 0) % FREQ
-    spread[...] = (comp == freq).astype(f32).astype(bf16)
+    comp = lax.broadcasted_iota(jnp.int32, (32, 384), 1) // NDIR
+    freq = lax.broadcasted_iota(jnp.int32, (32, 384), 0) % 16
+    for half in range(2):
+        spread[:, 384 * half : 384 * half + 384] = (comp == freq - 8 * half).astype(f32).astype(bf16)
 
     chunk = lax.broadcasted_iota(jnp.int32, (16, 128), 0)
     lane = lax.broadcasted_iota(jnp.int32, (16, 128), 1)
@@ -192,21 +223,35 @@
                 gather[at : at + 128, 128 * half : 128 * half + 128] = moved
 
 
-def corner_kernel(cols_second, cols_first, rows_second, rows_first, consts, rim):
+def unpack(even, first, second, pairs, out, back):
+    full = slots(pairs)
+    for i in range(SENT):
+        got = jnp.where(even, first[i], second[i])
+        if i < len(full):
+            out[full[i]] = got
+        else:
+            pair = pairs[i - len(full)]
+            out[pair[0]] = got
+            out[pair[1]] = roll(got, back)
+
+
+def unpack_kernel(cols_second, cols_first, rows_second, rows_first, consts, west, east):
     del rows_second, rows_first, consts
-    low = lanes() % 16 < 8
-    even_lon = is_even("lon")
-    west_low = low == is_even("lat")
+    even = is_even("lon")
+    unpack(even, cols_second, cols_first, EAST_PAIRS, west, 4)
+    unpack(even, cols_first, cols_second, WEST_PAIRS, east, -4)
+
+
+def unpack_rows_kernel(rows_second, rows_first, south, north):
+    even = is_even("lat")
+    unpack(even, rows_second, rows_first, NORTH_PAIRS, south, 64)
+    unpack(even, rows_first, rows_second, SOUTH_PAIRS, north, 64)
+
+
+def rim_kernel(second, west, east, rim):
+    west_low = (lanes() % 16 < 8) == (is_even("lat") != second)
     for slab in range(SLABS):
-        one, two = cols_first[slab], cols_second[slab]
-        east = jnp.where(even_lon, one, two)
-        west = jnp.where(even_lon, two, one)
-        rim[0, slab] = jnp.where(west_low, west, east)
-        rim[1, slab] = jnp.where(west_low, east, west)
-
-
-def relay_kernel(rims_pair, beyond):
-    beyond[...] = rims_pair[1]
+        rim[slab] = jnp.where(west_low, west[slab], east[slab])
 
 
 def split(x):
@@ -221,15 +266,13 @@
     lhs[:, 128 * (count + s) : 128 * (count + s) + 128] = low
 
 
-def place_kernel(own, cols_second, cols_first, rows_second, rows_first, matrix, q, lhs):
-    even_lon = is_even("lon")
-    even_lat = is_even("lat")
+def place_kernel(own, west, east, south, north, matrix, q, lhs):
     fill_parts(lhs, 6, 0, own[0])
     fill_parts(lhs, 6, 1, own[1])
-    fill_parts(lhs, 6, 2, jnp.where(even_lon, cols_second[...], cols_first[...]))
-    fill_parts(lhs, 6, 3, jnp.where(even_lon, cols_first[...], cols_second[...]))
-    fill_parts(lhs, 6, 4, jnp.where(even_lat, rows_second[...], rows_first[...]))
-    fill_parts(lhs, 6, 5, jnp.where(even_lat, rows_first[...], rows_second[...]))
+    fill_parts(lhs, 6, 2, west[...])
+    fill_parts(lhs, 6, 3, east[...])
+    fill_parts(lhs, 6, 4, south[...])
+    fill_parts(lhs, 6, 5, north[...])
     for pair in range(4):
         moved = jnp.dot(lhs[...], matrix[:, 256 * pair : 256 * pair + 256], preferred_element_type=f32)
         for i in range(2):
@@ -244,19 +287,25 @@
     return value * point[SEA : SEA + 1]
 
 
-def rims_kernel(partial, rims_second, rims_pair, consts, matrix, q, taps, ky, tx, ty, lhs):
+def rims_kernel(partial, rims_second, rims_first, consts, matrix, q, taps, ky, tx, ty, lhs):
     even_lat = is_even("lat")
-    fill_parts(lhs, 2, 0, jnp.where(even_lat, rims_second[...], rims_pair[0]))
-    fill_parts(lhs, 2, 1, jnp.where(even_lat, rims_pair[0], rims_second[...]))
-    for pair in range(4):
-        moved = jnp.dot(lhs[...], matrix[:, 256 * pair : 256 * pair + 256], preferred_element_type=f32)
-        for i in range(2):
-            t = 2 * pair + i
-            q[:, t] = partial[:, t] + moved[: 8 * SLABS, 128 * i : 128 * i + 128].reshape(SLABS, 8, 128)
-
+    south = jnp.where(even_lat, rims_second[...], rims_first[...])
+    north = jnp.where(even_lat, rims_first[...], rims_second[...])
+    for s, array in ((0, south), (1, north)):
+        high, low = split(array[:NDIR].reshape(8 * NDIR, 128))
+        lhs[:, 128 * s : 128 * s + 128] = high
+        lhs[:, 128 * (2 + s) : 128 * (2 + s) + 128] = low
+    lane = lanes()
+    south, north = south[STATIC], north[STATIC]
     speed = []
     for t in range(8):
-        point = q[STATIC, t]
+        if t % 2 == 0:
+            moved = jnp.dot(lhs[...], matrix[:, 128 * t : 128 * t + 256], preferred_element_type=f32)
+            for i in range(2):
+                q[:, t + i] = partial[:NDIR, t + i] + moved[:, 128 * i : 128 * i + 128].reshape(NDIR, 8, 128)
+        point = partial[STATIC, t]
+        for low, array, shift in ((0, south, 0), (24, south, 16), (96, north, 88), (120, north, 120)):
+            point = jnp.where((lane >= low) & (lane < low + 8), roll(array, shift - 16 * t), point)
         pace = lookup(point, consts, TAB_SPEED)
         turning = lookup(point, consts, TAB_TURN)
         speed.append(pace)
@@ -472,18 +521,21 @@
 
 def finish_kernel(early, static, sums, other, consts, spread, out, ready, sems):
     total = sums[...] + other[...]
+    level = consts[LEVEL]
+    losses = []
     for half in range(2):
         energy = total[half : half + 1]
         moment = total[2 + half : 3 + half]
         mean_level = jnp.maximum(moment, 1.0) / jnp.maximum(energy, 1.0)
         mean = energy / NCOMP
-        level = consts[LEVEL]
         breaking = break_coef * level * level / mean_level * (mean * mean)
         damping = static[half, 0, ICE : ICE + 1] * consts[ICE_RATE]
-        loss = jnp.exp(-breaking - damping)
-        parts = jnp.concatenate(split(loss.T), axis=1)
-        wide = jnp.dot(parts, spread[...], preferred_element_type=f32)
-        result = early[128 * half : 128 * half + 128, :] * wide
+        losses.append(jnp.exp(-breaking - damping))
+    turned = jnp.concatenate(losses, axis=0).T
+    wide = jnp.dot(jnp.concatenate(split(turned), axis=1), spread[...], preferred_element_type=f32)
+    for half in range(2):
+        loss = wide[:, 384 * half : 384 * half + NDIR * FREQ]
+        result = early[128 * half : 128 * half + 128, :] * loss
         mine = pl.ds(8 * half, 8)
         ready[mine] = result.reshape(8, 16, NDIR * FREQ)
         pltpu.make_async_copy(ready.at[mine], out.at[mine], sems.at[half]).start()
@@ -515,12 +567,6 @@
         if i + 1 < count or closed:
             j = (i + 1) % count
             pairs += [(i, j), (j, i)]
-    return lax.ppermute(array, axis, pairs)
-
-
-def skip(array, axis):
-    count = lax.axis_size(axis)
-    pairs = [(i, i + 2) for i in range(0, count - 2, 2)] + [(i, i - 2) for i in range(3, count, 2)]
     return lax.ppermute(array, axis, pairs)
 
 
@@ -539,6 +585,7 @@
     tile = (8, 128)
     block = (8,) + tile
     slabs = (SLABS,) + tile
+    sent = (SENT,) + tile
     inputs = [spectrum, sea_mask, ice_mask, depth_class, depth_slope, wind_speed, wind_dir]
     tables = [speed_table, refraction_table, ice_rate]
     own, speeds, turnings, ices = call(
@@ -551,42 +598,44 @@
         name="pack",
         space=pltpu.HBM,
     )(*[pltpu.with_memory_space_constraint(x, pltpu.HBM) for x in inputs + tables])
-    (to_second,) = call(functools.partial(column_kernel, True), 1, [slabs], name="column_far")(own)
+    (to_second,) = call(functools.partial(column_kernel, True), 1, [sent], name="column_far")(own)
     cols_second = swap(to_second, "lon", 1, True)
-    (to_first,) = call(functools.partial(column_kernel, False), 1, [slabs], name="column_near")(own)
+    (to_first,) = call(functools.partial(column_kernel, False), 1, [sent], name="column_near")(own)
     cols_first = swap(to_first, "lon", 0, True)
-    (edge_second,) = call(functools.partial(edge_kernel, True), 1, [slabs], name="edge_far")(own)
+    (edge_second,) = call(functools.partial(edge_kernel, True), 1, [sent], name="edge_far")(own)
     rows_second = swap(edge_second, "lat", 1)
-    (edge_first,) = call(functools.partial(edge_kernel, False), 1, [slabs], name="edge_near")(own)
+    (edge_first,) = call(functools.partial(edge_kernel, False), 1, [sent], name="edge_near")(own)
     rows_first = swap(edge_first, "lat", 0)
     place, rims, shifts, gather, spread, consts = call(
         tables_kernel,
         3,
-        [(1536, 1024), (512, 1024), (2, 256, 256), (2048, 256), (16, NDIR * FREQ), (20,) + tile],
+        [(1536, 1024), (512, 1024), (2, 256, 256), (2048, 256), (32, 768), (20,) + tile],
         name="tables",
         dtype=[bf16] * 5 + [f32],
     )(speeds, turnings, ices)
     (gain,) = call(growth_kernel, 2, [(NDIR, 2) + tile], name="growth")(own, consts)
-    (rim,) = call(corner_kernel, 5, [(2,) + slabs], name="corner")(
+    west, east = call(unpack_kernel, 5, [slabs] * 2, name="unpack")(
         cols_second, cols_first, rows_second, rows_first, consts
     )
-    rims_pair = swap(rim, "lat", 0)
-    (beyond,) = call(relay_kernel, 1, [slabs], name="relay")(rims_pair)
-    rims_second = skip(beyond, "lat")
+    (rim_second,) = call(functools.partial(rim_kernel, True), 2, [slabs], name="rim_far")(west, east)
+    rims_second = swap(rim_second, "lat", 1)
+    (rim_first,) = call(functools.partial(rim_kernel, False), 2, [slabs], name="rim_near")(west, east)
+    rims_first = swap(rim_first, "lat", 0)
+    south, north = call(unpack_rows_kernel, 2, [slabs] * 2, name="unpack_rows")(rows_second, rows_first)
     (partial,) = call(
         place_kernel,
         6,
         [(SLABS,) + block],
         [pltpu.VMEM((8 * SLABS + 8, 1536), bf16)],
         name="place",
-    )(own, cols_second, cols_first, rows_second, rows_first, place)
+    )(own, west, east, south, north, place)
     q, taps, ky, tx, ty = call(
         rims_kernel,
         5,
-        [(SLABS,) + block, (10, 2, 4) + block] + [block] * 3,
-        [pltpu.VMEM((8 * SLABS + 8, 512), bf16)],
+        [(NDIR,) + block, (10, 2, 4) + block] + [block] * 3,
+        [pltpu.VMEM((8 * NDIR, 512), bf16)],
         name="rims",
-    )(partial, rims_second, rims_pair, consts, rims)
+    )(partial, rims_second, rims_first, consts, rims)
     cells = [(NDIR,) + block]
     for substep in range(ITERS):
         (q,) = call(lon_kernel, 3, cells, [pltpu.VMEM((4, 576, 256), f32)], name="lon")(q, taps, shifts)

time: 34.7 us -> 31.7 us (0.914)
  waiting for transfers between devices: 11.7 us -> 7.97 us
  starting transfers between devices: 8.63 us -> 9.34 us
    ppermute x1 -> x0, waiting for transfers between devices: 4.61 us -> none  [skip(): return lax.ppermute(array, axis, pairs)]
    ppermute x6 -> x7, starting transfers between devices: 7.33 us -> 9.34 us  [swap(): return lax.ppermute(array, axis, pairs)]
    ppermute x1 -> x0, starting transfers between devices: 1.29 us -> none  [skip(): return lax.ppermute(array, axis, pairs)]
    ppermute x6 -> x7, waiting for transfers between devices: 7.1 us -> 7.97 us  [swap(): return lax.ppermute(array, axis, pairs)]
    pallas_call x7 -> x9, Pallas kernels: 1.43 us -> 1.6 us  [the longest x1 0.86 us: per_device(): call(rims_kernel, 5, [(NDIR,) + block, (10, 2, 4) + block] + [block] * 3,...]
  transfers between devices with their start and end apart: 7 -> 7, of which waited for: 5 -> 4; matrix products, arithmetic and copies ran while one was open for 0% -> 0% of each run, Pallas kernels for 8% -> 10%
where the time goes in v7:
time: 31.7 us; the launch traced here: 31.2 us
  Pallas kernels  13.7 us (43%)
  starting transfers between devices  9.34 us (29%)
  waiting for transfers between devices  7.97 us (25%)
    ppermute x7, starting transfers between devices, swap(): return lax.ppermute(array, axis, pairs)  9.34 us
    ppermute x7, waiting for transfers between devices, swap(): return lax.ppermute(array, axis, pairs)  7.97 us
    pallas_call x4, Pallas kernels, per_device(): call(lon_kernel, 3, cells, [pltpu.VMEM((4, 576, 256), f32)], name='lon')  2.85 us
    pallas_call x3, Pallas kernels, per_device(): q, = call(turn_kernel, 3, cells, name='turn')(q, tx, ty)  1.73 us
    pallas_call x3, Pallas kernels, per_device(): q, = call(lat_kernel, 3, cells, name='lat')(q, ky, consts)  1.63 us
    pallas_call x1, Pallas kernels, per_device(): call(pack_kernel, 10, [(2,) + slabs] + [x.shape for x in tables], [pltpu....  1.32 us
    pallas_call x1, Pallas kernels, per_device(): call(place_kernel, 6, [(SLABS,) + block], [pltpu.VMEM((8 * SLABS + 8, 153...  1.2 us
    pallas_call x1, Pallas kernels, per_device(): call(finish_kernel, 6, [spectrum.shape], [pltpu.VMEM(spectrum.shape, f32)...  1.13 us
  transfers between devices with their start and end apart: 7, of which 4 were waited for; matrix products, arithmetic and copies ran while one was open for 0% of the time, Pallas kernels for 10%

profile of v7, /device:TPU:2, one launch (start us, length us, event | category | flops | bytes accessed | tf_op | source)
XLA Modules:
  0.0 31.2 jit_solution(14713977912855391950)
XLA Ops:
  0.0 1.3 %pack.1 = (f32[2,37,8,128]{3,2,1,0:T(8,128)S(1)}, f32[8,16]{1,0:T(8,128)S(1)}, f32[8,16]{1,0:T(8,128)S(1)}, f32[16]{0:T(128)S(1)}) custom-call(f32[16,16,288]{2,1,0:T(8,128)} %refs_0_.1, s32[16,16]{1,0:T(8,128)} %refs_1_.1, s32[16,16]{1,0:T(8,128)} %refs_2_.1, s32[16,16]{1,0:T(8,128)} %refs_3_.1, f32[2,16,16]{2,1,0:T(8,128)} %refs_4_.1, f32[16,16]{1,0:T(8,128)} %refs_5_.1, ...), custom_call_target="tpu_custom_call" | custom-call | tf_op jit(solution)/shard_map/pack/pallas_call | solution.py:591
  1.3 0.2 column_far.1
  1.5 3.7 %collective-permute-start = (f32[34,8,128]{2,1,0:T(8,128)S(1)}, f32[34,8,128]{2,1,0:T(8,128)S(1)}, u32[]{:S(2)}, u32[]{:S(2)}) collective-permute-start(f32[34,8,128]{2,1,0:T(8,128)S(1)} %column_far.1), channel_id=1, source_target_pairs={{8,16},{16,8},{24,0},{0,24},{9,17},{17,9},{25,1},{1,25},{10,18},{1... | collective-permute-start | bytes 417800 | tf_op jit(solution)/shard_map/ppermute | solution.py:570
  5.1 0.1 column_near.1
  5.3 0.1 edge_far.1
  5.4 1.9 %collective-permute-start.2 = (f32[34,8,128]{2,1,0:T(8,128)S(1)}, f32[34,8,128]{2,1,0:T(8,128)S(1)}, u32[]{:S(2)}, u32[]{:S(2)}) collective-permute-start(f32[34,8,128]{2,1,0:T(8,128)S(1)} %edge_far.1), channel_id=1, source_target_pairs={{2,4},{4,2},{3,5},{5,3},{10,12},{12,10},{11,13},{13,11},{18,20},{2... | collective-permute-start | bytes 417800 | tf_op jit(solution)/shard_map/ppermute | solution.py:570
  7.5 0.6 %tables.1 = (bf16[1536,1024]{1,0:T(8,128)(2,1)S(1)}, bf16[512,1024]{1,0:T(8,128)(2,1)S(1)}, bf16[2,256,256]{2,1,0:T(8,128)(2,1)S(1)}, bf16[2048,256]{1,0:T(8,128...) custom-call(f32[8,16]{1,0:T(8,128)S(1)} %get-tuple-element.27.speed_table, ...), custom_call_target="tpu_custom_call" | custom-call | tf_op jit(solution)/shard_map/tables/pallas_call | solution.py:609
  8.0 1.9 %collective-permute-done.cols_second = f32[34,8,128]{2,1,0:T(8,128)S(1)} collective-permute-done((f32[34,8,128]{2,1,0:T(8,128)S(1)}, f32[34,8,128]{2,1,0:T(8,128)S(1)}, u32[]{:S(2)}, u32[]{:S(2)}) %collective-permute-start) | collective-permute-done | bytes 139296 | tf_op jit(solution)/shard_map/ppermute | solution.py:570
  9.9 2.0 %collective-permute-done.1.cols_first = f32[34,8,128]{2,1,0:T(8,128)S(1)} collective-permute-done((f32[34,8,128]{2,1,0:T(8,128)S(1)}, f32[34,8,128]{2,1,0:T(8,128)S(1)}, u32[]{:S(2)}, u32[]{:S(2)}) %collective-permute-start.1) | collective-permute-done | bytes 139296 | tf_op jit(solution)/shard_map/ppermute | solution.py:570
  11.9 0.1 unpack.1
  12.1 2.1 %collective-permute-start.4 = (f32[37,8,128]{2,1,0:T(8,128)S(1)}, f32[37,8,128]{2,1,0:T(8,128)S(1)}, u32[]{:S(2)}, u32[]{:S(2)}) collective-permute-start(f32[37,8,128]{2,1,0:T(8,128)S(1)} %rim_far.1), channel_id=1, source_target_pairs={{2,4},{4,2},{3,5},{5,3},{10,12},{12,10},{11,13},{13,11},{18,20},{2... | collective-permute-start | bytes 454664 | tf_op jit(solution)/shard_map/ppermute | solution.py:570
  14.3 0.1 unpack_rows.1
  14.4 1.2 %place.1.partial = f32[37,8,8,128]{3,2,1,0:T(8,128)S(1)} custom-call(f32[2,37,8,128]{3,2,1,0:T(8,128)S(1)} %get-tuple-element.26.own, f32[37,8,128]{2,1,0:T(8,128)S(1)} %get-tuple-element.31.west, f32[37,8,128]{2,1,0:T(8,128)S(1)} %get-tuple-element.32.east, f32[37,8,128]{2,1,0:T(8,128)S(1)} %get-tuple-element.33.south, ...), custom_call_target="tpu_custom_call" | custom-call | tf_op jit(solution)/shard_map/place/pallas_call | solution.py:625
  15.6 3.0 %collective-permute-done.4.rims_second = f32[37,8,128]{2,1,0:T(8,128)S(1)} collective-permute-done((f32[37,8,128]{2,1,0:T(8,128)S(1)}, f32[37,8,128]{2,1,0:T(8,128)S(1)}, u32[]{:S(2)}, u32[]{:S(2)}) %collective-permute-start.4) | collective-permute-done | bytes 151584 | tf_op jit(solution)/shard_map/ppermute | solution.py:570
  18.6 0.9 %rims.1 = (f32[36,8,8,128]{3,2,1,0:T(8,128)S(1)}, f32[10,2,4,8,8,128]{5,4,3,2,1,0:T(8,128)S(1)}, f32[8,8,128]{2,1,0:T(8,128)S(1)}, f32[8,8,128]{2,1,0:T(8,128)S(1)}, f32[8,8,128]{2,1,0:T(8,128)S(1)}) custom-call(f32[37,8,8,128]{3,2,1,0:T(8,128)S(1)} %place.1.partial, f32[37,8,128]{2,1,0:T(8,128)S(1)} %collective-permute-done.4.rims_second, ...), custom_call_target="tpu_custom_call" | custom-call | tf_op jit(solution)/shard_map/rims/pallas_call | solution.py:632
  19.5 0.7 %lon.4.q = f32[36,8,8,128]{3,2,1,0:T(8,128)S(1)} custom-call(f32[36,8,8,128]{3,2,1,0:T(8,128)S(1)} %get-tuple-element.37.q, f32[10,2,4,8,8,128]{5,4,3,2,1,0:T(8,128)S(1)} %get-tuple-element.38.taps, bf16[2,256,256]{2,1,0:T(8,128)(2,1)S(1)} %get-tuple-element.39.shifts), custom_call_target="tpu_custom_call" | custom-call | tf_op jit(solution)/shard_map/lon/pallas_call | solution.py:641
  20.2 0.5 %lat.3.q = f32[36,8,8,128]{3,2,1,0:T(8,128)S(1)} custom-call(f32[36,8,8,128]{3,2,1,0:T(8,128)S(1)} %lon.4.q, f32[8,8,128]{2,1,0:T(8,128)S(1)} %get-tuple-element.40.ky, f32[20,8,128]{2,1,0:T(8,128)S(1)} %get-tuple-element.30.consts), custom_call_target="tpu_custom_call" | custom-call | tf_op jit(solution)/shard_map/lat/pallas_call | solution.py:645
  20.7 0.6 %turn.3.q = f32[36,8,8,128]{3,2,1,0:T(8,128)S(1)} custom-call(f32[36,8,8,128]{3,2,1,0:T(8,128)S(1)} %lat.3.q, f32[8,8,128]{2,1,0:T(8,128)S(1)} %get-tuple-element.41.tx, f32[8,8,128]{2,1,0:T(8,128)S(1)} %get-tuple-element.42.ty), custom_call_target="tpu_custom_call" | custom-call | tf_op jit(solution)/shard_map/turn/pallas_call | solution.py:646
  21.3 0.7 %lon.5.q = f32[36,8,8,128]{3,2,1,0:T(8,128)S(1)} custom-call(f32[36,8,8,128]{3,2,1,0:T(8,128)S(1)} %turn.3.q, f32[10,2,4,8,8,128]{5,4,3,2,1,0:T(8,128)S(1)} %get-tuple-element.38.taps, bf16[2,256,256]{2,1,0:T(8,128)(2,1)S(1)} %get-tuple-element.39.shifts), custom_call_target="tpu_custom_call" | custom-call | tf_op jit(solution)/shard_map/lon/pallas_call | solution.py:641
  22.0 0.5 %lat.4.q = f32[36,8,8,128]{3,2,1,0:T(8,128)S(1)} custom-call(f32[36,8,8,128]{3,2,1,0:T(8,128)S(1)} %lon.5.q, f32[8,8,128]{2,1,0:T(8,128)S(1)} %get-tuple-element.40.ky, f32[20,8,128]{2,1,0:T(8,128)S(1)} %get-tuple-element.30.consts), custom_call_target="tpu_custom_call" | custom-call | tf_op jit(solution)/shard_map/lat/pallas_call | solution.py:645
  22.6 0.6 %turn.4.q = f32[36,8,8,128]{3,2,1,0:T(8,128)S(1)} custom-call(f32[36,8,8,128]{3,2,1,0:T(8,128)S(1)} %lat.4.q, f32[8,8,128]{2,1,0:T(8,128)S(1)} %get-tuple-element.41.tx, f32[8,8,128]{2,1,0:T(8,128)S(1)} %get-tuple-element.42.ty), custom_call_target="tpu_custom_call" | custom-call | tf_op jit(solution)/shard_map/turn/pallas_call | solution.py:646
  23.2 0.7 %lon.6.q = f32[36,8,8,128]{3,2,1,0:T(8,128)S(1)} custom-call(f32[36,8,8,128]{3,2,1,0:T(8,128)S(1)} %turn.4.q, f32[10,2,4,8,8,128]{5,4,3,2,1,0:T(8,128)S(1)} %get-tuple-element.38.taps, bf16[2,256,256]{2,1,0:T(8,128)(2,1)S(1)} %get-tuple-element.39.shifts), custom_call_target="tpu_custom_call" | custom-call | tf_op jit(solution)/shard_map/lon/pallas_call | solution.py:641
  23.9 0.5 %lat.5.q = f32[36,8,8,128]{3,2,1,0:T(8,128)S(1)} custom-call(f32[36,8,8,128]{3,2,1,0:T(8,128)S(1)} %lon.6.q, f32[8,8,128]{2,1,0:T(8,128)S(1)} %get-tuple-element.40.ky, f32[20,8,128]{2,1,0:T(8,128)S(1)} %get-tuple-element.30.consts), custom_call_target="tpu_custom_call" | custom-call | tf_op jit(solution)/shard_map/lat/pallas_call | solution.py:645
  24.4 0.6 %turn.5.q = f32[36,8,8,128]{3,2,1,0:T(8,128)S(1)} custom-call(f32[36,8,8,128]{3,2,1,0:T(8,128)S(1)} %lat.5.q, f32[8,8,128]{2,1,0:T(8,128)S(1)} %get-tuple-element.41.tx, f32[8,8,128]{2,1,0:T(8,128)S(1)} %get-tuple-element.42.ty), custom_call_target="tpu_custom_call" | custom-call | tf_op jit(solution)/shard_map/turn/pallas_call | solution.py:646
  25.0 0.7 %lon.7.q = f32[36,8,8,128]{3,2,1,0:T(8,128)S(1)} custom-call(f32[36,8,8,128]{3,2,1,0:T(8,128)S(1)} %turn.5.q, f32[10,2,4,8,8,128]{5,4,3,2,1,0:T(8,128)S(1)} %get-tuple-element.38.taps, bf16[2,256,256]{2,1,0:T(8,128)(2,1)S(1)} %get-tuple-element.39.shifts), custom_call_target="tpu_custom_call" | custom-call | tf_op jit(solution)/shard_map/lon/pallas_call | solution.py:641
  25.7 0.7 %lat_sums.1 = (f32[36,8,8,128]{3,2,1,0:T(8,128)S(1)}, f32[8,128]{1,0:T(8,128)S(1)}) custom-call(f32[36,8,8,128]{3,2,1,0:T(8,128)S(1)} %lon.7.q, f32[8,8,128]{2,1,0:T(8,128)S(1)} %get-tuple-element.40.ky, f32[20,8,128]{2,1,0:T(8,128)S(1)} %get-tuple-element.30.consts), custom_call_target="tpu_custom_call" | custom-call | tf_op jit(solution)/shard_map/lat_sums/pallas_call | solution.py:643
  26.5 1.5 %collective-permute-start.6 = (f32[8,128]{1,0:T(8,128)S(1)}, f32[8,128]{1,0:T(8,128)S(1)}, u32[]{:S(2)}, u32[]{:S(2)}) collective-permute-start(f32[8,128]{1,0:T(8,128)S(1)} %get-tuple-element.45.sums), channel_id=1, source_target_pairs={{0,1},{1,0},{2,3},{3,2},{4,5},{5,4},{6,7},{7,6},{8,9},{9,8},{10,11... | collective-permute-start | bytes 12296 | tf_op jit(solution)/shard_map/ppermute | solution.py:570
  28.0 0.1 growth.1.gain
  28.1 0.5 %gather.1.own = f32[2,36,8,128]{3,2,1,0:T(8,128)S(1)} custom-call(f32[36,8,8,128]{3,2,1,0:T(8,128)S(1)} %get-tuple-element.43.q, bf16[2048,256]{1,0:T(8,128)(2,1)S(1)} %get-tuple-element.44.matrix), custom_call_target="tpu_custom_call" | custom-call | tf_op jit(solution)/shard_map/gather/pallas_call | solution.py:648
  28.7 0.3 %last_turn.1.early = f32[256,288]{1,0:T(8,128)S(1)} custom-call(f32[2,36,8,128]{3,2,1,0:T(8,128)S(1)} %gather.1.own, f32[2,1,8,128]{3,2,1,0:T(8,128)S(1)} %slice.3.static, f32[36,2,8,128]{3,2,1,0:T(8,128)S(1)} %growth.1.gain, f32[20,8,128]{2,1,0:T(8,128)S(1)} %get-tuple-element.30.consts), custom_call_target="tpu_custom_call" | custom-call | tf_op jit(solution)/shard_map/last_turn/pallas_call | solution.py:652
  29.0 1.1 %collective-permute-done.6.other = f32[8,128]{1,0:T(8,128)S(1)} collective-permute-done((f32[8,128]{1,0:T(8,128)S(1)}, f32[8,128]{1,0:T(8,128)S(1)}, u32[]{:S(2)}, u32[]{:S(2)}) %collective-permute-start.6) | collective-permute-done | bytes 4128 | tf_op jit(solution)/shard_map/ppermute | solution.py:570
  30.1 1.1 %finish.1 = f32[16,16,288]{2,1,0:T(8,128)} custom-call(f32[256,288]{1,0:T(8,128)S(1)} %last_turn.1.early, f32[2,1,8,128]{3,2,1,0:T(8,128)S(1)} %slice.3.static, f32[8,128]{1,0:T(8,128)S(1)} %get-tuple-element.45.sums, f32[8,128]{1,0:T(8,128)S(1)} %collective-permute-done.6.other, f32[20,8,128]{2,1,0:T(8,128)S(1)} %get-tuple-element.30.consts, ...), custom_call_target="tpu_custom_call" | custom-call | tf_op jit(solution)/shard_map/finish/pallas_call | solution.py:659
  (10 shorter events, 0.3 us)
Async XLA Ops:
  1.5 8.4 %collective-permute-start = (f32[34,8,128]{2,1,0:T(8,128)S(1)}, f32[34,8,128]{2,1,0:T(8,128)S(1)}, u32[]{:S(2)}, u32[]{:S(2)}) collective-permute-start(f32[34,8,128]{2,1,0:T(8,128)S(1)} %column_far.1), channel_id=1, source_target_pairs={{8,16},{16,8},{24,0},{0,24},{9,17},{17,9},{25,1},{1,25},{10,18},{1... | collective-permute-start | bytes 417800 | tf_op jit(solution)/shard_map/ppermute | solution.py:570
  5.3 6.6 %collective-permute-start.1 = (f32[34,8,128]{2,1,0:T(8,128)S(1)}, f32[34,8,128]{2,1,0:T(8,128)S(1)}, u32[]{:S(2)}, u32[]{:S(2)}) collective-permute-start(f32[34,8,128]{2,1,0:T(8,128)S(1)} %column_near.1), channel_id=1, source_target_pairs={{0,8},{8,0},{16,24},{24,16},{1,9},{9,1},{17,25},{25,17},{2,10},{10... | collective-permute-start | bytes 417800 | tf_op jit(solution)/shard_map/ppermute | solution.py:570
  5.4 6.5 %collective-permute-start.2 = (f32[34,8,128]{2,1,0:T(8,128)S(1)}, f32[34,8,128]{2,1,0:T(8,128)S(1)}, u32[]{:S(2)}, u32[]{:S(2)}) collective-permute-start(f32[34,8,128]{2,1,0:T(8,128)S(1)} %edge_far.1), channel_id=1, source_target_pairs={{2,4},{4,2},{3,5},{5,3},{10,12},{12,10},{11,13},{13,11},{18,20},{2... | collective-permute-start | bytes 417800 | tf_op jit(solution)/shard_map/ppermute | solution.py:570
  7.4 4.5 %collective-permute-start.3 = (f32[34,8,128]{2,1,0:T(8,128)S(1)}, f32[34,8,128]{2,1,0:T(8,128)S(1)}, u32[]{:S(2)}, u32[]{:S(2)}) collective-permute-start(f32[34,8,128]{2,1,0:T(8,128)S(1)} %edge_near.1), channel_id=1, source_target_pairs={{0,2},{2,0},{4,6},{6,4},{1,3},{3,1},{5,7},{7,5},{8,10},{10,8},{12,... | collective-permute-start | bytes 417800 | tf_op jit(solution)/shard_map/ppermute | solution.py:570
  12.1 6.5 %collective-permute-start.4 = (f32[37,8,128]{2,1,0:T(8,128)S(1)}, f32[37,8,128]{2,1,0:T(8,128)S(1)}, u32[]{:S(2)}, u32[]{:S(2)}) collective-permute-start(f32[37,8,128]{2,1,0:T(8,128)S(1)} %rim_far.1), channel_id=1, source_target_pairs={{2,4},{4,2},{3,5},{5,3},{10,12},{12,10},{11,13},{13,11},{18,20},{2... | collective-permute-start | bytes 454664 | tf_op jit(solution)/shard_map/ppermute | solution.py:570
  14.2 4.4 %collective-permute-start.5 = (f32[37,8,128]{2,1,0:T(8,128)S(1)}, f32[37,8,128]{2,1,0:T(8,128)S(1)}, u32[]{:S(2)}, u32[]{:S(2)}) collective-permute-start(f32[37,8,128]{2,1,0:T(8,128)S(1)} %rim_near.1), channel_id=1, source_target_pairs={{0,2},{2,0},{4,6},{6,4},{1,3},{3,1},{5,7},{7,5},{8,10},{10,8},{12,... | collective-permute-start | bytes 454664 | tf_op jit(solution)/shard_map/ppermute | solution.py:570
  26.5 3.6 %collective-permute-start.6 = (f32[8,128]{1,0:T(8,128)S(1)}, f32[8,128]{1,0:T(8,128)S(1)}, u32[]{:S(2)}, u32[]{:S(2)}) collective-permute-start(f32[8,128]{1,0:T(8,128)S(1)} %get-tuple-element.45.sums), channel_id=1, source_target_pairs={{0,1},{1,0},{2,3},{3,2},{4,5},{5,4},{6,7},{7,6},{8,9},{9,8},{10,11... | collective-permute-start | bytes 12296 | tf_op jit(solution)/shard_map/ppermute | solution.py:570

commit v8 on v7

--- a/solution.py
+++ b/solution.py
@@ -55,8 +55,12 @@
     landed = refs[14:21]
     flat0, flat1, wide, sems = refs[21:]
     copies = [
-        pltpu.make_async_copy(src, dst, sems.at[i]) for i, (src, dst) in enumerate(zip(sources, landed + tables))
+        pltpu.make_async_copy(src, dst, sems.at[i])
+        for i, (src, dst) in enumerate(zip(sources[1:], landed[1:] + tables))
     ]
+    for i in range(4):
+        mine = pl.ds(4 * i, 4)
+        copies.append(pltpu.make_async_copy(sources[0].at[mine], landed[0].at[mine], sems.at[9 + i]))
     for copy in copies:
         copy.start()
     wide[...] = jnp.zeros_like(wide)
@@ -344,87 +348,97 @@
     return k - k * u + 2.0 * bend, k * u - bend, -bend
 
 
-FORTH_TAPS = (-1, -2)
-BACK_TAPS = (-1, 2)
-
-
-def lon_kernel(q, taps, shifts, out, moved):
-    for quadrant, sign in ((0, 0), (3, 0), (1, 1), (2, 1)):
+FORTH_TAPS = (1, -1, -2)
+BACK_TAPS = (1, -1, 2)
+
+
+def lat_north(tiles, ks, us, ws):
+    diff = [tiles[t + 1] - tiles[t] for t in range(7)]
+    diff.append(roll(tiles[0], -32) - tiles[7])
+    before = roll(diff[7], 32)
+    fluxes = []
+    for t in range(8):
+        fluxes.append(flux(tiles[t], diff[t], diff[t] - before, ks[t], us[t], ws[t]))
+        before = diff[t]
+    behind = roll(fluxes[7], 32)
+    out = []
+    for t in range(8):
+        out.append(tiles[t] - fluxes[t] + behind)
+        behind = fluxes[t]
+    return out
+
+
+def lat_south(tiles, ks, us, ws):
+    ahead = tiles[1:] + [roll(tiles[0], -32)]
+    diff = [tiles[t] - ahead[t] for t in range(8)]
+    after = diff[1:] + [roll(diff[0], -32)]
+    fluxes = [flux(ahead[t], diff[t], diff[t] - after[t], ks[t], us[t], ws[t]) for t in range(8)]
+    behind = roll(fluxes[7], 32)
+    out = []
+    for t in range(8):
+        out.append(tiles[t] + fluxes[t] - behind)
+        behind = fluxes[t]
+    return out
+
+
+def sweep_kernel(with_sums, q, taps, ky, consts, shifts, *refs):
+    if with_sums:
+        out, sums, moved = refs
+    else:
+        out, moved = refs
+    live = consts[LIVE]
+    totals = [jnp.zeros((8, 128), f32)] * 8
+
+    def shifted(quadrant, sign):
         x = q[9 * quadrant : 9 * quadrant + 9].reshape(576, 128)
         lhs = jnp.concatenate(split(x), axis=1)
         moved[quadrant] = jnp.dot(lhs, shifts[sign], preferred_element_type=f32)
-    for sign in range(2):
-        for base in range(10):
-            if base == 0:
-                dirs = [[0], [18]][sign]
-            elif base == 9:
-                dirs = [[27], [9]][sign]
-            else:
-                dirs = [[base, 36 - base], [18 - base, 18 + base]][sign]
-            for t in range(8):
-                tap = [taps[base, sign, i, t] for i in range(4)]
-                for d in dirs:
-                    at = 64 * (d % 9) + 8 * t
-                    cell = q[d, t]
-                    near = [moved[d // 9, at : at + 8, 128 * i : 128 * i + 128] for i in range(2)]
-                    out[d, t] = (tap[0] * cell + tap[1] * roll(cell, -1)) + (tap[2] * near[0] + tap[3] * near[1])
-
-
-def lat_kernel(q, ky, consts, out, sums=None):
-    live = consts[LIVE]
-    totals = [jnp.zeros((8, 128), f32)] * 8
-
-    def put(d, t, value):
-        out[d, t] = value
-        if sums is not None:
-            totals[t] = totals[t] + value
-
-    def forth(d, ks, us, ws):
-        tiles = [q[d, t] for t in range(8)]
-        diff = [tiles[t + 1] - tiles[t] for t in range(7)]
-        diff.append(roll(tiles[0], -32) - tiles[7])
-        before = roll(diff[7], 32)
-        fluxes = []
+
+    def lon(d, t, tap):
+        at = 64 * (d % 9) + 8 * t
+        near = [moved[d // 9, at : at + 8, 128 * i : 128 * i + 128] for i in range(3)]
+        return (tap[0] * q[d, t] + tap[1] * near[0]) + (tap[2] * near[1] + tap[3] * near[2])
+
+    def both(sign, base):
+        if base == 0:
+            dirs = [[0], [18]][sign]
+        elif base == 9:
+            dirs = [[27], [9]][sign]
+        else:
+            dirs = [[base, 36 - base], [18 - base, 18 + base]][sign]
+        tiles = [[] for _ in dirs]
         for t in range(8):
-            fluxes.append(flux(tiles[t], diff[t], diff[t] - before, ks[t], us[t], ws[t]))
-            before = diff[t]
-        behind = roll(fluxes[7], 32)
-        for t in range(8):
-            put(d, t, (tiles[t] - fluxes[t] + behind) * live)
-            behind = fluxes[t]
-
-    def back(d, ks, us, ws):
-        tiles = [q[d, t] for t in range(8)]
-        ahead = tiles[1:] + [roll(tiles[0], -32)]
-        diff = [tiles[t] - ahead[t] for t in range(8)]
-        after = diff[1:] + [roll(diff[0], -32)]
-        fluxes = [flux(ahead[t], diff[t], diff[t] - after[t], ks[t], us[t], ws[t]) for t in range(8)]
-        behind = roll(fluxes[7], 32)
-        for t in range(8):
-            put(d, t, (tiles[t] + fluxes[t] - behind) * live)
-            behind = fluxes[t]
-
-    for base in range(10):
+            tap = [taps[base, sign, i, t] for i in range(4)]
+            for cells, d in zip(tiles, dirs):
+                cells.append(lon(d, t, tap))
         ks = [SIN[base] * ky[t] for t in range(8)]
         us, ws = zip(*[halves(k) for k in ks])
-        if base == 0:
-            north, south = [0], [18]
-        elif base == 9:
-            north, south = [9], [27]
-        else:
-            north, south = [base, 18 - base], [18 + base, 36 - base]
-        for d in north:
-            forth(d, ks, us, ws)
-        for d in south:
-            back(d, ks, us, ws)
-    if sums is None:
+        for cells, d in zip(tiles, dirs):
+            lat = lat_north if d < 18 else lat_south
+            for t, value in enumerate(lat(cells, ks, us, ws)):
+                value = value * live
+                out[d, t] = value
+                if with_sums:
+                    totals[t] = totals[t] + value
+
+    shifted(0, 0)
+    shifted(3, 0)
+    shifted(1, 1)
+    for base in range(5):
+        both(0, base)
+    shifted(2, 1)
+    for base in range(5, 10):
+        both(0, base)
+    for base in range(10):
+        both(1, base)
+    if not with_sums:
         return
     lane = lanes()
     halves_of = [jnp.zeros((8, 128), f32)] * 2
     for t in range(8):
-        moved = roll(totals[t], 16 * t - 40)
-        halves_of[0] = jnp.where(lane // 16 == t, moved, halves_of[0])
-        halves_of[1] = jnp.where(lane // 16 == (t + 2) % 8, moved, halves_of[1])
+        rolled = roll(totals[t], 16 * t - 40)
+        halves_of[0] = jnp.where(lane // 16 == t, rolled, halves_of[0])
+        halves_of[1] = jnp.where(lane // 16 == (t + 2) % 8, rolled, halves_of[1])
     halves_of[1] = roll(halves_of[1], -32)
     sums[...] = jnp.zeros((8, 128), f32)
     for half in range(2):
@@ -536,12 +550,13 @@
     for half in range(2):
         loss = wide[:, 384 * half : 384 * half + NDIR * FREQ]
         result = early[128 * half : 128 * half + 128, :] * loss
-        mine = pl.ds(8 * half, 8)
-        ready[mine] = result.reshape(8, 16, NDIR * FREQ)
-        pltpu.make_async_copy(ready.at[mine], out.at[mine], sems.at[half]).start()
-    for half in range(2):
-        mine = pl.ds(8 * half, 8)
-        pltpu.make_async_copy(ready.at[mine], out.at[mine], sems.at[half]).wait()
+        ready[8 * half : 8 * half + 8] = result.reshape(8, 16, NDIR * FREQ)
+        for i in range(4 * half, 4 * half + 4):
+            mine = pl.ds(2 * i, 2)
+            pltpu.make_async_copy(ready.at[mine], out.at[mine], sems.at[i]).start()
+    for i in range(8):
+        mine = pl.ds(2 * i, 2)
+        pltpu.make_async_copy(ready.at[mine], out.at[mine], sems.at[i]).wait()
 
 
 PARAMS = pltpu.CompilerParams(vmem_limit_bytes=40 * 2**20)
@@ -594,7 +609,7 @@
         [(2,) + slabs] + [x.shape for x in tables],
         [pltpu.VMEM(x.shape, x.dtype) for x in inputs]
         + [pltpu.VMEM((NDIR * FREQ, 128), f32)] * 2
-        + [pltpu.VMEM((16, 128), f32), pltpu.SemaphoreType.DMA((10,))],
+        + [pltpu.VMEM((16, 128), f32), pltpu.SemaphoreType.DMA((13,))],
         name="pack",
         space=pltpu.HBM,
     )(*[pltpu.with_memory_space_constraint(x, pltpu.HBM) for x in inputs + tables])
@@ -609,7 +624,7 @@
     place, rims, shifts, gather, spread, consts = call(
         tables_kernel,
         3,
-        [(1536, 1024), (512, 1024), (2, 256, 256), (2048, 256), (32, 768), (20,) + tile],
+        [(1536, 1024), (512, 1024), (2, 256, 384), (2048, 256), (32, 768), (20,) + tile],
         name="tables",
         dtype=[bf16] * 5 + [f32],
     )(speeds, turnings, ices)
@@ -638,12 +653,17 @@
     )(partial, rims_second, rims_first, consts, rims)
     cells = [(NDIR,) + block]
     for substep in range(ITERS):
-        (q,) = call(lon_kernel, 3, cells, [pltpu.VMEM((4, 576, 256), f32)], name="lon")(q, taps, shifts)
-        if substep == ITERS - 1:
-            q, sums = call(lat_kernel, 3, cells + [tile], name="lat_sums")(q, ky, consts)
-        else:
-            (q,) = call(lat_kernel, 3, cells, name="lat")(q, ky, consts)
+        final = substep == ITERS - 1
+        q, *sums = call(
+            functools.partial(sweep_kernel, final),
+            5,
+            cells + [tile] * final,
+            [pltpu.VMEM((4, 576, 384), f32)],
+            name="sweep_sums" if final else "sweep",
+        )(q, taps, ky, consts, shifts)
+        if not final:
             (q,) = call(turn_kernel, 3, cells, name="turn")(q, tx, ty)
+    (sums,) = sums
     other = swap(sums, "band", 0)
     (last,) = call(
         gather_kernel, 2, [(2, NDIR) + tile], [pltpu.VMEM((8 * NDIR, 2048), bf16)], name="gather"
@@ -660,7 +680,7 @@
         finish_kernel,
         6,
         [spectrum.shape],
-        [pltpu.VMEM(spectrum.shape, f32), pltpu.SemaphoreType.DMA((2,))],
+        [pltpu.VMEM(spectrum.shape, f32), pltpu.SemaphoreType.DMA((8,))],
         name="finish",
         result=pltpu.HBM,
     )(early, static, sums, other, consts, spread)

time: 31.7 us -> 32.3 us (1.019)
  Pallas kernels: 13.7 us -> 14.2 us
    pallas_call x9 -> x5, Pallas kernels: 5.77 us -> 6.09 us  [the longest x4 5.51 us: per_device(): call(functools.partial(sweep_kernel, final), 5, cells + [tile] * final, [...]
where the time goes in v8:
time: 32.3 us; the launch traced here: 31.7 us
  Pallas kernels  14.2 us (44%)
  starting transfers between devices  9.35 us (29%)
  waiting for transfers between devices  7.98 us (25%)
    ppermute x7, starting transfers between devices, swap(): return lax.ppermute(array, axis, pairs)  9.35 us
    ppermute x7, waiting for transfers between devices, swap(): return lax.ppermute(array, axis, pairs)  7.98 us
    pallas_call x4, Pallas kernels, per_device(): call(functools.partial(sweep_kernel, final), 5, cells + [tile] * final, [...  5.51 us
    pallas_call x3, Pallas kernels, per_device(): q, = call(turn_kernel, 3, cells, name='turn')(q, tx, ty)  1.73 us
    pallas_call x1, Pallas kernels, per_device(): call(pack_kernel, 10, [(2,) + slabs] + [x.shape for x in tables], [pltpu....  1.51 us
    pallas_call x1, Pallas kernels, per_device(): call(finish_kernel, 6, [spectrum.shape], [pltpu.VMEM(spectrum.shape, f32)...  1.17 us
    pallas_call x1, Pallas kernels, per_device(): call(place_kernel, 6, [(SLABS,) + block], [pltpu.VMEM((8 * SLABS + 8, 153...  1.16 us
    pallas_call x1, Pallas kernels, per_device(): call(rims_kernel, 5, [(NDIR,) + block, (10, 2, 4) + block] + [block] * 3,...  0.86 us
  transfers between devices with their start and end apart: 7, of which 4 were waited for; matrix products, arithmetic and copies ran while one was open for 0% of the time, Pallas kernels for 10%

profile of v8, /device:TPU:2, one launch (start us, length us, event | category | flops | bytes accessed | tf_op | source)
XLA Modules:
  0.0 31.7 jit_solution(6696650536822751182)
XLA Ops:
  0.0 1.5 %pack.1 = (f32[2,37,8,128]{3,2,1,0:T(8,128)S(1)}, f32[8,16]{1,0:T(8,128)S(1)}, f32[8,16]{1,0:T(8,128)S(1)}, f32[16]{0:T(128)S(1)}) custom-call(f32[16,16,288]{2,1,0:T(8,128)} %refs_0_.1, s32[16,16]{1,0:T(8,128)} %refs_1_.1, s32[16,16]{1,0:T(8,128)} %refs_2_.1, s32[16,16]{1,0:T(8,128)} %refs_3_.1, f32[2,16,16]{2,1,0:T(8,128)} %refs_4_.1, f32[16,16]{1,0:T(8,128)} %refs_5_.1, ...), custom_call_target="tpu_custom_call" | custom-call | tf_op jit(solution)/shard_map/pack/pallas_call | solution.py:606
  1.5 0.2 column_far.1
  1.7 3.7 %collective-permute-start = (f32[34,8,128]{2,1,0:T(8,128)S(1)}, f32[34,8,128]{2,1,0:T(8,128)S(1)}, u32[]{:S(2)}, u32[]{:S(2)}) collective-permute-start(f32[34,8,128]{2,1,0:T(8,128)S(1)} %column_far.1), channel_id=1, source_target_pairs={{8,16},{16,8},{24,0},{0,24},{9,17},{17,9},{25,1},{1,25},{10,18},{1... | collective-permute-start | bytes 417800 | tf_op jit(solution)/shard_map/ppermute | solution.py:585
  5.3 0.1 column_near.1
  5.5 0.0 collective-permute-start.1
  5.5 0.1 edge_far.1
  5.6 1.9 %collective-permute-start.2 = (f32[34,8,128]{2,1,0:T(8,128)S(1)}, f32[34,8,128]{2,1,0:T(8,128)S(1)}, u32[]{:S(2)}, u32[]{:S(2)}) collective-permute-start(f32[34,8,128]{2,1,0:T(8,128)S(1)} %edge_far.1), channel_id=1, source_target_pairs={{2,4},{4,2},{3,5},{5,3},{10,12},{12,10},{11,13},{13,11},{18,20},{2... | collective-permute-start | bytes 417800 | tf_op jit(solution)/shard_map/ppermute | solution.py:585
  7.5 0.1 edge_near.1
  7.6 0.0 collective-permute-start.3
  7.6 0.6 %tables.1 = (bf16[1536,1024]{1,0:T(8,128)(2,1)S(1)}, bf16[512,1024]{1,0:T(8,128)(2,1)S(1)}, bf16[2,256,384]{2,1,0:T(8,128)(2,1)S(1)}, bf16[2048,256]{1,0:T(8,128...) custom-call(f32[8,16]{1,0:T(8,128)S(1)} %get-tuple-element.27.speed_table, ...), custom_call_target="tpu_custom_call" | custom-call | tf_op jit(solution)/shard_map/tables/pallas_call | solution.py:624
  8.2 1.8 %collective-permute-done.cols_second = f32[34,8,128]{2,1,0:T(8,128)S(1)} collective-permute-done((f32[34,8,128]{2,1,0:T(8,128)S(1)}, f32[34,8,128]{2,1,0:T(8,128)S(1)}, u32[]{:S(2)}, u32[]{:S(2)}) %collective-permute-start) | collective-permute-done | bytes 139296 | tf_op jit(solution)/shard_map/ppermute | solution.py:585
  10.1 2.0 %collective-permute-done.1.cols_first = f32[34,8,128]{2,1,0:T(8,128)S(1)} collective-permute-done((f32[34,8,128]{2,1,0:T(8,128)S(1)}, f32[34,8,128]{2,1,0:T(8,128)S(1)}, u32[]{:S(2)}, u32[]{:S(2)}) %collective-permute-start.1) | collective-permute-done | bytes 139296 | tf_op jit(solution)/shard_map/ppermute | solution.py:585
  12.1 0.1 unpack.1
  12.3 2.1 %collective-permute-start.4 = (f32[37,8,128]{2,1,0:T(8,128)S(1)}, f32[37,8,128]{2,1,0:T(8,128)S(1)}, u32[]{:S(2)}, u32[]{:S(2)}) collective-permute-start(f32[37,8,128]{2,1,0:T(8,128)S(1)} %rim_far.1), channel_id=1, source_target_pairs={{2,4},{4,2},{3,5},{5,3},{10,12},{12,10},{11,13},{13,11},{18,20},{2... | collective-permute-start | bytes 454664 | tf_op jit(solution)/shard_map/ppermute | solution.py:585
  14.4 0.1 collective-permute-start.5
  14.5 0.1 unpack_rows.1
  14.6 1.2 %place.1.partial = f32[37,8,8,128]{3,2,1,0:T(8,128)S(1)} custom-call(f32[2,37,8,128]{3,2,1,0:T(8,128)S(1)} %get-tuple-element.26.own, f32[37,8,128]{2,1,0:T(8,128)S(1)} %get-tuple-element.31.west, f32[37,8,128]{2,1,0:T(8,128)S(1)} %get-tuple-element.32.east, f32[37,8,128]{2,1,0:T(8,128)S(1)} %get-tuple-element.33.south, ...), custom_call_target="tpu_custom_call" | custom-call | tf_op jit(solution)/shard_map/place/pallas_call | solution.py:640
  15.7 3.0 %collective-permute-done.4.rims_second = f32[37,8,128]{2,1,0:T(8,128)S(1)} collective-permute-done((f32[37,8,128]{2,1,0:T(8,128)S(1)}, f32[37,8,128]{2,1,0:T(8,128)S(1)}, u32[]{:S(2)}, u32[]{:S(2)}) %collective-permute-start.4) | collective-permute-done | bytes 151584 | tf_op jit(solution)/shard_map/ppermute | solution.py:585
  18.8 0.9 %rims.1 = (f32[36,8,8,128]{3,2,1,0:T(8,128)S(1)}, f32[10,2,4,8,8,128]{5,4,3,2,1,0:T(8,128)S(1)}, f32[8,8,128]{2,1,0:T(8,128)S(1)}, f32[8,8,128]{2,1,0:T(8,128)S(1)}, f32[8,8,128]{2,1,0:T(8,128)S(1)}) custom-call(f32[37,8,8,128]{3,2,1,0:T(8,128)S(1)} %place.1.partial, f32[37,8,128]{2,1,0:T(8,128)S(1)} %collective-permute-done.4.rims_second, ...), custom_call_target="tpu_custom_call" | custom-call | tf_op jit(solution)/shard_map/rims/pallas_call | solution.py:647
  19.6 1.3 %sweep.3.q = f32[36,8,8,128]{3,2,1,0:T(8,128)S(1)} custom-call(f32[36,8,8,128]{3,2,1,0:T(8,128)S(1)} %get-tuple-element.37.q, f32[10,2,4,8,8,128]{5,4,3,2,1,0:T(8,128)S(1)} %get-tuple-element.38.taps, f32[8,8,128]{2,1,0:T(8,128)S(1)} %get-tuple-element.39.ky, f32[20,8,128]{2,1,0:T(8,128)S(1)} %get-tuple-element.30.consts, ...), custom_call_target="tpu_custom_call" | custom-call | tf_op jit(solution)/shard_map/sweep/pallas_call | solution.py:657
  21.0 0.6 %turn.3.q = f32[36,8,8,128]{3,2,1,0:T(8,128)S(1)} custom-call(f32[36,8,8,128]{3,2,1,0:T(8,128)S(1)} %sweep.3.q, f32[8,8,128]{2,1,0:T(8,128)S(1)} %get-tuple-element.41.tx, f32[8,8,128]{2,1,0:T(8,128)S(1)} %get-tuple-element.42.ty), custom_call_target="tpu_custom_call" | custom-call | tf_op jit(solution)/shard_map/turn/pallas_call | solution.py:665
  21.6 1.3 %sweep.4.q = f32[36,8,8,128]{3,2,1,0:T(8,128)S(1)} custom-call(f32[36,8,8,128]{3,2,1,0:T(8,128)S(1)} %turn.3.q, f32[10,2,4,8,8,128]{5,4,3,2,1,0:T(8,128)S(1)} %get-tuple-element.38.taps, f32[8,8,128]{2,1,0:T(8,128)S(1)} %get-tuple-element.39.ky, f32[20,8,128]{2,1,0:T(8,128)S(1)} %get-tuple-element.30.consts, bf16[2,256,384]{2,1,0:T(8,128)(2,1)S(1)} %get-tuple-element.40.shifts), custom_call_target="tpu_custom_call" | custom-call | tf_op jit(solution)/shard_map/sweep/pallas_call | solution.py:657
  22.9 0.6 %turn.4.q = f32[36,8,8,128]{3,2,1,0:T(8,128)S(1)} custom-call(f32[36,8,8,128]{3,2,1,0:T(8,128)S(1)} %sweep.4.q, f32[8,8,128]{2,1,0:T(8,128)S(1)} %get-tuple-element.41.tx, f32[8,8,128]{2,1,0:T(8,128)S(1)} %get-tuple-element.42.ty), custom_call_target="tpu_custom_call" | custom-call | tf_op jit(solution)/shard_map/turn/pallas_call | solution.py:665
  23.5 1.3 %sweep.5.q = f32[36,8,8,128]{3,2,1,0:T(8,128)S(1)} custom-call(f32[36,8,8,128]{3,2,1,0:T(8,128)S(1)} %turn.4.q, f32[10,2,4,8,8,128]{5,4,3,2,1,0:T(8,128)S(1)} %get-tuple-element.38.taps, f32[8,8,128]{2,1,0:T(8,128)S(1)} %get-tuple-element.39.ky, f32[20,8,128]{2,1,0:T(8,128)S(1)} %get-tuple-element.30.consts, bf16[2,256,384]{2,1,0:T(8,128)(2,1)S(1)} %get-tuple-element.40.shifts), custom_call_target="tpu_custom_call" | custom-call | tf_op jit(solution)/shard_map/sweep/pallas_call | solution.py:657
  24.8 0.6 %turn.5.q = f32[36,8,8,128]{3,2,1,0:T(8,128)S(1)} custom-call(f32[36,8,8,128]{3,2,1,0:T(8,128)S(1)} %sweep.5.q, f32[8,8,128]{2,1,0:T(8,128)S(1)} %get-tuple-element.41.tx, f32[8,8,128]{2,1,0:T(8,128)S(1)} %get-tuple-element.42.ty), custom_call_target="tpu_custom_call" | custom-call | tf_op jit(solution)/shard_map/turn/pallas_call | solution.py:665
  25.4 1.5 %sweep_sums.1 = (f32[36,8,8,128]{3,2,1,0:T(8,128)S(1)}, f32[8,128]{1,0:T(8,128)S(1)}) custom-call(f32[36,8,8,128]{3,2,1,0:T(8,128)S(1)} %turn.5.q, f32[10,2,4,8,8,128]{5,4,3,2,1,0:T(8,128)S(1)} %get-tuple-element.38.taps, f32[8,8,128]{2,1,0:T(8,128)S(1)} %get-tuple-element.39.ky, f32[20,8,128]{2,1,0:T(8,128)S(1)} %get-tuple-element.30.consts, ...), custom_call_target="tpu_custom_call" | custom-call | tf_op jit(solution)/shard_map/sweep_sums/pallas_call | solution.py:657
  26.9 1.5 %collective-permute-start.6 = (f32[8,128]{1,0:T(8,128)S(1)}, f32[8,128]{1,0:T(8,128)S(1)}, u32[]{:S(2)}, u32[]{:S(2)}) collective-permute-start(f32[8,128]{1,0:T(8,128)S(1)} %get-tuple-element.45.sums), channel_id=1, source_target_pairs={{0,1},{1,0},{2,3},{3,2},{4,5},{5,4},{6,7},{7,6},{8,9},{9,8},{10,11... | collective-permute-start | bytes 12296 | tf_op jit(solution)/shard_map/ppermute | solution.py:585
  28.5 0.1 growth.1.gain
  28.6 0.5 %gather.1.own = f32[2,36,8,128]{3,2,1,0:T(8,128)S(1)} custom-call(f32[36,8,8,128]{3,2,1,0:T(8,128)S(1)} %get-tuple-element.43.q, bf16[2048,256]{1,0:T(8,128)(2,1)S(1)} %get-tuple-element.44.matrix), custom_call_target="tpu_custom_call" | custom-call | tf_op jit(solution)/shard_map/gather/pallas_call | solution.py:668
  29.1 0.3 %last_turn.1.early = f32[256,288]{1,0:T(8,128)S(1)} custom-call(f32[2,36,8,128]{3,2,1,0:T(8,128)S(1)} %gather.1.own, f32[2,1,8,128]{3,2,1,0:T(8,128)S(1)} %slice.3.static, f32[36,2,8,128]{3,2,1,0:T(8,128)S(1)} %growth.1.gain, f32[20,8,128]{2,1,0:T(8,128)S(1)} %get-tuple-element.30.consts), custom_call_target="tpu_custom_call" | custom-call | tf_op jit(solution)/shard_map/last_turn/pallas_call | solution.py:672
  29.5 1.1 %collective-permute-done.6.other = f32[8,128]{1,0:T(8,128)S(1)} collective-permute-done((f32[8,128]{1,0:T(8,128)S(1)}, f32[8,128]{1,0:T(8,128)S(1)}, u32[]{:S(2)}, u32[]{:S(2)}) %collective-permute-start.6) | collective-permute-done | bytes 4128 | tf_op jit(solution)/shard_map/ppermute | solution.py:585
  30.5 1.2 %finish.1 = f32[16,16,288]{2,1,0:T(8,128)} custom-call(f32[256,288]{1,0:T(8,128)S(1)} %last_turn.1.early, f32[2,1,8,128]{3,2,1,0:T(8,128)S(1)} %slice.3.static, f32[8,128]{1,0:T(8,128)S(1)} %get-tuple-element.45.sums, f32[8,128]{1,0:T(8,128)S(1)} %collective-permute-done.6.other, f32[20,8,128]{2,1,0:T(8,128)S(1)} %get-tuple-element.30.consts, ...), custom_call_target="tpu_custom_call" | custom-call | tf_op jit(solution)/shard_map/finish/pallas_call | solution.py:679
  (6 shorter events, 0.1 us)
Async XLA Ops:
  1.7 8.4 %collective-permute-start = (f32[34,8,128]{2,1,0:T(8,128)S(1)}, f32[34,8,128]{2,1,0:T(8,128)S(1)}, u32[]{:S(2)}, u32[]{:S(2)}) collective-permute-start(f32[34,8,128]{2,1,0:T(8,128)S(1)} %column_far.1), channel_id=1, source_target_pairs={{8,16},{16,8},{24,0},{0,24},{9,17},{17,9},{25,1},{1,25},{10,18},{1... | collective-permute-start | bytes 417800 | tf_op jit(solution)/shard_map/ppermute | solution.py:585
  5.5 6.6 %collective-permute-start.1 = (f32[34,8,128]{2,1,0:T(8,128)S(1)}, f32[34,8,128]{2,1,0:T(8,128)S(1)}, u32[]{:S(2)}, u32[]{:S(2)}) collective-permute-start(f32[34,8,128]{2,1,0:T(8,128)S(1)} %column_near.1), channel_id=1, source_target_pairs={{0,8},{8,0},{16,24},{24,16},{1,9},{9,1},{17,25},{25,17},{2,10},{10... | collective-permute-start | bytes 417800 | tf_op jit(solution)/shard_map/ppermute | solution.py:585
  5.6 6.5 %collective-permute-start.2 = (f32[34,8,128]{2,1,0:T(8,128)S(1)}, f32[34,8,128]{2,1,0:T(8,128)S(1)}, u32[]{:S(2)}, u32[]{:S(2)}) collective-permute-start(f32[34,8,128]{2,1,0:T(8,128)S(1)} %edge_far.1), channel_id=1, source_target_pairs={{2,4},{4,2},{3,5},{5,3},{10,12},{12,10},{11,13},{13,11},{18,20},{2... | collective-permute-start | bytes 417800 | tf_op jit(solution)/shard_map/ppermute | solution.py:585
  7.6 4.5 %collective-permute-start.3 = (f32[34,8,128]{2,1,0:T(8,128)S(1)}, f32[34,8,128]{2,1,0:T(8,128)S(1)}, u32[]{:S(2)}, u32[]{:S(2)}) collective-permute-start(f32[34,8,128]{2,1,0:T(8,128)S(1)} %edge_near.1), channel_id=1, source_target_pairs={{0,2},{2,0},{4,6},{6,4},{1,3},{3,1},{5,7},{7,5},{8,10},{10,8},{12,... | collective-permute-start | bytes 417800 | tf_op jit(solution)/shard_map/ppermute | solution.py:585
  12.3 6.5 %collective-permute-start.4 = (f32[37,8,128]{2,1,0:T(8,128)S(1)}, f32[37,8,128]{2,1,0:T(8,128)S(1)}, u32[]{:S(2)}, u32[]{:S(2)}) collective-permute-start(f32[37,8,128]{2,1,0:T(8,128)S(1)} %rim_far.1), channel_id=1, source_target_pairs={{2,4},{4,2},{3,5},{5,3},{10,12},{12,10},{11,13},{13,11},{18,20},{2... | collective-permute-start | bytes 454664 | tf_op jit(solution)/shard_map/ppermute | solution.py:585
  14.4 4.4 %collective-permute-start.5 = (f32[37,8,128]{2,1,0:T(8,128)S(1)}, f32[37,8,128]{2,1,0:T(8,128)S(1)}, u32[]{:S(2)}, u32[]{:S(2)}) collective-permute-start(f32[37,8,128]{2,1,0:T(8,128)S(1)} %rim_near.1), channel_id=1, source_target_pairs={{0,2},{2,0},{4,6},{6,4},{1,3},{3,1},{5,7},{7,5},{8,10},{10,8},{12,... | collective-permute-start | bytes 454664 | tf_op jit(solution)/shard_map/ppermute | solution.py:585
  26.9 3.6 %collective-permute-start.6 = (f32[8,128]{1,0:T(8,128)S(1)}, f32[8,128]{1,0:T(8,128)S(1)}, u32[]{:S(2)}, u32[]{:S(2)}) collective-permute-start(f32[8,128]{1,0:T(8,128)S(1)} %get-tuple-element.45.sums), channel_id=1, source_target_pairs={{0,1},{1,0},{2,3},{3,2},{4,5},{5,4},{6,7},{7,6},{8,9},{9,8},{10,11... | collective-permute-start | bytes 12296 | tf_op jit(solution)/shard_map/ppermute | solution.py:585

commit v9 on v7

--- a/solution.py
+++ b/solution.py
@@ -50,46 +50,44 @@
     return lax.axis_index(axis) % 2 == 0
 
 
-def pack_kernel(*refs):
-    sources, own, tables = refs[:10], refs[10], refs[11:14]
-    landed = refs[14:21]
-    flat0, flat1, wide, sems = refs[21:]
-    copies = [
-        pltpu.make_async_copy(src, dst, sems.at[i]) for i, (src, dst) in enumerate(zip(sources, landed + tables))
-    ]
+def place_field(wide, values, static, field):
+    group = lax.broadcasted_iota(jnp.int32, (16, 128), 1) // 16
+    row = lax.broadcasted_iota(jnp.int32, (16, 128), 0) % 8
+    wide[:, :16] = values
+    moved = pltpu.roll(wide[...], 0, 1, stride=16, stride_axis=0)
+    kept = jnp.where(group == row, moved, 0.0)
+    for half in range(2):
+        static[half, field : field + 1, :] = jnp.sum(kept[8 * half : 8 * half + 8], axis=0, keepdims=True)
+
+
+def fetch(sources, landed, sems):
+    copies = [pltpu.make_async_copy(src, dst, sems.at[i]) for i, (src, dst) in enumerate(zip(sources, landed))]
     for copy in copies:
         copy.start()
+    return copies
+
+
+def pack_kernel(*refs):
+    sources, own, landed = refs[:4], refs[4], refs[5:9]
+    flat0, flat1, wide, static, sems = refs[9:]
+    copies = fetch(sources, landed, sems)
     wide[...] = jnp.zeros_like(wide)
-    group = lax.broadcasted_iota(jnp.int32, (16, 128), 1) // 16
-    row = lax.broadcasted_iota(jnp.int32, (16, 128), 0) % 8
-    own[:, STATIC] = jnp.zeros((2, 8, 128), f32)
+    static[...] = jnp.zeros_like(static)
     for copy in copies:
         copy.wait()
-    spec, sea, ice, depth, slope, wspeed, wdir = landed
-
-    def place(field, values):
-        wide[:, :16] = values
-        moved = pltpu.roll(wide[...], 0, 1, stride=16, stride_axis=0)
-        kept = jnp.where(group == row, moved, 0.0)
-        for half in range(2):
-            own[half, STATIC, field : field + 1, :] = jnp.sum(
-                kept[8 * half : 8 * half + 8], axis=0, keepdims=True
-            )
-
-    place(SEA, sea[...].astype(f32))
-    place(DEPTH, depth[...].astype(f32))
-    place(SLOPE_X, slope[0])
-    place(SLOPE_Y, slope[1])
-    place(ICE, ice[...].astype(f32))
-    place(WIND, wspeed[...])
-    place(WDIR, wdir[...])
+    spec, sea, depth, slope = landed
+    place_field(wide, sea[...].astype(f32), static, SEA)
+    place_field(wide, depth[...].astype(f32), static, DEPTH)
+    place_field(wide, slope[0], static, SLOPE_X)
+    place_field(wide, slope[1], static, SLOPE_Y)
+    own[:, STATIC] = static[...]
     grid = spec[...].reshape(256, NDIR * FREQ)
     for low, high in ((0, 128), (128, 256), (256, 288)):
         turned = grid[:, low:high].T
         flat0[low:high, :] = turned[:, :128]
         flat1[low:high, :] = turned[:, 128:]
-    sea0 = own[0, STATIC, SEA : SEA + 1, :]
-    sea1 = own[1, STATIC, SEA : SEA + 1, :]
+    sea0 = static[0, SEA : SEA + 1, :]
+    sea1 = static[1, SEA : SEA + 1, :]
     for d in range(NDIR):
         own[0, d] = flat0[pl.ds(d, FREQ, stride=NDIR), :] * sea0
         own[1, d] = flat1[pl.ds(d, FREQ, stride=NDIR), :] * sea1
@@ -143,20 +141,24 @@
         message[SENT - 3 + i] = jnp.where(near, one, roll(two, 64))
 
 
-def growth_kernel(own, consts, gain):
+def growth_kernel(own, local, consts, gain):
     for half in range(2):
-        point = own[half, STATIC]
+        point = local[half]
         turn = point[WDIR : WDIR + 1]
         cos_w = jnp.cos(turn)
         sin_w = jnp.sin(turn)
         force = wind_gain * point[WIND : WIND + 1] * consts[LEVEL]
-        share = point[SEA : SEA + 1]
+        share = own[half, STATIC, SEA : SEA + 1]
         for d in range(NDIR):
             along = jnp.maximum(COS[d] * cos_w + SIN[d] * sin_w, 0.0)
             gain[d, half] = jnp.exp(force * along) * share
 
 
-def tables_kernel(speed_table, refraction_table, ice_rate, place, rims, shifts, gather, spread, consts):
+def tables_kernel(*refs):
+    sources, (place, rims, shifts, gather, local, consts), landed = refs[:6], refs[6:12], refs[12:18]
+    wide, sems = refs[18:]
+    speed_table, refraction_table, ice_rate, ice, wspeed, wdir = landed
+    copies = fetch(sources, landed, sems)
     first = lax.axis_index("band") * FREQ
     sub = lax.broadcasted_iota(jnp.int32, (8, 128), 0)
     mine = lanes() == first + sub
@@ -168,11 +170,6 @@
     def widen(values):
         return jnp.concatenate([values, jnp.zeros((values.shape[0], 112), f32)], axis=1)
 
-    for at, table in ((TAB_SPEED, speed_table), (TAB_TURN, refraction_table)):
-        wide = widen(table[...])
-        for c in range(NCLASS):
-            consts[at + c] = column(wide[c : c + 1])
-    consts[ICE_RATE] = column(widen(ice_rate[...].reshape(1, 16)))
     consts[LEVEL] = jnp.exp(math.log(freq_ratio) * (first + sub).astype(f32))
     lat = lax.axis_index("lat")
     lats = lax.axis_size("lat")
@@ -182,11 +179,6 @@
     consts[STRETCH] = 1.0 / jnp.cos(latitude)
     ghost = ((group == 0) & (lat == 0)) | ((group == 3) & (lat == lats - 1))
     consts[LIVE] = jnp.where(ghost, 0.0, 1.0)
-    comp = lax.broadcasted_iota(jnp.int32, (32, 384), 1) // NDIR
-    freq = lax.broadcasted_iota(jnp.int32, (32, 384), 0) % 16
-    for half in range(2):
-        spread[:, 384 * half : 384 * half + 384] = (comp == freq - 8 * half).astype(f32).astype(bf16)
-
     chunk = lax.broadcasted_iota(jnp.int32, (16, 128), 0)
     lane = lax.broadcasted_iota(jnp.int32, (16, 128), 1)
     low = chunk < 8
@@ -221,6 +213,18 @@
             for part in range(2):
                 at = part * 1024 + 128 * t
                 gather[at : at + 128, 128 * half : 128 * half + 128] = moved
+    local[...] = jnp.zeros_like(local)
+    wide[...] = jnp.zeros_like(wide)
+    for copy in copies:
+        copy.wait()
+    for at, table in ((TAB_SPEED, speed_table), (TAB_TURN, refraction_table)):
+        padded = widen(table[...])
+        for c in range(NCLASS):
+            consts[at + c] = column(padded[c : c + 1])
+    consts[ICE_RATE] = column(widen(ice_rate[...].reshape(1, 16)))
+    place_field(wide, ice[...].astype(f32), local, ICE)
+    place_field(wide, wspeed[...], local, WIND)
+    place_field(wide, wdir[...], local, WDIR)
 
 
 def unpack(even, first, second, pairs, out, back):
@@ -348,11 +352,7 @@
 BACK_TAPS = (-1, 2)
 
 
-def lon_kernel(q, taps, shifts, out, moved):
-    for quadrant, sign in ((0, 0), (3, 0), (1, 1), (2, 1)):
-        x = q[9 * quadrant : 9 * quadrant + 9].reshape(576, 128)
-        lhs = jnp.concatenate(split(x), axis=1)
-        moved[quadrant] = jnp.dot(lhs, shifts[sign], preferred_element_type=f32)
+def lon_kernel(q, taps, shifts, out):
     for sign in range(2):
         for base in range(10):
             if base == 0:
@@ -361,13 +361,17 @@
                 dirs = [[27], [9]][sign]
             else:
                 dirs = [[base, 36 - base], [18 - base, 18 + base]][sign]
+            x = jnp.concatenate([q[d].reshape(64, 128) for d in dirs], axis=0)
+            lhs = jnp.concatenate(split(x), axis=1)
+            moved = jnp.dot(lhs, shifts[sign], preferred_element_type=f32)
             for t in range(8):
                 tap = [taps[base, sign, i, t] for i in range(4)]
-                for d in dirs:
-                    at = 64 * (d % 9) + 8 * t
+                for i, d in enumerate(dirs):
                     cell = q[d, t]
-                    near = [moved[d // 9, at : at + 8, 128 * i : 128 * i + 128] for i in range(2)]
-                    out[d, t] = (tap[0] * cell + tap[1] * roll(cell, -1)) + (tap[2] * near[0] + tap[3] * near[1])
+                    near = moved[64 * i + 8 * t : 64 * i + 8 * t + 8]
+                    out[d, t] = (tap[0] * cell + tap[1] * roll(cell, -1)) + (
+                        tap[2] * near[:, :128] + tap[3] * near[:, 128:]
+                    )
 
 
 def lat_kernel(q, ky, consts, out, sums=None):
@@ -501,13 +505,13 @@
         own[half] = moved[:, 128 * half : 128 * half + 128].reshape(NDIR, 8, 128)
 
 
-def last_turn_kernel(own, static, gain, consts, early, flat0, flat1):
-    for half, flat in ((0, flat0), (1, flat1)):
+def last_turn_kernel(own, static, gain, consts, early):
+    for half in range(2):
         point = static[half, 0]
         turning = lookup(point, consts, TAB_TURN)
 
-        def put(d, value, half=half, flat=flat):
-            flat[pl.ds(d, FREQ, stride=NDIR), :] = value * gain[d, half]
+        def put(d, value, half=half):
+            early[half, d] = value * gain[d, half]
 
         turn_around(
             lambda d, half=half: own[half, d],
@@ -515,33 +519,23 @@
             turning * point[SLOPE_X : SLOPE_X + 1],
             turning * point[SLOPE_Y : SLOPE_Y + 1],
         )
-        for low, high in ((0, 128), (128, 256), (256, 288)):
-            early[128 * half : 128 * half + 128, low:high] = flat[low:high, :].T
-
-
-def finish_kernel(early, static, sums, other, consts, spread, out, ready, sems):
+
+
+def finish_kernel(early, local, sums, other, consts, out, flat0, flat1):
     total = sums[...] + other[...]
     level = consts[LEVEL]
-    losses = []
-    for half in range(2):
+    for half, flat in ((0, flat0), (1, flat1)):
         energy = total[half : half + 1]
         moment = total[2 + half : 3 + half]
         mean_level = jnp.maximum(moment, 1.0) / jnp.maximum(energy, 1.0)
         mean = energy / NCOMP
         breaking = break_coef * level * level / mean_level * (mean * mean)
-        damping = static[half, 0, ICE : ICE + 1] * consts[ICE_RATE]
-        losses.append(jnp.exp(-breaking - damping))
-    turned = jnp.concatenate(losses, axis=0).T
-    wide = jnp.dot(jnp.concatenate(split(turned), axis=1), spread[...], preferred_element_type=f32)
-    for half in range(2):
-        loss = wide[:, 384 * half : 384 * half + NDIR * FREQ]
-        result = early[128 * half : 128 * half + 128, :] * loss
-        mine = pl.ds(8 * half, 8)
-        ready[mine] = result.reshape(8, 16, NDIR * FREQ)
-        pltpu.make_async_copy(ready.at[mine], out.at[mine], sems.at[half]).start()
-    for half in range(2):
-        mine = pl.ds(8 * half, 8)
-        pltpu.make_async_copy(ready.at[mine], out.at[mine], sems.at[half]).wait()
+        damping = local[half, ICE : ICE + 1] * consts[ICE_RATE]
+        loss = jnp.exp(-breaking - damping)
+        for d in range(NDIR):
+            flat[pl.ds(d, FREQ, stride=NDIR), :] = early[half, d] * loss
+        for low, high in ((0, 128), (128, 256), (256, 288)):
+            out[8 * half : 8 * half + 8, :, low:high] = flat[low:high, :].T.reshape(8, 16, high - low)
 
 
 PARAMS = pltpu.CompilerParams(vmem_limit_bytes=40 * 2**20)
@@ -586,18 +580,17 @@
     block = (8,) + tile
     slabs = (SLABS,) + tile
     sent = (SENT,) + tile
-    inputs = [spectrum, sea_mask, ice_mask, depth_class, depth_slope, wind_speed, wind_dir]
-    tables = [speed_table, refraction_table, ice_rate]
-    own, speeds, turnings, ices = call(
+    inputs = [spectrum, sea_mask, depth_class, depth_slope]
+    (own,) = call(
         pack_kernel,
-        10,
-        [(2,) + slabs] + [x.shape for x in tables],
+        4,
+        [(2,) + slabs],
         [pltpu.VMEM(x.shape, x.dtype) for x in inputs]
         + [pltpu.VMEM((NDIR * FREQ, 128), f32)] * 2
-        + [pltpu.VMEM((16, 128), f32), pltpu.SemaphoreType.DMA((10,))],
+        + [pltpu.VMEM((16, 128), f32), pltpu.VMEM((2,) + tile, f32), pltpu.SemaphoreType.DMA((4,))],
         name="pack",
         space=pltpu.HBM,
-    )(*[pltpu.with_memory_space_constraint(x, pltpu.HBM) for x in inputs + tables])
+    )(*[pltpu.with_memory_space_constraint(x, pltpu.HBM) for x in inputs])
     (to_second,) = call(functools.partial(column_kernel, True), 1, [sent], name="column_far")(own)
     cols_second = swap(to_second, "lon", 1, True)
     (to_first,) = call(functools.partial(column_kernel, False), 1, [sent], name="column_near")(own)
@@ -606,14 +599,18 @@
     rows_second = swap(edge_second, "lat", 1)
     (edge_first,) = call(functools.partial(edge_kernel, False), 1, [sent], name="edge_near")(own)
     rows_first = swap(edge_first, "lat", 0)
-    place, rims, shifts, gather, spread, consts = call(
+    inputs = [speed_table, refraction_table, ice_rate, ice_mask, wind_speed, wind_dir]
+    place, rims, shifts, gather, local, consts = call(
         tables_kernel,
-        3,
-        [(1536, 1024), (512, 1024), (2, 256, 256), (2048, 256), (32, 768), (20,) + tile],
+        6,
+        [(1536, 1024), (512, 1024), (2, 256, 256), (2048, 256), (2,) + tile, (20,) + tile],
+        [pltpu.VMEM(x.shape, x.dtype) for x in inputs]
+        + [pltpu.VMEM((16, 128), f32), pltpu.SemaphoreType.DMA((6,))],
         name="tables",
-        dtype=[bf16] * 5 + [f32],
-    )(speeds, turnings, ices)
-    (gain,) = call(growth_kernel, 2, [(NDIR, 2) + tile], name="growth")(own, consts)
+        space=pltpu.HBM,
+        dtype=[bf16] * 4 + [f32] * 2,
+    )(*[pltpu.with_memory_space_constraint(x, pltpu.HBM) for x in inputs])
+    (gain,) = call(growth_kernel, 3, [(NDIR, 2) + tile], name="growth")(own, local, consts)
     west, east = call(unpack_kernel, 5, [slabs] * 2, name="unpack")(
         cols_second, cols_first, rows_second, rows_first, consts
     )
@@ -638,7 +635,7 @@
     )(partial, rims_second, rims_first, consts, rims)
     cells = [(NDIR,) + block]
     for substep in range(ITERS):
-        (q,) = call(lon_kernel, 3, cells, [pltpu.VMEM((4, 576, 256), f32)], name="lon")(q, taps, shifts)
+        (q,) = call(lon_kernel, 3, cells, name="lon")(q, taps, shifts)
         if substep == ITERS - 1:
             q, sums = call(lat_kernel, 3, cells + [tile], name="lat_sums")(q, ky, consts)
         else:
@@ -649,21 +646,10 @@
         gather_kernel, 2, [(2, NDIR) + tile], [pltpu.VMEM((8 * NDIR, 2048), bf16)], name="gather"
     )(q, gather)
     static = own[:, STATIC:]
-    (early,) = call(
-        last_turn_kernel,
-        4,
-        [(256, NDIR * FREQ)],
-        [pltpu.VMEM((NDIR * FREQ, 128), f32)] * 2,
-        name="last_turn",
-    )(last, static, gain, consts)
+    (early,) = call(last_turn_kernel, 4, [(2, NDIR) + tile], name="last_turn")(last, static, gain, consts)
     (out,) = call(
-        finish_kernel,
-        6,
-        [spectrum.shape],
-        [pltpu.VMEM(spectrum.shape, f32), pltpu.SemaphoreType.DMA((2,))],
-        name="finish",
-        result=pltpu.HBM,
-    )(early, static, sums, other, consts, spread)
+        finish_kernel, 5, [spectrum.shape], [pltpu.VMEM((NDIR * FREQ, 128), f32)] * 2, name="finish"
+    )(early, local, sums, other, consts)
     return out
 
 

time: 31.7 us -> 31.5 us (level)
  transfers between devices with their start and end apart: 7 -> 7, of which waited for: 4 -> 4; matrix products, arithmetic and copies ran while one was open for 0% -> 0% of each run, Pallas kernels for 10% -> 11%
where the time goes in v9:
time: 31.5 us; the launch traced here: 31 us
  Pallas kernels  13.7 us (43%)
  starting transfers between devices  9.34 us (30%)
  waiting for transfers between devices  7.78 us (25%)
    ppermute x7, starting transfers between devices, swap(): return lax.ppermute(array, axis, pairs)  9.34 us
    ppermute x7, waiting for transfers between devices, swap(): return lax.ppermute(array, axis, pairs)  7.78 us
    pallas_call x4, Pallas kernels, per_device(): q, = call(lon_kernel, 3, cells, name='lon')(q, taps, shifts)  2.86 us
    pallas_call x3, Pallas kernels, per_device(): q, = call(turn_kernel, 3, cells, name='turn')(q, tx, ty)  1.73 us
    pallas_call x3, Pallas kernels, per_device(): q, = call(lat_kernel, 3, cells, name='lat')(q, ky, consts)  1.64 us
    pallas_call x1, Pallas kernels, per_device(): call(pack_kernel, 4, [(2,) + slabs], [pltpu.VMEM(x.shape, x.dtype) for x...  1.24 us
    pallas_call x1, Pallas kernels, per_device(): call(place_kernel, 6, [(SLABS,) + block], [pltpu.VMEM((8 * SLABS + 8, 153...  1.15 us
    pallas_call x1, Pallas kernels, per_device(): call(tables_kernel, 6, [(1536, 1024), (512, 1024), (2, 256, 256), (2048,...  0.96 us
  transfers between devices with their start and end apart: 7, of which 4 were waited for; matrix products, arithmetic and copies ran while one was open for 0% of the time, Pallas kernels for 11%

profile of v9, /device:TPU:2, one launch (start us, length us, event | category | flops | bytes accessed | tf_op | source)
XLA Modules:
  0.0 31.0 jit_solution(3456291327873297488)
XLA Ops:
  0.0 1.2 %pack.1.own = f32[2,37,8,128]{3,2,1,0:T(8,128)S(1)} custom-call(f32[16,16,288]{2,1,0:T(8,128)} %refs_0_.2, s32[16,16]{1,0:T(8,128)} %refs_1_.2, s32[16,16]{1,0:T(8,128)} %refs_2_.2, f32[2,16,16]{2,1,0:T(8,128)} %refs_3_.2), custom_call_target="tpu_custom_call" | custom-call | tf_op jit(solution)/shard_map/pack/pallas_call | solution.py:584
  1.3 0.2 column_far.1
  1.4 3.7 %collective-permute-start = (f32[34,8,128]{2,1,0:T(8,128)S(1)}, f32[34,8,128]{2,1,0:T(8,128)S(1)}, u32[]{:S(2)}, u32[]{:S(2)}) collective-permute-start(f32[34,8,128]{2,1,0:T(8,128)S(1)} %column_far.1), channel_id=1, source_target_pairs={{8,16},{16,8},{24,0},{0,24},{9,17},{17,9},{25,1},{1,25},{10,18},{1... | collective-permute-start | bytes 417800 | tf_op jit(solution)/shard_map/ppermute | solution.py:564
  5.1 0.1 column_near.1
  5.3 0.1 edge_far.1
  5.4 1.9 %collective-permute-start.2 = (f32[34,8,128]{2,1,0:T(8,128)S(1)}, f32[34,8,128]{2,1,0:T(8,128)S(1)}, u32[]{:S(2)}, u32[]{:S(2)}) collective-permute-start(f32[34,8,128]{2,1,0:T(8,128)S(1)} %edge_far.1), channel_id=1, source_target_pairs={{2,4},{4,2},{3,5},{5,3},{10,12},{12,10},{11,13},{13,11},{18,20},{2... | collective-permute-start | bytes 417800 | tf_op jit(solution)/shard_map/ppermute | solution.py:564
  7.4 1.0 %tables.1 = (bf16[1536,1024]{1,0:T(8,128)(2,1)S(1)}, bf16[512,1024]{1,0:T(8,128)(2,1)S(1)}, bf16[2,256,256]{2,1,0:T(8,128)(2,1)S(1)}, bf16[2048,256]{1,0:T(8,128...) custom-call(f32[8,16]{1,0:T(8,128)} %refs_0_.3, f32[8,16]{1,0:T(8,128)} %refs_1_.3, f32[16]{0:T(128)} %refs_2_.3, ...), custom_call_target="tpu_custom_call" | custom-call | tf_op jit(solution)/shard_map/tables/pallas_call | solution.py:603
  8.4 1.5 %collective-permute-done.cols_second = f32[34,8,128]{2,1,0:T(8,128)S(1)} collective-permute-done((f32[34,8,128]{2,1,0:T(8,128)S(1)}, f32[34,8,128]{2,1,0:T(8,128)S(1)}, u32[]{:S(2)}, u32[]{:S(2)}) %collective-permute-start) | collective-permute-done | bytes 139296 | tf_op jit(solution)/shard_map/ppermute | solution.py:564
  9.8 2.0 %collective-permute-done.1.cols_first = f32[34,8,128]{2,1,0:T(8,128)S(1)} collective-permute-done((f32[34,8,128]{2,1,0:T(8,128)S(1)}, f32[34,8,128]{2,1,0:T(8,128)S(1)}, u32[]{:S(2)}, u32[]{:S(2)}) %collective-permute-start.1) | collective-permute-done | bytes 139296 | tf_op jit(solution)/shard_map/ppermute | solution.py:564
  11.8 0.1 unpack.1
  12.0 2.1 %collective-permute-start.4 = (f32[37,8,128]{2,1,0:T(8,128)S(1)}, f32[37,8,128]{2,1,0:T(8,128)S(1)}, u32[]{:S(2)}, u32[]{:S(2)}) collective-permute-start(f32[37,8,128]{2,1,0:T(8,128)S(1)} %rim_far.1), channel_id=1, source_target_pairs={{2,4},{4,2},{3,5},{5,3},{10,12},{12,10},{11,13},{13,11},{18,20},{2... | collective-permute-start | bytes 454664 | tf_op jit(solution)/shard_map/ppermute | solution.py:564
  14.2 0.1 unpack_rows.1
  14.3 1.2 %place.1.partial = f32[37,8,8,128]{3,2,1,0:T(8,128)S(1)} custom-call(f32[2,37,8,128]{3,2,1,0:T(8,128)S(1)} %pack.1.own, f32[37,8,128]{2,1,0:T(8,128)S(1)} %get-tuple-element.23.west, f32[37,8,128]{2,1,0:T(8,128)S(1)} %get-tuple-element.24.east, f32[37,8,128]{2,1,0:T(8,128)S(1)} %get-tuple-element.25.south, f32[37,8,128]{2,1,0:T(8,128)S(1)} %get-tuple-element.26.north, ...), custom_call_target="tpu_custom_call" | custom-call | tf_op jit(solution)/shard_map/place/pallas_call | solution.py:622
  15.5 3.0 %collective-permute-done.4.rims_second = f32[37,8,128]{2,1,0:T(8,128)S(1)} collective-permute-done((f32[37,8,128]{2,1,0:T(8,128)S(1)}, f32[37,8,128]{2,1,0:T(8,128)S(1)}, u32[]{:S(2)}, u32[]{:S(2)}) %collective-permute-start.4) | collective-permute-done | bytes 151584 | tf_op jit(solution)/shard_map/ppermute | solution.py:564
  18.5 0.9 %rims.1 = (f32[36,8,8,128]{3,2,1,0:T(8,128)S(1)}, f32[10,2,4,8,8,128]{5,4,3,2,1,0:T(8,128)S(1)}, f32[8,8,128]{2,1,0:T(8,128)S(1)}, f32[8,8,128]{2,1,0:T(8,128)S(1)}, f32[8,8,128]{2,1,0:T(8,128)S(1)}) custom-call(f32[37,8,8,128]{3,2,1,0:T(8,128)S(1)} %place.1.partial, f32[37,8,128]{2,1,0:T(8,128)S(1)} %collective-permute-done.4.rims_second, ...), custom_call_target="tpu_custom_call" | custom-call | tf_op jit(solution)/shard_map/rims/pallas_call | solution.py:629
  19.4 0.7 %lon.4.q = f32[36,8,8,128]{3,2,1,0:T(8,128)S(1)} custom-call(f32[36,8,8,128]{3,2,1,0:T(8,128)S(1)} %get-tuple-element.29.q, f32[10,2,4,8,8,128]{5,4,3,2,1,0:T(8,128)S(1)} %get-tuple-element.30.taps, bf16[2,256,256]{2,1,0:T(8,128)(2,1)S(1)} %get-tuple-element.31.shifts), custom_call_target="tpu_custom_call" | custom-call | tf_op jit(solution)/shard_map/lon/pallas_call | solution.py:638
  20.1 0.5 %lat.3.q = f32[36,8,8,128]{3,2,1,0:T(8,128)S(1)} custom-call(f32[36,8,8,128]{3,2,1,0:T(8,128)S(1)} %lon.4.q, f32[8,8,128]{2,1,0:T(8,128)S(1)} %get-tuple-element.32.ky, f32[20,8,128]{2,1,0:T(8,128)S(1)} %get-tuple-element.22.consts), custom_call_target="tpu_custom_call" | custom-call | tf_op jit(solution)/shard_map/lat/pallas_call | solution.py:642
  20.6 0.6 %turn.3.q = f32[36,8,8,128]{3,2,1,0:T(8,128)S(1)} custom-call(f32[36,8,8,128]{3,2,1,0:T(8,128)S(1)} %lat.3.q, f32[8,8,128]{2,1,0:T(8,128)S(1)} %get-tuple-element.33.tx, f32[8,8,128]{2,1,0:T(8,128)S(1)} %get-tuple-element.34.ty), custom_call_target="tpu_custom_call" | custom-call | tf_op jit(solution)/shard_map/turn/pallas_call | solution.py:643
  21.2 0.7 %lon.5.q = f32[36,8,8,128]{3,2,1,0:T(8,128)S(1)} custom-call(f32[36,8,8,128]{3,2,1,0:T(8,128)S(1)} %turn.3.q, f32[10,2,4,8,8,128]{5,4,3,2,1,0:T(8,128)S(1)} %get-tuple-element.30.taps, bf16[2,256,256]{2,1,0:T(8,128)(2,1)S(1)} %get-tuple-element.31.shifts), custom_call_target="tpu_custom_call" | custom-call | tf_op jit(solution)/shard_map/lon/pallas_call | solution.py:638
  21.9 0.5 %lat.4.q = f32[36,8,8,128]{3,2,1,0:T(8,128)S(1)} custom-call(f32[36,8,8,128]{3,2,1,0:T(8,128)S(1)} %lon.5.q, f32[8,8,128]{2,1,0:T(8,128)S(1)} %get-tuple-element.32.ky, f32[20,8,128]{2,1,0:T(8,128)S(1)} %get-tuple-element.22.consts), custom_call_target="tpu_custom_call" | custom-call | tf_op jit(solution)/shard_map/lat/pallas_call | solution.py:642
  22.5 0.6 %turn.4.q = f32[36,8,8,128]{3,2,1,0:T(8,128)S(1)} custom-call(f32[36,8,8,128]{3,2,1,0:T(8,128)S(1)} %lat.4.q, f32[8,8,128]{2,1,0:T(8,128)S(1)} %get-tuple-element.33.tx, f32[8,8,128]{2,1,0:T(8,128)S(1)} %get-tuple-element.34.ty), custom_call_target="tpu_custom_call" | custom-call | tf_op jit(solution)/shard_map/turn/pallas_call | solution.py:643
  23.1 0.7 %lon.6.q = f32[36,8,8,128]{3,2,1,0:T(8,128)S(1)} custom-call(f32[36,8,8,128]{3,2,1,0:T(8,128)S(1)} %turn.4.q, f32[10,2,4,8,8,128]{5,4,3,2,1,0:T(8,128)S(1)} %get-tuple-element.30.taps, bf16[2,256,256]{2,1,0:T(8,128)(2,1)S(1)} %get-tuple-element.31.shifts), custom_call_target="tpu_custom_call" | custom-call | tf_op jit(solution)/shard_map/lon/pallas_call | solution.py:638
  23.8 0.5 %lat.5.q = f32[36,8,8,128]{3,2,1,0:T(8,128)S(1)} custom-call(f32[36,8,8,128]{3,2,1,0:T(8,128)S(1)} %lon.6.q, f32[8,8,128]{2,1,0:T(8,128)S(1)} %get-tuple-element.32.ky, f32[20,8,128]{2,1,0:T(8,128)S(1)} %get-tuple-element.22.consts), custom_call_target="tpu_custom_call" | custom-call | tf_op jit(solution)/shard_map/lat/pallas_call | solution.py:642
  24.4 0.6 %turn.5.q = f32[36,8,8,128]{3,2,1,0:T(8,128)S(1)} custom-call(f32[36,8,8,128]{3,2,1,0:T(8,128)S(1)} %lat.5.q, f32[8,8,128]{2,1,0:T(8,128)S(1)} %get-tuple-element.33.tx, f32[8,8,128]{2,1,0:T(8,128)S(1)} %get-tuple-element.34.ty), custom_call_target="tpu_custom_call" | custom-call | tf_op jit(solution)/shard_map/turn/pallas_call | solution.py:643
  24.9 0.7 %lon.7.q = f32[36,8,8,128]{3,2,1,0:T(8,128)S(1)} custom-call(f32[36,8,8,128]{3,2,1,0:T(8,128)S(1)} %turn.5.q, f32[10,2,4,8,8,128]{5,4,3,2,1,0:T(8,128)S(1)} %get-tuple-element.30.taps, bf16[2,256,256]{2,1,0:T(8,128)(2,1)S(1)} %get-tuple-element.31.shifts), custom_call_target="tpu_custom_call" | custom-call | tf_op jit(solution)/shard_map/lon/pallas_call | solution.py:638
  25.7 0.7 %lat_sums.1 = (f32[36,8,8,128]{3,2,1,0:T(8,128)S(1)}, f32[8,128]{1,0:T(8,128)S(1)}) custom-call(f32[36,8,8,128]{3,2,1,0:T(8,128)S(1)} %lon.7.q, f32[8,8,128]{2,1,0:T(8,128)S(1)} %get-tuple-element.32.ky, f32[20,8,128]{2,1,0:T(8,128)S(1)} %get-tuple-element.22.consts), custom_call_target="tpu_custom_call" | custom-call | tf_op jit(solution)/shard_map/lat_sums/pallas_call | solution.py:640
  26.4 1.5 %collective-permute-start.6 = (f32[8,128]{1,0:T(8,128)S(1)}, f32[8,128]{1,0:T(8,128)S(1)}, u32[]{:S(2)}, u32[]{:S(2)}) collective-permute-start(f32[8,128]{1,0:T(8,128)S(1)} %get-tuple-element.38.sums), channel_id=1, source_target_pairs={{0,1},{1,0},{2,3},{3,2},{4,5},{5,4},{6,7},{7,6},{8,9},{9,8},{10,11... | collective-permute-start | bytes 12296 | tf_op jit(solution)/shard_map/ppermute | solution.py:564
  27.9 0.1 growth.1.gain
  28.0 0.5 %gather.1.own = f32[2,36,8,128]{3,2,1,0:T(8,128)S(1)} custom-call(f32[36,8,8,128]{3,2,1,0:T(8,128)S(1)} %get-tuple-element.35.q, bf16[2048,256]{1,0:T(8,128)(2,1)S(1)} %get-tuple-element.36.matrix), custom_call_target="tpu_custom_call" | custom-call | tf_op jit(solution)/shard_map/gather/pallas_call | solution.py:645
  28.6 0.2 last_turn.1.early
  28.7 1.3 %collective-permute-done.6.other = f32[8,128]{1,0:T(8,128)S(1)} collective-permute-done((f32[8,128]{1,0:T(8,128)S(1)}, f32[8,128]{1,0:T(8,128)S(1)}, u32[]{:S(2)}, u32[]{:S(2)}) %collective-permute-start.6) | collective-permute-done | bytes 4128 | tf_op jit(solution)/shard_map/ppermute | solution.py:564
  30.0 1.0 %finish.1 = f32[16,16,288]{2,1,0:T(8,128)} custom-call(f32[2,36,8,128]{3,2,1,0:T(8,128)S(1)} %last_turn.1.early, f32[2,8,128]{2,1,0:T(8,128)S(1)} %get-tuple-element.37.local, f32[8,128]{1,0:T(8,128)S(1)} %get-tuple-element.38.sums, f32[8,128]{1,0:T(8,128)S(1)} %collective-permute-done.6.other, f32[20,8,128]{2,1,0:T(8,128)S(1)} %get-tuple-element.22.consts), custom_call_target="tpu_custom_call" | custom-call | tf_op jit(solution)/shard_map/finish/pallas_call | solution.py:650
  (10 shorter events, 0.3 us)
Async XLA Ops:
  1.4 8.4 %collective-permute-start = (f32[34,8,128]{2,1,0:T(8,128)S(1)}, f32[34,8,128]{2,1,0:T(8,128)S(1)}, u32[]{:S(2)}, u32[]{:S(2)}) collective-permute-start(f32[34,8,128]{2,1,0:T(8,128)S(1)} %column_far.1), channel_id=1, source_target_pairs={{8,16},{16,8},{24,0},{0,24},{9,17},{17,9},{25,1},{1,25},{10,18},{1... | collective-permute-start | bytes 417800 | tf_op jit(solution)/shard_map/ppermute | solution.py:564
  5.2 6.6 %collective-permute-start.1 = (f32[34,8,128]{2,1,0:T(8,128)S(1)}, f32[34,8,128]{2,1,0:T(8,128)S(1)}, u32[]{:S(2)}, u32[]{:S(2)}) collective-permute-start(f32[34,8,128]{2,1,0:T(8,128)S(1)} %column_near.1), channel_id=1, source_target_pairs={{0,8},{8,0},{16,24},{24,16},{1,9},{9,1},{17,25},{25,17},{2,10},{10... | collective-permute-start | bytes 417800 | tf_op jit(solution)/shard_map/ppermute | solution.py:564
  5.4 6.5 %collective-permute-start.2 = (f32[34,8,128]{2,1,0:T(8,128)S(1)}, f32[34,8,128]{2,1,0:T(8,128)S(1)}, u32[]{:S(2)}, u32[]{:S(2)}) collective-permute-start(f32[34,8,128]{2,1,0:T(8,128)S(1)} %edge_far.1), channel_id=1, source_target_pairs={{2,4},{4,2},{3,5},{5,3},{10,12},{12,10},{11,13},{13,11},{18,20},{2... | collective-permute-start | bytes 417800 | tf_op jit(solution)/shard_map/ppermute | solution.py:564
  7.4 4.5 %collective-permute-start.3 = (f32[34,8,128]{2,1,0:T(8,128)S(1)}, f32[34,8,128]{2,1,0:T(8,128)S(1)}, u32[]{:S(2)}, u32[]{:S(2)}) collective-permute-start(f32[34,8,128]{2,1,0:T(8,128)S(1)} %edge_near.1), channel_id=1, source_target_pairs={{0,2},{2,0},{4,6},{6,4},{1,3},{3,1},{5,7},{7,5},{8,10},{10,8},{12,... | collective-permute-start | bytes 417800 | tf_op jit(solution)/shard_map/ppermute | solution.py:564
  12.0 6.5 %collective-permute-start.4 = (f32[37,8,128]{2,1,0:T(8,128)S(1)}, f32[37,8,128]{2,1,0:T(8,128)S(1)}, u32[]{:S(2)}, u32[]{:S(2)}) collective-permute-start(f32[37,8,128]{2,1,0:T(8,128)S(1)} %rim_far.1), channel_id=1, source_target_pairs={{2,4},{4,2},{3,5},{5,3},{10,12},{12,10},{11,13},{13,11},{18,20},{2... | collective-permute-start | bytes 454664 | tf_op jit(solution)/shard_map/ppermute | solution.py:564
  14.1 4.4 %collective-permute-start.5 = (f32[37,8,128]{2,1,0:T(8,128)S(1)}, f32[37,8,128]{2,1,0:T(8,128)S(1)}, u32[]{:S(2)}, u32[]{:S(2)}) collective-permute-start(f32[37,8,128]{2,1,0:T(8,128)S(1)} %rim_near.1), channel_id=1, source_target_pairs={{0,2},{2,0},{4,6},{6,4},{1,3},{3,1},{5,7},{7,5},{8,10},{10,8},{12,... | collective-permute-start | bytes 454664 | tf_op jit(solution)/shard_map/ppermute | solution.py:564
  26.4 3.6 %collective-permute-start.6 = (f32[8,128]{1,0:T(8,128)S(1)}, f32[8,128]{1,0:T(8,128)S(1)}, u32[]{:S(2)}, u32[]{:S(2)}) collective-permute-start(f32[8,128]{1,0:T(8,128)S(1)} %get-tuple-element.38.sums), channel_id=1, source_target_pairs={{0,1},{1,0},{2,3},{3,2},{4,5},{5,4},{6,7},{7,6},{8,9},{9,8},{10,11... | collective-permute-start | bytes 12296 | tf_op jit(solution)/shard_map/ppermute | solution.py:564

commit v10 on v9

--- a/solution.py
+++ b/solution.py
@@ -93,16 +93,64 @@
         own[1, d] = flat1[pl.ds(d, FREQ, stride=NDIR), :] * sea1
 
 
-WEST_PAIRS = [(33, 0), (34, 1), (35, 2)]
-EAST_PAIRS = [(15, 18), (16, 19), (17, 20)]
-
-
-def slots(pairs):
-    paired = [d for pair in pairs for d in pair]
-    return [d for d in range(SLABS) if d not in paired]
-
-
-SENT = SLABS - 3
+NEEDS = (7, 7, 6, 6, 5, 5, 4, 4, 4, 4, 4, 4, 5, 5, 6, 6, 7, 7)
+PACKED = {
+    0: [(12, 3, 7, 1)],
+    1: [(12, 4, 7, 1)],
+    2: [(15, 0, 6, 2)],
+    3: [(15, 2, 6, 2)],
+    4: [(12, 0, 5, 3)],
+    5: [(13, 0, 5, 3)],
+    6: [(9, 0, 4, 4)],
+    7: [(10, 0, 4, 4)],
+    8: [(11, 0, 4, 4)],
+    14: [(15, 4, 6, 2)],
+    16: [(13, 3, 7, 1)],
+    17: [(13, 4, 7, 1)],
+}
+TO_WEST, TO_EAST, TO_NORTH, TO_SOUTH = 27, 9, 18, 0
+SENT = 18 + 1 + len(PACKED)
+
+
+def downstream(first):
+    return [(first + i) % NDIR for i in range(18)]
+
+
+def whole(first):
+    return [d for d in range(NDIR) if d not in downstream(first)] + [STATIC]
+
+
+def write_message(message, get, rising, rising_first, falling_first, place, unit):
+    for i, pair in enumerate(zip(whole(rising_first), whole(falling_first))):
+        message[i] = get(*pair)
+    up, down = downstream(rising_first), downstream(falling_first)
+    cell = jnp.where(rising, place, 7 - place)
+    for i, (main, pieces) in enumerate(PACKED.items()):
+        value = get(up[main], down[main])
+        for other, start, to, count in pieces:
+            shift = (to - start) * unit
+            moved = pltpu.roll(get(up[other], down[other]), jnp.where(rising, shift, 128 - shift), 1)
+            value = jnp.where((cell >= to) & (cell < to + count), moved, value)
+        message[19 + i] = value
+
+
+def read_message(message, out, rising, first, place, unit):
+    for i, d in enumerate(whole(first)):
+        out[d] = message(i)
+    dirs = downstream(first)
+    cell = place if rising else 7 - place
+    parts = {}
+    for i, (main, pieces) in enumerate(PACKED.items()):
+        value = message(19 + i)
+        out[dirs[main]] = value
+        for other, start, to, count in pieces:
+            shift = (start - to) * unit
+            moved = roll(value, shift if rising else -shift)
+            if other in parts:
+                moved = jnp.where((cell >= start) & (cell < start + count), moved, parts[other])
+            parts[other] = moved
+    for other, value in parts.items():
+        out[dirs[other]] = value
 
 
 def column_kernel(second, own, message):
@@ -111,34 +159,20 @@
     from_own0 = (inner >= 8) == to_east
     shift = jnp.where(to_east, 120, 8)
 
-    def edge(slab):
+    def get(west, east):
+        slab = west if west == east else jnp.where(to_east, east, west)
         return jnp.where(from_own0, own[0, slab], pltpu.roll(own[1, slab], shift, 1))
 
-    for i, (east, west) in enumerate(zip(slots(EAST_PAIRS), slots(WEST_PAIRS))):
-        if east == west:
-            message[i] = edge(east)
-        else:
-            message[i] = edge(jnp.where(to_east, east, west))
-    near = (inner % 8 >= 4) == to_east
-    for i, (east, west) in enumerate(zip(EAST_PAIRS, WEST_PAIRS)):
-        one = edge(jnp.where(to_east, east[0], west[0]))
-        two = edge(jnp.where(to_east, east[1], west[1]))
-        message[SENT - 3 + i] = jnp.where(near, one, pltpu.roll(two, jnp.where(to_east, 124, 4), 1))
-
-
-NORTH_PAIRS = [(24, 27), (25, 28), (26, 29)]
-SOUTH_PAIRS = [(6, 9), (7, 10), (8, 11)]
+    write_message(message, get, ~to_east, TO_WEST, TO_EAST, inner % 8, 1)
 
 
 def edge_kernel(second, own, message):
     to_north = is_even("lat") != second
-    for i, (north, south) in enumerate(zip(slots(NORTH_PAIRS), slots(SOUTH_PAIRS))):
-        message[i] = jnp.where(to_north, own[1, north], own[0, south])
-    near = (lanes() >= 64) == to_north
-    for i, (north, south) in enumerate(zip(NORTH_PAIRS, SOUTH_PAIRS)):
-        one = jnp.where(to_north, own[1, north[0]], own[0, south[0]])
-        two = jnp.where(to_north, own[1, north[1]], own[0, south[1]])
-        message[SENT - 3 + i] = jnp.where(near, one, roll(two, 64))
+
+    def get(south, north):
+        return jnp.where(to_north, own[1, north], own[0, south])
+
+    write_message(message, get, ~to_north, TO_SOUTH, TO_NORTH, lanes() // 16, 16)
 
 
 def growth_kernel(own, local, consts, gain):
@@ -227,29 +261,19 @@
     place_field(wide, wdir[...], local, WDIR)
 
 
-def unpack(even, first, second, pairs, out, back):
-    full = slots(pairs)
-    for i in range(SENT):
-        got = jnp.where(even, first[i], second[i])
-        if i < len(full):
-            out[full[i]] = got
-        else:
-            pair = pairs[i - len(full)]
-            out[pair[0]] = got
-            out[pair[1]] = roll(got, back)
-
-
 def unpack_kernel(cols_second, cols_first, rows_second, rows_first, consts, west, east):
     del rows_second, rows_first, consts
     even = is_even("lon")
-    unpack(even, cols_second, cols_first, EAST_PAIRS, west, 4)
-    unpack(even, cols_first, cols_second, WEST_PAIRS, east, -4)
+    place = lanes() % 8
+    read_message(lambda i: jnp.where(even, cols_second[i], cols_first[i]), west, False, TO_EAST, place, 1)
+    read_message(lambda i: jnp.where(even, cols_first[i], cols_second[i]), east, True, TO_WEST, place, 1)
 
 
 def unpack_rows_kernel(rows_second, rows_first, south, north):
     even = is_even("lat")
-    unpack(even, rows_second, rows_first, NORTH_PAIRS, south, 64)
-    unpack(even, rows_first, rows_second, SOUTH_PAIRS, north, 64)
+    place = lanes() // 16
+    read_message(lambda i: jnp.where(even, rows_second[i], rows_first[i]), south, False, TO_NORTH, place, 16)
+    read_message(lambda i: jnp.where(even, rows_first[i], rows_second[i]), north, True, TO_SOUTH, place, 16)
 
 
 def rim_kernel(second, west, east, rim):
@@ -348,8 +372,8 @@
     return k - k * u + 2.0 * bend, k * u - bend, -bend
 
 
-FORTH_TAPS = (-1, -2)
-BACK_TAPS = (-1, 2)
+FORTH_TAPS = (1, -1, -2)
+BACK_TAPS = (1, -1, 2)
 
 
 def lon_kernel(q, taps, shifts, out):
@@ -369,8 +393,8 @@
                 for i, d in enumerate(dirs):
                     cell = q[d, t]
                     near = moved[64 * i + 8 * t : 64 * i + 8 * t + 8]
-                    out[d, t] = (tap[0] * cell + tap[1] * roll(cell, -1)) + (
-                        tap[2] * near[:, :128] + tap[3] * near[:, 128:]
+                    out[d, t] = (tap[0] * cell + tap[1] * near[:, :128]) + (
+                        tap[2] * near[:, 128:256] + tap[3] * near[:, 256:]
                     )
 
 
@@ -603,7 +627,7 @@
     place, rims, shifts, gather, local, consts = call(
         tables_kernel,
         6,
-        [(1536, 1024), (512, 1024), (2, 256, 256), (2048, 256), (2,) + tile, (20,) + tile],
+        [(1536, 1024), (512, 1024), (2, 256, 384), (2048, 256), (2,) + tile, (20,) + tile],
         [pltpu.VMEM(x.shape, x.dtype) for x in inputs]
         + [pltpu.VMEM((16, 128), f32), pltpu.SemaphoreType.DMA((6,))],
         name="tables",

time: 31.5 us -> 32.1 us (1.019)
  the two profiles are of different devices: /device:TPU:2 before, /device:TPU:10 now
where the time goes in v10:
time: 32.1 us; the launch traced here: 31.8 us
  Pallas kernels  14.3 us (45%)
  starting transfers between devices  9.66 us (30%)
  waiting for transfers between devices  7.68 us (24%)
    ppermute x7, starting transfers between devices, swap(): return lax.ppermute(array, axis, pairs)  9.66 us
    ppermute x7, waiting for transfers between devices, swap(): return lax.ppermute(array, axis, pairs)  7.68 us
    pallas_call x4, Pallas kernels, per_device(): q, = call(lon_kernel, 3, cells, name='lon')(q, taps, shifts)  3.47 us
    pallas_call x3, Pallas kernels, per_device(): q, = call(turn_kernel, 3, cells, name='turn')(q, tx, ty)  1.73 us
    pallas_call x3, Pallas kernels, per_device(): q, = call(lat_kernel, 3, cells, name='lat')(q, ky, consts)  1.63 us
    pallas_call x1, Pallas kernels, per_device(): call(pack_kernel, 4, [(2,) + slabs], [pltpu.VMEM(x.shape, x.dtype) for x...  1.24 us
    pallas_call x1, Pallas kernels, per_device(): call(place_kernel, 6, [(SLABS,) + block], [pltpu.VMEM((8 * SLABS + 8, 153...  1.16 us
    pallas_call x1, Pallas kernels, per_device(): call(tables_kernel, 6, [(1536, 1024), (512, 1024), (2, 256, 384), (2048,...  0.96 us
  transfers between devices with their start and end apart: 7, of which 5 were waited for; matrix products, arithmetic and copies ran while one was open for 0% of the time, Pallas kernels for 11%

profile of v10, /device:TPU:10, one launch (start us, length us, event | category | flops | bytes accessed | tf_op | source)
XLA Modules:
  0.0 31.8 jit_solution(14071966815537342559)
XLA Ops:
  0.0 1.2 %pack.1.own = f32[2,37,8,128]{3,2,1,0:T(8,128)S(1)} custom-call(f32[16,16,288]{2,1,0:T(8,128)} %refs_0_.2, s32[16,16]{1,0:T(8,128)} %refs_1_.2, s32[16,16]{1,0:T(8,128)} %refs_2_.2, f32[2,16,16]{2,1,0:T(8,128)} %refs_3_.2), custom_call_target="tpu_custom_call" | custom-call | tf_op jit(solution)/shard_map/pack/pallas_call | solution.py:608
  1.3 0.2 column_far.1
  1.4 1.6 %collective-permute-start = (f32[31,8,128]{2,1,0:T(8,128)S(1)}, f32[31,8,128]{2,1,0:T(8,128)S(1)}, u32[]{:S(2)}, u32[]{:S(2)}) collective-permute-start(f32[31,8,128]{2,1,0:T(8,128)S(1)} %column_far.1), channel_id=1, source_target_pairs={{8,16},{16,8},{24,0},{0,24},{9,17},{17,9},{25,1},{1,25},{10,18},{1... | collective-permute-start | bytes 380936 | tf_op jit(solution)/shard_map/ppermute | solution.py:588
  3.1 0.1 column_near.1
  3.2 2.5 %collective-permute-start.1 = (f32[31,8,128]{2,1,0:T(8,128)S(1)}, f32[31,8,128]{2,1,0:T(8,128)S(1)}, u32[]{:S(2)}, u32[]{:S(2)}) collective-permute-start(f32[31,8,128]{2,1,0:T(8,128)S(1)} %column_near.1), channel_id=1, source_target_pairs={{0,8},{8,0},{16,24},{24,16},{1,9},{9,1},{17,25},{25,17},{2,10},{10... | collective-permute-start | bytes 380936 | tf_op jit(solution)/shard_map/ppermute | solution.py:588
  5.8 1.9 %collective-permute-start.2 = (f32[31,8,128]{2,1,0:T(8,128)S(1)}, f32[31,8,128]{2,1,0:T(8,128)S(1)}, u32[]{:S(2)}, u32[]{:S(2)}) collective-permute-start(f32[31,8,128]{2,1,0:T(8,128)S(1)} %edge_far.1), channel_id=1, source_target_pairs={{2,4},{4,2},{3,5},{5,3},{10,12},{12,10},{11,13},{13,11},{18,20},{2... | collective-permute-start | bytes 380936 | tf_op jit(solution)/shard_map/ppermute | solution.py:588
  7.9 1.0 %tables.1 = (bf16[1536,1024]{1,0:T(8,128)(2,1)S(1)}, bf16[512,1024]{1,0:T(8,128)(2,1)S(1)}, bf16[2,256,384]{2,1,0:T(8,128)(2,1)S(1)}, bf16[2048,256]{1,0:T(8,128...) custom-call(f32[8,16]{1,0:T(8,128)} %refs_0_.3, f32[8,16]{1,0:T(8,128)} %refs_1_.3, f32[16]{0:T(128)} %refs_2_.3, ...), custom_call_target="tpu_custom_call" | custom-call | tf_op jit(solution)/shard_map/tables/pallas_call | solution.py:627
  8.9 0.4 %collective-permute-done.cols_second = f32[31,8,128]{2,1,0:T(8,128)S(1)} collective-permute-done((f32[31,8,128]{2,1,0:T(8,128)S(1)}, f32[31,8,128]{2,1,0:T(8,128)S(1)}, u32[]{:S(2)}, u32[]{:S(2)}) %collective-permute-start) | collective-permute-done | bytes 127008 | tf_op jit(solution)/shard_map/ppermute | solution.py:588
  9.4 2.1 %collective-permute-done.1.cols_first = f32[31,8,128]{2,1,0:T(8,128)S(1)} collective-permute-done((f32[31,8,128]{2,1,0:T(8,128)S(1)}, f32[31,8,128]{2,1,0:T(8,128)S(1)}, u32[]{:S(2)}, u32[]{:S(2)}) %collective-permute-start.1) | collective-permute-done | bytes 127008 | tf_op jit(solution)/shard_map/ppermute | solution.py:588
  11.4 0.7 %collective-permute-done.2.rows_second = f32[31,8,128]{2,1,0:T(8,128)S(1)} collective-permute-done((f32[31,8,128]{2,1,0:T(8,128)S(1)}, f32[31,8,128]{2,1,0:T(8,128)S(1)}, u32[]{:S(2)}, u32[]{:S(2)}) %collective-permute-start.2) | collective-permute-done | bytes 127008 | tf_op jit(solution)/shard_map/ppermute | solution.py:588
  12.3 1.9 %collective-permute-start.4 = (f32[37,8,128]{2,1,0:T(8,128)S(1)}, f32[37,8,128]{2,1,0:T(8,128)S(1)}, u32[]{:S(2)}, u32[]{:S(2)}) collective-permute-start(f32[37,8,128]{2,1,0:T(8,128)S(1)} %rim_far.1), channel_id=1, source_target_pairs={{2,4},{4,2},{3,5},{5,3},{10,12},{12,10},{11,13},{13,11},{18,20},{2... | collective-permute-start | bytes 454664 | tf_op jit(solution)/shard_map/ppermute | solution.py:588
  14.3 0.1 unpack_rows.1
  14.4 1.2 %place.1.partial = f32[37,8,8,128]{3,2,1,0:T(8,128)S(1)} custom-call(f32[2,37,8,128]{3,2,1,0:T(8,128)S(1)} %pack.1.own, f32[37,8,128]{2,1,0:T(8,128)S(1)} %get-tuple-element.23.west, f32[37,8,128]{2,1,0:T(8,128)S(1)} %get-tuple-element.24.east, f32[37,8,128]{2,1,0:T(8,128)S(1)} %get-tuple-element.25.south, f32[37,8,128]{2,1,0:T(8,128)S(1)} %get-tuple-element.26.north, ...), custom_call_target="tpu_custom_call" | custom-call | tf_op jit(solution)/shard_map/place/pallas_call | solution.py:646
  15.6 3.2 %collective-permute-done.4.rims_second = f32[37,8,128]{2,1,0:T(8,128)S(1)} collective-permute-done((f32[37,8,128]{2,1,0:T(8,128)S(1)}, f32[37,8,128]{2,1,0:T(8,128)S(1)}, u32[]{:S(2)}, u32[]{:S(2)}) %collective-permute-start.4) | collective-permute-done | bytes 151584 | tf_op jit(solution)/shard_map/ppermute | solution.py:588
  18.8 0.9 %rims.1 = (f32[36,8,8,128]{3,2,1,0:T(8,128)S(1)}, f32[10,2,4,8,8,128]{5,4,3,2,1,0:T(8,128)S(1)}, f32[8,8,128]{2,1,0:T(8,128)S(1)}, f32[8,8,128]{2,1,0:T(8,128)S(1)}, f32[8,8,128]{2,1,0:T(8,128)S(1)}) custom-call(f32[37,8,8,128]{3,2,1,0:T(8,128)S(1)} %place.1.partial, f32[37,8,128]{2,1,0:T(8,128)S(1)} %collective-permute-done.4.rims_second, ...), custom_call_target="tpu_custom_call" | custom-call | tf_op jit(solution)/shard_map/rims/pallas_call | solution.py:653
  19.7 0.9 %lon.4.q = f32[36,8,8,128]{3,2,1,0:T(8,128)S(1)} custom-call(f32[36,8,8,128]{3,2,1,0:T(8,128)S(1)} %get-tuple-element.29.q, f32[10,2,4,8,8,128]{5,4,3,2,1,0:T(8,128)S(1)} %get-tuple-element.30.taps, bf16[2,256,384]{2,1,0:T(8,128)(2,1)S(1)} %get-tuple-element.31.shifts), custom_call_target="tpu_custom_call" | custom-call | tf_op jit(solution)/shard_map/lon/pallas_call | solution.py:662
  20.5 0.5 %lat.3.q = f32[36,8,8,128]{3,2,1,0:T(8,128)S(1)} custom-call(f32[36,8,8,128]{3,2,1,0:T(8,128)S(1)} %lon.4.q, f32[8,8,128]{2,1,0:T(8,128)S(1)} %get-tuple-element.32.ky, f32[20,8,128]{2,1,0:T(8,128)S(1)} %get-tuple-element.22.consts), custom_call_target="tpu_custom_call" | custom-call | tf_op jit(solution)/shard_map/lat/pallas_call | solution.py:666
  21.1 0.6 %turn.3.q = f32[36,8,8,128]{3,2,1,0:T(8,128)S(1)} custom-call(f32[36,8,8,128]{3,2,1,0:T(8,128)S(1)} %lat.3.q, f32[8,8,128]{2,1,0:T(8,128)S(1)} %get-tuple-element.33.tx, f32[8,8,128]{2,1,0:T(8,128)S(1)} %get-tuple-element.34.ty), custom_call_target="tpu_custom_call" | custom-call | tf_op jit(solution)/shard_map/turn/pallas_call | solution.py:667
  21.7 0.9 %lon.5.q = f32[36,8,8,128]{3,2,1,0:T(8,128)S(1)} custom-call(f32[36,8,8,128]{3,2,1,0:T(8,128)S(1)} %turn.3.q, f32[10,2,4,8,8,128]{5,4,3,2,1,0:T(8,128)S(1)} %get-tuple-element.30.taps, bf16[2,256,384]{2,1,0:T(8,128)(2,1)S(1)} %get-tuple-element.31.shifts), custom_call_target="tpu_custom_call" | custom-call | tf_op jit(solution)/shard_map/lon/pallas_call | solution.py:662
  22.5 0.5 %lat.4.q = f32[36,8,8,128]{3,2,1,0:T(8,128)S(1)} custom-call(f32[36,8,8,128]{3,2,1,0:T(8,128)S(1)} %lon.5.q, f32[8,8,128]{2,1,0:T(8,128)S(1)} %get-tuple-element.32.ky, f32[20,8,128]{2,1,0:T(8,128)S(1)} %get-tuple-element.22.consts), custom_call_target="tpu_custom_call" | custom-call | tf_op jit(solution)/shard_map/lat/pallas_call | solution.py:666
  23.1 0.6 %turn.4.q = f32[36,8,8,128]{3,2,1,0:T(8,128)S(1)} custom-call(f32[36,8,8,128]{3,2,1,0:T(8,128)S(1)} %lat.4.q, f32[8,8,128]{2,1,0:T(8,128)S(1)} %get-tuple-element.33.tx, f32[8,8,128]{2,1,0:T(8,128)S(1)} %get-tuple-element.34.ty), custom_call_target="tpu_custom_call" | custom-call | tf_op jit(solution)/shard_map/turn/pallas_call | solution.py:667
  23.7 0.9 %lon.6.q = f32[36,8,8,128]{3,2,1,0:T(8,128)S(1)} custom-call(f32[36,8,8,128]{3,2,1,0:T(8,128)S(1)} %turn.4.q, f32[10,2,4,8,8,128]{5,4,3,2,1,0:T(8,128)S(1)} %get-tuple-element.30.taps, bf16[2,256,384]{2,1,0:T(8,128)(2,1)S(1)} %get-tuple-element.31.shifts), custom_call_target="tpu_custom_call" | custom-call | tf_op jit(solution)/shard_map/lon/pallas_call | solution.py:662
  24.5 0.5 %lat.5.q = f32[36,8,8,128]{3,2,1,0:T(8,128)S(1)} custom-call(f32[36,8,8,128]{3,2,1,0:T(8,128)S(1)} %lon.6.q, f32[8,8,128]{2,1,0:T(8,128)S(1)} %get-tuple-element.32.ky, f32[20,8,128]{2,1,0:T(8,128)S(1)} %get-tuple-element.22.consts), custom_call_target="tpu_custom_call" | custom-call | tf_op jit(solution)/shard_map/lat/pallas_call | solution.py:666
  25.1 0.6 %turn.5.q = f32[36,8,8,128]{3,2,1,0:T(8,128)S(1)} custom-call(f32[36,8,8,128]{3,2,1,0:T(8,128)S(1)} %lat.5.q, f32[8,8,128]{2,1,0:T(8,128)S(1)} %get-tuple-element.33.tx, f32[8,8,128]{2,1,0:T(8,128)S(1)} %get-tuple-element.34.ty), custom_call_target="tpu_custom_call" | custom-call | tf_op jit(solution)/shard_map/turn/pallas_call | solution.py:667
  25.7 0.9 %lon.7.q = f32[36,8,8,128]{3,2,1,0:T(8,128)S(1)} custom-call(f32[36,8,8,128]{3,2,1,0:T(8,128)S(1)} %turn.5.q, f32[10,2,4,8,8,128]{5,4,3,2,1,0:T(8,128)S(1)} %get-tuple-element.30.taps, bf16[2,256,384]{2,1,0:T(8,128)(2,1)S(1)} %get-tuple-element.31.shifts), custom_call_target="tpu_custom_call" | custom-call | tf_op jit(solution)/shard_map/lon/pallas_call | solution.py:662
  26.5 0.7 %lat_sums.1 = (f32[36,8,8,128]{3,2,1,0:T(8,128)S(1)}, f32[8,128]{1,0:T(8,128)S(1)}) custom-call(f32[36,8,8,128]{3,2,1,0:T(8,128)S(1)} %lon.7.q, f32[8,8,128]{2,1,0:T(8,128)S(1)} %get-tuple-element.32.ky, f32[20,8,128]{2,1,0:T(8,128)S(1)} %get-tuple-element.22.consts), custom_call_target="tpu_custom_call" | custom-call | tf_op jit(solution)/shard_map/lat_sums/pallas_call | solution.py:664
  27.3 1.5 %collective-permute-start.6 = (f32[8,128]{1,0:T(8,128)S(1)}, f32[8,128]{1,0:T(8,128)S(1)}, u32[]{:S(2)}, u32[]{:S(2)}) collective-permute-start(f32[8,128]{1,0:T(8,128)S(1)} %get-tuple-element.38.sums), channel_id=1, source_target_pairs={{0,1},{1,0},{2,3},{3,2},{4,5},{5,4},{6,7},{7,6},{8,9},{9,8},{10,11... | collective-permute-start | bytes 12296 | tf_op jit(solution)/shard_map/ppermute | solution.py:588
  28.8 0.1 growth.1.gain
  28.9 0.5 %gather.1.own = f32[2,36,8,128]{3,2,1,0:T(8,128)S(1)} custom-call(f32[36,8,8,128]{3,2,1,0:T(8,128)S(1)} %get-tuple-element.35.q, bf16[2048,256]{1,0:T(8,128)(2,1)S(1)} %get-tuple-element.36.matrix), custom_call_target="tpu_custom_call" | custom-call | tf_op jit(solution)/shard_map/gather/pallas_call | solution.py:669
  29.4 0.2 last_turn.1.early
  29.6 1.3 %collective-permute-done.6.other = f32[8,128]{1,0:T(8,128)S(1)} collective-permute-done((f32[8,128]{1,0:T(8,128)S(1)}, f32[8,128]{1,0:T(8,128)S(1)}, u32[]{:S(2)}, u32[]{:S(2)}) %collective-permute-start.6) | collective-permute-done | bytes 4128 | tf_op jit(solution)/shard_map/ppermute | solution.py:588
  30.9 1.0 %finish.1 = f32[16,16,288]{2,1,0:T(8,128)} custom-call(f32[2,36,8,128]{3,2,1,0:T(8,128)S(1)} %last_turn.1.early, f32[2,8,128]{2,1,0:T(8,128)S(1)} %get-tuple-element.37.local, f32[8,128]{1,0:T(8,128)S(1)} %get-tuple-element.38.sums, f32[8,128]{1,0:T(8,128)S(1)} %collective-permute-done.6.other, f32[20,8,128]{2,1,0:T(8,128)S(1)} %get-tuple-element.22.consts), custom_call_target="tpu_custom_call" | custom-call | tf_op jit(solution)/shard_map/finish/pallas_call | solution.py:674
  (10 shorter events, 0.5 us)
Async XLA Ops:
  1.4 7.9 %collective-permute-start = (f32[31,8,128]{2,1,0:T(8,128)S(1)}, f32[31,8,128]{2,1,0:T(8,128)S(1)}, u32[]{:S(2)}, u32[]{:S(2)}) collective-permute-start(f32[31,8,128]{2,1,0:T(8,128)S(1)} %column_far.1), channel_id=1, source_target_pairs={{8,16},{16,8},{24,0},{0,24},{9,17},{17,9},{25,1},{1,25},{10,18},{1... | collective-permute-start | bytes 380936 | tf_op jit(solution)/shard_map/ppermute | solution.py:588
  3.2 8.2 %collective-permute-start.1 = (f32[31,8,128]{2,1,0:T(8,128)S(1)}, f32[31,8,128]{2,1,0:T(8,128)S(1)}, u32[]{:S(2)}, u32[]{:S(2)}) collective-permute-start(f32[31,8,128]{2,1,0:T(8,128)S(1)} %column_near.1), channel_id=1, source_target_pairs={{0,8},{8,0},{16,24},{24,16},{1,9},{9,1},{17,25},{25,17},{2,10},{10... | collective-permute-start | bytes 380936 | tf_op jit(solution)/shard_map/ppermute | solution.py:588
  5.8 6.2 %collective-permute-start.2 = (f32[31,8,128]{2,1,0:T(8,128)S(1)}, f32[31,8,128]{2,1,0:T(8,128)S(1)}, u32[]{:S(2)}, u32[]{:S(2)}) collective-permute-start(f32[31,8,128]{2,1,0:T(8,128)S(1)} %edge_far.1), channel_id=1, source_target_pairs={{2,4},{4,2},{3,5},{5,3},{10,12},{12,10},{11,13},{13,11},{18,20},{2... | collective-permute-start | bytes 380936 | tf_op jit(solution)/shard_map/ppermute | solution.py:588
  7.9 4.2 %collective-permute-start.3 = (f32[31,8,128]{2,1,0:T(8,128)S(1)}, f32[31,8,128]{2,1,0:T(8,128)S(1)}, u32[]{:S(2)}, u32[]{:S(2)}) collective-permute-start(f32[31,8,128]{2,1,0:T(8,128)S(1)} %edge_near.1), channel_id=1, source_target_pairs={{0,2},{2,0},{4,6},{6,4},{1,3},{3,1},{5,7},{7,5},{8,10},{10,8},{12,... | collective-permute-start | bytes 380936 | tf_op jit(solution)/shard_map/ppermute | solution.py:588
  12.3 6.5 %collective-permute-start.4 = (f32[37,8,128]{2,1,0:T(8,128)S(1)}, f32[37,8,128]{2,1,0:T(8,128)S(1)}, u32[]{:S(2)}, u32[]{:S(2)}) collective-permute-start(f32[37,8,128]{2,1,0:T(8,128)S(1)} %rim_far.1), channel_id=1, source_target_pairs={{2,4},{4,2},{3,5},{5,3},{10,12},{12,10},{11,13},{13,11},{18,20},{2... | collective-permute-start | bytes 454664 | tf_op jit(solution)/shard_map/ppermute | solution.py:588
  14.2 4.6 %collective-permute-start.5 = (f32[37,8,128]{2,1,0:T(8,128)S(1)}, f32[37,8,128]{2,1,0:T(8,128)S(1)}, u32[]{:S(2)}, u32[]{:S(2)}) collective-permute-start(f32[37,8,128]{2,1,0:T(8,128)S(1)} %rim_near.1), channel_id=1, source_target_pairs={{0,2},{2,0},{4,6},{6,4},{1,3},{3,1},{5,7},{7,5},{8,10},{10,8},{12,... | collective-permute-start | bytes 454664 | tf_op jit(solution)/shard_map/ppermute | solution.py:588
  27.3 3.6 %collective-permute-start.6 = (f32[8,128]{1,0:T(8,128)S(1)}, f32[8,128]{1,0:T(8,128)S(1)}, u32[]{:S(2)}, u32[]{:S(2)}) collective-permute-start(f32[8,128]{1,0:T(8,128)S(1)} %get-tuple-element.38.sums), channel_id=1, source_target_pairs={{0,1},{1,0},{2,3},{3,2},{4,5},{5,4},{6,7},{7,6},{8,9},{9,8},{10,11... | collective-permute-start | bytes 12296 | tf_op jit(solution)/shard_map/ppermute | solution.py:588

commit v11 on v10

--- a/solution.py
+++ b/solution.py
@@ -261,8 +261,8 @@
     place_field(wide, wdir[...], local, WDIR)
 
 
-def unpack_kernel(cols_second, cols_first, rows_second, rows_first, consts, west, east):
-    del rows_second, rows_first, consts
+def unpack_kernel(cols_second, cols_first, consts, west, east):
+    del consts
     even = is_even("lon")
     place = lanes() % 8
     read_message(lambda i: jnp.where(even, cols_second[i], cols_first[i]), west, False, TO_EAST, place, 1)
@@ -276,7 +276,8 @@
     read_message(lambda i: jnp.where(even, rows_first[i], rows_second[i]), north, True, TO_SOUTH, place, 16)
 
 
-def rim_kernel(second, west, east, rim):
+def rim_kernel(second, west, east, *refs):
+    rim = refs[-1]
     west_low = (lanes() % 16 < 8) == (is_even("lat") != second)
     for slab in range(SLABS):
         rim[slab] = jnp.where(west_low, west[slab], east[slab])
@@ -372,8 +373,8 @@
     return k - k * u + 2.0 * bend, k * u - bend, -bend
 
 
-FORTH_TAPS = (1, -1, -2)
-BACK_TAPS = (1, -1, 2)
+FORTH_TAPS = (-1, -2)
+BACK_TAPS = (-1, 2)
 
 
 def lon_kernel(q, taps, shifts, out):
@@ -393,8 +394,8 @@
                 for i, d in enumerate(dirs):
                     cell = q[d, t]
                     near = moved[64 * i + 8 * t : 64 * i + 8 * t + 8]
-                    out[d, t] = (tap[0] * cell + tap[1] * near[:, :128]) + (
-                        tap[2] * near[:, 128:256] + tap[3] * near[:, 256:]
+                    out[d, t] = (tap[0] * cell + tap[1] * roll(cell, -1)) + (
+                        tap[2] * near[:, :128] + tap[3] * near[:, 128:]
                     )
 
 
@@ -627,7 +628,7 @@
     place, rims, shifts, gather, local, consts = call(
         tables_kernel,
         6,
-        [(1536, 1024), (512, 1024), (2, 256, 384), (2048, 256), (2,) + tile, (20,) + tile],
+        [(1536, 1024), (512, 1024), (2, 256, 256), (2048, 256), (2,) + tile, (20,) + tile],
         [pltpu.VMEM(x.shape, x.dtype) for x in inputs]
         + [pltpu.VMEM((16, 128), f32), pltpu.SemaphoreType.DMA((6,))],
         name="tables",
@@ -635,12 +636,12 @@
         dtype=[bf16] * 4 + [f32] * 2,
     )(*[pltpu.with_memory_space_constraint(x, pltpu.HBM) for x in inputs])
     (gain,) = call(growth_kernel, 3, [(NDIR, 2) + tile], name="growth")(own, local, consts)
-    west, east = call(unpack_kernel, 5, [slabs] * 2, name="unpack")(
-        cols_second, cols_first, rows_second, rows_first, consts
-    )
+    west, east = call(unpack_kernel, 3, [slabs] * 2, name="unpack")(cols_second, cols_first, consts)
     (rim_second,) = call(functools.partial(rim_kernel, True), 2, [slabs], name="rim_far")(west, east)
     rims_second = swap(rim_second, "lat", 1)
-    (rim_first,) = call(functools.partial(rim_kernel, False), 2, [slabs], name="rim_near")(west, east)
+    (rim_first,) = call(functools.partial(rim_kernel, False), 4, [slabs], name="rim_near")(
+        west, east, rows_second, rows_first
+    )
     rims_first = swap(rim_first, "lat", 0)
     south, north = call(unpack_rows_kernel, 2, [slabs] * 2, name="unpack_rows")(rows_second, rows_first)
     (partial,) = call(

time: 32.1 us -> 30.8 us (0.960)
  the two profiles are of different devices: /device:TPU:10 before, /device:TPU:2 now
where the time goes in v11:
time: 30.8 us; the launch traced here: 30.4 us
  Pallas kernels  13.7 us (44%)
  starting transfers between devices  9.24 us (30%)
  waiting for transfers between devices  7.26 us (24%)
    ppermute x7, starting transfers between devices, swap(): return lax.ppermute(array, axis, pairs)  9.24 us
    ppermute x7, waiting for transfers between devices, swap(): return lax.ppermute(array, axis, pairs)  7.26 us
    pallas_call x4, Pallas kernels, per_device(): q, = call(lon_kernel, 3, cells, name='lon')(q, taps, shifts)  2.86 us
    pallas_call x3, Pallas kernels, per_device(): q, = call(turn_kernel, 3, cells, name='turn')(q, tx, ty)  1.73 us
    pallas_call x3, Pallas kernels, per_device(): q, = call(lat_kernel, 3, cells, name='lat')(q, ky, consts)  1.64 us
    pallas_call x1, Pallas kernels, per_device(): call(pack_kernel, 4, [(2,) + slabs], [pltpu.VMEM(x.shape, x.dtype) for x...  1.24 us
    pallas_call x1, Pallas kernels, per_device(): call(place_kernel, 6, [(SLABS,) + block], [pltpu.VMEM((8 * SLABS + 8, 153...  1.16 us
    pallas_call x1, Pallas kernels, per_device(): call(tables_kernel, 6, [(1536, 1024), (512, 1024), (2, 256, 256), (2048,...  0.96 us
  transfers between devices with their start and end apart: 7, of which 4 were waited for; matrix products, arithmetic and copies ran while one was open for 0% of the time, Pallas kernels for 12%

profile of v11, /device:TPU:2, one launch (start us, length us, event | category | flops | bytes accessed | tf_op | source)
XLA Modules:
  0.0 30.4 jit_solution(8144301791545733632)
XLA Ops:
  0.0 1.2 %pack.1.own = f32[2,37,8,128]{3,2,1,0:T(8,128)S(1)} custom-call(f32[16,16,288]{2,1,0:T(8,128)} %refs_0_.2, s32[16,16]{1,0:T(8,128)} %refs_1_.2, s32[16,16]{1,0:T(8,128)} %refs_2_.2, f32[2,16,16]{2,1,0:T(8,128)} %refs_3_.2), custom_call_target="tpu_custom_call" | custom-call | tf_op jit(solution)/shard_map/pack/pallas_call | solution.py:609
  1.3 0.2 column_far.1
  1.4 3.7 %collective-permute-start = (f32[31,8,128]{2,1,0:T(8,128)S(1)}, f32[31,8,128]{2,1,0:T(8,128)S(1)}, u32[]{:S(2)}, u32[]{:S(2)}) collective-permute-start(f32[31,8,128]{2,1,0:T(8,128)S(1)} %column_far.1), channel_id=1, source_target_pairs={{8,16},{16,8},{24,0},{0,24},{9,17},{17,9},{25,1},{1,25},{10,18},{1... | collective-permute-start | bytes 380936 | tf_op jit(solution)/shard_map/ppermute | solution.py:589
  5.1 0.1 column_near.1
  5.3 0.1 edge_far.1
  5.4 1.9 %collective-permute-start.2 = (f32[31,8,128]{2,1,0:T(8,128)S(1)}, f32[31,8,128]{2,1,0:T(8,128)S(1)}, u32[]{:S(2)}, u32[]{:S(2)}) collective-permute-start(f32[31,8,128]{2,1,0:T(8,128)S(1)} %edge_far.1), channel_id=1, source_target_pairs={{2,4},{4,2},{3,5},{5,3},{10,12},{12,10},{11,13},{13,11},{18,20},{2... | collective-permute-start | bytes 380936 | tf_op jit(solution)/shard_map/ppermute | solution.py:589
  7.5 1.0 %tables.1 = (bf16[1536,1024]{1,0:T(8,128)(2,1)S(1)}, bf16[512,1024]{1,0:T(8,128)(2,1)S(1)}, bf16[2,256,256]{2,1,0:T(8,128)(2,1)S(1)}, bf16[2048,256]{1,0:T(8,128...) custom-call(f32[8,16]{1,0:T(8,128)} %refs_0_.3, f32[8,16]{1,0:T(8,128)} %refs_1_.3, f32[16]{0:T(128)} %refs_2_.3, ...), custom_call_target="tpu_custom_call" | custom-call | tf_op jit(solution)/shard_map/tables/pallas_call | solution.py:628
  8.5 1.1 %collective-permute-done.cols_second = f32[31,8,128]{2,1,0:T(8,128)S(1)} collective-permute-done((f32[31,8,128]{2,1,0:T(8,128)S(1)}, f32[31,8,128]{2,1,0:T(8,128)S(1)}, u32[]{:S(2)}, u32[]{:S(2)}) %collective-permute-start) | collective-permute-done | bytes 127008 | tf_op jit(solution)/shard_map/ppermute | solution.py:589
  9.6 1.7 %collective-permute-done.1.cols_first = f32[31,8,128]{2,1,0:T(8,128)S(1)} collective-permute-done((f32[31,8,128]{2,1,0:T(8,128)S(1)}, f32[31,8,128]{2,1,0:T(8,128)S(1)}, u32[]{:S(2)}, u32[]{:S(2)}) %collective-permute-start.1) | collective-permute-done | bytes 127008 | tf_op jit(solution)/shard_map/ppermute | solution.py:589
  11.3 0.1 unpack.1
  11.5 1.9 %collective-permute-start.4 = (f32[37,8,128]{2,1,0:T(8,128)S(1)}, f32[37,8,128]{2,1,0:T(8,128)S(1)}, u32[]{:S(2)}, u32[]{:S(2)}) collective-permute-start(f32[37,8,128]{2,1,0:T(8,128)S(1)} %rim_far.1), channel_id=1, source_target_pairs={{2,4},{4,2},{3,5},{5,3},{10,12},{12,10},{11,13},{13,11},{18,20},{2... | collective-permute-start | bytes 454664 | tf_op jit(solution)/shard_map/ppermute | solution.py:589
  13.5 0.1 unpack_rows.1
  13.7 1.2 %place.1.partial = f32[37,8,8,128]{3,2,1,0:T(8,128)S(1)} custom-call(f32[2,37,8,128]{3,2,1,0:T(8,128)S(1)} %pack.1.own, f32[37,8,128]{2,1,0:T(8,128)S(1)} %get-tuple-element.23.west, f32[37,8,128]{2,1,0:T(8,128)S(1)} %get-tuple-element.24.east, f32[37,8,128]{2,1,0:T(8,128)S(1)} %get-tuple-element.25.south, f32[37,8,128]{2,1,0:T(8,128)S(1)} %get-tuple-element.26.north, ...), custom_call_target="tpu_custom_call" | custom-call | tf_op jit(solution)/shard_map/place/pallas_call | solution.py:647
  14.8 3.2 %collective-permute-done.4.rims_second = f32[37,8,128]{2,1,0:T(8,128)S(1)} collective-permute-done((f32[37,8,128]{2,1,0:T(8,128)S(1)}, f32[37,8,128]{2,1,0:T(8,128)S(1)}, u32[]{:S(2)}, u32[]{:S(2)}) %collective-permute-start.4) | collective-permute-done | bytes 151584 | tf_op jit(solution)/shard_map/ppermute | solution.py:589
  18.0 0.9 %rims.1 = (f32[36,8,8,128]{3,2,1,0:T(8,128)S(1)}, f32[10,2,4,8,8,128]{5,4,3,2,1,0:T(8,128)S(1)}, f32[8,8,128]{2,1,0:T(8,128)S(1)}, f32[8,8,128]{2,1,0:T(8,128)S(1)}, f32[8,8,128]{2,1,0:T(8,128)S(1)}) custom-call(f32[37,8,8,128]{3,2,1,0:T(8,128)S(1)} %place.1.partial, f32[37,8,128]{2,1,0:T(8,128)S(1)} %collective-permute-done.4.rims_second, ...), custom_call_target="tpu_custom_call" | custom-call | tf_op jit(solution)/shard_map/rims/pallas_call | solution.py:654
  18.9 0.7 %lon.4.q = f32[36,8,8,128]{3,2,1,0:T(8,128)S(1)} custom-call(f32[36,8,8,128]{3,2,1,0:T(8,128)S(1)} %get-tuple-element.29.q, f32[10,2,4,8,8,128]{5,4,3,2,1,0:T(8,128)S(1)} %get-tuple-element.30.taps, bf16[2,256,256]{2,1,0:T(8,128)(2,1)S(1)} %get-tuple-element.31.shifts), custom_call_target="tpu_custom_call" | custom-call | tf_op jit(solution)/shard_map/lon/pallas_call | solution.py:663
  19.6 0.5 %lat.3.q = f32[36,8,8,128]{3,2,1,0:T(8,128)S(1)} custom-call(f32[36,8,8,128]{3,2,1,0:T(8,128)S(1)} %lon.4.q, f32[8,8,128]{2,1,0:T(8,128)S(1)} %get-tuple-element.32.ky, f32[20,8,128]{2,1,0:T(8,128)S(1)} %get-tuple-element.22.consts), custom_call_target="tpu_custom_call" | custom-call | tf_op jit(solution)/shard_map/lat/pallas_call | solution.py:667
  20.1 0.6 %turn.3.q = f32[36,8,8,128]{3,2,1,0:T(8,128)S(1)} custom-call(f32[36,8,8,128]{3,2,1,0:T(8,128)S(1)} %lat.3.q, f32[8,8,128]{2,1,0:T(8,128)S(1)} %get-tuple-element.33.tx, f32[8,8,128]{2,1,0:T(8,128)S(1)} %get-tuple-element.34.ty), custom_call_target="tpu_custom_call" | custom-call | tf_op jit(solution)/shard_map/turn/pallas_call | solution.py:668
  20.7 0.7 %lon.5.q = f32[36,8,8,128]{3,2,1,0:T(8,128)S(1)} custom-call(f32[36,8,8,128]{3,2,1,0:T(8,128)S(1)} %turn.3.q, f32[10,2,4,8,8,128]{5,4,3,2,1,0:T(8,128)S(1)} %get-tuple-element.30.taps, bf16[2,256,256]{2,1,0:T(8,128)(2,1)S(1)} %get-tuple-element.31.shifts), custom_call_target="tpu_custom_call" | custom-call | tf_op jit(solution)/shard_map/lon/pallas_call | solution.py:663
  21.4 0.5 %lat.4.q = f32[36,8,8,128]{3,2,1,0:T(8,128)S(1)} custom-call(f32[36,8,8,128]{3,2,1,0:T(8,128)S(1)} %lon.5.q, f32[8,8,128]{2,1,0:T(8,128)S(1)} %get-tuple-element.32.ky, f32[20,8,128]{2,1,0:T(8,128)S(1)} %get-tuple-element.22.consts), custom_call_target="tpu_custom_call" | custom-call | tf_op jit(solution)/shard_map/lat/pallas_call | solution.py:667
  22.0 0.6 %turn.4.q = f32[36,8,8,128]{3,2,1,0:T(8,128)S(1)} custom-call(f32[36,8,8,128]{3,2,1,0:T(8,128)S(1)} %lat.4.q, f32[8,8,128]{2,1,0:T(8,128)S(1)} %get-tuple-element.33.tx, f32[8,8,128]{2,1,0:T(8,128)S(1)} %get-tuple-element.34.ty), custom_call_target="tpu_custom_call" | custom-call | tf_op jit(solution)/shard_map/turn/pallas_call | solution.py:668
  22.6 0.7 %lon.6.q = f32[36,8,8,128]{3,2,1,0:T(8,128)S(1)} custom-call(f32[36,8,8,128]{3,2,1,0:T(8,128)S(1)} %turn.4.q, f32[10,2,4,8,8,128]{5,4,3,2,1,0:T(8,128)S(1)} %get-tuple-element.30.taps, bf16[2,256,256]{2,1,0:T(8,128)(2,1)S(1)} %get-tuple-element.31.shifts), custom_call_target="tpu_custom_call" | custom-call | tf_op jit(solution)/shard_map/lon/pallas_call | solution.py:663
  23.3 0.5 %lat.5.q = f32[36,8,8,128]{3,2,1,0:T(8,128)S(1)} custom-call(f32[36,8,8,128]{3,2,1,0:T(8,128)S(1)} %lon.6.q, f32[8,8,128]{2,1,0:T(8,128)S(1)} %get-tuple-element.32.ky, f32[20,8,128]{2,1,0:T(8,128)S(1)} %get-tuple-element.22.consts), custom_call_target="tpu_custom_call" | custom-call | tf_op jit(solution)/shard_map/lat/pallas_call | solution.py:667
  23.8 0.6 %turn.5.q = f32[36,8,8,128]{3,2,1,0:T(8,128)S(1)} custom-call(f32[36,8,8,128]{3,2,1,0:T(8,128)S(1)} %lat.5.q, f32[8,8,128]{2,1,0:T(8,128)S(1)} %get-tuple-element.33.tx, f32[8,8,128]{2,1,0:T(8,128)S(1)} %get-tuple-element.34.ty), custom_call_target="tpu_custom_call" | custom-call | tf_op jit(solution)/shard_map/turn/pallas_call | solution.py:668
  24.4 0.7 %lon.7.q = f32[36,8,8,128]{3,2,1,0:T(8,128)S(1)} custom-call(f32[36,8,8,128]{3,2,1,0:T(8,128)S(1)} %turn.5.q, f32[10,2,4,8,8,128]{5,4,3,2,1,0:T(8,128)S(1)} %get-tuple-element.30.taps, bf16[2,256,256]{2,1,0:T(8,128)(2,1)S(1)} %get-tuple-element.31.shifts), custom_call_target="tpu_custom_call" | custom-call | tf_op jit(solution)/shard_map/lon/pallas_call | solution.py:663
  25.1 0.7 %lat_sums.1 = (f32[36,8,8,128]{3,2,1,0:T(8,128)S(1)}, f32[8,128]{1,0:T(8,128)S(1)}) custom-call(f32[36,8,8,128]{3,2,1,0:T(8,128)S(1)} %lon.7.q, f32[8,8,128]{2,1,0:T(8,128)S(1)} %get-tuple-element.32.ky, f32[20,8,128]{2,1,0:T(8,128)S(1)} %get-tuple-element.22.consts), custom_call_target="tpu_custom_call" | custom-call | tf_op jit(solution)/shard_map/lat_sums/pallas_call | solution.py:665
  25.9 1.5 %collective-permute-start.6 = (f32[8,128]{1,0:T(8,128)S(1)}, f32[8,128]{1,0:T(8,128)S(1)}, u32[]{:S(2)}, u32[]{:S(2)}) collective-permute-start(f32[8,128]{1,0:T(8,128)S(1)} %get-tuple-element.38.sums), channel_id=1, source_target_pairs={{0,1},{1,0},{2,3},{3,2},{4,5},{5,4},{6,7},{7,6},{8,9},{9,8},{10,11... | collective-permute-start | bytes 12296 | tf_op jit(solution)/shard_map/ppermute | solution.py:589
  27.4 0.1 growth.1.gain
  27.5 0.5 %gather.1.own = f32[2,36,8,128]{3,2,1,0:T(8,128)S(1)} custom-call(f32[36,8,8,128]{3,2,1,0:T(8,128)S(1)} %get-tuple-element.35.q, bf16[2048,256]{1,0:T(8,128)(2,1)S(1)} %get-tuple-element.36.matrix), custom_call_target="tpu_custom_call" | custom-call | tf_op jit(solution)/shard_map/gather/pallas_call | solution.py:670
  28.0 0.2 last_turn.1.early
  28.2 1.3 %collective-permute-done.6.other = f32[8,128]{1,0:T(8,128)S(1)} collective-permute-done((f32[8,128]{1,0:T(8,128)S(1)}, f32[8,128]{1,0:T(8,128)S(1)}, u32[]{:S(2)}, u32[]{:S(2)}) %collective-permute-start.6) | collective-permute-done | bytes 4128 | tf_op jit(solution)/shard_map/ppermute | solution.py:589
  29.5 1.0 %finish.1 = f32[16,16,288]{2,1,0:T(8,128)} custom-call(f32[2,36,8,128]{3,2,1,0:T(8,128)S(1)} %last_turn.1.early, f32[2,8,128]{2,1,0:T(8,128)S(1)} %get-tuple-element.37.local, f32[8,128]{1,0:T(8,128)S(1)} %get-tuple-element.38.sums, f32[8,128]{1,0:T(8,128)S(1)} %collective-permute-done.6.other, f32[20,8,128]{2,1,0:T(8,128)S(1)} %get-tuple-element.22.consts), custom_call_target="tpu_custom_call" | custom-call | tf_op jit(solution)/shard_map/finish/pallas_call | solution.py:675
  (10 shorter events, 0.4 us)
Async XLA Ops:
  1.4 8.2 %collective-permute-start = (f32[31,8,128]{2,1,0:T(8,128)S(1)}, f32[31,8,128]{2,1,0:T(8,128)S(1)}, u32[]{:S(2)}, u32[]{:S(2)}) collective-permute-start(f32[31,8,128]{2,1,0:T(8,128)S(1)} %column_far.1), channel_id=1, source_target_pairs={{8,16},{16,8},{24,0},{0,24},{9,17},{17,9},{25,1},{1,25},{10,18},{1... | collective-permute-start | bytes 380936 | tf_op jit(solution)/shard_map/ppermute | solution.py:589
  5.2 6.1 %collective-permute-start.1 = (f32[31,8,128]{2,1,0:T(8,128)S(1)}, f32[31,8,128]{2,1,0:T(8,128)S(1)}, u32[]{:S(2)}, u32[]{:S(2)}) collective-permute-start(f32[31,8,128]{2,1,0:T(8,128)S(1)} %column_near.1), channel_id=1, source_target_pairs={{0,8},{8,0},{16,24},{24,16},{1,9},{9,1},{17,25},{25,17},{2,10},{10... | collective-permute-start | bytes 380936 | tf_op jit(solution)/shard_map/ppermute | solution.py:589
  5.4 8.0 %collective-permute-start.2 = (f32[31,8,128]{2,1,0:T(8,128)S(1)}, f32[31,8,128]{2,1,0:T(8,128)S(1)}, u32[]{:S(2)}, u32[]{:S(2)}) collective-permute-start(f32[31,8,128]{2,1,0:T(8,128)S(1)} %edge_far.1), channel_id=1, source_target_pairs={{2,4},{4,2},{3,5},{5,3},{10,12},{12,10},{11,13},{13,11},{18,20},{2... | collective-permute-start | bytes 380936 | tf_op jit(solution)/shard_map/ppermute | solution.py:589
  7.4 6.0 %collective-permute-start.3 = (f32[31,8,128]{2,1,0:T(8,128)S(1)}, f32[31,8,128]{2,1,0:T(8,128)S(1)}, u32[]{:S(2)}, u32[]{:S(2)}) collective-permute-start(f32[31,8,128]{2,1,0:T(8,128)S(1)} %edge_near.1), channel_id=1, source_target_pairs={{0,2},{2,0},{4,6},{6,4},{1,3},{3,1},{5,7},{7,5},{8,10},{10,8},{12,... | collective-permute-start | bytes 380936 | tf_op jit(solution)/shard_map/ppermute | solution.py:589
  11.5 6.5 %collective-permute-start.4 = (f32[37,8,128]{2,1,0:T(8,128)S(1)}, f32[37,8,128]{2,1,0:T(8,128)S(1)}, u32[]{:S(2)}, u32[]{:S(2)}) collective-permute-start(f32[37,8,128]{2,1,0:T(8,128)S(1)} %rim_far.1), channel_id=1, source_target_pairs={{2,4},{4,2},{3,5},{5,3},{10,12},{12,10},{11,13},{13,11},{18,20},{2... | collective-permute-start | bytes 454664 | tf_op jit(solution)/shard_map/ppermute | solution.py:589
  13.5 4.5 %collective-permute-start.5 = (f32[37,8,128]{2,1,0:T(8,128)S(1)}, f32[37,8,128]{2,1,0:T(8,128)S(1)}, u32[]{:S(2)}, u32[]{:S(2)}) collective-permute-start(f32[37,8,128]{2,1,0:T(8,128)S(1)} %rim_near.1), channel_id=1, source_target_pairs={{0,2},{2,0},{4,6},{6,4},{1,3},{3,1},{5,7},{7,5},{8,10},{10,8},{12,... | collective-permute-start | bytes 454664 | tf_op jit(solution)/shard_map/ppermute | solution.py:589
  25.9 3.6 %collective-permute-start.6 = (f32[8,128]{1,0:T(8,128)S(1)}, f32[8,128]{1,0:T(8,128)S(1)}, u32[]{:S(2)}, u32[]{:S(2)}) collective-permute-start(f32[8,128]{1,0:T(8,128)S(1)} %get-tuple-element.38.sums), channel_id=1, source_target_pairs={{0,1},{1,0},{2,3},{3,2},{4,5},{5,4},{6,7},{7,6},{8,9},{9,8},{10,11... | collective-permute-start | bytes 12296 | tf_op jit(solution)/shard_map/ppermute | solution.py:589

commit v12 on v11

--- a/solution.py
+++ b/solution.py
@@ -261,7 +261,7 @@
     place_field(wide, wdir[...], local, WDIR)
 
 
-def unpack_kernel(cols_second, cols_first, consts, west, east):
+def unpack_kernel(cols_first, cols_second, consts, west, east):
     del consts
     even = is_even("lon")
     place = lanes() % 8
@@ -316,7 +316,7 @@
     return value * point[SEA : SEA + 1]
 
 
-def rims_kernel(partial, rims_second, rims_first, consts, matrix, q, taps, ky, tx, ty, lhs):
+def rims_kernel(partial, rims_second, rims_first, consts, matrix, q, kx, ky, tx, ty, lhs):
     even_lat = is_even("lat")
     south = jnp.where(even_lat, rims_second[...], rims_first[...])
     north = jnp.where(even_lat, rims_first[...], rims_second[...])
@@ -341,19 +341,8 @@
         tx[t] = turning * point[SLOPE_X : SLOPE_X + 1]
         ty[t] = turning * point[SLOPE_Y : SLOPE_Y + 1]
         stretch = consts[STRETCH, t : t + 1, :]
-        right = 0.5 * (pace + roll(pace, -1)) * stretch
-        left = 0.5 * (pace + roll(pace, 1)) * stretch
-        for base in range(10):
-            a1, b1, c1 = weights(COS[base] * right)
-            a0, b0, c0 = weights(COS[base] * left)
-            taps[base, 0, 0, t] = 1.0 - a1 + b0
-            taps[base, 0, 1, t] = -b1
-            taps[base, 0, 2, t] = a0 - c1
-            taps[base, 0, 3, t] = c0
-            taps[base, 1, 0, t] = 1.0 + b1 - a0
-            taps[base, 1, 1, t] = a1 - c0
-            taps[base, 1, 2, t] = -b0
-            taps[base, 1, 3, t] = c1
+        kx[0, t] = 0.5 * (pace + roll(pace, -1)) * stretch
+        kx[1, t] = 0.5 * (pace + roll(pace, 1)) * stretch
     for t in range(8):
         ahead = speed[t + 1] if t < 7 else roll(speed[0], -32)
         ky[t] = 0.5 * (speed[t] + ahead)
@@ -377,26 +366,47 @@
 BACK_TAPS = (-1, 2)
 
 
+def lon_dirs(sign, base):
+    if base == 0:
+        return [[0], [18]][sign]
+    if base == 9:
+        return [[27], [9]][sign]
+    return [[base, 36 - base], [18 - base, 18 + base]][sign]
+
+
+def lon_pair(q, shifts, out, sign, base, tap_of):
+    dirs = lon_dirs(sign, base)
+    x = jnp.concatenate([q[d].reshape(64, 128) for d in dirs], axis=0)
+    lhs = jnp.concatenate(split(x), axis=1)
+    moved = jnp.dot(lhs, shifts[sign], preferred_element_type=f32)
+    for t in range(8):
+        tap = tap_of(t)
+        for i, d in enumerate(dirs):
+            cell = q[d, t]
+            near = moved[64 * i + 8 * t : 64 * i + 8 * t + 8]
+            out[d, t] = (tap[0] * cell + tap[1] * roll(cell, -1)) + (
+                tap[2] * near[:, :128] + tap[3] * near[:, 128:]
+            )
+
+
+def first_lon_kernel(q, kx, shifts, out, taps):
+    for base in range(10):
+        for t in range(8):
+            a1, b1, c1 = weights(COS[base] * kx[0, t])
+            a0, b0, c0 = weights(COS[base] * kx[1, t])
+            for sign, tap in enumerate(
+                ((1.0 - a1 + b0, -b1, a0 - c1, c0), (1.0 + b1 - a0, a1 - c0, -b0, c1))
+            ):
+                for i in range(4):
+                    taps[base, sign, i, t] = tap[i]
+        for sign in range(2):
+            lon_pair(q, shifts, out, sign, base, lambda t: [taps[base, sign, i, t] for i in range(4)])
+
+
 def lon_kernel(q, taps, shifts, out):
     for sign in range(2):
         for base in range(10):
-            if base == 0:
-                dirs = [[0], [18]][sign]
-            elif base == 9:
-                dirs = [[27], [9]][sign]
-            else:
-                dirs = [[base, 36 - base], [18 - base, 18 + base]][sign]
-            x = jnp.concatenate([q[d].reshape(64, 128) for d in dirs], axis=0)
-            lhs = jnp.concatenate(split(x), axis=1)
-            moved = jnp.dot(lhs, shifts[sign], preferred_element_type=f32)
-            for t in range(8):
-                tap = [taps[base, sign, i, t] for i in range(4)]
-                for i, d in enumerate(dirs):
-                    cell = q[d, t]
-                    near = moved[64 * i + 8 * t : 64 * i + 8 * t + 8]
-                    out[d, t] = (tap[0] * cell + tap[1] * roll(cell, -1)) + (
-                        tap[2] * near[:, :128] + tap[3] * near[:, 128:]
-                    )
+            lon_pair(q, shifts, out, sign, base, lambda t: [taps[base, sign, i, t] for i in range(4)])
 
 
 def lat_kernel(q, ky, consts, out, sums=None):
@@ -464,11 +474,13 @@
 def turn_around(get, put, x, y):
     def factors(d):
         k = SIN_FACE[d] * x - COS_FACE[d] * y
-        half, third = 0.5 * k, (1.0 / 3.0) * k
-        return k, 0.5 - half, 1.0 / 3.0 + third, 0.5 + half, 1.0 / 3.0 - third
+        return (k, *halves(k))
+
+    def opposite(cell, diff, curve, k, u, w):
+        return k * (cell + w * (1.5 * diff - u * curve))
 
     half_turn = NDIR // 2
-    k, u, w, u_back, w_back = factors(half_turn - 1)
+    k, u, w = factors(half_turn - 1)
     state = []
     ends = []
     for at in (0, half_turn):
@@ -479,7 +491,7 @@
         curve = diff - diff1
         curve1 = diff1 - (before - last)
         if at == 0:
-            f = flux(before, diff1, jnp.where(k >= 0.0, curve, curve1), k, u_back, w_back)
+            f = opposite(before, diff1, jnp.where(k >= 0.0, curve, curve1), k, u, w)
         else:
             f = flux(before, diff1, jnp.where(k >= 0.0, curve1, curve), k, u, w)
         state.append([cell, ahead, diff, curve])
@@ -487,7 +499,7 @@
     f_first, f_second = -ends[0], -ends[1]
     for d in range(half_turn):
         if d < half_turn - 1:
-            k, u, w, u_back, w_back = factors(d)
+            k, u, w = factors(d)
             positive = k >= 0.0
         for at in (0, half_turn):
             cell, ahead, diff, curve = state[at // half_turn]
@@ -503,7 +515,7 @@
                 f_first = f
             else:
                 if d < half_turn - 1:
-                    f = flux(cell, diff, jnp.where(positive, curve_ahead, curve), k, u_back, w_back)
+                    f = opposite(cell, diff, jnp.where(positive, curve_ahead, curve), k, u, w)
                 else:
                     f = ends[0]
                 put(at + d, cell + f - f_second)
@@ -616,10 +628,10 @@
         name="pack",
         space=pltpu.HBM,
     )(*[pltpu.with_memory_space_constraint(x, pltpu.HBM) for x in inputs])
+    (to_first,) = call(functools.partial(column_kernel, False), 1, [sent], name="column_near")(own)
+    cols_first = swap(to_first, "lon", 0, True)
     (to_second,) = call(functools.partial(column_kernel, True), 1, [sent], name="column_far")(own)
     cols_second = swap(to_second, "lon", 1, True)
-    (to_first,) = call(functools.partial(column_kernel, False), 1, [sent], name="column_near")(own)
-    cols_first = swap(to_first, "lon", 0, True)
     (edge_second,) = call(functools.partial(edge_kernel, True), 1, [sent], name="edge_far")(own)
     rows_second = swap(edge_second, "lat", 1)
     (edge_first,) = call(functools.partial(edge_kernel, False), 1, [sent], name="edge_near")(own)
@@ -636,11 +648,11 @@
         dtype=[bf16] * 4 + [f32] * 2,
     )(*[pltpu.with_memory_space_constraint(x, pltpu.HBM) for x in inputs])
     (gain,) = call(growth_kernel, 3, [(NDIR, 2) + tile], name="growth")(own, local, consts)
-    west, east = call(unpack_kernel, 3, [slabs] * 2, name="unpack")(cols_second, cols_first, consts)
+    west, east = call(unpack_kernel, 3, [slabs] * 2, name="unpack")(cols_first, cols_second, consts)
     (rim_second,) = call(functools.partial(rim_kernel, True), 2, [slabs], name="rim_far")(west, east)
     rims_second = swap(rim_second, "lat", 1)
-    (rim_first,) = call(functools.partial(rim_kernel, False), 4, [slabs], name="rim_near")(
-        west, east, rows_second, rows_first
+    (rim_first,) = call(functools.partial(rim_kernel, False), 5, [slabs], name="rim_near")(
+        west, east, rows_second, rows_first, rim_second
     )
     rims_first = swap(rim_first, "lat", 0)
     south, north = call(unpack_rows_kernel, 2, [slabs] * 2, name="unpack_rows")(rows_second, rows_first)
@@ -651,16 +663,19 @@
         [pltpu.VMEM((8 * SLABS + 8, 1536), bf16)],
         name="place",
     )(own, west, east, south, north, place)
-    q, taps, ky, tx, ty = call(
+    q, kx, ky, tx, ty = call(
         rims_kernel,
         5,
-        [(NDIR,) + block, (10, 2, 4) + block] + [block] * 3,
+        [(NDIR,) + block, (2,) + block] + [block] * 3,
         [pltpu.VMEM((8 * NDIR, 512), bf16)],
         name="rims",
     )(partial, rims_second, rims_first, consts, rims)
     cells = [(NDIR,) + block]
     for substep in range(ITERS):
-        (q,) = call(lon_kernel, 3, cells, name="lon")(q, taps, shifts)
+        if substep == 0:
+            q, taps = call(first_lon_kernel, 3, cells + [(10, 2, 4) + block], name="first_lon")(q, kx, shifts)
+        else:
+            (q,) = call(lon_kernel, 3, cells, name="lon")(q, taps, shifts)
         if substep == ITERS - 1:
             q, sums = call(lat_kernel, 3, cells + [tile], name="lat_sums")(q, ky, consts)
         else:

time: 30.8 us -> 30.8 us (level)
  starting transfers between devices: 9.24 us -> 9.69 us
    pallas_call x4 -> x3, Pallas kernels: 2.86 us -> 2.09 us  [per_device(): q, = call(lon_kernel, 3, cells, name='lon')(q, taps, shifts)]
    pallas_call x2 -> x3, Pallas kernels: 0.9 us -> 1.66 us  [the longest x1 1.13 us: per_device(): call(first_lon_kernel, 3, cells + [(10, 2, 4) + block], name='first_lon')]
    ppermute x7, starting transfers between devices: 9.24 us -> 9.69 us  [swap(): return lax.ppermute(array, axis, pairs)]
  transfers between devices with their start and end apart: 7 -> 7, of which waited for: 4 -> 3; matrix products, arithmetic and copies ran while one was open for 0% -> 0% of each run, Pallas kernels for 12% -> 12%
where the time goes in v12:
time: 30.8 us; the launch traced here: 30.5 us
  Pallas kernels  13.7 us (44%)
  starting transfers between devices  9.69 us (31%)
  waiting for transfers between devices  6.98 us (23%)
    ppermute x7, starting transfers between devices, swap(): return lax.ppermute(array, axis, pairs)  9.69 us
    ppermute x7, waiting for transfers between devices, swap(): return lax.ppermute(array, axis, pairs)  6.98 us
    pallas_call x3, Pallas kernels, per_device(): q, = call(lon_kernel, 3, cells, name='lon')(q, taps, shifts)  2.09 us
    pallas_call x3, Pallas kernels, per_device(): q, = call(turn_kernel, 3, cells, name='turn')(q, tx, ty)  1.67 us
    pallas_call x3, Pallas kernels, per_device(): q, = call(lat_kernel, 3, cells, name='lat')(q, ky, consts)  1.64 us
    pallas_call x1, Pallas kernels, per_device(): call(pack_kernel, 4, [(2,) + slabs], [pltpu.VMEM(x.shape, x.dtype) for x...  1.24 us
    pallas_call x1, Pallas kernels, per_device(): call(place_kernel, 6, [(SLABS,) + block], [pltpu.VMEM((8 * SLABS + 8, 153...  1.16 us
    pallas_call x1, Pallas kernels, per_device(): call(first_lon_kernel, 3, cells + [(10, 2, 4) + block], name='first_lon')  1.13 us
  transfers between devices with their start and end apart: 7, of which 3 were waited for; matrix products, arithmetic and copies ran while one was open for 0% of the time, Pallas kernels for 12%

profile of v12, /device:TPU:2, one launch (start us, length us, event | category | flops | bytes accessed | tf_op | source)
XLA Modules:
  0.0 30.5 jit_solution(3493030976502360414)
XLA Ops:
  0.0 1.2 %pack.1.own = f32[2,37,8,128]{3,2,1,0:T(8,128)S(1)} custom-call(f32[16,16,288]{2,1,0:T(8,128)} %refs_0_.2, s32[16,16]{1,0:T(8,128)} %refs_1_.2, s32[16,16]{1,0:T(8,128)} %refs_2_.2, f32[2,16,16]{2,1,0:T(8,128)} %refs_3_.2), custom_call_target="tpu_custom_call" | custom-call | tf_op jit(solution)/shard_map/pack/pallas_call | solution.py:621
  1.3 0.2 column_near.1
  1.4 1.6 %collective-permute-start = (f32[31,8,128]{2,1,0:T(8,128)S(1)}, f32[31,8,128]{2,1,0:T(8,128)S(1)}, u32[]{:S(2)}, u32[]{:S(2)}) collective-permute-start(f32[31,8,128]{2,1,0:T(8,128)S(1)} %column_near.1), channel_id=1, source_target_pairs={{0,8},{8,0},{16,24},{24,16},{1,9},{9,1},{17,25},{25,17},{2,10},{10... | collective-permute-start | bytes 380936 | tf_op jit(solution)/shard_map/ppermute | solution.py:601
  3.1 0.1 column_far.1
  3.2 2.5 %collective-permute-start.1 = (f32[31,8,128]{2,1,0:T(8,128)S(1)}, f32[31,8,128]{2,1,0:T(8,128)S(1)}, u32[]{:S(2)}, u32[]{:S(2)}) collective-permute-start(f32[31,8,128]{2,1,0:T(8,128)S(1)} %column_far.1), channel_id=1, source_target_pairs={{8,16},{16,8},{24,0},{0,24},{9,17},{17,9},{25,1},{1,25},{10,18},{1... | collective-permute-start | bytes 380936 | tf_op jit(solution)/shard_map/ppermute | solution.py:601
  5.8 1.9 %collective-permute-start.2 = (f32[31,8,128]{2,1,0:T(8,128)S(1)}, f32[31,8,128]{2,1,0:T(8,128)S(1)}, u32[]{:S(2)}, u32[]{:S(2)}) collective-permute-start(f32[31,8,128]{2,1,0:T(8,128)S(1)} %edge_far.1), channel_id=1, source_target_pairs={{2,4},{4,2},{3,5},{5,3},{10,12},{12,10},{11,13},{13,11},{18,20},{2... | collective-permute-start | bytes 380936 | tf_op jit(solution)/shard_map/ppermute | solution.py:601
  7.8 0.1 edge_near.1
  7.9 1.0 %tables.1 = (bf16[1536,1024]{1,0:T(8,128)(2,1)S(1)}, bf16[512,1024]{1,0:T(8,128)(2,1)S(1)}, bf16[2,256,256]{2,1,0:T(8,128)(2,1)S(1)}, bf16[2048,256]{1,0:T(8,128...) custom-call(f32[8,16]{1,0:T(8,128)} %refs_0_.3, f32[8,16]{1,0:T(8,128)} %refs_1_.3, f32[16]{0:T(128)} %refs_2_.3, ...), custom_call_target="tpu_custom_call" | custom-call | tf_op jit(solution)/shard_map/tables/pallas_call | solution.py:640
  8.9 2.6 %collective-permute-done.1.cols_second = f32[31,8,128]{2,1,0:T(8,128)S(1)} collective-permute-done((f32[31,8,128]{2,1,0:T(8,128)S(1)}, f32[31,8,128]{2,1,0:T(8,128)S(1)}, u32[]{:S(2)}, u32[]{:S(2)}) %collective-permute-start.1) | collective-permute-done | bytes 127008 | tf_op jit(solution)/shard_map/ppermute | solution.py:601
  11.5 0.1 unpack.1
  11.6 1.9 %collective-permute-start.4 = (f32[37,8,128]{2,1,0:T(8,128)S(1)}, f32[37,8,128]{2,1,0:T(8,128)S(1)}, u32[]{:S(2)}, u32[]{:S(2)}) collective-permute-start(f32[37,8,128]{2,1,0:T(8,128)S(1)} %rim_far.1.refs_2_), channel_id=1, source_target_pairs={{2,4},{4,2},{3,5},{5,3},{10,12},{12,10},{11,13},{13,11},{18,20},{2... | collective-permute-start | bytes 454664 | tf_op jit(solution)/shard_map/ppermute | solution.py:601
  13.7 0.1 unpack_rows.1
  13.8 1.2 %place.1.partial = f32[37,8,8,128]{3,2,1,0:T(8,128)S(1)} custom-call(f32[2,37,8,128]{3,2,1,0:T(8,128)S(1)} %pack.1.own, f32[37,8,128]{2,1,0:T(8,128)S(1)} %get-tuple-element.25.west, f32[37,8,128]{2,1,0:T(8,128)S(1)} %get-tuple-element.26.east, f32[37,8,128]{2,1,0:T(8,128)S(1)} %get-tuple-element.27.south, f32[37,8,128]{2,1,0:T(8,128)S(1)} %get-tuple-element.28.north, ...), custom_call_target="tpu_custom_call" | custom-call | tf_op jit(solution)/shard_map/place/pallas_call | solution.py:659
  15.0 3.2 %collective-permute-done.4.rims_second = f32[37,8,128]{2,1,0:T(8,128)S(1)} collective-permute-done((f32[37,8,128]{2,1,0:T(8,128)S(1)}, f32[37,8,128]{2,1,0:T(8,128)S(1)}, u32[]{:S(2)}, u32[]{:S(2)}) %collective-permute-start.4) | collective-permute-done | bytes 151584 | tf_op jit(solution)/shard_map/ppermute | solution.py:601
  18.1 0.5 %rims.1 = (f32[36,8,8,128]{3,2,1,0:T(8,128)S(1)}, f32[2,8,8,128]{3,2,1,0:T(8,128)S(1)}, f32[8,8,128]{2,1,0:T(8,128)S(1)}, f32[8,8,128]{2,1,0:T(8,128)S(1)}, f32[8,8,128]{2,1,0:T(8,128)S(1)}) custom-call(f32[37,8,8,128]{3,2,1,0:T(8,128)S(1)} %place.1.partial, f32[37,8,128]{2,1,0:T(8,128)S(1)} %collective-permute-done.4.rims_second, ...), custom_call_target="tpu_custom_call" | custom-call | tf_op jit(solution)/shard_map/rims/pallas_call | solution.py:666
  18.7 1.1 %first_lon.1 = (f32[36,8,8,128]{3,2,1,0:T(8,128)S(1)}, f32[10,2,4,8,8,128]{5,4,3,2,1,0:T(8,128)S(1)}) custom-call(f32[36,8,8,128]{3,2,1,0:T(8,128)S(1)} %get-tuple-element.31.q, f32[2,8,8,128]{3,2,1,0:T(8,128)S(1)} %get-tuple-element.32.kx, bf16[2,256,256]{2,1,0:T(8,128)(2,1)S(1)} %get-tuple-element.33.shifts), custom_call_target="tpu_custom_call" | custom-call | tf_op jit(solution)/shard_map/first_lon/pallas_call | solution.py:676
  19.8 0.5 %lat.3.q = f32[36,8,8,128]{3,2,1,0:T(8,128)S(1)} custom-call(f32[36,8,8,128]{3,2,1,0:T(8,128)S(1)} %get-tuple-element.34.q, f32[8,8,128]{2,1,0:T(8,128)S(1)} %get-tuple-element.35.ky, f32[20,8,128]{2,1,0:T(8,128)S(1)} %get-tuple-element.24.consts), custom_call_target="tpu_custom_call" | custom-call | tf_op jit(solution)/shard_map/lat/pallas_call | solution.py:682
  20.3 0.6 %turn.3.q = f32[36,8,8,128]{3,2,1,0:T(8,128)S(1)} custom-call(f32[36,8,8,128]{3,2,1,0:T(8,128)S(1)} %lat.3.q, f32[8,8,128]{2,1,0:T(8,128)S(1)} %get-tuple-element.36.tx, f32[8,8,128]{2,1,0:T(8,128)S(1)} %get-tuple-element.37.ty), custom_call_target="tpu_custom_call" | custom-call | tf_op jit(solution)/shard_map/turn/pallas_call | solution.py:683
  20.9 0.7 %lon.3.q = f32[36,8,8,128]{3,2,1,0:T(8,128)S(1)} custom-call(f32[36,8,8,128]{3,2,1,0:T(8,128)S(1)} %turn.3.q, f32[10,2,4,8,8,128]{5,4,3,2,1,0:T(8,128)S(1)} %get-tuple-element.38.taps, bf16[2,256,256]{2,1,0:T(8,128)(2,1)S(1)} %get-tuple-element.33.shifts), custom_call_target="tpu_custom_call" | custom-call | tf_op jit(solution)/shard_map/lon/pallas_call | solution.py:678
  21.6 0.5 %lat.4.q = f32[36,8,8,128]{3,2,1,0:T(8,128)S(1)} custom-call(f32[36,8,8,128]{3,2,1,0:T(8,128)S(1)} %lon.3.q, f32[8,8,128]{2,1,0:T(8,128)S(1)} %get-tuple-element.35.ky, f32[20,8,128]{2,1,0:T(8,128)S(1)} %get-tuple-element.24.consts), custom_call_target="tpu_custom_call" | custom-call | tf_op jit(solution)/shard_map/lat/pallas_call | solution.py:682
  22.2 0.6 %turn.4.q = f32[36,8,8,128]{3,2,1,0:T(8,128)S(1)} custom-call(f32[36,8,8,128]{3,2,1,0:T(8,128)S(1)} %lat.4.q, f32[8,8,128]{2,1,0:T(8,128)S(1)} %get-tuple-element.36.tx, f32[8,8,128]{2,1,0:T(8,128)S(1)} %get-tuple-element.37.ty), custom_call_target="tpu_custom_call" | custom-call | tf_op jit(solution)/shard_map/turn/pallas_call | solution.py:683
  22.7 0.7 %lon.4.q = f32[36,8,8,128]{3,2,1,0:T(8,128)S(1)} custom-call(f32[36,8,8,128]{3,2,1,0:T(8,128)S(1)} %turn.4.q, f32[10,2,4,8,8,128]{5,4,3,2,1,0:T(8,128)S(1)} %get-tuple-element.38.taps, bf16[2,256,256]{2,1,0:T(8,128)(2,1)S(1)} %get-tuple-element.33.shifts), custom_call_target="tpu_custom_call" | custom-call | tf_op jit(solution)/shard_map/lon/pallas_call | solution.py:678
  23.4 0.5 %lat.5.q = f32[36,8,8,128]{3,2,1,0:T(8,128)S(1)} custom-call(f32[36,8,8,128]{3,2,1,0:T(8,128)S(1)} %lon.4.q, f32[8,8,128]{2,1,0:T(8,128)S(1)} %get-tuple-element.35.ky, f32[20,8,128]{2,1,0:T(8,128)S(1)} %get-tuple-element.24.consts), custom_call_target="tpu_custom_call" | custom-call | tf_op jit(solution)/shard_map/lat/pallas_call | solution.py:682
  24.0 0.6 %turn.5.q = f32[36,8,8,128]{3,2,1,0:T(8,128)S(1)} custom-call(f32[36,8,8,128]{3,2,1,0:T(8,128)S(1)} %lat.5.q, f32[8,8,128]{2,1,0:T(8,128)S(1)} %get-tuple-element.36.tx, f32[8,8,128]{2,1,0:T(8,128)S(1)} %get-tuple-element.37.ty), custom_call_target="tpu_custom_call" | custom-call | tf_op jit(solution)/shard_map/turn/pallas_call | solution.py:683
  24.5 0.7 %lon.5.q = f32[36,8,8,128]{3,2,1,0:T(8,128)S(1)} custom-call(f32[36,8,8,128]{3,2,1,0:T(8,128)S(1)} %turn.5.q, f32[10,2,4,8,8,128]{5,4,3,2,1,0:T(8,128)S(1)} %get-tuple-element.38.taps, bf16[2,256,256]{2,1,0:T(8,128)(2,1)S(1)} %get-tuple-element.33.shifts), custom_call_target="tpu_custom_call" | custom-call | tf_op jit(solution)/shard_map/lon/pallas_call | solution.py:678
  25.2 0.7 %lat_sums.1 = (f32[36,8,8,128]{3,2,1,0:T(8,128)S(1)}, f32[8,128]{1,0:T(8,128)S(1)}) custom-call(f32[36,8,8,128]{3,2,1,0:T(8,128)S(1)} %lon.5.q, f32[8,8,128]{2,1,0:T(8,128)S(1)} %get-tuple-element.35.ky, f32[20,8,128]{2,1,0:T(8,128)S(1)} %get-tuple-element.24.consts), custom_call_target="tpu_custom_call" | custom-call | tf_op jit(solution)/shard_map/lat_sums/pallas_call | solution.py:680
  26.0 1.5 %collective-permute-start.6 = (f32[8,128]{1,0:T(8,128)S(1)}, f32[8,128]{1,0:T(8,128)S(1)}, u32[]{:S(2)}, u32[]{:S(2)}) collective-permute-start(f32[8,128]{1,0:T(8,128)S(1)} %get-tuple-element.42.sums), channel_id=1, source_target_pairs={{0,1},{1,0},{2,3},{3,2},{4,5},{5,4},{6,7},{7,6},{8,9},{9,8},{10,11... | collective-permute-start | bytes 12296 | tf_op jit(solution)/shard_map/ppermute | solution.py:601
  27.5 0.1 growth.1.gain
  27.6 0.5 %gather.1.own = f32[2,36,8,128]{3,2,1,0:T(8,128)S(1)} custom-call(f32[36,8,8,128]{3,2,1,0:T(8,128)S(1)} %get-tuple-element.39.q, bf16[2048,256]{1,0:T(8,128)(2,1)S(1)} %get-tuple-element.40.matrix), custom_call_target="tpu_custom_call" | custom-call | tf_op jit(solution)/shard_map/gather/pallas_call | solution.py:685
  28.2 0.2 last_turn.1.early
  28.3 1.2 %collective-permute-done.6.other = f32[8,128]{1,0:T(8,128)S(1)} collective-permute-done((f32[8,128]{1,0:T(8,128)S(1)}, f32[8,128]{1,0:T(8,128)S(1)}, u32[]{:S(2)}, u32[]{:S(2)}) %collective-permute-start.6) | collective-permute-done | bytes 4128 | tf_op jit(solution)/shard_map/ppermute | solution.py:601
  29.6 1.0 %finish.1 = f32[16,16,288]{2,1,0:T(8,128)} custom-call(f32[2,36,8,128]{3,2,1,0:T(8,128)S(1)} %last_turn.1.early, f32[2,8,128]{2,1,0:T(8,128)S(1)} %get-tuple-element.41.local, f32[8,128]{1,0:T(8,128)S(1)} %get-tuple-element.42.sums, f32[8,128]{1,0:T(8,128)S(1)} %collective-permute-done.6.other, f32[20,8,128]{2,1,0:T(8,128)S(1)} %get-tuple-element.24.consts), custom_call_target="tpu_custom_call" | custom-call | tf_op jit(solution)/shard_map/finish/pallas_call | solution.py:690
  (10 shorter events, 0.3 us)
Async XLA Ops:
  1.4 7.5 %collective-permute-start = (f32[31,8,128]{2,1,0:T(8,128)S(1)}, f32[31,8,128]{2,1,0:T(8,128)S(1)}, u32[]{:S(2)}, u32[]{:S(2)}) collective-permute-start(f32[31,8,128]{2,1,0:T(8,128)S(1)} %column_near.1), channel_id=1, source_target_pairs={{0,8},{8,0},{16,24},{24,16},{1,9},{9,1},{17,25},{25,17},{2,10},{10... | collective-permute-start | bytes 380936 | tf_op jit(solution)/shard_map/ppermute | solution.py:601
  3.2 8.3 %collective-permute-start.1 = (f32[31,8,128]{2,1,0:T(8,128)S(1)}, f32[31,8,128]{2,1,0:T(8,128)S(1)}, u32[]{:S(2)}, u32[]{:S(2)}) collective-permute-start(f32[31,8,128]{2,1,0:T(8,128)S(1)} %column_far.1), channel_id=1, source_target_pairs={{8,16},{16,8},{24,0},{0,24},{9,17},{17,9},{25,1},{1,25},{10,18},{1... | collective-permute-start | bytes 380936 | tf_op jit(solution)/shard_map/ppermute | solution.py:601
  5.8 7.7 %collective-permute-start.2 = (f32[31,8,128]{2,1,0:T(8,128)S(1)}, f32[31,8,128]{2,1,0:T(8,128)S(1)}, u32[]{:S(2)}, u32[]{:S(2)}) collective-permute-start(f32[31,8,128]{2,1,0:T(8,128)S(1)} %edge_far.1), channel_id=1, source_target_pairs={{2,4},{4,2},{3,5},{5,3},{10,12},{12,10},{11,13},{13,11},{18,20},{2... | collective-permute-start | bytes 380936 | tf_op jit(solution)/shard_map/ppermute | solution.py:601
  7.9 5.7 %collective-permute-start.3 = (f32[31,8,128]{2,1,0:T(8,128)S(1)}, f32[31,8,128]{2,1,0:T(8,128)S(1)}, u32[]{:S(2)}, u32[]{:S(2)}) collective-permute-start(f32[31,8,128]{2,1,0:T(8,128)S(1)} %edge_near.1), channel_id=1, source_target_pairs={{0,2},{2,0},{4,6},{6,4},{1,3},{3,1},{5,7},{7,5},{8,10},{10,8},{12,... | collective-permute-start | bytes 380936 | tf_op jit(solution)/shard_map/ppermute | solution.py:601
  11.6 6.5 %collective-permute-start.4 = (f32[37,8,128]{2,1,0:T(8,128)S(1)}, f32[37,8,128]{2,1,0:T(8,128)S(1)}, u32[]{:S(2)}, u32[]{:S(2)}) collective-permute-start(f32[37,8,128]{2,1,0:T(8,128)S(1)} %rim_far.1.refs_2_), channel_id=1, source_target_pairs={{2,4},{4,2},{3,5},{5,3},{10,12},{12,10},{11,13},{13,11},{18,20},{2... | collective-permute-start | bytes 454664 | tf_op jit(solution)/shard_map/ppermute | solution.py:601
  13.6 4.5 %collective-permute-start.5 = (f32[37,8,128]{2,1,0:T(8,128)S(1)}, f32[37,8,128]{2,1,0:T(8,128)S(1)}, u32[]{:S(2)}, u32[]{:S(2)}) collective-permute-start(f32[37,8,128]{2,1,0:T(8,128)S(1)} %rim_near.1), channel_id=1, source_target_pairs={{0,2},{2,0},{4,6},{6,4},{1,3},{3,1},{5,7},{7,5},{8,10},{10,8},{12,... | collective-permute-start | bytes 454664 | tf_op jit(solution)/shard_map/ppermute | solution.py:601
  26.0 3.6 %collective-permute-start.6 = (f32[8,128]{1,0:T(8,128)S(1)}, f32[8,128]{1,0:T(8,128)S(1)}, u32[]{:S(2)}, u32[]{:S(2)}) collective-permute-start(f32[8,128]{1,0:T(8,128)S(1)} %get-tuple-element.42.sums), channel_id=1, source_target_pairs={{0,1},{1,0},{2,3},{3,2},{4,5},{5,4},{6,7},{7,6},{8,9},{9,8},{10,11... | collective-permute-start | bytes 12296 | tf_op jit(solution)/shard_map/ppermute | solution.py:601

commit v13 on v12

--- a/solution.py
+++ b/solution.py
@@ -277,10 +277,16 @@
 
 
 def rim_kernel(second, west, east, *refs):
-    rim = refs[-1]
-    west_low = (lanes() % 16 < 8) == (is_even("lat") != second)
-    for slab in range(SLABS):
-        rim[slab] = jnp.where(west_low, west[slab], east[slab])
+    to_north = is_even("lat") != second
+    west_low = (lanes() % 16 < 8) == to_north
+
+    def get(south, north):
+        slab = south if south == north else jnp.where(to_north, north, south)
+        return jnp.where(west_low, west[slab], east[slab])
+
+    write_message(refs[-1], get, ~to_north, TO_SOUTH, TO_NORTH, lanes() // 16, 16)
+    if second:
+        refs[-1][SENT] = jnp.zeros((8, 128), f32)
 
 
 def split(x):
@@ -316,10 +322,11 @@
     return value * point[SEA : SEA + 1]
 
 
-def rims_kernel(partial, rims_second, rims_first, consts, matrix, q, kx, ky, tx, ty, lhs):
+def rims_kernel(partial, rims_second, rims_first, consts, matrix, q, kx, ky, tx, ty, lhs, south, north):
     even_lat = is_even("lat")
-    south = jnp.where(even_lat, rims_second[...], rims_first[...])
-    north = jnp.where(even_lat, rims_first[...], rims_second[...])
+    place = lanes() // 16
+    read_message(lambda i: jnp.where(even_lat, rims_second[i], rims_first[i]), south, False, TO_NORTH, place, 16)
+    read_message(lambda i: jnp.where(even_lat, rims_first[i], rims_second[i]), north, True, TO_SOUTH, place, 16)
     for s, array in ((0, south), (1, north)):
         high, low = split(array[:NDIR].reshape(8 * NDIR, 128))
         lhs[:, 128 * s : 128 * s + 128] = high
@@ -374,24 +381,32 @@
     return [[base, 36 - base], [18 - base, 18 + base]][sign]
 
 
-def lon_pair(q, shifts, out, sign, base, tap_of):
-    dirs = lon_dirs(sign, base)
-    x = jnp.concatenate([q[d].reshape(64, 128) for d in dirs], axis=0)
+def lon_products(q, shifts, sign, base):
+    x = jnp.concatenate([q[d].reshape(64, 128) for d in lon_dirs(sign, base)], axis=0)
     lhs = jnp.concatenate(split(x), axis=1)
-    moved = jnp.dot(lhs, shifts[sign], preferred_element_type=f32)
-    for t in range(8):
-        tap = tap_of(t)
-        for i, d in enumerate(dirs):
-            cell = q[d, t]
-            near = moved[64 * i + 8 * t : 64 * i + 8 * t + 8]
-            out[d, t] = (tap[0] * cell + tap[1] * roll(cell, -1)) + (
-                tap[2] * near[:, :128] + tap[3] * near[:, 128:]
-            )
+    return jnp.dot(lhs, shifts[sign], preferred_element_type=f32)
+
+
+def lon_stages(q, taps, shifts, out, order, before):
+    ahead = lon_products(q, shifts, *order[0])
+    for step, (sign, base) in enumerate(order):
+        moved = ahead
+        if step + 1 < len(order):
+            ahead = lon_products(q, shifts, *order[step + 1])
+        before(step)
+        for t in range(8):
+            tap = [taps[base, sign, i, t] for i in range(4)]
+            for i, d in enumerate(lon_dirs(sign, base)):
+                cell = q[d, t]
+                near = moved[64 * i + 8 * t : 64 * i + 8 * t + 8]
+                out[d, t] = (tap[0] * cell + tap[1] * roll(cell, -1)) + (
+                    tap[2] * near[:, :128] + tap[3] * near[:, 128:]
+                )
 
 
 def first_lon_kernel(q, kx, shifts, out, taps):
-    for base in range(10):
-        for t in range(8):
+    def prepare(base, tiles):
+        for t in tiles:
             a1, b1, c1 = weights(COS[base] * kx[0, t])
             a0, b0, c0 = weights(COS[base] * kx[1, t])
             for sign, tap in enumerate(
@@ -399,14 +414,18 @@
             ):
                 for i in range(4):
                     taps[base, sign, i, t] = tap[i]
-        for sign in range(2):
-            lon_pair(q, shifts, out, sign, base, lambda t: [taps[base, sign, i, t] for i in range(4)])
+
+    def before(step):
+        if step // 2 < 9:
+            prepare(step // 2 + 1, range(4 * (step % 2), 4 * (step % 2) + 4))
+
+    prepare(0, range(8))
+    lon_stages(q, taps, shifts, out, [(sign, base) for base in range(10) for sign in range(2)], before)
 
 
 def lon_kernel(q, taps, shifts, out):
-    for sign in range(2):
-        for base in range(10):
-            lon_pair(q, shifts, out, sign, base, lambda t: [taps[base, sign, i, t] for i in range(4)])
+    order = [(sign, base) for sign in range(2) for base in range(10)]
+    lon_stages(q, taps, shifts, out, order, lambda step: None)
 
 
 def lat_kernel(q, ky, consts, out, sums=None):
@@ -649,9 +668,9 @@
     )(*[pltpu.with_memory_space_constraint(x, pltpu.HBM) for x in inputs])
     (gain,) = call(growth_kernel, 3, [(NDIR, 2) + tile], name="growth")(own, local, consts)
     west, east = call(unpack_kernel, 3, [slabs] * 2, name="unpack")(cols_first, cols_second, consts)
-    (rim_second,) = call(functools.partial(rim_kernel, True), 2, [slabs], name="rim_far")(west, east)
+    (rim_second,) = call(functools.partial(rim_kernel, True), 2, [(SENT + 1,) + tile], name="rim_far")(west, east)
     rims_second = swap(rim_second, "lat", 1)
-    (rim_first,) = call(functools.partial(rim_kernel, False), 5, [slabs], name="rim_near")(
+    (rim_first,) = call(functools.partial(rim_kernel, False), 5, [sent], name="rim_near")(
         west, east, rows_second, rows_first, rim_second
     )
     rims_first = swap(rim_first, "lat", 0)
@@ -667,7 +686,7 @@
         rims_kernel,
         5,
         [(NDIR,) + block, (2,) + block] + [block] * 3,
-        [pltpu.VMEM((8 * NDIR, 512), bf16)],
+        [pltpu.VMEM((8 * NDIR, 512), bf16)] + [pltpu.VMEM(slabs, f32)] * 2,
         name="rims",
     )(partial, rims_second, rims_first, consts, rims)
     cells = [(NDIR,) + block]

time: 30.8 us -> 30.9 us (level)
  no operation moved by 1% of the time
where the time goes in v13:
time: 30.9 us; the launch traced here: 30.5 us
  Pallas kernels  13.9 us (45%)
  starting transfers between devices  9.68 us (31%)
  waiting for transfers between devices  6.7 us (22%)
    ppermute x7, starting transfers between devices, swap(): return lax.ppermute(array, axis, pairs)  9.68 us
    ppermute x7, waiting for transfers between devices, swap(): return lax.ppermute(array, axis, pairs)  6.7 us
    pallas_call x3, Pallas kernels, per_device(): q, = call(lon_kernel, 3, cells, name='lon')(q, taps, shifts)  2.1 us
    pallas_call x3, Pallas kernels, per_device(): q, = call(turn_kernel, 3, cells, name='turn')(q, tx, ty)  1.67 us
    pallas_call x3, Pallas kernels, per_device(): q, = call(lat_kernel, 3, cells, name='lat')(q, ky, consts)  1.64 us
    pallas_call x1, Pallas kernels, per_device(): call(pack_kernel, 4, [(2,) + slabs], [pltpu.VMEM(x.shape, x.dtype) for x...  1.24 us
    pallas_call x1, Pallas kernels, per_device(): call(place_kernel, 6, [(SLABS,) + block], [pltpu.VMEM((8 * SLABS + 8, 153...  1.16 us
    pallas_call x1, Pallas kernels, per_device(): call(first_lon_kernel, 3, cells + [(10, 2, 4) + block], name='first_lon')  1.14 us
  transfers between devices with their start and end apart: 7, of which 3 were waited for; matrix products, arithmetic and copies ran while one was open for 0% of the time, Pallas kernels for 12%

profile of v13, /device:TPU:2, one launch (start us, length us, event | category | flops | bytes accessed | tf_op | source)
XLA Modules:
  0.0 30.5 jit_solution(15293516437776713940)
XLA Ops:
  0.0 1.2 %pack.1.own = f32[2,37,8,128]{3,2,1,0:T(8,128)S(1)} custom-call(f32[16,16,288]{2,1,0:T(8,128)} %refs_0_.2, s32[16,16]{1,0:T(8,128)} %refs_1_.2, s32[16,16]{1,0:T(8,128)} %refs_2_.2, f32[2,16,16]{2,1,0:T(8,128)} %refs_3_.2), custom_call_target="tpu_custom_call" | custom-call | tf_op jit(solution)/shard_map/pack/pallas_call | solution.py:640
  1.3 0.2 column_near.1
  1.4 1.6 %collective-permute-start = (f32[31,8,128]{2,1,0:T(8,128)S(1)}, f32[31,8,128]{2,1,0:T(8,128)S(1)}, u32[]{:S(2)}, u32[]{:S(2)}) collective-permute-start(f32[31,8,128]{2,1,0:T(8,128)S(1)} %column_near.1), channel_id=1, source_target_pairs={{0,8},{8,0},{16,24},{24,16},{1,9},{9,1},{17,25},{25,17},{2,10},{10... | collective-permute-start | bytes 380936 | tf_op jit(solution)/shard_map/ppermute | solution.py:620
  3.1 0.1 column_far.1
  3.2 2.5 %collective-permute-start.1 = (f32[31,8,128]{2,1,0:T(8,128)S(1)}, f32[31,8,128]{2,1,0:T(8,128)S(1)}, u32[]{:S(2)}, u32[]{:S(2)}) collective-permute-start(f32[31,8,128]{2,1,0:T(8,128)S(1)} %column_far.1), channel_id=1, source_target_pairs={{8,16},{16,8},{24,0},{0,24},{9,17},{17,9},{25,1},{1,25},{10,18},{1... | collective-permute-start | bytes 380936 | tf_op jit(solution)/shard_map/ppermute | solution.py:620
  5.8 1.9 %collective-permute-start.2 = (f32[31,8,128]{2,1,0:T(8,128)S(1)}, f32[31,8,128]{2,1,0:T(8,128)S(1)}, u32[]{:S(2)}, u32[]{:S(2)}) collective-permute-start(f32[31,8,128]{2,1,0:T(8,128)S(1)} %edge_far.1), channel_id=1, source_target_pairs={{2,4},{4,2},{3,5},{5,3},{10,12},{12,10},{11,13},{13,11},{18,20},{2... | collective-permute-start | bytes 380936 | tf_op jit(solution)/shard_map/ppermute | solution.py:620
  7.9 1.0 %tables.1 = (bf16[1536,1024]{1,0:T(8,128)(2,1)S(1)}, bf16[512,1024]{1,0:T(8,128)(2,1)S(1)}, bf16[2,256,256]{2,1,0:T(8,128)(2,1)S(1)}, bf16[2048,256]{1,0:T(8,128...) custom-call(f32[8,16]{1,0:T(8,128)} %refs_0_.3, f32[8,16]{1,0:T(8,128)} %refs_1_.3, f32[16]{0:T(128)} %refs_2_.3, ...), custom_call_target="tpu_custom_call" | custom-call | tf_op jit(solution)/shard_map/tables/pallas_call | solution.py:659
  8.9 2.6 %collective-permute-done.1.cols_second = f32[31,8,128]{2,1,0:T(8,128)S(1)} collective-permute-done((f32[31,8,128]{2,1,0:T(8,128)S(1)}, f32[31,8,128]{2,1,0:T(8,128)S(1)}, u32[]{:S(2)}, u32[]{:S(2)}) %collective-permute-start.1) | collective-permute-done | bytes 127008 | tf_op jit(solution)/shard_map/ppermute | solution.py:620
  11.5 0.1 unpack.1
  11.7 1.9 %collective-permute-start.4 = (f32[32,8,128]{2,1,0:T(8,128)S(1)}, f32[32,8,128]{2,1,0:T(8,128)S(1)}, u32[]{:S(2)}, u32[]{:S(2)}) collective-permute-start(f32[32,8,128]{2,1,0:T(8,128)S(1)} %rim_far.1.refs_2_), channel_id=1, source_target_pairs={{2,4},{4,2},{3,5},{5,3},{10,12},{12,10},{11,13},{13,11},{18,20},{2... | collective-permute-start | bytes 393224 | tf_op jit(solution)/shard_map/ppermute | solution.py:620
  13.7 0.1 rim_near.1
  13.8 0.1 unpack_rows.1
  14.0 1.2 %place.1.partial = f32[37,8,8,128]{3,2,1,0:T(8,128)S(1)} custom-call(f32[2,37,8,128]{3,2,1,0:T(8,128)S(1)} %pack.1.own, f32[37,8,128]{2,1,0:T(8,128)S(1)} %get-tuple-element.25.west, f32[37,8,128]{2,1,0:T(8,128)S(1)} %get-tuple-element.26.east, f32[37,8,128]{2,1,0:T(8,128)S(1)} %get-tuple-element.27.south, f32[37,8,128]{2,1,0:T(8,128)S(1)} %get-tuple-element.28.north, ...), custom_call_target="tpu_custom_call" | custom-call | tf_op jit(solution)/shard_map/place/pallas_call | solution.py:678
  15.2 2.8 %collective-permute-done.4.rims_second = f32[32,8,128]{2,1,0:T(8,128)S(1)} collective-permute-done((f32[32,8,128]{2,1,0:T(8,128)S(1)}, f32[32,8,128]{2,1,0:T(8,128)S(1)}, u32[]{:S(2)}, u32[]{:S(2)}) %collective-permute-start.4) | collective-permute-done | bytes 131104 | tf_op jit(solution)/shard_map/ppermute | solution.py:620
  18.0 0.6 %rims.1 = (f32[36,8,8,128]{3,2,1,0:T(8,128)S(1)}, f32[2,8,8,128]{3,2,1,0:T(8,128)S(1)}, f32[8,8,128]{2,1,0:T(8,128)S(1)}, f32[8,8,128]{2,1,0:T(8,128)S(1)}, f32[8,8,128]{2,1,0:T(8,128)S(1)}) custom-call(f32[37,8,8,128]{3,2,1,0:T(8,128)S(1)} %place.1.partial, f32[32,8,128]{2,1,0:T(8,128)S(1)} %collective-permute-done.4.rims_second, ...), custom_call_target="tpu_custom_call" | custom-call | tf_op jit(solution)/shard_map/rims/pallas_call | solution.py:685
  18.6 1.1 %first_lon.1 = (f32[36,8,8,128]{3,2,1,0:T(8,128)S(1)}, f32[10,2,4,8,8,128]{5,4,3,2,1,0:T(8,128)S(1)}) custom-call(f32[36,8,8,128]{3,2,1,0:T(8,128)S(1)} %get-tuple-element.31.q, f32[2,8,8,128]{3,2,1,0:T(8,128)S(1)} %get-tuple-element.32.kx, bf16[2,256,256]{2,1,0:T(8,128)(2,1)S(1)} %get-tuple-element.33.shifts), custom_call_target="tpu_custom_call" | custom-call | tf_op jit(solution)/shard_map/first_lon/pallas_call | solution.py:695
  19.7 0.5 %lat.3.q = f32[36,8,8,128]{3,2,1,0:T(8,128)S(1)} custom-call(f32[36,8,8,128]{3,2,1,0:T(8,128)S(1)} %get-tuple-element.34.q, f32[8,8,128]{2,1,0:T(8,128)S(1)} %get-tuple-element.35.ky, f32[20,8,128]{2,1,0:T(8,128)S(1)} %get-tuple-element.24.consts), custom_call_target="tpu_custom_call" | custom-call | tf_op jit(solution)/shard_map/lat/pallas_call | solution.py:701
  20.2 0.6 %turn.3.q = f32[36,8,8,128]{3,2,1,0:T(8,128)S(1)} custom-call(f32[36,8,8,128]{3,2,1,0:T(8,128)S(1)} %lat.3.q, f32[8,8,128]{2,1,0:T(8,128)S(1)} %get-tuple-element.36.tx, f32[8,8,128]{2,1,0:T(8,128)S(1)} %get-tuple-element.37.ty), custom_call_target="tpu_custom_call" | custom-call | tf_op jit(solution)/shard_map/turn/pallas_call | solution.py:702
  20.8 0.7 %lon.3.q = f32[36,8,8,128]{3,2,1,0:T(8,128)S(1)} custom-call(f32[36,8,8,128]{3,2,1,0:T(8,128)S(1)} %turn.3.q, f32[10,2,4,8,8,128]{5,4,3,2,1,0:T(8,128)S(1)} %get-tuple-element.38.taps, bf16[2,256,256]{2,1,0:T(8,128)(2,1)S(1)} %get-tuple-element.33.shifts), custom_call_target="tpu_custom_call" | custom-call | tf_op jit(solution)/shard_map/lon/pallas_call | solution.py:697
  21.5 0.5 %lat.4.q = f32[36,8,8,128]{3,2,1,0:T(8,128)S(1)} custom-call(f32[36,8,8,128]{3,2,1,0:T(8,128)S(1)} %lon.3.q, f32[8,8,128]{2,1,0:T(8,128)S(1)} %get-tuple-element.35.ky, f32[20,8,128]{2,1,0:T(8,128)S(1)} %get-tuple-element.24.consts), custom_call_target="tpu_custom_call" | custom-call | tf_op jit(solution)/shard_map/lat/pallas_call | solution.py:701
  22.1 0.6 %turn.4.q = f32[36,8,8,128]{3,2,1,0:T(8,128)S(1)} custom-call(f32[36,8,8,128]{3,2,1,0:T(8,128)S(1)} %lat.4.q, f32[8,8,128]{2,1,0:T(8,128)S(1)} %get-tuple-element.36.tx, f32[8,8,128]{2,1,0:T(8,128)S(1)} %get-tuple-element.37.ty), custom_call_target="tpu_custom_call" | custom-call | tf_op jit(solution)/shard_map/turn/pallas_call | solution.py:702
  22.6 0.7 %lon.4.q = f32[36,8,8,128]{3,2,1,0:T(8,128)S(1)} custom-call(f32[36,8,8,128]{3,2,1,0:T(8,128)S(1)} %turn.4.q, f32[10,2,4,8,8,128]{5,4,3,2,1,0:T(8,128)S(1)} %get-tuple-element.38.taps, bf16[2,256,256]{2,1,0:T(8,128)(2,1)S(1)} %get-tuple-element.33.shifts), custom_call_target="tpu_custom_call" | custom-call | tf_op jit(solution)/shard_map/lon/pallas_call | solution.py:697
  23.3 0.5 %lat.5.q = f32[36,8,8,128]{3,2,1,0:T(8,128)S(1)} custom-call(f32[36,8,8,128]{3,2,1,0:T(8,128)S(1)} %lon.4.q, f32[8,8,128]{2,1,0:T(8,128)S(1)} %get-tuple-element.35.ky, f32[20,8,128]{2,1,0:T(8,128)S(1)} %get-tuple-element.24.consts), custom_call_target="tpu_custom_call" | custom-call | tf_op jit(solution)/shard_map/lat/pallas_call | solution.py:701
  23.9 0.6 %turn.5.q = f32[36,8,8,128]{3,2,1,0:T(8,128)S(1)} custom-call(f32[36,8,8,128]{3,2,1,0:T(8,128)S(1)} %lat.5.q, f32[8,8,128]{2,1,0:T(8,128)S(1)} %get-tuple-element.36.tx, f32[8,8,128]{2,1,0:T(8,128)S(1)} %get-tuple-element.37.ty), custom_call_target="tpu_custom_call" | custom-call | tf_op jit(solution)/shard_map/turn/pallas_call | solution.py:702
  24.4 0.7 %lon.5.q = f32[36,8,8,128]{3,2,1,0:T(8,128)S(1)} custom-call(f32[36,8,8,128]{3,2,1,0:T(8,128)S(1)} %turn.5.q, f32[10,2,4,8,8,128]{5,4,3,2,1,0:T(8,128)S(1)} %get-tuple-element.38.taps, bf16[2,256,256]{2,1,0:T(8,128)(2,1)S(1)} %get-tuple-element.33.shifts), custom_call_target="tpu_custom_call" | custom-call | tf_op jit(solution)/shard_map/lon/pallas_call | solution.py:697
  25.2 0.7 %lat_sums.1 = (f32[36,8,8,128]{3,2,1,0:T(8,128)S(1)}, f32[8,128]{1,0:T(8,128)S(1)}) custom-call(f32[36,8,8,128]{3,2,1,0:T(8,128)S(1)} %lon.5.q, f32[8,8,128]{2,1,0:T(8,128)S(1)} %get-tuple-element.35.ky, f32[20,8,128]{2,1,0:T(8,128)S(1)} %get-tuple-element.24.consts), custom_call_target="tpu_custom_call" | custom-call | tf_op jit(solution)/shard_map/lat_sums/pallas_call | solution.py:699
  25.9 1.5 %collective-permute-start.6 = (f32[8,128]{1,0:T(8,128)S(1)}, f32[8,128]{1,0:T(8,128)S(1)}, u32[]{:S(2)}, u32[]{:S(2)}) collective-permute-start(f32[8,128]{1,0:T(8,128)S(1)} %get-tuple-element.42.sums), channel_id=1, source_target_pairs={{0,1},{1,0},{2,3},{3,2},{4,5},{5,4},{6,7},{7,6},{8,9},{9,8},{10,11... | collective-permute-start | bytes 12296 | tf_op jit(solution)/shard_map/ppermute | solution.py:620
  27.4 0.1 growth.1.gain
  27.5 0.5 %gather.1.own = f32[2,36,8,128]{3,2,1,0:T(8,128)S(1)} custom-call(f32[36,8,8,128]{3,2,1,0:T(8,128)S(1)} %get-tuple-element.39.q, bf16[2048,256]{1,0:T(8,128)(2,1)S(1)} %get-tuple-element.40.matrix), custom_call_target="tpu_custom_call" | custom-call | tf_op jit(solution)/shard_map/gather/pallas_call | solution.py:704
  28.1 0.2 last_turn.1.early
  28.2 1.3 %collective-permute-done.6.other = f32[8,128]{1,0:T(8,128)S(1)} collective-permute-done((f32[8,128]{1,0:T(8,128)S(1)}, f32[8,128]{1,0:T(8,128)S(1)}, u32[]{:S(2)}, u32[]{:S(2)}) %collective-permute-start.6) | collective-permute-done | bytes 4128 | tf_op jit(solution)/shard_map/ppermute | solution.py:620
  29.5 1.0 %finish.1 = f32[16,16,288]{2,1,0:T(8,128)} custom-call(f32[2,36,8,128]{3,2,1,0:T(8,128)S(1)} %last_turn.1.early, f32[2,8,128]{2,1,0:T(8,128)S(1)} %get-tuple-element.41.local, f32[8,128]{1,0:T(8,128)S(1)} %get-tuple-element.42.sums, f32[8,128]{1,0:T(8,128)S(1)} %collective-permute-done.6.other, f32[20,8,128]{2,1,0:T(8,128)S(1)} %get-tuple-element.24.consts), custom_call_target="tpu_custom_call" | custom-call | tf_op jit(solution)/shard_map/finish/pallas_call | solution.py:709
  (10 shorter events, 0.5 us)
Async XLA Ops:
  1.4 7.5 %collective-permute-start = (f32[31,8,128]{2,1,0:T(8,128)S(1)}, f32[31,8,128]{2,1,0:T(8,128)S(1)}, u32[]{:S(2)}, u32[]{:S(2)}) collective-permute-start(f32[31,8,128]{2,1,0:T(8,128)S(1)} %column_near.1), channel_id=1, source_target_pairs={{0,8},{8,0},{16,24},{24,16},{1,9},{9,1},{17,25},{25,17},{2,10},{10... | collective-permute-start | bytes 380936 | tf_op jit(solution)/shard_map/ppermute | solution.py:620
  3.2 8.3 %collective-permute-start.1 = (f32[31,8,128]{2,1,0:T(8,128)S(1)}, f32[31,8,128]{2,1,0:T(8,128)S(1)}, u32[]{:S(2)}, u32[]{:S(2)}) collective-permute-start(f32[31,8,128]{2,1,0:T(8,128)S(1)} %column_far.1), channel_id=1, source_target_pairs={{8,16},{16,8},{24,0},{0,24},{9,17},{17,9},{25,1},{1,25},{10,18},{1... | collective-permute-start | bytes 380936 | tf_op jit(solution)/shard_map/ppermute | solution.py:620
  5.8 7.8 %collective-permute-start.2 = (f32[31,8,128]{2,1,0:T(8,128)S(1)}, f32[31,8,128]{2,1,0:T(8,128)S(1)}, u32[]{:S(2)}, u32[]{:S(2)}) collective-permute-start(f32[31,8,128]{2,1,0:T(8,128)S(1)} %edge_far.1), channel_id=1, source_target_pairs={{2,4},{4,2},{3,5},{5,3},{10,12},{12,10},{11,13},{13,11},{18,20},{2... | collective-permute-start | bytes 380936 | tf_op jit(solution)/shard_map/ppermute | solution.py:620
  7.9 5.8 %collective-permute-start.3 = (f32[31,8,128]{2,1,0:T(8,128)S(1)}, f32[31,8,128]{2,1,0:T(8,128)S(1)}, u32[]{:S(2)}, u32[]{:S(2)}) collective-permute-start(f32[31,8,128]{2,1,0:T(8,128)S(1)} %edge_near.1), channel_id=1, source_target_pairs={{0,2},{2,0},{4,6},{6,4},{1,3},{3,1},{5,7},{7,5},{8,10},{10,8},{12,... | collective-permute-start | bytes 380936 | tf_op jit(solution)/shard_map/ppermute | solution.py:620
  11.7 6.3 %collective-permute-start.4 = (f32[32,8,128]{2,1,0:T(8,128)S(1)}, f32[32,8,128]{2,1,0:T(8,128)S(1)}, u32[]{:S(2)}, u32[]{:S(2)}) collective-permute-start(f32[32,8,128]{2,1,0:T(8,128)S(1)} %rim_far.1.refs_2_), channel_id=1, source_target_pairs={{2,4},{4,2},{3,5},{5,3},{10,12},{12,10},{11,13},{13,11},{18,20},{2... | collective-permute-start | bytes 393224 | tf_op jit(solution)/shard_map/ppermute | solution.py:620
  13.8 1.4 %collective-permute-start.5 = (f32[31,8,128]{2,1,0:T(8,128)S(1)}, f32[31,8,128]{2,1,0:T(8,128)S(1)}, u32[]{:S(2)}, u32[]{:S(2)}) collective-permute-start(f32[31,8,128]{2,1,0:T(8,128)S(1)} %rim_near.1), channel_id=1, source_target_pairs={{0,2},{2,0},{4,6},{6,4},{1,3},{3,1},{5,7},{7,5},{8,10},{10,8},{12,... | collective-permute-start | bytes 380936 | tf_op jit(solution)/shard_map/ppermute | solution.py:620
  25.9 3.6 %collective-permute-start.6 = (f32[8,128]{1,0:T(8,128)S(1)}, f32[8,128]{1,0:T(8,128)S(1)}, u32[]{:S(2)}, u32[]{:S(2)}) collective-permute-start(f32[8,128]{1,0:T(8,128)S(1)} %get-tuple-element.42.sums), channel_id=1, source_target_pairs={{0,1},{1,0},{2,3},{3,2},{4,5},{5,4},{6,7},{7,6},{8,9},{9,8},{10,11... | collective-permute-start | bytes 12296 | tf_op jit(solution)/shard_map/ppermute | solution.py:620

commit v14 on v12

--- a/solution.py
+++ b/solution.py
@@ -261,12 +261,15 @@
     place_field(wide, wdir[...], local, WDIR)
 
 
-def unpack_kernel(cols_first, cols_second, consts, west, east):
-    del consts
+def read_columns(cols_first, cols_second, west, east):
     even = is_even("lon")
     place = lanes() % 8
     read_message(lambda i: jnp.where(even, cols_second[i], cols_first[i]), west, False, TO_EAST, place, 1)
     read_message(lambda i: jnp.where(even, cols_first[i], cols_second[i]), east, True, TO_WEST, place, 1)
+
+
+def unpack_kernel(cols_first, cols_second, west, east):
+    read_columns(cols_first, cols_second, west, east)
 
 
 def unpack_rows_kernel(rows_second, rows_first, south, north):
@@ -276,11 +279,30 @@
     read_message(lambda i: jnp.where(even, rows_first[i], rows_second[i]), north, True, TO_SOUTH, place, 16)
 
 
-def rim_kernel(second, west, east, *refs):
-    rim = refs[-1]
-    west_low = (lanes() % 16 < 8) == (is_even("lat") != second)
-    for slab in range(SLABS):
-        rim[slab] = jnp.where(west_low, west[slab], east[slab])
+def write_rim(second, west, east, message):
+    to_north = is_even("lat") != second
+    west_low = (lanes() % 16 < 8) == to_north
+
+    def pick(side, south, north):
+        return side[south] if south == north else jnp.where(to_north, side[north], side[south])
+
+    def get(south, north):
+        return jnp.where(west_low, pick(west, south, north), pick(east, south, north))
+
+    write_message(message, get, ~to_north, TO_SOUTH, TO_NORTH, lanes() // 16, 16)
+
+
+def far_rim_kernel(cols_first, cols_second, consts, message):
+    del consts
+    west, east = {}, {}
+    read_columns(cols_first, cols_second, west, east)
+    write_rim(True, west, east, message)
+    message[SENT] = jnp.zeros((8, 128), f32)
+
+
+def near_rim_kernel(west, east, rows_second, rows_first, far, message):
+    del rows_second, rows_first, far
+    write_rim(False, west, east, message)
 
 
 def split(x):
@@ -316,10 +338,11 @@
     return value * point[SEA : SEA + 1]
 
 
-def rims_kernel(partial, rims_second, rims_first, consts, matrix, q, kx, ky, tx, ty, lhs):
+def rims_kernel(partial, rims_second, rims_first, consts, matrix, q, taps, ky, tx, ty, lhs, south, north):
     even_lat = is_even("lat")
-    south = jnp.where(even_lat, rims_second[...], rims_first[...])
-    north = jnp.where(even_lat, rims_first[...], rims_second[...])
+    place = lanes() // 16
+    read_message(lambda i: jnp.where(even_lat, rims_second[i], rims_first[i]), south, False, TO_NORTH, place, 16)
+    read_message(lambda i: jnp.where(even_lat, rims_first[i], rims_second[i]), north, True, TO_SOUTH, place, 16)
     for s, array in ((0, south), (1, north)):
         high, low = split(array[:NDIR].reshape(8 * NDIR, 128))
         lhs[:, 128 * s : 128 * s + 128] = high
@@ -341,8 +364,14 @@
         tx[t] = turning * point[SLOPE_X : SLOPE_X + 1]
         ty[t] = turning * point[SLOPE_Y : SLOPE_Y + 1]
         stretch = consts[STRETCH, t : t + 1, :]
-        kx[0, t] = 0.5 * (pace + roll(pace, -1)) * stretch
-        kx[1, t] = 0.5 * (pace + roll(pace, 1)) * stretch
+        right = powers(0.5 * (pace + roll(pace, -1)) * stretch)
+        left = powers(0.5 * (pace + roll(pace, 1)) * stretch)
+        for base in range(10):
+            a1, b1, c1 = weights(COS[base], right)
+            a0, b0, c0 = weights(COS[base], left)
+            for sign, tap in enumerate(((1.0 - a1 + b0, b1, a0 + c1, c0), (1.0 + b1 - a0, a1 + c0, b0, c1))):
+                for i in range(4):
+                    taps[base, sign, i, t] = tap[i]
     for t in range(8):
         ahead = speed[t + 1] if t < 7 else roll(speed[0], -32)
         ky[t] = 0.5 * (speed[t] + ahead)
@@ -356,10 +385,16 @@
     return 0.5 - 0.5 * k, (1.0 / 3.0) + (1.0 / 3.0) * k
 
 
-def weights(k):
-    u, w = halves(k)
-    bend = k * u * w
-    return k - k * u + 2.0 * bend, k * u - bend, -bend
+def powers(face):
+    square = face * face
+    return (1.0 / 6.0) * face, 0.5 * square, (1.0 / 6.0) * (square * face)
+
+
+def weights(cos_d, face_powers):
+    p, s, c = face_powers
+    bend = cos_d * p - cos_d**3 * c
+    rest = cos_d**2 * s - cos_d**3 * c
+    return (5.0 * cos_d * p - cos_d**3 * c) + rest, 2.0 * cos_d * p - rest, bend
 
 
 FORTH_TAPS = (-1, -2)
@@ -374,39 +409,24 @@
     return [[base, 36 - base], [18 - base, 18 + base]][sign]
 
 
-def lon_pair(q, shifts, out, sign, base, tap_of):
-    dirs = lon_dirs(sign, base)
-    x = jnp.concatenate([q[d].reshape(64, 128) for d in dirs], axis=0)
-    lhs = jnp.concatenate(split(x), axis=1)
-    moved = jnp.dot(lhs, shifts[sign], preferred_element_type=f32)
-    for t in range(8):
-        tap = tap_of(t)
-        for i, d in enumerate(dirs):
-            cell = q[d, t]
-            near = moved[64 * i + 8 * t : 64 * i + 8 * t + 8]
-            out[d, t] = (tap[0] * cell + tap[1] * roll(cell, -1)) + (
-                tap[2] * near[:, :128] + tap[3] * near[:, 128:]
-            )
-
-
-def first_lon_kernel(q, kx, shifts, out, taps):
-    for base in range(10):
-        for t in range(8):
-            a1, b1, c1 = weights(COS[base] * kx[0, t])
-            a0, b0, c0 = weights(COS[base] * kx[1, t])
-            for sign, tap in enumerate(
-                ((1.0 - a1 + b0, -b1, a0 - c1, c0), (1.0 + b1 - a0, a1 - c0, -b0, c1))
-            ):
-                for i in range(4):
-                    taps[base, sign, i, t] = tap[i]
-        for sign in range(2):
-            lon_pair(q, shifts, out, sign, base, lambda t: [taps[base, sign, i, t] for i in range(4)])
-
-
 def lon_kernel(q, taps, shifts, out):
     for sign in range(2):
         for base in range(10):
-            lon_pair(q, shifts, out, sign, base, lambda t: [taps[base, sign, i, t] for i in range(4)])
+            dirs = lon_dirs(sign, base)
+            x = jnp.concatenate([q[d].reshape(64, 128) for d in dirs], axis=0)
+            lhs = jnp.concatenate(split(x), axis=1)
+            moved = jnp.dot(lhs, shifts[sign], preferred_element_type=f32)
+            for t in range(8):
+                tap = [taps[base, sign, i, t] for i in range(4)]
+                for i, d in enumerate(dirs):
+                    cell = q[d, t]
+                    ahead = roll(cell, -1)
+                    near = moved[64 * i + 8 * t : 64 * i + 8 * t + 8]
+                    behind, beyond = near[:, :128], near[:, 128:]
+                    if sign == 0:
+                        out[d, t] = (tap[0] * cell - tap[1] * ahead) + (tap[2] * behind - tap[3] * beyond)
+                    else:
+                        out[d, t] = (tap[0] * cell + tap[1] * ahead) - (tap[2] * behind + tap[3] * beyond)
 
 
 def lat_kernel(q, ky, consts, out, sums=None):
@@ -648,10 +668,10 @@
         dtype=[bf16] * 4 + [f32] * 2,
     )(*[pltpu.with_memory_space_constraint(x, pltpu.HBM) for x in inputs])
     (gain,) = call(growth_kernel, 3, [(NDIR, 2) + tile], name="growth")(own, local, consts)
-    west, east = call(unpack_kernel, 3, [slabs] * 2, name="unpack")(cols_first, cols_second, consts)
-    (rim_second,) = call(functools.partial(rim_kernel, True), 2, [slabs], name="rim_far")(west, east)
+    (rim_second,) = call(far_rim_kernel, 3, [(SENT + 1,) + tile], name="rim_far")(cols_first, cols_second, consts)
     rims_second = swap(rim_second, "lat", 1)
-    (rim_first,) = call(functools.partial(rim_kernel, False), 5, [slabs], name="rim_near")(
+    west, east = call(unpack_kernel, 2, [slabs] * 2, name="unpack")(cols_first, cols_second)
+    (rim_first,) = call(near_rim_kernel, 5, [sent], name="rim_near")(
         west, east, rows_second, rows_first, rim_second
     )
     rims_first = swap(rim_first, "lat", 0)
@@ -663,19 +683,16 @@
         [pltpu.VMEM((8 * SLABS + 8, 1536), bf16)],
         name="place",
     )(own, west, east, south, north, place)
-    q, kx, ky, tx, ty = call(
+    q, taps, ky, tx, ty = call(
         rims_kernel,
         5,
-        [(NDIR,) + block, (2,) + block] + [block] * 3,
-        [pltpu.VMEM((8 * NDIR, 512), bf16)],
+        [(NDIR,) + block, (10, 2, 4) + block] + [block] * 3,
+        [pltpu.VMEM((8 * NDIR, 512), bf16)] + [pltpu.VMEM(slabs, f32)] * 2,
         name="rims",
     )(partial, rims_second, rims_first, consts, rims)
     cells = [(NDIR,) + block]
     for substep in range(ITERS):
-        if substep == 0:
-            q, taps = call(first_lon_kernel, 3, cells + [(10, 2, 4) + block], name="first_lon")(q, kx, shifts)
-        else:
-            (q,) = call(lon_kernel, 3, cells, name="lon")(q, taps, shifts)
+        (q,) = call(lon_kernel, 3, cells, name="lon")(q, taps, shifts)
         if substep == ITERS - 1:
             q, sums = call(lat_kernel, 3, cells + [tile], name="lat_sums")(q, ky, consts)
         else:

time: 30.8 us -> 30.9 us (level)
  waiting for transfers between devices: 6.98 us -> 6.6 us
    pallas_call x3 -> x4, Pallas kernels: 2.09 us -> 2.92 us  [per_device(): q, = call(lon_kernel, 3, cells, name='lon')(q, taps, shifts)]
    pallas_call x5 -> x4, Pallas kernels: 1.8 us -> 1.24 us  [the longest x1 0.91 us: per_device(): call(rims_kernel, 5, [(NDIR,) + block, (10, 2, 4) + block] + [block] * 3,...]
    ppermute x7, waiting for transfers between devices: 6.98 us -> 6.6 us  [swap(): return lax.ppermute(array, axis, pairs)]
where the time goes in v14:
time: 30.9 us; the launch traced here: 30.4 us
  Pallas kernels  13.9 us (45%)
  starting transfers between devices  9.68 us (31%)
  waiting for transfers between devices  6.6 us (21%)
    ppermute x7, starting transfers between devices, swap(): return lax.ppermute(array, axis, pairs)  9.68 us
    ppermute x7, waiting for transfers between devices, swap(): return lax.ppermute(array, axis, pairs)  6.6 us
    pallas_call x4, Pallas kernels, per_device(): q, = call(lon_kernel, 3, cells, name='lon')(q, taps, shifts)  2.92 us
    pallas_call x3, Pallas kernels, per_device(): q, = call(turn_kernel, 3, cells, name='turn')(q, tx, ty)  1.68 us
    pallas_call x3, Pallas kernels, per_device(): q, = call(lat_kernel, 3, cells, name='lat')(q, ky, consts)  1.64 us
    pallas_call x1, Pallas kernels, per_device(): call(pack_kernel, 4, [(2,) + slabs], [pltpu.VMEM(x.shape, x.dtype) for x...  1.24 us
    pallas_call x1, Pallas kernels, per_device(): call(place_kernel, 6, [(SLABS,) + block], [pltpu.VMEM((8 * SLABS + 8, 153...  1.16 us
    pallas_call x1, Pallas kernels, per_device(): call(tables_kernel, 6, [(1536, 1024), (512, 1024), (2, 256, 256), (2048,...  0.96 us
  transfers between devices with their start and end apart: 7, of which 3 were waited for; matrix products, arithmetic and copies ran while one was open for 0% of the time, Pallas kernels for 12%

profile of v14, /device:TPU:2, one launch (start us, length us, event | category | flops | bytes accessed | tf_op | source)
XLA Modules:
  0.0 30.4 jit_solution(178172126428408093)
XLA Ops:
  0.0 1.2 %pack.1.own = f32[2,37,8,128]{3,2,1,0:T(8,128)S(1)} custom-call(f32[16,16,288]{2,1,0:T(8,128)} %refs_0_.2, s32[16,16]{1,0:T(8,128)} %refs_1_.2, s32[16,16]{1,0:T(8,128)} %refs_2_.2, f32[2,16,16]{2,1,0:T(8,128)} %refs_3_.2), custom_call_target="tpu_custom_call" | custom-call | tf_op jit(solution)/shard_map/pack/pallas_call | solution.py:641
  1.3 0.2 column_near.1
  1.4 1.6 %collective-permute-start = (f32[31,8,128]{2,1,0:T(8,128)S(1)}, f32[31,8,128]{2,1,0:T(8,128)S(1)}, u32[]{:S(2)}, u32[]{:S(2)}) collective-permute-start(f32[31,8,128]{2,1,0:T(8,128)S(1)} %column_near.1), channel_id=1, source_target_pairs={{0,8},{8,0},{16,24},{24,16},{1,9},{9,1},{17,25},{25,17},{2,10},{10... | collective-permute-start | bytes 380936 | tf_op jit(solution)/shard_map/ppermute | solution.py:621
  3.1 0.1 column_far.1
  3.2 2.5 %collective-permute-start.1 = (f32[31,8,128]{2,1,0:T(8,128)S(1)}, f32[31,8,128]{2,1,0:T(8,128)S(1)}, u32[]{:S(2)}, u32[]{:S(2)}) collective-permute-start(f32[31,8,128]{2,1,0:T(8,128)S(1)} %column_far.1), channel_id=1, source_target_pairs={{8,16},{16,8},{24,0},{0,24},{9,17},{17,9},{25,1},{1,25},{10,18},{1... | collective-permute-start | bytes 380936 | tf_op jit(solution)/shard_map/ppermute | solution.py:621
  5.8 1.9 %collective-permute-start.2 = (f32[31,8,128]{2,1,0:T(8,128)S(1)}, f32[31,8,128]{2,1,0:T(8,128)S(1)}, u32[]{:S(2)}, u32[]{:S(2)}) collective-permute-start(f32[31,8,128]{2,1,0:T(8,128)S(1)} %edge_far.1), channel_id=1, source_target_pairs={{2,4},{4,2},{3,5},{5,3},{10,12},{12,10},{11,13},{13,11},{18,20},{2... | collective-permute-start | bytes 380936 | tf_op jit(solution)/shard_map/ppermute | solution.py:621
  7.9 1.0 %tables.1 = (bf16[1536,1024]{1,0:T(8,128)(2,1)S(1)}, bf16[512,1024]{1,0:T(8,128)(2,1)S(1)}, bf16[2,256,256]{2,1,0:T(8,128)(2,1)S(1)}, bf16[2048,256]{1,0:T(8,128...) custom-call(f32[8,16]{1,0:T(8,128)} %refs_0_.3, f32[8,16]{1,0:T(8,128)} %refs_1_.3, f32[16]{0:T(128)} %refs_2_.3, ...), custom_call_target="tpu_custom_call" | custom-call | tf_op jit(solution)/shard_map/tables/pallas_call | solution.py:660
  8.9 2.6 %collective-permute-done.1.cols_second = f32[31,8,128]{2,1,0:T(8,128)S(1)} collective-permute-done((f32[31,8,128]{2,1,0:T(8,128)S(1)}, f32[31,8,128]{2,1,0:T(8,128)S(1)}, u32[]{:S(2)}, u32[]{:S(2)}) %collective-permute-start.1) | collective-permute-done | bytes 127008 | tf_op jit(solution)/shard_map/ppermute | solution.py:621
  11.5 0.1 rim_far.1.far
  11.6 1.9 %collective-permute-start.4 = (f32[32,8,128]{2,1,0:T(8,128)S(1)}, f32[32,8,128]{2,1,0:T(8,128)S(1)}, u32[]{:S(2)}, u32[]{:S(2)}) collective-permute-start(f32[32,8,128]{2,1,0:T(8,128)S(1)} %rim_far.1.far), channel_id=1, source_target_pairs={{2,4},{4,2},{3,5},{5,3},{10,12},{12,10},{11,13},{13,11},{18,20},{2... | collective-permute-start | bytes 393224 | tf_op jit(solution)/shard_map/ppermute | solution.py:621
  13.5 0.1 unpack.1
  13.9 0.1 unpack_rows.1
  14.0 1.2 %place.1.partial = f32[37,8,8,128]{3,2,1,0:T(8,128)S(1)} custom-call(f32[2,37,8,128]{3,2,1,0:T(8,128)S(1)} %pack.1.own, f32[37,8,128]{2,1,0:T(8,128)S(1)} %get-tuple-element.22.west, f32[37,8,128]{2,1,0:T(8,128)S(1)} %get-tuple-element.23.east, f32[37,8,128]{2,1,0:T(8,128)S(1)} %get-tuple-element.24.south, f32[37,8,128]{2,1,0:T(8,128)S(1)} %get-tuple-element.25.north, ...), custom_call_target="tpu_custom_call" | custom-call | tf_op jit(solution)/shard_map/place/pallas_call | solution.py:679
  15.2 2.7 %collective-permute-done.4.rims_second = f32[32,8,128]{2,1,0:T(8,128)S(1)} collective-permute-done((f32[32,8,128]{2,1,0:T(8,128)S(1)}, f32[32,8,128]{2,1,0:T(8,128)S(1)}, u32[]{:S(2)}, u32[]{:S(2)}) %collective-permute-start.4) | collective-permute-done | bytes 131104 | tf_op jit(solution)/shard_map/ppermute | solution.py:621
  17.9 0.9 %rims.1 = (f32[36,8,8,128]{3,2,1,0:T(8,128)S(1)}, f32[10,2,4,8,8,128]{5,4,3,2,1,0:T(8,128)S(1)}, f32[8,8,128]{2,1,0:T(8,128)S(1)}, f32[8,8,128]{2,1,0:T(8,128)S(1)}, f32[8,8,128]{2,1,0:T(8,128)S(1)}) custom-call(f32[37,8,8,128]{3,2,1,0:T(8,128)S(1)} %place.1.partial, f32[32,8,128]{2,1,0:T(8,128)S(1)} %collective-permute-done.4.rims_second, ...), custom_call_target="tpu_custom_call" | custom-call | tf_op jit(solution)/shard_map/rims/pallas_call | solution.py:686
  18.8 0.7 %lon.4.q = f32[36,8,8,128]{3,2,1,0:T(8,128)S(1)} custom-call(f32[36,8,8,128]{3,2,1,0:T(8,128)S(1)} %get-tuple-element.29.q, f32[10,2,4,8,8,128]{5,4,3,2,1,0:T(8,128)S(1)} %get-tuple-element.30.taps, bf16[2,256,256]{2,1,0:T(8,128)(2,1)S(1)} %get-tuple-element.31.shifts), custom_call_target="tpu_custom_call" | custom-call | tf_op jit(solution)/shard_map/lon/pallas_call | solution.py:695
  19.6 0.5 %lat.3.q = f32[36,8,8,128]{3,2,1,0:T(8,128)S(1)} custom-call(f32[36,8,8,128]{3,2,1,0:T(8,128)S(1)} %lon.4.q, f32[8,8,128]{2,1,0:T(8,128)S(1)} %get-tuple-element.32.ky, f32[20,8,128]{2,1,0:T(8,128)S(1)} %get-tuple-element.27.consts), custom_call_target="tpu_custom_call" | custom-call | tf_op jit(solution)/shard_map/lat/pallas_call | solution.py:699
  20.1 0.6 %turn.3.q = f32[36,8,8,128]{3,2,1,0:T(8,128)S(1)} custom-call(f32[36,8,8,128]{3,2,1,0:T(8,128)S(1)} %lat.3.q, f32[8,8,128]{2,1,0:T(8,128)S(1)} %get-tuple-element.33.tx, f32[8,8,128]{2,1,0:T(8,128)S(1)} %get-tuple-element.34.ty), custom_call_target="tpu_custom_call" | custom-call | tf_op jit(solution)/shard_map/turn/pallas_call | solution.py:700
  20.7 0.7 %lon.5.q = f32[36,8,8,128]{3,2,1,0:T(8,128)S(1)} custom-call(f32[36,8,8,128]{3,2,1,0:T(8,128)S(1)} %turn.3.q, f32[10,2,4,8,8,128]{5,4,3,2,1,0:T(8,128)S(1)} %get-tuple-element.30.taps, bf16[2,256,256]{2,1,0:T(8,128)(2,1)S(1)} %get-tuple-element.31.shifts), custom_call_target="tpu_custom_call" | custom-call | tf_op jit(solution)/shard_map/lon/pallas_call | solution.py:695
  21.4 0.5 %lat.4.q = f32[36,8,8,128]{3,2,1,0:T(8,128)S(1)} custom-call(f32[36,8,8,128]{3,2,1,0:T(8,128)S(1)} %lon.5.q, f32[8,8,128]{2,1,0:T(8,128)S(1)} %get-tuple-element.32.ky, f32[20,8,128]{2,1,0:T(8,128)S(1)} %get-tuple-element.27.consts), custom_call_target="tpu_custom_call" | custom-call | tf_op jit(solution)/shard_map/lat/pallas_call | solution.py:699
  21.9 0.6 %turn.4.q = f32[36,8,8,128]{3,2,1,0:T(8,128)S(1)} custom-call(f32[36,8,8,128]{3,2,1,0:T(8,128)S(1)} %lat.4.q, f32[8,8,128]{2,1,0:T(8,128)S(1)} %get-tuple-element.33.tx, f32[8,8,128]{2,1,0:T(8,128)S(1)} %get-tuple-element.34.ty), custom_call_target="tpu_custom_call" | custom-call | tf_op jit(solution)/shard_map/turn/pallas_call | solution.py:700
  22.5 0.7 %lon.6.q = f32[36,8,8,128]{3,2,1,0:T(8,128)S(1)} custom-call(f32[36,8,8,128]{3,2,1,0:T(8,128)S(1)} %turn.4.q, f32[10,2,4,8,8,128]{5,4,3,2,1,0:T(8,128)S(1)} %get-tuple-element.30.taps, bf16[2,256,256]{2,1,0:T(8,128)(2,1)S(1)} %get-tuple-element.31.shifts), custom_call_target="tpu_custom_call" | custom-call | tf_op jit(solution)/shard_map/lon/pallas_call | solution.py:695
  23.2 0.5 %lat.5.q = f32[36,8,8,128]{3,2,1,0:T(8,128)S(1)} custom-call(f32[36,8,8,128]{3,2,1,0:T(8,128)S(1)} %lon.6.q, f32[8,8,128]{2,1,0:T(8,128)S(1)} %get-tuple-element.32.ky, f32[20,8,128]{2,1,0:T(8,128)S(1)} %get-tuple-element.27.consts), custom_call_target="tpu_custom_call" | custom-call | tf_op jit(solution)/shard_map/lat/pallas_call | solution.py:699
  23.8 0.6 %turn.5.q = f32[36,8,8,128]{3,2,1,0:T(8,128)S(1)} custom-call(f32[36,8,8,128]{3,2,1,0:T(8,128)S(1)} %lat.5.q, f32[8,8,128]{2,1,0:T(8,128)S(1)} %get-tuple-element.33.tx, f32[8,8,128]{2,1,0:T(8,128)S(1)} %get-tuple-element.34.ty), custom_call_target="tpu_custom_call" | custom-call | tf_op jit(solution)/shard_map/turn/pallas_call | solution.py:700
  24.4 0.7 %lon.7.q = f32[36,8,8,128]{3,2,1,0:T(8,128)S(1)} custom-call(f32[36,8,8,128]{3,2,1,0:T(8,128)S(1)} %turn.5.q, f32[10,2,4,8,8,128]{5,4,3,2,1,0:T(8,128)S(1)} %get-tuple-element.30.taps, bf16[2,256,256]{2,1,0:T(8,128)(2,1)S(1)} %get-tuple-element.31.shifts), custom_call_target="tpu_custom_call" | custom-call | tf_op jit(solution)/shard_map/lon/pallas_call | solution.py:695
  25.1 0.7 %lat_sums.1 = (f32[36,8,8,128]{3,2,1,0:T(8,128)S(1)}, f32[8,128]{1,0:T(8,128)S(1)}) custom-call(f32[36,8,8,128]{3,2,1,0:T(8,128)S(1)} %lon.7.q, f32[8,8,128]{2,1,0:T(8,128)S(1)} %get-tuple-element.32.ky, f32[20,8,128]{2,1,0:T(8,128)S(1)} %get-tuple-element.27.consts), custom_call_target="tpu_custom_call" | custom-call | tf_op jit(solution)/shard_map/lat_sums/pallas_call | solution.py:697
  25.8 1.5 %collective-permute-start.6 = (f32[8,128]{1,0:T(8,128)S(1)}, f32[8,128]{1,0:T(8,128)S(1)}, u32[]{:S(2)}, u32[]{:S(2)}) collective-permute-start(f32[8,128]{1,0:T(8,128)S(1)} %get-tuple-element.38.sums), channel_id=1, source_target_pairs={{0,1},{1,0},{2,3},{3,2},{4,5},{5,4},{6,7},{7,6},{8,9},{9,8},{10,11... | collective-permute-start | bytes 12296 | tf_op jit(solution)/shard_map/ppermute | solution.py:621
  27.3 0.1 growth.1.gain
  27.5 0.5 %gather.1.own = f32[2,36,8,128]{3,2,1,0:T(8,128)S(1)} custom-call(f32[36,8,8,128]{3,2,1,0:T(8,128)S(1)} %get-tuple-element.35.q, bf16[2048,256]{1,0:T(8,128)(2,1)S(1)} %get-tuple-element.36.matrix), custom_call_target="tpu_custom_call" | custom-call | tf_op jit(solution)/shard_map/gather/pallas_call | solution.py:702
  28.0 0.2 last_turn.1.early
  28.2 1.3 %collective-permute-done.6.other = f32[8,128]{1,0:T(8,128)S(1)} collective-permute-done((f32[8,128]{1,0:T(8,128)S(1)}, f32[8,128]{1,0:T(8,128)S(1)}, u32[]{:S(2)}, u32[]{:S(2)}) %collective-permute-start.6) | collective-permute-done | bytes 4128 | tf_op jit(solution)/shard_map/ppermute | solution.py:621
  29.4 1.0 %finish.1 = f32[16,16,288]{2,1,0:T(8,128)} custom-call(f32[2,36,8,128]{3,2,1,0:T(8,128)S(1)} %last_turn.1.early, f32[2,8,128]{2,1,0:T(8,128)S(1)} %get-tuple-element.37.local, f32[8,128]{1,0:T(8,128)S(1)} %get-tuple-element.38.sums, f32[8,128]{1,0:T(8,128)S(1)} %collective-permute-done.6.other, f32[20,8,128]{2,1,0:T(8,128)S(1)} %get-tuple-element.27.consts), custom_call_target="tpu_custom_call" | custom-call | tf_op jit(solution)/shard_map/finish/pallas_call | solution.py:707
  (10 shorter events, 0.5 us)
Async XLA Ops:
  1.4 7.5 %collective-permute-start = (f32[31,8,128]{2,1,0:T(8,128)S(1)}, f32[31,8,128]{2,1,0:T(8,128)S(1)}, u32[]{:S(2)}, u32[]{:S(2)}) collective-permute-start(f32[31,8,128]{2,1,0:T(8,128)S(1)} %column_near.1), channel_id=1, source_target_pairs={{0,8},{8,0},{16,24},{24,16},{1,9},{9,1},{17,25},{25,17},{2,10},{10... | collective-permute-start | bytes 380936 | tf_op jit(solution)/shard_map/ppermute | solution.py:621
  3.2 8.3 %collective-permute-start.1 = (f32[31,8,128]{2,1,0:T(8,128)S(1)}, f32[31,8,128]{2,1,0:T(8,128)S(1)}, u32[]{:S(2)}, u32[]{:S(2)}) collective-permute-start(f32[31,8,128]{2,1,0:T(8,128)S(1)} %column_far.1), channel_id=1, source_target_pairs={{8,16},{16,8},{24,0},{0,24},{9,17},{17,9},{25,1},{1,25},{10,18},{1... | collective-permute-start | bytes 380936 | tf_op jit(solution)/shard_map/ppermute | solution.py:621
  5.8 7.8 %collective-permute-start.2 = (f32[31,8,128]{2,1,0:T(8,128)S(1)}, f32[31,8,128]{2,1,0:T(8,128)S(1)}, u32[]{:S(2)}, u32[]{:S(2)}) collective-permute-start(f32[31,8,128]{2,1,0:T(8,128)S(1)} %edge_far.1), channel_id=1, source_target_pairs={{2,4},{4,2},{3,5},{5,3},{10,12},{12,10},{11,13},{13,11},{18,20},{2... | collective-permute-start | bytes 380936 | tf_op jit(solution)/shard_map/ppermute | solution.py:621
  7.9 5.8 %collective-permute-start.3 = (f32[31,8,128]{2,1,0:T(8,128)S(1)}, f32[31,8,128]{2,1,0:T(8,128)S(1)}, u32[]{:S(2)}, u32[]{:S(2)}) collective-permute-start(f32[31,8,128]{2,1,0:T(8,128)S(1)} %edge_near.1), channel_id=1, source_target_pairs={{0,2},{2,0},{4,6},{6,4},{1,3},{3,1},{5,7},{7,5},{8,10},{10,8},{12,... | collective-permute-start | bytes 380936 | tf_op jit(solution)/shard_map/ppermute | solution.py:621
  11.6 6.3 %collective-permute-start.4 = (f32[32,8,128]{2,1,0:T(8,128)S(1)}, f32[32,8,128]{2,1,0:T(8,128)S(1)}, u32[]{:S(2)}, u32[]{:S(2)}) collective-permute-start(f32[32,8,128]{2,1,0:T(8,128)S(1)} %rim_far.1.far), channel_id=1, source_target_pairs={{2,4},{4,2},{3,5},{5,3},{10,12},{12,10},{11,13},{13,11},{18,20},{2... | collective-permute-start | bytes 393224 | tf_op jit(solution)/shard_map/ppermute | solution.py:621
  13.8 1.4 %collective-permute-start.5 = (f32[31,8,128]{2,1,0:T(8,128)S(1)}, f32[31,8,128]{2,1,0:T(8,128)S(1)}, u32[]{:S(2)}, u32[]{:S(2)}) collective-permute-start(f32[31,8,128]{2,1,0:T(8,128)S(1)} %rim_near.1), channel_id=1, source_target_pairs={{0,2},{2,0},{4,6},{6,4},{1,3},{3,1},{5,7},{7,5},{8,10},{10,8},{12,... | collective-permute-start | bytes 380936 | tf_op jit(solution)/shard_map/ppermute | solution.py:621
  25.8 3.6 %collective-permute-start.6 = (f32[8,128]{1,0:T(8,128)S(1)}, f32[8,128]{1,0:T(8,128)S(1)}, u32[]{:S(2)}, u32[]{:S(2)}) collective-permute-start(f32[8,128]{1,0:T(8,128)S(1)} %get-tuple-element.38.sums), channel_id=1, source_target_pairs={{0,1},{1,0},{2,3},{3,2},{4,5},{5,4},{6,7},{7,6},{8,9},{9,8},{10,11... | collective-permute-start | bytes 12296 | tf_op jit(solution)/shard_map/ppermute | solution.py:621

commit v15 on v13

--- a/solution.py
+++ b/solution.py
@@ -73,7 +73,7 @@
     copies = fetch(sources, landed, sems)
     wide[...] = jnp.zeros_like(wide)
     static[...] = jnp.zeros_like(static)
-    for copy in copies:
+    for copy in copies[1:]:
         copy.wait()
     spec, sea, depth, slope = landed
     place_field(wide, sea[...].astype(f32), static, SEA)
@@ -81,6 +81,7 @@
     place_field(wide, slope[0], static, SLOPE_X)
     place_field(wide, slope[1], static, SLOPE_Y)
     own[:, STATIC] = static[...]
+    copies[0].wait()
     grid = spec[...].reshape(256, NDIR * FREQ)
     for low, high in ((0, 128), (128, 256), (256, 288)):
         turned = grid[:, low:high].T

time: 30.9 us -> 30.9 us (level)
  no operation moved by 1% of the time
where the time goes in v15:
time: 30.9 us; the launch traced here: 30.4 us
  Pallas kernels  13.8 us (45%)
  starting transfers between devices  9.68 us (31%)
  waiting for transfers between devices  6.7 us (22%)
    ppermute x7, starting transfers between devices, swap(): return lax.ppermute(array, axis, pairs)  9.68 us
    ppermute x7, waiting for transfers between devices, swap(): return lax.ppermute(array, axis, pairs)  6.7 us
    pallas_call x3, Pallas kernels, per_device(): q, = call(lon_kernel, 3, cells, name='lon')(q, taps, shifts)  2.1 us
    pallas_call x3, Pallas kernels, per_device(): q, = call(turn_kernel, 3, cells, name='turn')(q, tx, ty)  1.67 us
    pallas_call x3, Pallas kernels, per_device(): q, = call(lat_kernel, 3, cells, name='lat')(q, ky, consts)  1.64 us
    pallas_call x1, Pallas kernels, per_device(): call(pack_kernel, 4, [(2,) + slabs], [pltpu.VMEM(x.shape, x.dtype) for x...  1.19 us
    pallas_call x1, Pallas kernels, per_device(): call(place_kernel, 6, [(SLABS,) + block], [pltpu.VMEM((8 * SLABS + 8, 153...  1.16 us
    pallas_call x1, Pallas kernels, per_device(): call(first_lon_kernel, 3, cells + [(10, 2, 4) + block], name='first_lon')  1.14 us
  transfers between devices with their start and end apart: 7, of which 3 were waited for; matrix products, arithmetic and copies ran while one was open for 0% of the time, Pallas kernels for 12%

profile of v15, /device:TPU:2, one launch (start us, length us, event | category | flops | bytes accessed | tf_op | source)
XLA Modules:
  0.0 30.4 jit_solution(12792960323391407442)
XLA Ops:
  0.0 1.2 %pack.1.own = f32[2,37,8,128]{3,2,1,0:T(8,128)S(1)} custom-call(f32[16,16,288]{2,1,0:T(8,128)} %refs_0_.2, s32[16,16]{1,0:T(8,128)} %refs_1_.2, s32[16,16]{1,0:T(8,128)} %refs_2_.2, f32[2,16,16]{2,1,0:T(8,128)} %refs_3_.2), custom_call_target="tpu_custom_call" | custom-call | tf_op jit(solution)/shard_map/pack/pallas_call | solution.py:641
  1.2 0.2 column_near.1
  1.4 1.6 %collective-permute-start = (f32[31,8,128]{2,1,0:T(8,128)S(1)}, f32[31,8,128]{2,1,0:T(8,128)S(1)}, u32[]{:S(2)}, u32[]{:S(2)}) collective-permute-start(f32[31,8,128]{2,1,0:T(8,128)S(1)} %column_near.1), channel_id=1, source_target_pairs={{0,8},{8,0},{16,24},{24,16},{1,9},{9,1},{17,25},{25,17},{2,10},{10... | collective-permute-start | bytes 380936 | tf_op jit(solution)/shard_map/ppermute | solution.py:621
  3.0 0.1 column_far.1
  3.2 2.5 %collective-permute-start.1 = (f32[31,8,128]{2,1,0:T(8,128)S(1)}, f32[31,8,128]{2,1,0:T(8,128)S(1)}, u32[]{:S(2)}, u32[]{:S(2)}) collective-permute-start(f32[31,8,128]{2,1,0:T(8,128)S(1)} %column_far.1), channel_id=1, source_target_pairs={{8,16},{16,8},{24,0},{0,24},{9,17},{17,9},{25,1},{1,25},{10,18},{1... | collective-permute-start | bytes 380936 | tf_op jit(solution)/shard_map/ppermute | solution.py:621
  5.8 1.9 %collective-permute-start.2 = (f32[31,8,128]{2,1,0:T(8,128)S(1)}, f32[31,8,128]{2,1,0:T(8,128)S(1)}, u32[]{:S(2)}, u32[]{:S(2)}) collective-permute-start(f32[31,8,128]{2,1,0:T(8,128)S(1)} %edge_far.1), channel_id=1, source_target_pairs={{2,4},{4,2},{3,5},{5,3},{10,12},{12,10},{11,13},{13,11},{18,20},{2... | collective-permute-start | bytes 380936 | tf_op jit(solution)/shard_map/ppermute | solution.py:621
  7.9 1.0 %tables.1 = (bf16[1536,1024]{1,0:T(8,128)(2,1)S(1)}, bf16[512,1024]{1,0:T(8,128)(2,1)S(1)}, bf16[2,256,256]{2,1,0:T(8,128)(2,1)S(1)}, bf16[2048,256]{1,0:T(8,128...) custom-call(f32[8,16]{1,0:T(8,128)} %refs_0_.3, f32[8,16]{1,0:T(8,128)} %refs_1_.3, f32[16]{0:T(128)} %refs_2_.3, ...), custom_call_target="tpu_custom_call" | custom-call | tf_op jit(solution)/shard_map/tables/pallas_call | solution.py:660
  8.9 2.6 %collective-permute-done.1.cols_second = f32[31,8,128]{2,1,0:T(8,128)S(1)} collective-permute-done((f32[31,8,128]{2,1,0:T(8,128)S(1)}, f32[31,8,128]{2,1,0:T(8,128)S(1)}, u32[]{:S(2)}, u32[]{:S(2)}) %collective-permute-start.1) | collective-permute-done | bytes 127008 | tf_op jit(solution)/shard_map/ppermute | solution.py:621
  11.4 0.1 unpack.1
  11.7 1.9 %collective-permute-start.4 = (f32[32,8,128]{2,1,0:T(8,128)S(1)}, f32[32,8,128]{2,1,0:T(8,128)S(1)}, u32[]{:S(2)}, u32[]{:S(2)}) collective-permute-start(f32[32,8,128]{2,1,0:T(8,128)S(1)} %rim_far.1.refs_2_), channel_id=1, source_target_pairs={{2,4},{4,2},{3,5},{5,3},{10,12},{12,10},{11,13},{13,11},{18,20},{2... | collective-permute-start | bytes 393224 | tf_op jit(solution)/shard_map/ppermute | solution.py:621
  13.6 0.1 rim_near.1
  13.8 0.1 unpack_rows.1
  13.9 1.2 %place.1.partial = f32[37,8,8,128]{3,2,1,0:T(8,128)S(1)} custom-call(f32[2,37,8,128]{3,2,1,0:T(8,128)S(1)} %pack.1.own, f32[37,8,128]{2,1,0:T(8,128)S(1)} %get-tuple-element.25.west, f32[37,8,128]{2,1,0:T(8,128)S(1)} %get-tuple-element.26.east, f32[37,8,128]{2,1,0:T(8,128)S(1)} %get-tuple-element.27.south, f32[37,8,128]{2,1,0:T(8,128)S(1)} %get-tuple-element.28.north, ...), custom_call_target="tpu_custom_call" | custom-call | tf_op jit(solution)/shard_map/place/pallas_call | solution.py:679
  15.1 2.8 %collective-permute-done.4.rims_second = f32[32,8,128]{2,1,0:T(8,128)S(1)} collective-permute-done((f32[32,8,128]{2,1,0:T(8,128)S(1)}, f32[32,8,128]{2,1,0:T(8,128)S(1)}, u32[]{:S(2)}, u32[]{:S(2)}) %collective-permute-start.4) | collective-permute-done | bytes 131104 | tf_op jit(solution)/shard_map/ppermute | solution.py:621
  17.9 0.6 %rims.1 = (f32[36,8,8,128]{3,2,1,0:T(8,128)S(1)}, f32[2,8,8,128]{3,2,1,0:T(8,128)S(1)}, f32[8,8,128]{2,1,0:T(8,128)S(1)}, f32[8,8,128]{2,1,0:T(8,128)S(1)}, f32[8,8,128]{2,1,0:T(8,128)S(1)}) custom-call(f32[37,8,8,128]{3,2,1,0:T(8,128)S(1)} %place.1.partial, f32[32,8,128]{2,1,0:T(8,128)S(1)} %collective-permute-done.4.rims_second, ...), custom_call_target="tpu_custom_call" | custom-call | tf_op jit(solution)/shard_map/rims/pallas_call | solution.py:686
  18.5 1.1 %first_lon.1 = (f32[36,8,8,128]{3,2,1,0:T(8,128)S(1)}, f32[10,2,4,8,8,128]{5,4,3,2,1,0:T(8,128)S(1)}) custom-call(f32[36,8,8,128]{3,2,1,0:T(8,128)S(1)} %get-tuple-element.31.q, f32[2,8,8,128]{3,2,1,0:T(8,128)S(1)} %get-tuple-element.32.kx, bf16[2,256,256]{2,1,0:T(8,128)(2,1)S(1)} %get-tuple-element.33.shifts), custom_call_target="tpu_custom_call" | custom-call | tf_op jit(solution)/shard_map/first_lon/pallas_call | solution.py:696
  19.6 0.5 %lat.3.q = f32[36,8,8,128]{3,2,1,0:T(8,128)S(1)} custom-call(f32[36,8,8,128]{3,2,1,0:T(8,128)S(1)} %get-tuple-element.34.q, f32[8,8,128]{2,1,0:T(8,128)S(1)} %get-tuple-element.35.ky, f32[20,8,128]{2,1,0:T(8,128)S(1)} %get-tuple-element.24.consts), custom_call_target="tpu_custom_call" | custom-call | tf_op jit(solution)/shard_map/lat/pallas_call | solution.py:702
  20.2 0.6 %turn.3.q = f32[36,8,8,128]{3,2,1,0:T(8,128)S(1)} custom-call(f32[36,8,8,128]{3,2,1,0:T(8,128)S(1)} %lat.3.q, f32[8,8,128]{2,1,0:T(8,128)S(1)} %get-tuple-element.36.tx, f32[8,8,128]{2,1,0:T(8,128)S(1)} %get-tuple-element.37.ty), custom_call_target="tpu_custom_call" | custom-call | tf_op jit(solution)/shard_map/turn/pallas_call | solution.py:703
  20.8 0.7 %lon.3.q = f32[36,8,8,128]{3,2,1,0:T(8,128)S(1)} custom-call(f32[36,8,8,128]{3,2,1,0:T(8,128)S(1)} %turn.3.q, f32[10,2,4,8,8,128]{5,4,3,2,1,0:T(8,128)S(1)} %get-tuple-element.38.taps, bf16[2,256,256]{2,1,0:T(8,128)(2,1)S(1)} %get-tuple-element.33.shifts), custom_call_target="tpu_custom_call" | custom-call | tf_op jit(solution)/shard_map/lon/pallas_call | solution.py:698
  21.5 0.5 %lat.4.q = f32[36,8,8,128]{3,2,1,0:T(8,128)S(1)} custom-call(f32[36,8,8,128]{3,2,1,0:T(8,128)S(1)} %lon.3.q, f32[8,8,128]{2,1,0:T(8,128)S(1)} %get-tuple-element.35.ky, f32[20,8,128]{2,1,0:T(8,128)S(1)} %get-tuple-element.24.consts), custom_call_target="tpu_custom_call" | custom-call | tf_op jit(solution)/shard_map/lat/pallas_call | solution.py:702
  22.0 0.6 %turn.4.q = f32[36,8,8,128]{3,2,1,0:T(8,128)S(1)} custom-call(f32[36,8,8,128]{3,2,1,0:T(8,128)S(1)} %lat.4.q, f32[8,8,128]{2,1,0:T(8,128)S(1)} %get-tuple-element.36.tx, f32[8,8,128]{2,1,0:T(8,128)S(1)} %get-tuple-element.37.ty), custom_call_target="tpu_custom_call" | custom-call | tf_op jit(solution)/shard_map/turn/pallas_call | solution.py:703
  22.6 0.7 %lon.4.q = f32[36,8,8,128]{3,2,1,0:T(8,128)S(1)} custom-call(f32[36,8,8,128]{3,2,1,0:T(8,128)S(1)} %turn.4.q, f32[10,2,4,8,8,128]{5,4,3,2,1,0:T(8,128)S(1)} %get-tuple-element.38.taps, bf16[2,256,256]{2,1,0:T(8,128)(2,1)S(1)} %get-tuple-element.33.shifts), custom_call_target="tpu_custom_call" | custom-call | tf_op jit(solution)/shard_map/lon/pallas_call | solution.py:698
  23.3 0.5 %lat.5.q = f32[36,8,8,128]{3,2,1,0:T(8,128)S(1)} custom-call(f32[36,8,8,128]{3,2,1,0:T(8,128)S(1)} %lon.4.q, f32[8,8,128]{2,1,0:T(8,128)S(1)} %get-tuple-element.35.ky, f32[20,8,128]{2,1,0:T(8,128)S(1)} %get-tuple-element.24.consts), custom_call_target="tpu_custom_call" | custom-call | tf_op jit(solution)/shard_map/lat/pallas_call | solution.py:702
  23.8 0.6 %turn.5.q = f32[36,8,8,128]{3,2,1,0:T(8,128)S(1)} custom-call(f32[36,8,8,128]{3,2,1,0:T(8,128)S(1)} %lat.5.q, f32[8,8,128]{2,1,0:T(8,128)S(1)} %get-tuple-element.36.tx, f32[8,8,128]{2,1,0:T(8,128)S(1)} %get-tuple-element.37.ty), custom_call_target="tpu_custom_call" | custom-call | tf_op jit(solution)/shard_map/turn/pallas_call | solution.py:703
  24.4 0.7 %lon.5.q = f32[36,8,8,128]{3,2,1,0:T(8,128)S(1)} custom-call(f32[36,8,8,128]{3,2,1,0:T(8,128)S(1)} %turn.5.q, f32[10,2,4,8,8,128]{5,4,3,2,1,0:T(8,128)S(1)} %get-tuple-element.38.taps, bf16[2,256,256]{2,1,0:T(8,128)(2,1)S(1)} %get-tuple-element.33.shifts), custom_call_target="tpu_custom_call" | custom-call | tf_op jit(solution)/shard_map/lon/pallas_call | solution.py:698
  25.1 0.7 %lat_sums.1 = (f32[36,8,8,128]{3,2,1,0:T(8,128)S(1)}, f32[8,128]{1,0:T(8,128)S(1)}) custom-call(f32[36,8,8,128]{3,2,1,0:T(8,128)S(1)} %lon.5.q, f32[8,8,128]{2,1,0:T(8,128)S(1)} %get-tuple-element.35.ky, f32[20,8,128]{2,1,0:T(8,128)S(1)} %get-tuple-element.24.consts), custom_call_target="tpu_custom_call" | custom-call | tf_op jit(solution)/shard_map/lat_sums/pallas_call | solution.py:700
  25.8 1.5 %collective-permute-start.6 = (f32[8,128]{1,0:T(8,128)S(1)}, f32[8,128]{1,0:T(8,128)S(1)}, u32[]{:S(2)}, u32[]{:S(2)}) collective-permute-start(f32[8,128]{1,0:T(8,128)S(1)} %get-tuple-element.42.sums), channel_id=1, source_target_pairs={{0,1},{1,0},{2,3},{3,2},{4,5},{5,4},{6,7},{7,6},{8,9},{9,8},{10,11... | collective-permute-start | bytes 12296 | tf_op jit(solution)/shard_map/ppermute | solution.py:621
  27.4 0.1 growth.1.gain
  27.5 0.5 %gather.1.own = f32[2,36,8,128]{3,2,1,0:T(8,128)S(1)} custom-call(f32[36,8,8,128]{3,2,1,0:T(8,128)S(1)} %get-tuple-element.39.q, bf16[2048,256]{1,0:T(8,128)(2,1)S(1)} %get-tuple-element.40.matrix), custom_call_target="tpu_custom_call" | custom-call | tf_op jit(solution)/shard_map/gather/pallas_call | solution.py:705
  28.0 0.2 last_turn.1.early
  28.2 1.2 %collective-permute-done.6.other = f32[8,128]{1,0:T(8,128)S(1)} collective-permute-done((f32[8,128]{1,0:T(8,128)S(1)}, f32[8,128]{1,0:T(8,128)S(1)}, u32[]{:S(2)}, u32[]{:S(2)}) %collective-permute-start.6) | collective-permute-done | bytes 4128 | tf_op jit(solution)/shard_map/ppermute | solution.py:621
  29.4 1.0 %finish.1 = f32[16,16,288]{2,1,0:T(8,128)} custom-call(f32[2,36,8,128]{3,2,1,0:T(8,128)S(1)} %last_turn.1.early, f32[2,8,128]{2,1,0:T(8,128)S(1)} %get-tuple-element.41.local, f32[8,128]{1,0:T(8,128)S(1)} %get-tuple-element.42.sums, f32[8,128]{1,0:T(8,128)S(1)} %collective-permute-done.6.other, f32[20,8,128]{2,1,0:T(8,128)S(1)} %get-tuple-element.24.consts), custom_call_target="tpu_custom_call" | custom-call | tf_op jit(solution)/shard_map/finish/pallas_call | solution.py:710
  (10 shorter events, 0.5 us)
Async XLA Ops:
  1.4 7.5 %collective-permute-start = (f32[31,8,128]{2,1,0:T(8,128)S(1)}, f32[31,8,128]{2,1,0:T(8,128)S(1)}, u32[]{:S(2)}, u32[]{:S(2)}) collective-permute-start(f32[31,8,128]{2,1,0:T(8,128)S(1)} %column_near.1), channel_id=1, source_target_pairs={{0,8},{8,0},{16,24},{24,16},{1,9},{9,1},{17,25},{25,17},{2,10},{10... | collective-permute-start | bytes 380936 | tf_op jit(solution)/shard_map/ppermute | solution.py:621
  3.2 8.3 %collective-permute-start.1 = (f32[31,8,128]{2,1,0:T(8,128)S(1)}, f32[31,8,128]{2,1,0:T(8,128)S(1)}, u32[]{:S(2)}, u32[]{:S(2)}) collective-permute-start(f32[31,8,128]{2,1,0:T(8,128)S(1)} %column_far.1), channel_id=1, source_target_pairs={{8,16},{16,8},{24,0},{0,24},{9,17},{17,9},{25,1},{1,25},{10,18},{1... | collective-permute-start | bytes 380936 | tf_op jit(solution)/shard_map/ppermute | solution.py:621
  5.8 7.8 %collective-permute-start.2 = (f32[31,8,128]{2,1,0:T(8,128)S(1)}, f32[31,8,128]{2,1,0:T(8,128)S(1)}, u32[]{:S(2)}, u32[]{:S(2)}) collective-permute-start(f32[31,8,128]{2,1,0:T(8,128)S(1)} %edge_far.1), channel_id=1, source_target_pairs={{2,4},{4,2},{3,5},{5,3},{10,12},{12,10},{11,13},{13,11},{18,20},{2... | collective-permute-start | bytes 380936 | tf_op jit(solution)/shard_map/ppermute | solution.py:621
  7.8 5.8 %collective-permute-start.3 = (f32[31,8,128]{2,1,0:T(8,128)S(1)}, f32[31,8,128]{2,1,0:T(8,128)S(1)}, u32[]{:S(2)}, u32[]{:S(2)}) collective-permute-start(f32[31,8,128]{2,1,0:T(8,128)S(1)} %edge_near.1), channel_id=1, source_target_pairs={{0,2},{2,0},{4,6},{6,4},{1,3},{3,1},{5,7},{7,5},{8,10},{10,8},{12,... | collective-permute-start | bytes 380936 | tf_op jit(solution)/shard_map/ppermute | solution.py:621
  11.7 6.3 %collective-permute-start.4 = (f32[32,8,128]{2,1,0:T(8,128)S(1)}, f32[32,8,128]{2,1,0:T(8,128)S(1)}, u32[]{:S(2)}, u32[]{:S(2)}) collective-permute-start(f32[32,8,128]{2,1,0:T(8,128)S(1)} %rim_far.1.refs_2_), channel_id=1, source_target_pairs={{2,4},{4,2},{3,5},{5,3},{10,12},{12,10},{11,13},{13,11},{18,20},{2... | collective-permute-start | bytes 393224 | tf_op jit(solution)/shard_map/ppermute | solution.py:621
  13.7 1.4 %collective-permute-start.5 = (f32[31,8,128]{2,1,0:T(8,128)S(1)}, f32[31,8,128]{2,1,0:T(8,128)S(1)}, u32[]{:S(2)}, u32[]{:S(2)}) collective-permute-start(f32[31,8,128]{2,1,0:T(8,128)S(1)} %rim_near.1), channel_id=1, source_target_pairs={{0,2},{2,0},{4,6},{6,4},{1,3},{3,1},{5,7},{7,5},{8,10},{10,8},{12,... | collective-permute-start | bytes 380936 | tf_op jit(solution)/shard_map/ppermute | solution.py:621
  25.8 3.6 %collective-permute-start.6 = (f32[8,128]{1,0:T(8,128)S(1)}, f32[8,128]{1,0:T(8,128)S(1)}, u32[]{:S(2)}, u32[]{:S(2)}) collective-permute-start(f32[8,128]{1,0:T(8,128)S(1)} %get-tuple-element.42.sums), channel_id=1, source_target_pairs={{0,1},{1,0},{2,3},{3,2},{4,5},{5,4},{6,7},{7,6},{8,9},{9,8},{10,11... | collective-permute-start | bytes 12296 | tf_op jit(solution)/shard_map/ppermute | solution.py:621
